TPU v7x, 32 devices: a whole 2x2x4 slice. The times are simulated.
32 devices in a mesh: grp: 2 (over x), band: 16 (over z, y, core).
Axes of the slice: x: 2, y: 2, z: 4, core: 2. Of those that a mesh axis runs over, the one named last changes fastest.
Arguments:
- samples: float32 [2, 192, 8192], P(None, None, ('grp', 'band')), parts along dimension 2, may hold values from -6 to 6
- prototype: float32 [16, 128], replicated, may hold values from -1.5 to 1.5
- dish_filter: float32 [2, 8, 192, 128], replicated, may hold values from -1.5 to 1.5
- beam_weights: float32 [16, 8, 2, 192, 192], P('band'), may hold values from -0.3125 to 0.3125
- dish_order: int32 [192], replicated, may hold values from 0 to 191, each once
Outputs:
- power: float32 [32, 8, 192, 8], P(('grp', 'band')), parts along dimension 0
There are 2 independent parts, one for each index of `grp`. A program takes and returns all parts, laid end to end along the dimension named above; an argument that names none is the same for every part. Nothing has to cross between parts.
Inputs may be any that keep to these rules, and one draw needn't show every extreme that they name: `dish_order`: each of the 192 dishes stands in exactly one panel slot.
All inputs are finite; a program needn't handle non-finite values.
Results may differ from a plain program's by a relative error of at most 0.0003.
Values sent between devices are 32-bit elements; how exact they have to be, the bound alone decides.
No kernel may reach another device: no remote copies, remote signals or barrier semaphores. Data moves between devices by JAX's collectives and lax.ppermute only.
A program may use at most 64 MiB of HBM per device.

v0:
```python
import math

import jax
import jax.numpy as jnp
from jax import lax
from jax.sharding import PartitionSpec as P

INTEG = 4


def shifted(value, axis, steps):
    count = lax.axis_size(axis)
    leading, last = (max(0, -steps), min(count, count - steps))
    return lax.ppermute(value, axis, [(source, source + steps) for source in range(leading, last)])


def swapped(value, axis, bit):
    mask = 2**bit
    pairs = [(source, source ^ mask) for source in range(lax.axis_size(axis))]
    return lax.ppermute(value, axis, pairs)


def fourier_tables(length):
    counter = jnp.arange(length, dtype=jnp.int32)
    product = counter[:, None] * counter[None, :] % length
    angles = product.astype(jnp.float32) * (2.0 * math.pi / length)
    factor = 1.0 / math.sqrt(length)
    return (jnp.cos(angles) * factor, jnp.sin(angles) * factor)


def filter_frames(real_in, imag_in, tap_real, tap_imag, frame_count):
    tap_count = tap_real.shape[0]
    out_real = jnp.zeros(real_in.shape[:-1] + (frame_count,), real_in.dtype)
    out_imag = jnp.zeros(real_in.shape[:-1] + (frame_count,), real_in.dtype)
    for tap_index in range(tap_count):
        offset = tap_count - 1 - tap_index
        part_real = real_in[..., offset : offset + frame_count]
        part_imag = imag_in[..., offset : offset + frame_count]
        factor_real = tap_real[tap_index][..., None]
        factor_imag = tap_imag[tap_index][..., None]
        out_real = out_real + factor_real * part_real - factor_imag * part_imag
        out_imag = out_imag + factor_real * part_imag + factor_imag * part_real
    return (out_real, out_imag)


def detect(weights, field_real, field_imag):
    highest = lax.Precision.HIGHEST

    def contract(weight_part, field_part):
        return jnp.einsum("qds,dqf->qsf", weight_part, field_part, precision=highest)

    beam_real = contract(weights[:, 0], field_real) - contract(weights[:, 1], field_imag)
    beam_imag = contract(weights[:, 0], field_imag) + contract(weights[:, 1], field_real)
    energy = beam_real * beam_real + beam_imag * beam_imag
    shaped = energy.reshape(energy.shape[:-1] + (energy.shape[-1] // INTEG, INTEG))
    return jnp.mean(shaped, axis=-1)


def history(blocks, needed, frames_dev):
    pieces = [blocks]
    rounds = -(-needed // frames_dev)
    for step_count in range(1, rounds + 1):
        keeping = min(frames_dev, needed - (step_count - 1) * frames_dev)
        tail_part = blocks[:, :, frames_dev - keeping :, :]
        arrived_tail = shifted(tail_part, "band", step_count)
        pieces = [arrived_tail] + pieces
    return jnp.concatenate(pieces, axis=2)


def body(samples, prototype, dish_filter, beam_weights, dish_order):
    highest = lax.Precision.HIGHEST
    devices = lax.axis_size("band")
    position = lax.axis_index("band")
    pfb_count = prototype.shape[0]
    channels = prototype.shape[1]
    fir_count = dish_filter.shape[1]
    dishes = dish_filter.shape[2]
    band_chans = beam_weights.shape[1]
    bands = channels // band_chans
    owners = devices // bands
    panel_size = dishes // owners
    frames_dev = samples.shape[2] // channels
    band_id = position // owners
    owner_id = position % owners
    zero_index = jnp.zeros((), jnp.int32)
    ordered = jnp.take(samples, dish_order, axis=1)
    taps_ordered = jnp.take(dish_filter, dish_order, axis=2)
    blocks = ordered.reshape(2, dishes, frames_dev, channels)
    extended = history(blocks, pfb_count - 1, frames_dev)
    polyphase = jnp.zeros((2, dishes, frames_dev, channels), jnp.float32)
    for tap_index in range(pfb_count):
        offset = pfb_count - 1 - tap_index
        polyphase = (
            polyphase + prototype[tap_index] * extended[:, :, offset : offset + frames_dev, :]
        )
    cosine_table, sine_table = fourier_tables(channels)
    spec_real = jnp.dot(polyphase[0], cosine_table, precision=highest) + jnp.dot(
        polyphase[1], sine_table, precision=highest
    )
    spec_imag = jnp.dot(polyphase[1], cosine_table, precision=highest) - jnp.dot(
        polyphase[0], sine_table, precision=highest
    )
    spec_real = jnp.transpose(spec_real, (0, 2, 1))
    spec_imag = jnp.transpose(spec_imag, (0, 2, 1))
    stacked = jnp.stack([spec_real, spec_imag])
    pieces = stacked.reshape(2, owners, panel_size, bands, band_chans, frames_dev)
    pieces = jnp.transpose(pieces, (3, 1, 0, 2, 4, 5))
    pieces = pieces.reshape(devices, 2, panel_size, band_chans, frames_dev)
    arrived = lax.all_to_all(pieces, "band", split_axis=0, concat_axis=4, tiled=True)[0]
    total_frames = arrived.shape[3]
    dish_count = arrived.shape[1]
    if dish_count == dishes:
        dish_start = zero_index
    else:
        dish_start = owner_id * panel_size
    local_taps = lax.dynamic_slice(
        taps_ordered,
        (zero_index, zero_index, dish_start, band_id * band_chans),
        (2, fir_count, dish_count, band_chans),
    )
    padded = jnp.pad(arrived, ((0, 0), (0, 0), (0, 0), (fir_count - 1, 0)))
    filtered_real, filtered_imag = filter_frames(
        padded[0], padded[1], local_taps[0], local_taps[1], total_frames
    )
    arrived = jnp.stack([filtered_real, filtered_imag])
    collected = arrived[:, None]
    for bit_pos in range(owners.bit_length() - 1):
        partner = swapped(collected, "band", bit_pos)
        upper_half = owner_id // (1 << bit_pos) % 2 == 1
        collected = jnp.where(
            upper_half,
            jnp.concatenate([partner, collected], axis=1),
            jnp.concatenate([collected, partner], axis=1),
        )
    gathered = collected.reshape(2, dishes, band_chans, total_frames)
    power = detect(beam_weights[0], gathered[0], gathered[1])
    return power[None]


def solution(mesh):
    placed = (P(None, None, ("grp", "band")), P(), P(), P("band", None, None, None, None), P())
    return jax.shard_map(
        body,
        mesh=mesh,
        in_specs=placed,
        out_specs=P(("grp", "band"), None, None, None),
        check_vma=False,
    )
```

profile of v0, /device:TPU:0, one launch (start us, length us, event | category | flops | bytes accessed | tf_op | source)
XLA Modules:
  0.0 127.6 jit_solution(12866249529802294853)
XLA Ops:
  0.0 0.0 copy-start
  0.0 0.8 compare_and_fusion
  0.8 0.7 compare_select_fusion
  1.5 2.4 %gather_fusion.1 = f32[192,2,256]{2,0,1:T(8,128)S(1)} fusion(f32[2,192,256]{2,1,0:T(8,128)} %param.5, s32[1024]{0:T(1024)S(1)} %pad_clamp_fusion), kind=kCustom, calls=%fused_computation.1 | custom fusion | bytes 787200 | tf_op jit(solution)/shard_map/jit(_take)/gather | solution.py:86
  3.9 0.1 bitcast_select_fusion
  4.0 5.3 %collective-permute-start.6 = (f32[2,192,2,128]{3,1,2,0:T(8,128)S(1)}, f32[2,192,2,128]{3,1,2,0:T(8,128)S(1)}, u32[]{:S(2)}, u32[]{:S(2)}) collective-permute-start(f32[2,192,2,128]{3,1,2,0:T(8,128)S(1)} %bitcast_select_fusion), channel_id=1, source_target_pairs={{0,7},{1,8},{2,9},{3,10},{4,11},{5,12},{6,13},{7,14},{8,15},{16,23... | collective-permute-start | bytes 1179656 | tf_op jit(solution)/shard_map/ppermute | solution.py:14
  9.4 4.5 %collective-permute-start.5 = (f32[2,192,2,128]{3,1,2,0:T(8,128)S(1)}, f32[2,192,2,128]{3,1,2,0:T(8,128)S(1)}, u32[]{:S(2)}, u32[]{:S(2)}) collective-permute-start(f32[2,192,2,128]{3,1,2,0:T(8,128)S(1)} %bitcast_select_fusion), channel_id=1, source_target_pairs={{0,6},{1,7},{2,8},{3,9},{4,10},{5,11},{6,12},{7,13},{8,14},{9,15},... | collective-permute-start | bytes 1179656 | tf_op jit(solution)/shard_map/ppermute | solution.py:14
  13.9 1.9 %collective-permute-start.7 = (f32[2,192,1,128]{3,1,2,0:T(8,128)S(1)}, f32[2,192,1,128]{3,1,2,0:T(8,128)S(1)}, u32[]{:S(2)}, u32[]{:S(2)}) collective-permute-start(f32[2,192,1,128]{3,1,2,0:T(8,128)S(1)} %slice.303), channel_id=1, source_target_pairs={{0,8},{1,9},{2,10},{3,11},{4,12},{5,13},{6,14},{7,15},{16,24},{17,... | collective-permute-start | bytes 589832 | tf_op jit(solution)/shard_map/ppermute | solution.py:14
  15.8 1.3 %collective-permute-start.4 = (f32[2,192,2,128]{3,1,2,0:T(8,128)S(1)}, f32[2,192,2,128]{3,1,2,0:T(8,128)S(1)}, u32[]{:S(2)}, u32[]{:S(2)}) collective-permute-start(f32[2,192,2,128]{3,1,2,0:T(8,128)S(1)} %bitcast_select_fusion), channel_id=1, source_target_pairs={{0,5},{1,6},{2,7},{3,8},{4,9},{5,10},{6,11},{7,12},{8,13},{9,14},{... | collective-permute-start | bytes 1179656 | tf_op jit(solution)/shard_map/ppermute | solution.py:14
  17.2 1.6 %collective-permute-start.3 = (f32[2,192,2,128]{3,1,2,0:T(8,128)S(1)}, f32[2,192,2,128]{3,1,2,0:T(8,128)S(1)}, u32[]{:S(2)}, u32[]{:S(2)}) collective-permute-start(f32[2,192,2,128]{3,1,2,0:T(8,128)S(1)} %bitcast_select_fusion), channel_id=1, source_target_pairs={{0,4},{1,5},{2,6},{3,7},{4,8},{5,9},{6,10},{7,11},{8,12},{9,13},{1... | collective-permute-start | bytes 1179656 | tf_op jit(solution)/shard_map/ppermute | solution.py:14
  18.8 12.8 %collective-permute-done.7 = f32[2,192,1,128]{3,1,2,0:T(8,128)S(1)} collective-permute-done((f32[2,192,1,128]{3,1,2,0:T(8,128)S(1)}, f32[2,192,1,128]{3,1,2,0:T(8,128)S(1)}, u32[]{:S(2)}, u32[]{:S(2)}) %collective-permute-start.7) | collective-permute-done | bytes 196640 | tf_op jit(solution)/shard_map/ppermute | solution.py:14
  31.5 3.2 %collective-permute-start.2 = (f32[2,192,2,128]{3,1,2,0:T(8,128)S(1)}, f32[2,192,2,128]{3,1,2,0:T(8,128)S(1)}, u32[]{:S(2)}, u32[]{:S(2)}) collective-permute-start(f32[2,192,2,128]{3,1,2,0:T(8,128)S(1)} %bitcast_select_fusion), channel_id=1, source_target_pairs={{0,3},{1,4},{2,5},{3,6},{4,7},{5,8},{6,9},{7,10},{8,11},{9,12},{10... | collective-permute-start | bytes 1179656 | tf_op jit(solution)/shard_map/ppermute | solution.py:14
  34.8 0.0 collective-permute-done.6
  34.8 11.8 %collective-permute-start.1 = (f32[2,192,2,128]{3,1,2,0:T(8,128)S(1)}, f32[2,192,2,128]{3,1,2,0:T(8,128)S(1)}, u32[]{:S(2)}, u32[]{:S(2)}) collective-permute-start(f32[2,192,2,128]{3,1,2,0:T(8,128)S(1)} %bitcast_select_fusion), channel_id=1, source_target_pairs={{0,2},{1,3},{2,4},{3,5},{4,6},{5,7},{6,8},{7,9},{8,10},{9,11},{10,... | collective-permute-start | bytes 1179656 | tf_op jit(solution)/shard_map/ppermute | solution.py:14
  46.6 0.0 collective-permute-done.5
  46.6 18.8 %collective-permute-start = (f32[2,192,2,128]{3,1,2,0:T(8,128)S(1)}, f32[2,192,2,128]{3,1,2,0:T(8,128)S(1)}, u32[]{:S(2)}, u32[]{:S(2)}) collective-permute-start(f32[2,192,2,128]{3,1,2,0:T(8,128)S(1)} %bitcast_select_fusion), channel_id=1, source_target_pairs={{0,1},{1,2},{2,3},{3,4},{4,5},{5,6},{6,7},{7,8},{8,9},{9,10},{10,1... | collective-permute-start | bytes 1179656 | tf_op jit(solution)/shard_map/ppermute | solution.py:14
  65.4 0.0 copy-done.2
  65.5 0.0 collective-permute-done.4
  65.5 0.0 collective-permute-done.3
  65.5 0.0 collective-permute-done.2
  65.5 0.0 collective-permute-done.1
  65.5 1.2 collective-permute-done
  66.7 0.4 fusion.14
  67.2 0.6 fusion.43
  67.8 0.6 fusion.42
  68.3 0.6 fusion.11
  68.9 0.1 copy.72
  69.0 0.6 fusion.12
  69.6 0.1 copy.71
  69.8 0.8 copy.73
  70.6 33.8 %all-to-all-start = ((f32[16,2,192,8,2]{2,3,4,1,0:T(8,128)}), f32[16,2,192,8,2]{2,3,4,1,0:T(8,128)}, u32[]{:S(2)}, u32[]{:S(2)}) async-start(f32[16,2,192,8,2]{2,3,4,1,0:T(8,128)} %copy.73), calls=%async_computation | async-start | bytes 1048576 | tf_op jit(solution)/shard_map/all_to_all | solution.py:109
  104.4 0.0 copy-done
  104.4 4.4 %gather_fusion = f32[192,2,8,128]{3,0,2,1:T(8,128)S(1)} fusion(f32[2,8,192,128]{3,2,1,0:T(8,128)S(1)} %copy-done, s32[1024]{0:T(1024)S(1)} %pad_clamp_fusion), kind=kCustom, calls=%fused_computation | custom fusion | bytes 3146496 | tf_op jit(solution)/shard_map/jit(_take)/gather | solution.py:87
  108.8 0.5 fusion
  109.4 0.1 slice_bitcast_fusion.39
  109.5 0.1 copy.69
  109.5 0.1 copy.89
  109.6 0.1 copy.88
  109.7 0.1 copy.87
  109.7 0.1 copy.86
  109.8 0.1 copy.85
  109.9 0.1 copy.84
  109.9 0.1 copy.83
  110.0 0.1 copy.82
  110.1 0.1 copy.81
  110.2 0.1 copy.80
  110.2 0.1 copy.79
  110.3 0.1 copy.78
  110.4 0.1 copy.77
  110.4 0.1 copy.76
  110.5 0.1 copy.75
  110.6 3.8 %copy.106 = f32[1,8,2,192,192]{4,3,1,2,0:T(8,128)} copy(f32[1,8,2,192,192]{4,3,2,1,0:T(8,128)} %param.8) | data formatting | bytes 4718592 | tf_op args[3]
  114.4 4.5 %all-to-all-done = f32[16,2,192,8,2]{2,3,4,1,0:T(8,128)} async-done(((f32[16,2,192,8,2]{2,3,4,1,0:T(8,128)}), f32[16,2,192,8,2]{2,3,4,1,0:T(8,128)}, u32[]{:S(2)}, u32[]{:S(2)}) %all-to-all-start) | async-done | bytes 393248 | tf_op jit(solution)/shard_map/all_to_all | solution.py:109
  118.9 1.1 copy.74
  120.1 0.3 multiply_add_fusion
  120.4 0.3 multiply_subtract_fusion
  120.6 1.6 %copy-done.1 = f32[1,8,2,192,192]{4,3,1,2,0:T(8,128)S(1)} copy-done((f32[1,8,2,192,192]{4,3,1,2,0:T(8,128)S(1)}, f32[1,8,2,192,192]{4,3,1,2,0:T(8,128)}, u32[]{:S(2)}) %copy-start.1) | copy-done | bytes 2359320
  122.2 1.1 fusion.1
  123.4 1.1 fusion.2
  124.5 1.1 fusion.6
  125.6 1.1 fusion.10
  126.7 0.1 reshape.93
  126.8 0.2 reduce_sum.9
  127.0 0.6 multiply_bitcast_fusion
  (7 shorter events, 0.1 us)
Async XLA Ops:
  0.0 104.4 %copy-start = (f32[2,8,192,128]{3,2,1,0:T(8,128)S(1)}, f32[2,8,192,128]{3,2,1,0:T(8,128)}, u32[]{:S(2)}) copy-start(f32[2,8,192,128]{3,2,1,0:T(8,128)} %param.7) | copy-start | bytes 4718596
  1.5 63.9 %copy-start.2 = (f32[16,128]{1,0:T(8,128)S(1)}, f32[16,128]{1,0:T(8,128)}, u32[]{:S(2)}) copy-start(f32[16,128]{1,0:T(8,128)} %param.6) | copy-start | bytes 24580
  4.0 30.7 %collective-permute-start.6 = (f32[2,192,2,128]{3,1,2,0:T(8,128)S(1)}, f32[2,192,2,128]{3,1,2,0:T(8,128)S(1)}, u32[]{:S(2)}, u32[]{:S(2)}) collective-permute-start(f32[2,192,2,128]{3,1,2,0:T(8,128)S(1)} %bitcast_select_fusion), channel_id=1, source_target_pairs={{0,7},{1,8},{2,9},{3,10},{4,11},{5,12},{6,13},{7,14},{8,15},{16,23... | collective-permute-start | bytes 1179656 | tf_op jit(solution)/shard_map/ppermute | solution.py:14
  9.4 37.2 %collective-permute-start.5 = (f32[2,192,2,128]{3,1,2,0:T(8,128)S(1)}, f32[2,192,2,128]{3,1,2,0:T(8,128)S(1)}, u32[]{:S(2)}, u32[]{:S(2)}) collective-permute-start(f32[2,192,2,128]{3,1,2,0:T(8,128)S(1)} %bitcast_select_fusion), channel_id=1, source_target_pairs={{0,6},{1,7},{2,8},{3,9},{4,10},{5,11},{6,12},{7,13},{8,14},{9,15},... | collective-permute-start | bytes 1179656 | tf_op jit(solution)/shard_map/ppermute | solution.py:14
  13.9 17.6 %collective-permute-start.7 = (f32[2,192,1,128]{3,1,2,0:T(8,128)S(1)}, f32[2,192,1,128]{3,1,2,0:T(8,128)S(1)}, u32[]{:S(2)}, u32[]{:S(2)}) collective-permute-start(f32[2,192,1,128]{3,1,2,0:T(8,128)S(1)} %slice.303), channel_id=1, source_target_pairs={{0,8},{1,9},{2,10},{3,11},{4,12},{5,13},{6,14},{7,15},{16,24},{17,... | collective-permute-start | bytes 589832 | tf_op jit(solution)/shard_map/ppermute | solution.py:14
  15.8 49.6 %collective-permute-start.4 = (f32[2,192,2,128]{3,1,2,0:T(8,128)S(1)}, f32[2,192,2,128]{3,1,2,0:T(8,128)S(1)}, u32[]{:S(2)}, u32[]{:S(2)}) collective-permute-start(f32[2,192,2,128]{3,1,2,0:T(8,128)S(1)} %bitcast_select_fusion), channel_id=1, source_target_pairs={{0,5},{1,6},{2,7},{3,8},{4,9},{5,10},{6,11},{7,12},{8,13},{9,14},{... | collective-permute-start | bytes 1179656 | tf_op jit(solution)/shard_map/ppermute | solution.py:14
  17.2 48.3 %collective-permute-start.3 = (f32[2,192,2,128]{3,1,2,0:T(8,128)S(1)}, f32[2,192,2,128]{3,1,2,0:T(8,128)S(1)}, u32[]{:S(2)}, u32[]{:S(2)}) collective-permute-start(f32[2,192,2,128]{3,1,2,0:T(8,128)S(1)} %bitcast_select_fusion), channel_id=1, source_target_pairs={{0,4},{1,5},{2,6},{3,7},{4,8},{5,9},{6,10},{7,11},{8,12},{9,13},{1... | collective-permute-start | bytes 1179656 | tf_op jit(solution)/shard_map/ppermute | solution.py:14
  31.5 34.0 %collective-permute-start.2 = (f32[2,192,2,128]{3,1,2,0:T(8,128)S(1)}, f32[2,192,2,128]{3,1,2,0:T(8,128)S(1)}, u32[]{:S(2)}, u32[]{:S(2)}) collective-permute-start(f32[2,192,2,128]{3,1,2,0:T(8,128)S(1)} %bitcast_select_fusion), channel_id=1, source_target_pairs={{0,3},{1,4},{2,5},{3,6},{4,7},{5,8},{6,9},{7,10},{8,11},{9,12},{10... | collective-permute-start | bytes 1179656 | tf_op jit(solution)/shard_map/ppermute | solution.py:14
  34.8 30.7 %collective-permute-start.1 = (f32[2,192,2,128]{3,1,2,0:T(8,128)S(1)}, f32[2,192,2,128]{3,1,2,0:T(8,128)S(1)}, u32[]{:S(2)}, u32[]{:S(2)}) collective-permute-start(f32[2,192,2,128]{3,1,2,0:T(8,128)S(1)} %bitcast_select_fusion), channel_id=1, source_target_pairs={{0,2},{1,3},{2,4},{3,5},{4,6},{5,7},{6,8},{7,9},{8,10},{9,11},{10,... | collective-permute-start | bytes 1179656 | tf_op jit(solution)/shard_map/ppermute | solution.py:14
  46.6 20.1 %collective-permute-start = (f32[2,192,2,128]{3,1,2,0:T(8,128)S(1)}, f32[2,192,2,128]{3,1,2,0:T(8,128)S(1)}, u32[]{:S(2)}, u32[]{:S(2)}) collective-permute-start(f32[2,192,2,128]{3,1,2,0:T(8,128)S(1)} %bitcast_select_fusion), channel_id=1, source_target_pairs={{0,1},{1,2},{2,3},{3,4},{4,5},{5,6},{6,7},{7,8},{8,9},{9,10},{10,1... | collective-permute-start | bytes 1179656 | tf_op jit(solution)/shard_map/ppermute | solution.py:14
  70.6 48.3 %all-to-all-start = ((f32[16,2,192,8,2]{2,3,4,1,0:T(8,128)}), f32[16,2,192,8,2]{2,3,4,1,0:T(8,128)}, u32[]{:S(2)}, u32[]{:S(2)}) async-start(f32[16,2,192,8,2]{2,3,4,1,0:T(8,128)} %copy.73), calls=%async_computation | async-start | bytes 1048576 | tf_op jit(solution)/shard_map/all_to_all | solution.py:109
  120.4 1.9 %copy-start.1 = (f32[1,8,2,192,192]{4,3,1,2,0:T(8,128)S(1)}, f32[1,8,2,192,192]{4,3,1,2,0:T(8,128)}, u32[]{:S(2)}) copy-start(f32[1,8,2,192,192]{4,3,1,2,0:T(8,128)} %copy.106) | copy-start | bytes 7077892
where the time goes:
time: 128 us
  starting transfers between devices  82.3 us (64%)
  waiting for transfers between devices  18.5 us (14%)
  local copies, waits for them, and re-layouts  15.8 us (12%)
  matrix products  6.71 us (5%)
  other arithmetic  3.93 us (3%)
    ppermute x8, starting transfers between devices, shifted(): lax.ppermute(value, axis, [(source, source + steps) for source in range(l...  48.5 us
    all_to_all x1, starting transfers between devices, body(): lax.all_to_all(pieces, 'band', split_axis=0, concat_axis=4, tiled=True)[0]  33.8 us
    ppermute x8, waiting for transfers between devices, shifted(): lax.ppermute(value, axis, [(source, source + steps) for source in range(l...  14 us
    unnamed x7, local copies, waits for them, and re-layouts  5.42 us
    all_to_all x1, waiting for transfers between devices, body(): lax.all_to_all(pieces, 'band', split_axis=0, concat_axis=4, tiled=True)[0]  4.54 us
    dot_general x4, matrix products, contract(): jnp.einsum('qds,dqf->qsf', weight_part, field_part, precision=highest)  4.45 us
    gather x1, local copies, waits for them, and re-layouts, body(): taps_ordered = jnp.take(dish_filter, dish_order, axis=2)  4.4 us
  transfers between devices with their start and end apart: 9, of which 3 were waited for; matrix products, arithmetic and copies ran while one was open for 8% of the time, Pallas kernels for 0%

commit v1 on v0

v1 whole, which is shorter than its diff:
```python
import math

import jax
import jax.numpy as jnp
from jax import lax
from jax.sharding import PartitionSpec as P

INTEG = 4
HIGHEST = lax.Precision.HIGHEST


def fourier_tables(length):
    counter = jnp.arange(length, dtype=jnp.int32)
    product = counter[:, None] * counter[None, :] % length
    angles = product.astype(jnp.float32) * (2.0 * math.pi / length)
    factor = 1.0 / math.sqrt(length)
    return (jnp.cos(angles) * factor, jnp.sin(angles) * factor)


def detect(weights, field_real, field_imag):
    def contract(weight_part, field_part):
        return jnp.einsum("qds,dqf->qsf", weight_part, field_part, precision=HIGHEST)

    beam_real = contract(weights[:, 0], field_real) - contract(weights[:, 1], field_imag)
    beam_imag = contract(weights[:, 0], field_imag) + contract(weights[:, 1], field_real)
    energy = beam_real * beam_real + beam_imag * beam_imag
    shaped = energy.reshape(energy.shape[:-1] + (energy.shape[-1] // INTEG, INTEG))
    return jnp.mean(shaped, axis=-1)


def body(samples, prototype, dish_filter, beam_weights, dish_order):
    devices = lax.axis_size("band")
    position = lax.axis_index("band")
    pfb_count, channels = prototype.shape
    fir_count = dish_filter.shape[1]
    dishes = dish_filter.shape[2]
    band_chans = beam_weights.shape[1]
    bands = channels // band_chans
    owners = devices // bands
    frames_dev = samples.shape[2] // channels
    frames = frames_dev * devices
    share = -(-dishes // devices)
    extra = share * devices - dishes

    padded = jnp.pad(samples, ((0, 0), (0, extra), (0, 0)))
    pieces = padded.reshape(2, devices, share, frames_dev, channels)
    pieces = jnp.transpose(pieces, (1, 3, 0, 2, 4)).reshape(
        devices, frames_dev, 2 * share, channels
    )
    arrived = lax.all_to_all(pieces, "band", split_axis=0, concat_axis=0, tiled=True)
    blocks = arrived.reshape(frames, 2 * share, channels)

    history = jnp.pad(blocks, ((pfb_count - 1, 0), (0, 0), (0, 0)))
    polyphase = jnp.zeros_like(blocks)
    for tap_index in range(pfb_count):
        offset = pfb_count - 1 - tap_index
        polyphase = polyphase + prototype[tap_index] * history[offset : offset + frames]
    cosine, sine = fourier_tables(channels)
    both = jnp.dot(polyphase, jnp.concatenate([cosine, sine], axis=1), precision=HIGHEST)
    with_cos = both[..., :channels].reshape(frames, 2, share, channels)
    with_sin = both[..., channels:].reshape(frames, 2, share, channels)
    spec_real = with_cos[:, 0] + with_sin[:, 1]
    spec_imag = with_cos[:, 1] - with_sin[:, 0]

    taps = jnp.pad(dish_filter, ((0, 0), (0, 0), (0, extra), (0, 0)))
    taps = lax.dynamic_slice_in_dim(taps, position * share, share, 2)
    lead = ((fir_count - 1, 0), (0, 0), (0, 0))
    past_real, past_imag = jnp.pad(spec_real, lead), jnp.pad(spec_imag, lead)
    out_real = jnp.zeros_like(spec_real)
    out_imag = jnp.zeros_like(spec_imag)
    for tap_index in range(fir_count):
        offset = fir_count - 1 - tap_index
        part_real = past_real[offset : offset + frames]
        part_imag = past_imag[offset : offset + frames]
        factor_real, factor_imag = taps[0, tap_index], taps[1, tap_index]
        out_real = out_real + factor_real * part_real - factor_imag * part_imag
        out_imag = out_imag + factor_real * part_imag + factor_imag * part_real

    filtered = jnp.stack([out_real, out_imag])
    filtered = filtered.reshape(2, frames, share, bands, band_chans)
    filtered = jnp.transpose(filtered, (3, 0, 2, 4, 1)).reshape(
        bands, 2 * share, band_chans * frames
    )
    filtered = jnp.repeat(filtered, owners, axis=0)
    field = lax.all_to_all(filtered, "band", split_axis=0, concat_axis=0, tiled=True)
    field = field.reshape(devices, 2, share, band_chans, frames)
    field = jnp.transpose(field, (1, 0, 2, 3, 4))
    field = field.reshape(2, devices * share, band_chans, frames)
    field = jnp.take(field, dish_order, axis=1)
    power = detect(beam_weights[0], field[0], field[1])
    return power[None]


def solution(mesh):
    placed = (P(None, None, ("grp", "band")), P(), P(), P("band", None, None, None, None), P())
    return jax.shard_map(
        body,
        mesh=mesh,
        in_specs=placed,
        out_specs=P(("grp", "band"), None, None, None),
        check_vma=False,
    )
```

time: 128 us -> 59 us (0.46)
  starting transfers between devices: 82.3 us -> 10.9 us
  waiting for transfers between devices: 18.5 us -> 20.8 us
  local copies, waits for them, and re-layouts: 15.8 us -> 17.9 us
  matrix products: 6.71 us -> 5.32 us
    ppermute x8 -> x0, starting transfers between devices: 48.5 us -> none  [shifted(): lax.ppermute(value, axis, [(source, source + steps) for source in range(l...]
    all_to_all x1 -> x2, starting transfers between devices: 33.8 us -> 10.9 us  [the longest x1 7.39 us: body(): lax.all_to_all(pieces, 'band', split_axis=0, concat_axis=0, tiled=True)]
    all_to_all x1 -> x2, waiting for transfers between devices: 4.54 us -> 20.8 us  [the longest x1 10.9 us: body(): lax.all_to_all(pieces, 'band', split_axis=0, concat_axis=0, tiled=True)]
    ppermute x8 -> x0, waiting for transfers between devices: 14 us -> none  [shifted(): lax.ppermute(value, axis, [(source, source + steps) for source in range(l...]
    reshape x1 -> x4, local copies, waits for them, and re-layouts: 0.85 us -> 6.25 us  [the longest x2 4.2 us: body(): field = field.reshape(devices, 2, share, band_chans, frames)]
    unnamed x7 -> x5, local copies, waits for them, and re-layouts: 5.42 us -> 2.22 us
    another operation x0 -> x2, local copies, waits for them, and re-layouts: none -> 1.42 us  [body(): filtered = jnp.repeat(filtered, owners, axis=0)]
    dot_general x8 -> x5, matrix products: 6.71 us -> 5.32 us  [the longest x4 4.26 us: contract(): jnp.einsum('qds,dqf->qsf', weight_part, field_part, precision=HIGHEST)]
  transfers between devices with their start and end apart: 9 -> 2, of which waited for: 3 -> 2; matrix products, arithmetic and copies ran while one was open for 8% -> 6% of each run, Pallas kernels for 0% -> 0%
where the time goes in v1:
time: 59 us; the launch traced here: 58.4 us
  waiting for transfers between devices  20.8 us (35%)
  local copies, waits for them, and re-layouts  17.9 us (30%)
  starting transfers between devices  10.9 us (18%)
  matrix products  5.32 us (9%)
  other arithmetic  3.19 us (5%)
    all_to_all x1, waiting for transfers between devices, body(): lax.all_to_all(pieces, 'band', split_axis=0, concat_axis=0, tiled=True)  10.9 us
    all_to_all x1, waiting for transfers between devices, body(): lax.all_to_all(filtered, 'band', split_axis=0, concat_axis=0, tiled=True)  9.89 us
    all_to_all x1, starting transfers between devices, body(): lax.all_to_all(pieces, 'band', split_axis=0, concat_axis=0, tiled=True)  7.39 us
    gather x2, local copies, waits for them, and re-layouts, body(): field = jnp.take(field, dish_order, axis=1)  6.19 us
    dot_general x4, matrix products, contract(): jnp.einsum('qds,dqf->qsf', weight_part, field_part, precision=HIGHEST)  4.26 us
    reshape x2, local copies, waits for them, and re-layouts, body(): field = field.reshape(devices, 2, share, band_chans, frames)  4.2 us
    all_to_all x1, starting transfers between devices, body(): lax.all_to_all(filtered, 'band', split_axis=0, concat_axis=0, tiled=True)  3.55 us
    unnamed x5, local copies, waits for them, and re-layouts  2.22 us
  transfers between devices with their start and end apart: 2, of which 2 were waited for; matrix products, arithmetic and copies ran while one was open for 6% of the time, Pallas kernels for 0%

profile of v1, /device:TPU:0, one launch (start us, length us, event | category | flops | bytes accessed | tf_op | source)
XLA Modules:
  0.0 58.4 jit_solution(5629699336342908056)
XLA Ops:
  0.0 1.2 %reshape.77 = f32[2,16,12,2,128]{4,3,2,1,0:T(2,128)S(1)} reshape(f32[2,192,256]{2,1,0:T(8,128)} %param.5) | data formatting | bytes 786432 | tf_op jit(solution)/shard_map/reshape | solution.py:46
  1.2 0.0 copy-start
  1.2 0.1 copy.27
  1.3 0.9 %copy.28 = f32[16,2,24,128]{3,2,1,0:T(8,128)} copy(f32[16,2,24,128]{3,0,2,1:T(8,128)S(1)} %bitcast.133) | data formatting | bytes 786432 | tf_op jit(solution)/shard_map/reshape | solution.py:47
  2.2 7.4 %all-to-all-start = ((f32[16,2,24,128]{3,2,1,0:T(8,128)}), f32[16,2,24,128]{3,2,1,0:T(8,128)S(1)}, u32[]{:S(2)}, u32[]{:S(2)}) async-start(f32[16,2,24,128]{3,2,1,0:T(8,128)} %copy.28), calls=%async_computation | async-start | bytes 786432 | tf_op jit(solution)/shard_map/all_to_all | solution.py:50
  9.6 0.3 sine_multiply_fusion
  9.8 0.9 %dynamic-slice_bitcast_fusion.15 = (f32[12,128]{1,0:T(8,128)S(1)}, f32[12,128]{1,0:T(8,128)S(1)}, f32[12,128]{1,0:T(8,128)S(1)}, f32[12,128]{1,0:T(8,128)S(1)}, ...) fusion(f32[2,8,192,128]{3,2,1,0:T(8,128)} %param.7, ...), kind=kLoop, calls=%fused_computation.131 | loop fusion | bytes 196640 | tf_op jit(solution)/shard_map/mul | solution.py:76
  10.8 0.0 copy-done
  10.8 10.9 %all-to-all-done = f32[16,2,24,128]{3,2,1,0:T(8,128)S(1)} async-done(((f32[16,2,24,128]{3,2,1,0:T(8,128)}), f32[16,2,24,128]{3,2,1,0:T(8,128)S(1)}, u32[]{:S(2)}, u32[]{:S(2)}) %all-to-all-start) | async-done | bytes 393248 | tf_op jit(solution)/shard_map/all_to_all | solution.py:50
  21.7 1.1 %fusion.26 = f32[32,24,256]{2,1,0:T(8,128)S(1)} fusion(f32[32,24,128]{2,1,0:T(8,128)S(1)} %bitcast.137, f32[128]{0:T(128)S(1)} %get-tuple-element.39, f32[128]{0:T(128)S(1)} %get-tuple-element.40, f32[128]{0:T(128)S(1)} %get-tuple-element.26, f32[128]{0:T(128)S(1)} %get-tuple-element.27, f32[128]{0:T(128)S(1)} %get-tuple-element.28, ...), kind=kOutput, calls=%fused_computation.47 | convolution fusion | flops 305070080 | bytes 1318912 | tf_op jit(solution)/shard_map/dot_general | solution.py:59
  22.8 0.1 fusion.85
  22.9 0.1 copy.29
  23.0 0.1 copy.30
  23.0 0.1 fusion.57
  23.1 0.4 multiply_add_fusion
  23.5 0.4 multiply_subtract_fusion
  23.9 0.3 copy.31
  24.2 0.3 copy.32
  24.5 0.2 maximum_bitcast_fusion
  24.6 0.4 reshape.95
  25.1 1.0 %copy.37 = f32[16,24,256]{2,1,0:T(8,128)} copy(f32[16,24,256]{2,0,1:T(8,128)S(1)} %reshape.95) | data formatting | bytes 786432 | tf_op jit(solution)/shard_map/reshape;broadcast_in_dim;reshape | solution.py:84
  26.1 3.6 %all-to-all-start.1 = ((f32[16,24,256]{2,1,0:T(8,128)}), f32[16,24,256]{2,1,0:T(8,128)S(1)}, u32[]{:S(2)}, u32[]{:S(2)}) async-start(f32[16,24,256]{2,1,0:T(8,128)} %copy.37), calls=%async_computation.1 | async-start | bytes 786432 | tf_op jit(solution)/shard_map/all_to_all | solution.py:85
  29.6 0.0 copy-start.1
  29.6 2.2 %copy.39 = f32[1,8,2,192,192]{4,3,1,2,0:T(8,128)S(1)} copy(f32[1,8,2,192,192]{4,3,2,1,0:T(8,128)} %param.8) | data formatting | bytes 4718592 | tf_op args[3]
  31.8 0.0 copy-done.1
  31.9 9.9 %all-to-all-done.1 = f32[16,24,256]{2,1,0:T(8,128)S(1)} async-done(((f32[16,24,256]{2,1,0:T(8,128)}), f32[16,24,256]{2,1,0:T(8,128)S(1)}, u32[]{:S(2)}, u32[]{:S(2)}) %all-to-all-start.1) | async-done | bytes 393248 | tf_op jit(solution)/shard_map/all_to_all | solution.py:85
  41.8 1.5 %reshape.82 = f32[16,2,12,8,32]{4,3,2,1,0:T(8,128)} reshape(f32[16,24,256]{2,1,0:T(8,128)S(1)} %all-to-all-done.1) | data formatting | bytes 786432 | tf_op jit(solution)/shard_map/reshape | solution.py:86
  43.3 2.7 %copy.34 = f32[16,2,12,8,32]{4,3,2,0,1:T(8,128)} copy(f32[16,2,12,8,32]{4,3,2,1,0:T(8,128)} %reshape.82) | data formatting | bytes 786432 | tf_op jit(solution)/shard_map/reshape | solution.py:86
  46.0 3.3 %gather_fusion = f32[192,2,8,32]{3,2,1,0:T(8,128)} fusion(f32[2,192,8,32]{3,2,1,0:T(8,128)} %bitcast.130, s32[1024]{0:T(1024)S(1)} %pad_clamp_fusion), kind=kCustom, calls=%fused_computation | custom fusion | bytes 787200 | tf_op jit(solution)/shard_map/jit(_take)/gather | solution.py:89
  49.3 2.9 %copy.35 = f32[192,2,8,32]{0,3,2,1:T(8,128)} copy(f32[192,2,8,32]{3,2,1,0:T(8,128)} %gather_fusion) | data formatting | bytes 786432 | tf_op jit(solution)/shard_map/jit(_take)/gather | solution.py:89
  52.2 1.1 %select_bitcast_fusion = f32[2,192,8,32]{1,3,2,0:T(8,128)S(1)} fusion(f32[192,2,8,32]{0,3,2,1:T(8,128)} %copy.35, pred[192]{0:T(512)(128)(4,1)S(1)} %compare_and_fusion), kind=kLoop, calls=%fused_computation.30 | loop fusion | flops 98304 | bytes 786624 | tf_op jit(solution)/shard_map/jit(_take)/select_n | solution.py:89
  53.3 1.1 %fusion = f32[8,32,192]{2,1,0:T(8,128)S(1)} fusion(f32[8,2,192,192]{3,2,0,1:T(8,128)S(1)} %bitcast.126, f32[2,192,8,32]{1,3,2,0:T(8,128)S(1)} %select_bitcast_fusion), kind=kOutput, calls=%fused_computation.5 | convolution fusion | flops 113246208 | bytes 2031616 | tf_op jit(solution)/shard_map/qds,dqf->qsf/dot_general | solution.py:22
  54.3 1.1 %fusion.1 = f32[8,32,192]{2,1,0:T(8,128)S(1)} fusion(f32[8,2,192,192]{3,2,0,1:T(8,128)S(1)} %bitcast.127, f32[2,192,8,32]{1,3,2,0:T(8,128)S(1)} %select_bitcast_fusion), kind=kOutput, calls=%fused_computation.6 | convolution fusion | flops 113246208 | bytes 2031616 | tf_op jit(solution)/shard_map/qds,dqf->qsf/dot_general | solution.py:22
  55.4 1.1 %fusion.5 = f32[8,32,192]{2,1,0:T(8,128)S(1)} fusion(f32[8,32,192]{2,1,0:T(8,128)S(1)} %fusion.1, f32[8,2,192,192]{3,2,0,1:T(8,128)S(1)} %bitcast.128, f32[2,192,8,32]{1,3,2,0:T(8,128)S(1)} %select_bitcast_fusion), kind=kOutput, calls=%fused_computation.25 | convolution fusion | flops 113344512 | bytes 2293760 | tf_op jit(solution)/shard_map/qds,dqf->qsf/dot_general | solution.py:22
  56.5 1.1 %fusion.9 = f32[8,192,32]{1,2,0:T(8,128)S(1)} fusion(f32[8,32,192]{2,1,0:T(8,128)S(1)} %fusion.5, f32[8,32,192]{2,1,0:T(8,128)S(1)} %fusion, f32[8,2,192,192]{3,2,0,1:T(8,128)S(1)} %bitcast.129, f32[2,192,8,32]{1,3,2,0:T(8,128)S(1)} %select_bitcast_fusion), kind=kOutput, calls=%fused_computation.29 | convolution fusion | flops 113393664 | bytes 2555904 | tf_op jit(solution)/shard_map/qds,dqf->qsf/dot_general | solution.py:22
  57.5 0.1 reshape.84
  57.6 0.2 reduce_sum.9
  57.8 0.6 %multiply_bitcast_fusion = f32[1,8,192,8]{2,3,1,0:T(8,128)} fusion(f32[8,192,8]{1,2,0:T(8,128)S(1)} %reduce_sum.9), kind=kLoop, calls=%fused_computation.110 | loop fusion | flops 12288 | bytes 98304 | tf_op jit(solution)/shard_map/div | solution.py:28
  (4 shorter events, 0.0 us)
Async XLA Ops:
  1.2 9.6 %copy-start = (f32[16,128]{1,0:T(8,128)S(1)}, f32[16,128]{1,0:T(8,128)}, u32[]{:S(2)}) copy-start(f32[16,128]{1,0:T(8,128)} %param.6) | copy-start | bytes 24580
  2.2 19.6 %all-to-all-start = ((f32[16,2,24,128]{3,2,1,0:T(8,128)}), f32[16,2,24,128]{3,2,1,0:T(8,128)S(1)}, u32[]{:S(2)}, u32[]{:S(2)}) async-start(f32[16,2,24,128]{3,2,1,0:T(8,128)} %copy.28), calls=%async_computation | async-start | bytes 786432 | tf_op jit(solution)/shard_map/all_to_all | solution.py:50
  26.1 15.7 %all-to-all-start.1 = ((f32[16,24,256]{2,1,0:T(8,128)}), f32[16,24,256]{2,1,0:T(8,128)S(1)}, u32[]{:S(2)}, u32[]{:S(2)}) async-start(f32[16,24,256]{2,1,0:T(8,128)} %copy.37), calls=%async_computation.1 | async-start | bytes 786432 | tf_op jit(solution)/shard_map/all_to_all | solution.py:85
  29.6 2.2 %copy-start.1 = (s32[192]{0:T(256)S(1)}, s32[192]{0:T(256)}, u32[]{:S(2)}) copy-start(s32[192]{0:T(256)} %param.9) | copy-start | bytes 2308

commit v2 on v1

--- a/solution.py
+++ b/solution.py
@@ -2,11 +2,18 @@
 
 import jax
 import jax.numpy as jnp
+import numpy as np
 from jax import lax
+from jax.experimental import pallas as pl
+from jax.experimental.pallas import tpu as pltpu
 from jax.sharding import PartitionSpec as P
 
 INTEG = 4
 HIGHEST = lax.Precision.HIGHEST
+F32 = jnp.float32
+BF16 = jnp.bfloat16
+LANES = 128
+VMEM = pl.BlockSpec(memory_space=pltpu.VMEM)
 
 
 def fourier_tables(length):
@@ -17,6 +24,254 @@
     return (jnp.cos(angles) * factor, jnp.sin(angles) * factor)
 
 
+def split(value):
+    high = value.astype(BF16)
+    return high, (value - high.astype(F32)).astype(BF16)
+
+
+def share_row(part, dish):
+    return part * 8 + dish if dish < 8 else 16 + part * 4 + dish - 8
+
+
+def pieces_kernel(x_ref, out_ref):
+    devices, frames_dev = out_ref.shape[:2]
+    low = lax.broadcasted_iota(jnp.int32, (8, LANES), 0) < 4
+    for frame in range(frames_dev):
+        lanes = slice(frame * LANES, (frame + 1) * LANES)
+        for dev in range(0, devices, 2):
+            for one in (dev, dev + 1):
+                for part in range(2):
+                    out_ref[one, frame, part * 8 : part * 8 + 8, :] = x_ref[
+                        part, one * 8 : one * 8 + 8, lanes
+                    ]
+            start = devices * 8 + dev * 4
+            real = x_ref[0, start : start + 8, lanes]
+            imag = x_ref[1, start : start + 8, lanes]
+            out_ref[dev, frame, 16:24, :] = jnp.where(low, real, pltpu.roll(imag, 4, 0))
+            out_ref[dev + 1, frame, 16:24, :] = jnp.where(low, pltpu.roll(real, 4, 0), imag)
+
+
+def weights_kernel(w_ref, order_ref, slot_ref, out_ref):
+    order = order_ref[...]
+    beams = w_ref.shape[3]
+    for half in range(2):
+        hot = (order == slot_ref[half : half + 1, :]).astype(BF16)
+        for part in range(2):
+            turned = w_ref[0, part].T
+            value = split(turned)[half]
+            product = jnp.dot(value, hot, preferred_element_type=F32)
+            rows = slice(part * beams, (part + 1) * beams)
+            if half == 0:
+                out_ref[0, rows, :] = product.astype(BF16)
+            else:
+                out_ref[0, rows, :] += product.astype(BF16)
+
+
+def channel_kernel(x_ref, proto_ref, table_ref, taps_ref, out_ref, poly, spec, filt):
+    frames = x_ref.shape[0]
+    pfb_count = proto_ref.shape[0]
+    fir_count = taps_ref.shape[0]
+    group = 8
+    low = lax.broadcasted_iota(jnp.int32, (group, 8, LANES), 1) < 4
+
+    spec[0 : fir_count - 1] = jnp.zeros((fir_count - 1, 24, 2 * LANES), F32)
+    for first in range(0, frames, group):
+        found = []
+        for rows in range(0, 24, 8):
+            total = None
+            for tap in range(pfb_count):
+                begin = first - tap
+                lost = max(0, -begin)
+                if lost >= group:
+                    continue
+                block = x_ref[begin + lost : begin + group, rows : rows + 8, :]
+                term = block * proto_ref[tap : tap + 1, :][None]
+                if lost:
+                    term = jnp.concatenate([jnp.zeros((lost, 8, LANES), F32), term], axis=0)
+                total = term if total is None else total + term
+            found.append(total)
+        turned = pltpu.roll(found[2], 4, 1)
+        other = [found[1], -found[0], jnp.where(low, turned, -turned)]
+        for index in range(3):
+            rows = slice(index * 8, index * 8 + 8)
+            poly[first : first + group, rows, 0:LANES] = found[index]
+            poly[first : first + group, rows, LANES : 2 * LANES] = other[index]
+
+    for first in range(0, frames, group):
+        value = poly[first : first + group].reshape(group * 24, 2 * LANES)
+        high, rest = split(value)
+        stacked = jnp.concatenate([high, rest, high], axis=1)
+        product = jnp.dot(stacked, table_ref[...], preferred_element_type=F32)
+        begin = first + fir_count - 1
+        spec[begin : begin + group] = product.reshape(group, 24, 2 * LANES)
+
+    for rows in range(0, 24, 8):
+        for first in range(0, frames, group):
+            total = None
+            for tap in range(fir_count):
+                begin = first + fir_count - 1 - tap
+                near = spec[begin : begin + group, rows : rows + 8, 0:LANES]
+                cross = spec[begin : begin + group, rows : rows + 8, LANES : 2 * LANES]
+                term = taps_ref[tap, 0, rows : rows + 8, :][None] * near
+                term = term + taps_ref[tap, 1, rows : rows + 8, :][None] * cross
+                total = term if total is None else total + term
+            for frame in range(group):
+                begin = (first + frame) * 24 + rows
+                filt[begin : begin + 8, :] = total[frame]
+
+    per_band = out_ref.shape[1] // 6
+    for pair in range(6):
+        rows = [
+            filt[pl.ds(share_row(part, pair * 2 + odd), frames, stride=24), :]
+            for part in range(2)
+            for odd in range(2)
+        ]
+        turned = jnp.concatenate(rows, axis=0).T
+        for dev in range(out_ref.shape[0]):
+            out_ref[dev, pair * per_band : (pair + 1) * per_band, :] = turned[
+                dev * per_band : (dev + 1) * per_band
+            ]
+
+
+def beams_kernel(x_ref, w_ref, pool_ref, out_ref):
+    step = pl.program_id(0)
+    rows = x_ref.shape[0] // 8
+    beams = w_ref.shape[1] // 2
+    lane = lax.broadcasted_iota(jnp.int32, (rows, LANES), 1)
+    even = lane % 64 < 32
+    one = x_ref[pl.ds(2 * step, rows, stride=8), :]
+    two = x_ref[pl.ds(2 * step + 1, rows, stride=8), :]
+    first = jnp.where(even, one, pltpu.roll(two, 32, 1))
+    second = jnp.where(even, pltpu.roll(one, LANES - 32, 1), two)
+    field = jnp.concatenate([first, second], axis=0)
+    high, rest = split(field)
+    both = jnp.concatenate([high, rest], axis=1)
+    both = jnp.concatenate([both, both], axis=0)
+    sums = []
+    for index in range(2):
+        product = jnp.dot(w_ref[index], both, preferred_element_type=F32)
+        sums.append(product[:, 0:LANES] + product[:, LANES : 2 * LANES])
+    wide = lax.broadcasted_iota(jnp.int32, (beams, LANES), 1)
+    even = wide % 64 < 32
+    by_real = jnp.where(even, sums[0][:beams], sums[1][:beams])
+    by_imag = jnp.where(even, sums[0][beams:], sums[1][beams:])
+    crossed = pltpu.roll(by_imag, 64, 1)
+    beam = by_real + jnp.where(wide < 64, -crossed, crossed)
+    high, rest = split(beam * beam)
+    power = lax.dot_general(
+        pool_ref[...],
+        jnp.concatenate([high, rest], axis=1),
+        (((1,), (1,)), ((), ())),
+        preferred_element_type=F32,
+    )
+    out_ref[0] = power[0:8]
+    out_ref[1] = power[8:16]
+
+
+def slots_of(devices):
+    dishes = np.zeros((2, devices, 6), np.int32)
+    for odd in range(2):
+        for dev in range(devices):
+            for pair in range(6):
+                own = pair * 2 + odd
+                dishes[odd, dev, pair] = (
+                    dev * 8 + own if own < 8 else devices * 8 + dev * 4 + own - 8
+                )
+    flat = dishes.reshape(-1)
+    none = np.full_like(flat, -1)
+    return np.stack([np.concatenate([flat, none]), np.concatenate([none, flat])])
+
+
+def dft_parts(channels):
+    index = np.arange(channels)
+    angle = 2.0 * np.pi * (index[:, None] * index[None, :] % channels) / channels
+    cosine = np.cos(angle) / np.sqrt(channels)
+    sine = np.sin(angle) / np.sqrt(channels)
+    table = np.block([[cosine, sine], [sine, -cosine]]).astype(np.float32)
+    high = table.astype(jnp.bfloat16)
+    rest = (table - high.astype(np.float32)).astype(jnp.bfloat16)
+    return np.concatenate([high, high, rest], axis=0)
+
+
+def pool_parts(frames):
+    pool = np.zeros((2, 8, 2, 2, frames), np.float32)
+    for which in range(2):
+        for frame in range(frames):
+            pool[which, frame // INTEG, :, which, frame] = 1.0 / INTEG
+    pool = pool.reshape(16, LANES)
+    return np.concatenate([pool, pool], axis=1).astype(jnp.bfloat16)
+
+
+def close_body(samples, prototype, dish_filter, beam_weights, dish_order):
+    devices = lax.axis_size("band")
+    position = lax.axis_index("band")
+    channels = prototype.shape[1]
+    fir_count = dish_filter.shape[1]
+    dishes = dish_filter.shape[2]
+    band_chans = beam_weights.shape[1]
+    beams = beam_weights.shape[4]
+    frames_dev = samples.shape[2] // channels
+    frames = frames_dev * devices
+
+    pieces = pl.pallas_call(
+        pieces_kernel,
+        out_shape=jax.ShapeDtypeStruct((devices, frames_dev, 24, channels), F32),
+        in_specs=[VMEM],
+        out_specs=VMEM,
+        name="pieces",
+    )(samples)
+    arrived = lax.all_to_all(pieces, "band", split_axis=0, concat_axis=0, tiled=True)
+
+    eight = lax.dynamic_slice_in_dim(dish_filter, position * 8, 8, 2)
+    four = lax.dynamic_slice_in_dim(dish_filter, devices * 8 + position * 4, 4, 2)
+    taps = jnp.concatenate([eight, eight, four, four], axis=2)
+    taps = jnp.transpose(taps, (1, 0, 2, 3))
+    weights = pl.pallas_call(
+        weights_kernel,
+        grid=(band_chans,),
+        out_shape=jax.ShapeDtypeStruct((band_chans, 2 * beams, 2 * dishes), BF16),
+        in_specs=[
+            pl.BlockSpec((1, 2, dishes, beams), lambda i: (i, 0, 0, 0)),
+            pl.BlockSpec((dishes, 1), lambda i: (0, 0)),
+            pl.BlockSpec((2, 2 * dishes), lambda i: (0, 0)),
+        ],
+        out_specs=pl.BlockSpec((1, 2 * beams, 2 * dishes), lambda i: (i, 0, 0)),
+        name="weights",
+        cost_estimate=pl.CostEstimate(
+            flops=8 * 4 * 2 * 192 * 192 * 384, bytes_accessed=5 << 20, transcendentals=0
+        ),
+    )(beam_weights[0], dish_order.reshape(dishes, 1), slots_of(devices))
+
+    filtered = pl.pallas_call(
+        channel_kernel,
+        out_shape=jax.ShapeDtypeStruct((devices, 6 * band_chans, channels), F32),
+        in_specs=[VMEM] * 4,
+        out_specs=VMEM,
+        scratch_shapes=[
+            pltpu.VMEM((frames, 24, 2 * LANES), F32),
+            pltpu.VMEM((frames + fir_count - 1, 24, 2 * LANES), F32),
+            pltpu.VMEM((frames * 24, LANES), F32),
+        ],
+        name="channels",
+    )(arrived.reshape(frames, 24, channels), prototype, dft_parts(channels), taps)
+    field = lax.all_to_all(filtered, "band", split_axis=0, concat_axis=0, tiled=True)
+    field = field.reshape(devices * 6 * band_chans, channels)
+
+    power = pl.pallas_call(
+        beams_kernel,
+        grid=(band_chans // 2,),
+        out_shape=jax.ShapeDtypeStruct((band_chans, frames // INTEG, beams), F32),
+        in_specs=[
+            pl.BlockSpec(field.shape, lambda i: (0, 0)),
+            pl.BlockSpec((2, 2 * beams, 2 * dishes), lambda i: (i, 0, 0)),
+            pl.BlockSpec((16, 2 * LANES), lambda i: (0, 0)),
+        ],
+        out_specs=pl.BlockSpec((2, frames // INTEG, beams), lambda i: (i, 0, 0)),
+        name="beams",
+    )(field, weights, pool_parts(frames))
+    return jnp.transpose(power, (0, 2, 1))[None]
+
+
 def detect(weights, field_real, field_imag):
     def contract(weight_part, field_part):
         return jnp.einsum("qds,dqf->qsf", weight_part, field_part, precision=HIGHEST)
@@ -28,7 +283,7 @@
     return jnp.mean(shaped, axis=-1)
 
 
-def body(samples, prototype, dish_filter, beam_weights, dish_order):
+def wide_body(samples, prototype, dish_filter, beam_weights, dish_order):
     devices = lax.axis_size("band")
     position = lax.axis_index("band")
     pfb_count, channels = prototype.shape
@@ -92,6 +347,20 @@
 
 
 def solution(mesh):
+    devices = mesh.shape["band"]
+
+    def body(samples, prototype, dish_filter, beam_weights, dish_order):
+        channels = prototype.shape[1]
+        close = (
+            channels == LANES
+            and beam_weights.shape[1] == 8
+            and devices * 8 == channels
+            and dish_filter.shape[2] == 12 * devices
+            and samples.shape[2] * devices == 32 * channels
+        )
+        chosen = close_body if close else wide_body
+        return chosen(samples, prototype, dish_filter, beam_weights, dish_order)
+
     placed = (P(None, None, ("grp", "band")), P(), P(), P("band", None, None, None, None), P())
     return jax.shard_map(
         body,

time: 59 us -> 47.3 us (0.80)
  Pallas kernels: 0 us -> 17.5 us
  local copies, waits for them, and re-layouts: 17.9 us -> 2.29 us
  waiting for transfers between devices: 20.8 us -> 15 us
  matrix products: 5.32 us -> 0 us
  other arithmetic: 3.19 us -> 0.69 us
    pallas_call x0 -> x4, Pallas kernels: none -> 17.5 us  [the longest x1 7.8 us: close_body(): pl.pallas_call(weights_kernel, grid=(band_chans,), out_shape=jax.ShapeDty...]
    gather x2 -> x0, local copies, waits for them, and re-layouts: 6.19 us -> none  [body(): field = jnp.take(field, dish_order, axis=1)]
    all_to_all x2, waiting for transfers between devices: 20.8 us -> 15 us  [the longest x1 11.4 us: close_body(): lax.all_to_all(pieces, 'band', split_axis=0, concat_axis=0, tiled=True)]
    reshape x5 -> x1, local copies, waits for them, and re-layouts: 6.32 us -> 0.76 us  [close_body(): dish_order.reshape(dishes, 1)]
    dot_general x5 -> x0, matrix products: 5.32 us -> none  [the longest x4 4.26 us: contract(): jnp.einsum('qds,dqf->qsf', weight_part, field_part, precision=HIGHEST)]
    another operation x2 -> x0, local copies, waits for them, and re-layouts: 1.42 us -> none  [body(): filtered = jnp.repeat(filtered, owners, axis=0)]
    select_n x2 -> x0, other arithmetic: 1.09 us -> none  [body(): field = jnp.take(field, dish_order, axis=1)]
    mul x2 -> x0, local copies, waits for them, and re-layouts: 0.94 us -> none  [the longest x1 0.93 us: body(): out_real = out_real + factor_real * part_real - factor_imag * part_imag]
  transfers between devices with their start and end apart: 2 -> 2, of which waited for: 2 -> 2; matrix products, arithmetic and copies ran while one was open for 6% -> 3% of each run, Pallas kernels for 0% -> 17%
where the time goes in v2:
time: 47.3 us; the launch traced here: 46.7 us
  Pallas kernels  17.5 us (37%)
  waiting for transfers between devices  15 us (32%)
  starting transfers between devices  11.1 us (23%)
  local copies, waits for them, and re-layouts  2.29 us (5%)
  other arithmetic  0.69 us (1%)
    all_to_all x1, waiting for transfers between devices, close_body(): lax.all_to_all(pieces, 'band', split_axis=0, concat_axis=0, tiled=True)  11.4 us
    pallas_call x1, Pallas kernels, close_body(): pl.pallas_call(weights_kernel, grid=(band_chans,), out_shape=jax.ShapeDty...  7.8 us
    all_to_all x1, starting transfers between devices, close_body(): lax.all_to_all(pieces, 'band', split_axis=0, concat_axis=0, tiled=True)  7.52 us
    pallas_call x1, Pallas kernels, close_body(): pl.pallas_call(beams_kernel, grid=(band_chans // 2,), out_shape=jax.Shape...  4.81 us
    all_to_all x1, waiting for transfers between devices, close_body(): lax.all_to_all(filtered, 'band', split_axis=0, concat_axis=0, tiled=True)  3.59 us
    all_to_all x1, starting transfers between devices, close_body(): lax.all_to_all(filtered, 'band', split_axis=0, concat_axis=0, tiled=True)  3.55 us
    pallas_call x1, Pallas kernels, close_body(): pl.pallas_call(channel_kernel, out_shape=jax.ShapeDtypeStruct((devices, 6...  3.04 us
    pallas_call x1, Pallas kernels, close_body(): pl.pallas_call(pieces_kernel, out_shape=jax.ShapeDtypeStruct((devices, fr...  1.88 us
  transfers between devices with their start and end apart: 2, of which 2 were waited for; matrix products, arithmetic and copies ran while one was open for 3% of the time, Pallas kernels for 17%

profile of v2, /device:TPU:0, one launch (start us, length us, event | category | flops | bytes accessed | tf_op | source)
XLA Modules:
  0.0 46.7 jit_solution(508277261746458596)
XLA Ops:
  0.0 0.0 copy-start
  0.0 1.9 %pieces.1 = f32[16,2,24,128]{3,2,1,0:T(8,128)} custom-call(f32[2,192,256]{2,1,0:T(8,128)} %x_ref.1), custom_call_target="tpu_custom_call" | custom-call | tf_op jit(solution)/shard_map/pieces/pallas_call | solution.py:216
  1.9 0.0 copy-start.3
  1.9 7.5 %all-to-all-start = ((f32[16,2,24,128]{3,2,1,0:T(8,128)}), f32[16,2,24,128]{3,2,1,0:T(8,128)S(1)}, u32[]{:S(2)}, u32[]{:S(2)}) async-start(f32[16,2,24,128]{3,2,1,0:T(8,128)} %pieces.1), calls=%async_computation | async-start | bytes 786432 | tf_op jit(solution)/shard_map/all_to_all | solution.py:223
  9.4 0.0 copy-done
  9.5 0.7 %copy_bitcast_fusion.taps_ref = f32[8,2,24,128]{3,2,1,0:T(8,128)} fusion(f32[2,8,4,128]{3,2,1,0:T(4,128)S(1)} %constant_dynamic-slice_fusion, f32[2,8,8,128]{3,2,1,0:T(8,128)S(1)} %constant_dynamic-slice_fusion.1), kind=kLoop, calls=%fused_computation.1 | loop fusion | flops 147456 | bytes 294912 | tf_op jit(solution)/shard_map/transpose | solution.py:228
  10.2 11.4 %all-to-all-done = f32[16,2,24,128]{3,2,1,0:T(8,128)S(1)} async-done(((f32[16,2,24,128]{3,2,1,0:T(8,128)}), f32[16,2,24,128]{3,2,1,0:T(8,128)S(1)}, u32[]{:S(2)}, u32[]{:S(2)}) %all-to-all-start) | async-done | bytes 393248 | tf_op jit(solution)/shard_map/all_to_all | solution.py:223
  21.6 0.0 copy-start.1
  21.6 0.7 %copy-done.1 = f32[16,2,24,128]{3,2,1,0:T(8,128)} copy-done((f32[16,2,24,128]{3,2,1,0:T(8,128)}, f32[16,2,24,128]{3,2,1,0:T(8,128)S(1)}, u32[]{:S(2)}) %copy-start.1) | copy-done | bytes 393240
  22.4 3.0 %channels.1 = f32[16,48,128]{2,1,0:T(8,128)} custom-call(f32[32,24,128]{2,1,0:T(8,128)} %bitcast.10, f32[16,128]{1,0:T(8,128)} %proto_ref.1, bf16[768,256]{1,0:T(8,128)(2,1)} %constant.23.clone.table_ref, f32[8,2,24,128]{3,2,1,0:T(8,128)} %copy_bitcast_fusion.taps_ref), custom_call_target="tpu_custom_call" | custom-call | tf_op jit(solution)/shard_map/channels/pallas_call | solution.py:245
  25.4 3.6 %all-to-all-start.1 = ((f32[16,48,128]{2,1,0:T(8,128)}), f32[16,48,128]{2,1,0:T(8,128)S(1)}, u32[]{:S(2)}, u32[]{:S(2)}) async-start(f32[16,48,128]{2,1,0:T(8,128)} %channels.1), calls=%async_computation.1 | async-start | bytes 786432 | tf_op jit(solution)/shard_map/all_to_all | solution.py:257
  29.0 0.0 copy-done.3
  29.0 0.8 %copy.13.order_ref = s32[192,1]{1,0:T(8,128)} copy(s32[192,1]{0,1:T(1,128)S(1)} %bitcast.12) | data formatting | bytes 1536 | tf_op jit(solution)/shard_map/reshape | solution.py:243
  29.7 7.8 %weights.1.w_ref = bf16[8,384,384]{2,1,0:T(8,128)(2,1)} custom-call(f32[8,2,192,192]{3,2,1,0:T(8,128)} %bitcast.9, s32[192,1]{1,0:T(8,128)} %copy.13.order_ref, s32[2,384]{1,0:T(2,128)} %constant.22.clone.slot_ref), custom_call_target="tpu_custom_call" | custom-call | flops 905969664 | bytes 5242880 | tf_op jit(solution)/shard_map/weights/pallas_call | solution.py:229
  37.5 3.6 %all-to-all-done.1 = f32[16,48,128]{2,1,0:T(8,128)S(1)} async-done(((f32[16,48,128]{2,1,0:T(8,128)}), f32[16,48,128]{2,1,0:T(8,128)S(1)}, u32[]{:S(2)}, u32[]{:S(2)}) %all-to-all-start.1) | async-done | bytes 393248 | tf_op jit(solution)/shard_map/all_to_all | solution.py:257
  41.1 0.0 copy-start.2
  41.1 0.7 %copy-done.2 = f32[16,48,128]{2,1,0:T(8,128)} copy-done((f32[16,48,128]{2,1,0:T(8,128)}, f32[16,48,128]{2,1,0:T(8,128)S(1)}, u32[]{:S(2)}) %copy-start.2) | copy-done | bytes 393240
  41.9 4.8 %beams.1 = f32[8,8,192]{2,1,0:T(8,128)} custom-call(f32[768,128]{1,0:T(8,128)} %bitcast.11, bf16[8,384,384]{2,1,0:T(8,128)(2,1)} %weights.1.w_ref, bf16[16,256]{1,0:T(8,128)(2,1)} %constant.24.clone.pool_ref), custom_call_target="tpu_custom_call" | custom-call | tf_op jit(solution)/shard_map/beams/pallas_call | solution.py:260
  (2 shorter events, 0.0 us)
Async XLA Ops:
  0.0 9.4 %copy-start = (f32[2,8,192,128]{3,2,1,0:T(8,128)S(1)}, f32[2,8,192,128]{3,2,1,0:T(8,128)}, u32[]{:S(2)}) copy-start(f32[2,8,192,128]{3,2,1,0:T(8,128)} %param.10) | copy-start | bytes 4718596
  1.9 27.1 %copy-start.3 = (s32[192]{0:T(256)S(1)}, s32[192]{0:T(256)}, u32[]{:S(2)}) copy-start(s32[192]{0:T(256)} %param.12) | copy-start | bytes 2308
  1.9 19.7 %all-to-all-start = ((f32[16,2,24,128]{3,2,1,0:T(8,128)}), f32[16,2,24,128]{3,2,1,0:T(8,128)S(1)}, u32[]{:S(2)}, u32[]{:S(2)}) async-start(f32[16,2,24,128]{3,2,1,0:T(8,128)} %pieces.1), calls=%async_computation | async-start | bytes 786432 | tf_op jit(solution)/shard_map/all_to_all | solution.py:223
  21.6 0.7 %copy-start.1 = (f32[16,2,24,128]{3,2,1,0:T(8,128)}, f32[16,2,24,128]{3,2,1,0:T(8,128)S(1)}, u32[]{:S(2)}) copy-start(f32[16,2,24,128]{3,2,1,0:T(8,128)S(1)} %all-to-all-done) | copy-start | bytes 1179652
  25.4 15.7 %all-to-all-start.1 = ((f32[16,48,128]{2,1,0:T(8,128)}), f32[16,48,128]{2,1,0:T(8,128)S(1)}, u32[]{:S(2)}, u32[]{:S(2)}) async-start(f32[16,48,128]{2,1,0:T(8,128)} %channels.1), calls=%async_computation.1 | async-start | bytes 786432 | tf_op jit(solution)/shard_map/all_to_all | solution.py:257
  41.1 0.7 %copy-start.2 = (f32[16,48,128]{2,1,0:T(8,128)}, f32[16,48,128]{2,1,0:T(8,128)S(1)}, u32[]{:S(2)}) copy-start(f32[16,48,128]{2,1,0:T(8,128)S(1)} %all-to-all-done.1) | copy-start | bytes 1179652

commit v3 on v2

--- a/solution.py
+++ b/solution.py
@@ -14,6 +14,7 @@
 BF16 = jnp.bfloat16
 LANES = 128
 VMEM = pl.BlockSpec(memory_space=pltpu.VMEM)
+GRANT = pltpu.CompilerParams(vmem_limit_bytes=16 << 20)
 
 
 def fourier_tables(length):
@@ -55,7 +56,7 @@
     order = order_ref[...]
     beams = w_ref.shape[3]
     for half in range(2):
-        hot = (order == slot_ref[half : half + 1, :]).astype(BF16)
+        hot = (slot_ref[:, half : half + 1] == order).astype(F32).T.astype(BF16)
         for part in range(2):
             turned = w_ref[0, part].T
             value = split(turned)[half]
@@ -133,39 +134,42 @@
             ]
 
 
-def beams_kernel(x_ref, w_ref, pool_ref, out_ref):
-    step = pl.program_id(0)
+def beams_kernel(x_ref, w_ref, out_ref):
     rows = x_ref.shape[0] // 8
     beams = w_ref.shape[1] // 2
     lane = lax.broadcasted_iota(jnp.int32, (rows, LANES), 1)
     even = lane % 64 < 32
-    one = x_ref[pl.ds(2 * step, rows, stride=8), :]
-    two = x_ref[pl.ds(2 * step + 1, rows, stride=8), :]
-    first = jnp.where(even, one, pltpu.roll(two, 32, 1))
-    second = jnp.where(even, pltpu.roll(one, LANES - 32, 1), two)
-    field = jnp.concatenate([first, second], axis=0)
-    high, rest = split(field)
-    both = jnp.concatenate([high, rest], axis=1)
-    both = jnp.concatenate([both, both], axis=0)
-    sums = []
-    for index in range(2):
-        product = jnp.dot(w_ref[index], both, preferred_element_type=F32)
-        sums.append(product[:, 0:LANES] + product[:, LANES : 2 * LANES])
     wide = lax.broadcasted_iota(jnp.int32, (beams, LANES), 1)
-    even = wide % 64 < 32
-    by_real = jnp.where(even, sums[0][:beams], sums[1][:beams])
-    by_imag = jnp.where(even, sums[0][beams:], sums[1][beams:])
-    crossed = pltpu.roll(by_imag, 64, 1)
-    beam = by_real + jnp.where(wide < 64, -crossed, crossed)
-    high, rest = split(beam * beam)
-    power = lax.dot_general(
-        pool_ref[...],
-        jnp.concatenate([high, rest], axis=1),
-        (((1,), (1,)), ((), ())),
-        preferred_element_type=F32,
-    )
-    out_ref[0] = power[0:8]
-    out_ref[1] = power[8:16]
+    even_wide = wide % 64 < 32
+    row = lax.broadcasted_iota(jnp.int32, (16, 2 * LANES), 0)
+    column = lax.broadcasted_iota(jnp.int32, (16, 2 * LANES), 1)
+    pool = jnp.where(row == column % 64 // INTEG, 1.0 / INTEG, 0.0).astype(BF16)
+    for step in range(w_ref.shape[0] // 2):
+        one = x_ref[pl.ds(2 * step, rows, stride=8), :]
+        two = x_ref[pl.ds(2 * step + 1, rows, stride=8), :]
+        first = jnp.where(even, one, pltpu.roll(two, 32, 1))
+        second = jnp.where(even, pltpu.roll(one, LANES - 32, 1), two)
+        field = jnp.concatenate([first, second], axis=0)
+        high, rest = split(field)
+        both = jnp.concatenate([high, rest], axis=1)
+        both = jnp.concatenate([both, both], axis=0)
+        sums = []
+        for index in range(2):
+            product = jnp.dot(w_ref[2 * step + index], both, preferred_element_type=F32)
+            sums.append(product[:, 0:LANES] + product[:, LANES : 2 * LANES])
+        by_real = jnp.where(even_wide, sums[0][:beams], sums[1][:beams])
+        by_imag = jnp.where(even_wide, sums[0][beams:], sums[1][beams:])
+        crossed = pltpu.roll(by_imag, 64, 1)
+        beam = by_real + jnp.where(wide < 64, -crossed, crossed)
+        high, rest = split(beam * beam)
+        power = lax.dot_general(
+            pool,
+            jnp.concatenate([high, rest], axis=1),
+            (((1,), (1,)), ((), ())),
+            preferred_element_type=F32,
+        )
+        out_ref[2 * step] = power[0:8]
+        out_ref[2 * step + 1] = power[8:16]
 
 
 def slots_of(devices):
@@ -179,7 +183,7 @@
                 )
     flat = dishes.reshape(-1)
     none = np.full_like(flat, -1)
-    return np.stack([np.concatenate([flat, none]), np.concatenate([none, flat])])
+    return np.stack([np.concatenate([flat, none]), np.concatenate([none, flat])], axis=1)
 
 
 def dft_parts(channels):
@@ -191,15 +195,6 @@
     high = table.astype(jnp.bfloat16)
     rest = (table - high.astype(np.float32)).astype(jnp.bfloat16)
     return np.concatenate([high, high, rest], axis=0)
-
-
-def pool_parts(frames):
-    pool = np.zeros((2, 8, 2, 2, frames), np.float32)
-    for which in range(2):
-        for frame in range(frames):
-            pool[which, frame // INTEG, :, which, frame] = 1.0 / INTEG
-    pool = pool.reshape(16, LANES)
-    return np.concatenate([pool, pool], axis=1).astype(jnp.bfloat16)
 
 
 def close_body(samples, prototype, dish_filter, beam_weights, dish_order):
@@ -219,6 +214,7 @@
         in_specs=[VMEM],
         out_specs=VMEM,
         name="pieces",
+        compiler_params=GRANT,
     )(samples)
     arrived = lax.all_to_all(pieces, "band", split_axis=0, concat_axis=0, tiled=True)
 
@@ -232,15 +228,16 @@
         out_shape=jax.ShapeDtypeStruct((band_chans, 2 * beams, 2 * dishes), BF16),
         in_specs=[
             pl.BlockSpec((1, 2, dishes, beams), lambda i: (i, 0, 0, 0)),
-            pl.BlockSpec((dishes, 1), lambda i: (0, 0)),
-            pl.BlockSpec((2, 2 * dishes), lambda i: (0, 0)),
+            pl.BlockSpec((1, dishes), lambda i: (0, 0)),
+            pl.BlockSpec((2 * dishes, 2), lambda i: (0, 0)),
         ],
         out_specs=pl.BlockSpec((1, 2 * beams, 2 * dishes), lambda i: (i, 0, 0)),
         name="weights",
+        compiler_params=GRANT,
         cost_estimate=pl.CostEstimate(
             flops=8 * 4 * 2 * 192 * 192 * 384, bytes_accessed=5 << 20, transcendentals=0
         ),
-    )(beam_weights[0], dish_order.reshape(dishes, 1), slots_of(devices))
+    )(beam_weights[0], dish_order.reshape(1, dishes), slots_of(devices))
 
     filtered = pl.pallas_call(
         channel_kernel,
@@ -253,22 +250,19 @@
             pltpu.VMEM((frames * 24, LANES), F32),
         ],
         name="channels",
+        compiler_params=GRANT,
     )(arrived.reshape(frames, 24, channels), prototype, dft_parts(channels), taps)
     field = lax.all_to_all(filtered, "band", split_axis=0, concat_axis=0, tiled=True)
     field = field.reshape(devices * 6 * band_chans, channels)
 
     power = pl.pallas_call(
         beams_kernel,
-        grid=(band_chans // 2,),
         out_shape=jax.ShapeDtypeStruct((band_chans, frames // INTEG, beams), F32),
-        in_specs=[
-            pl.BlockSpec(field.shape, lambda i: (0, 0)),
-            pl.BlockSpec((2, 2 * beams, 2 * dishes), lambda i: (i, 0, 0)),
-            pl.BlockSpec((16, 2 * LANES), lambda i: (0, 0)),
-        ],
-        out_specs=pl.BlockSpec((2, frames // INTEG, beams), lambda i: (i, 0, 0)),
+        in_specs=[VMEM] * 2,
+        out_specs=VMEM,
         name="beams",
-    )(field, weights, pool_parts(frames))
+        compiler_params=GRANT,
+    )(field, weights)
     return jnp.transpose(power, (0, 2, 1))[None]
 
 

time: 47.3 us -> 43.9 us (0.928)
  Pallas kernels: 17.5 us -> 10.9 us
  local copies, waits for them, and re-layouts: 2.29 us -> 6.14 us
  other arithmetic: 0.69 us -> 0.02 us
    unnamed x8 -> x18, local copies, waits for them, and re-layouts: 1.49 us -> 6.1 us
    pallas_call x1, Pallas kernels: 4.81 us -> 2.6 us  [close_body(): pl.pallas_call(beams_kernel, out_shape=jax.ShapeDtypeStruct((band_chans,...]
    pallas_call x1, Pallas kernels: 7.8 us -> 5.69 us  [close_body(): pl.pallas_call(weights_kernel, grid=(band_chans,), out_shape=jax.ShapeDty...]
    pallas_call x1, Pallas kernels: 3.04 us -> 1.87 us  [close_body(): pl.pallas_call(channel_kernel, out_shape=jax.ShapeDtypeStruct((devices, 6...]
    pallas_call x1, Pallas kernels: 1.88 us -> 0.77 us  [close_body(): pl.pallas_call(pieces_kernel, out_shape=jax.ShapeDtypeStruct((devices, fr...]
    reshape x1 -> x0, local copies, waits for them, and re-layouts: 0.76 us -> none  [close_body(): dish_order.reshape(dishes, 1)]
    transpose x1, other arithmetic: 0.69 us -> 0.02 us  [close_body(): taps = jnp.transpose(taps, (1, 0, 2, 3))]
    all_to_all x1, waiting for transfers between devices: 11.4 us -> 12.1 us  [close_body(): lax.all_to_all(pieces, 'band', split_axis=0, concat_axis=0, tiled=True)]
  transfers between devices with their start and end apart: 2 -> 2, of which waited for: 2 -> 2; matrix products, arithmetic and copies ran while one was open for 3% -> 0% of each run, Pallas kernels for 17% -> 13%
where the time goes in v3:
time: 43.9 us; the launch traced here: 43.5 us
  waiting for transfers between devices  15.2 us (35%)
  starting transfers between devices  11.1 us (25%)
  Pallas kernels  10.9 us (25%)
  local copies, waits for them, and re-layouts  6.14 us (14%)
    all_to_all x1, waiting for transfers between devices, close_body(): lax.all_to_all(pieces, 'band', split_axis=0, concat_axis=0, tiled=True)  12.1 us
    all_to_all x1, starting transfers between devices, close_body(): lax.all_to_all(pieces, 'band', split_axis=0, concat_axis=0, tiled=True)  7.52 us
    unnamed x18, local copies, waits for them, and re-layouts  6.1 us
    pallas_call x1, Pallas kernels, close_body(): pl.pallas_call(weights_kernel, grid=(band_chans,), out_shape=jax.ShapeDty...  5.69 us
    all_to_all x1, starting transfers between devices, close_body(): lax.all_to_all(filtered, 'band', split_axis=0, concat_axis=0, tiled=True)  3.55 us
    all_to_all x1, waiting for transfers between devices, close_body(): lax.all_to_all(filtered, 'band', split_axis=0, concat_axis=0, tiled=True)  3.13 us
    pallas_call x1, Pallas kernels, close_body(): pl.pallas_call(beams_kernel, out_shape=jax.ShapeDtypeStruct((band_chans,...  2.6 us
    pallas_call x1, Pallas kernels, close_body(): pl.pallas_call(channel_kernel, out_shape=jax.ShapeDtypeStruct((devices, 6...  1.87 us
  transfers between devices with their start and end apart: 2, of which 2 were waited for; matrix products, arithmetic and copies ran while one was open for 0% of the time, Pallas kernels for 13%

profile of v3, /device:TPU:0, one launch (start us, length us, event | category | flops | bytes accessed | tf_op | source)
XLA Modules:
  0.0 43.5 jit_solution(14270870715584918559)
XLA Ops:
  0.0 0.0 copy-start
  0.0 0.0 copy-start.4
  0.0 1.1 %copy-done.4 = f32[2,192,256]{2,1,0:T(8,128)S(1)} copy-done((f32[2,192,256]{2,1,0:T(8,128)S(1)}, f32[2,192,256]{2,1,0:T(8,128)}, u32[]{:S(2)}) %copy-start.4) | copy-done | bytes 393240
  1.1 0.0 copy-start.5
  1.1 0.0 copy-start.7
  1.1 0.8 %pieces.1 = f32[16,2,24,128]{3,2,1,0:T(8,128)} custom-call(f32[2,192,256]{2,1,0:T(8,128)S(1)} %copy-done.4), custom_call_target="tpu_custom_call" | custom-call | tf_op jit(solution)/shard_map/pieces/pallas_call | solution.py:211
  1.9 0.0 copy-start.6
  1.9 0.0 copy-start.8
  1.9 7.5 %all-to-all-start = ((f32[16,2,24,128]{3,2,1,0:T(8,128)}), f32[16,2,24,128]{3,2,1,0:T(8,128)S(1)}, u32[]{:S(2)}, u32[]{:S(2)}) async-start(f32[16,2,24,128]{3,2,1,0:T(8,128)} %pieces.1), calls=%async_computation | async-start | bytes 786432 | tf_op jit(solution)/shard_map/all_to_all | solution.py:219
  9.4 0.0 copy-done
  9.5 12.1 %all-to-all-done = f32[16,2,24,128]{3,2,1,0:T(8,128)S(1)} async-done(((f32[16,2,24,128]{3,2,1,0:T(8,128)}), f32[16,2,24,128]{3,2,1,0:T(8,128)S(1)}, u32[]{:S(2)}, u32[]{:S(2)}) %all-to-all-start) | async-done | bytes 393248 | tf_op jit(solution)/shard_map/all_to_all | solution.py:219
  21.6 0.0 copy-done.5
  21.6 0.0 copy-done.7
  21.6 1.9 %channels.1 = f32[16,48,128]{2,1,0:T(8,128)} custom-call(f32[32,24,128]{2,1,0:T(8,128)S(1)} %bitcast.10, f32[16,128]{1,0:T(8,128)S(1)} %copy-done.7, bf16[768,256]{1,0:T(8,128)(2,1)S(1)} %copy-done.5, f32[8,2,24,128]{3,2,1,0:T(8,128)S(1)} %copy_bitcast_fusion.taps_ref), custom_call_target="tpu_custom_call" | custom-call | tf_op jit(solution)/shard_map/channels/pallas_call | solution.py:242
  23.5 3.6 %all-to-all-start.1 = ((f32[16,48,128]{2,1,0:T(8,128)}), f32[16,48,128]{2,1,0:T(8,128)S(1)}, u32[]{:S(2)}, u32[]{:S(2)}) async-start(f32[16,48,128]{2,1,0:T(8,128)} %channels.1), calls=%async_computation.1 | async-start | bytes 786432 | tf_op jit(solution)/shard_map/all_to_all | solution.py:255
  27.0 0.0 copy-done.6
  27.1 0.0 copy-done.8
  27.1 0.0 copy-start.3
  27.1 1.9 %copy-done.3 = f32[1,8,2,192,192]{4,3,2,1,0:T(8,128)S(1)} copy-done((f32[1,8,2,192,192]{4,3,2,1,0:T(8,128)S(1)}, f32[1,8,2,192,192]{4,3,2,1,0:T(8,128)}, u32[]{:S(2)}) %copy-start.3) | copy-done | bytes 2359320
  29.0 5.7 %weights.1.w_ref = bf16[8,384,384]{2,1,0:T(8,128)(2,1)S(1)} custom-call(f32[8,2,192,192]{3,2,1,0:T(8,128)S(1)} %bitcast.9, s32[1,192]{1,0:T(1,128)S(1)} %bitcast.12, s32[384,2]{1,0:T(8,128)S(1)} %copy-done.6), custom_call_target="tpu_custom_call" | custom-call | flops 905969664 | bytes 5242880 | tf_op jit(solution)/shard_map/weights/pallas_call | solution.py:225
  34.7 0.0 copy-start.1
  34.7 1.4 %copy-done.1 = bf16[8,384,384]{2,1,0:T(8,128)(2,1)} copy-done((bf16[8,384,384]{2,1,0:T(8,128)(2,1)}, bf16[8,384,384]{2,1,0:T(8,128)(2,1)S(1)}, u32[]{:S(2)}) %copy-start.1) | copy-done | bytes 2359320
  36.1 3.1 %all-to-all-done.1 = f32[16,48,128]{2,1,0:T(8,128)S(1)} async-done(((f32[16,48,128]{2,1,0:T(8,128)}), f32[16,48,128]{2,1,0:T(8,128)S(1)}, u32[]{:S(2)}, u32[]{:S(2)}) %all-to-all-start.1) | async-done | bytes 393248 | tf_op jit(solution)/shard_map/all_to_all | solution.py:255
  39.2 0.0 copy-start.2
  39.2 1.7 %copy-done.2 = bf16[8,384,384]{2,1,0:T(8,128)(2,1)S(1)} copy-done((bf16[8,384,384]{2,1,0:T(8,128)(2,1)S(1)}, bf16[8,384,384]{2,1,0:T(8,128)(2,1)}, u32[]{:S(2)}) %copy-start.2) | copy-done | bytes 2359320
  40.9 2.6 %beams.1 = f32[8,8,192]{2,1,0:T(8,128)} custom-call(f32[768,128]{1,0:T(8,128)S(1)} %bitcast.11, bf16[8,384,384]{2,1,0:T(8,128)(2,1)S(1)} %copy-done.2), custom_call_target="tpu_custom_call" | custom-call | tf_op jit(solution)/shard_map/beams/pallas_call | solution.py:258
  (3 shorter events, 0.1 us)
Async XLA Ops:
  0.0 9.4 %copy-start = (f32[2,8,192,128]{3,2,1,0:T(8,128)S(1)}, f32[2,8,192,128]{3,2,1,0:T(8,128)}, u32[]{:S(2)}) copy-start(f32[2,8,192,128]{3,2,1,0:T(8,128)} %param.9) | copy-start | bytes 4718596
  0.0 1.1 %copy-start.4 = (f32[2,192,256]{2,1,0:T(8,128)S(1)}, f32[2,192,256]{2,1,0:T(8,128)}, u32[]{:S(2)}) copy-start(f32[2,192,256]{2,1,0:T(8,128)} %x_ref.1) | copy-start | bytes 1179652
  1.1 20.5 %copy-start.5 = (bf16[768,256]{1,0:T(8,128)(2,1)S(1)}, bf16[768,256]{1,0:T(8,128)(2,1)}, u32[]{:S(2)}) copy-start(bf16[768,256]{1,0:T(8,128)(2,1)} %constant.21.clone.table_ref) | copy-start | bytes 1179652
  1.1 20.5 %copy-start.7 = (f32[16,128]{1,0:T(8,128)S(1)}, f32[16,128]{1,0:T(8,128)}, u32[]{:S(2)}) copy-start(f32[16,128]{1,0:T(8,128)} %proto_ref.1) | copy-start | bytes 24580
  1.9 25.2 %copy-start.6 = (s32[384,2]{1,0:T(8,128)S(1)}, s32[384,2]{1,0:T(8,128)}, u32[]{:S(2)}) copy-start(s32[384,2]{1,0:T(8,128)} %constant.20.clone.slot_ref) | copy-start | bytes 9220
  1.9 25.2 %copy-start.8 = (s32[192]{0:T(256)S(1)}, s32[192]{0:T(256)}, u32[]{:S(2)}) copy-start(s32[192]{0:T(256)} %param.11) | copy-start | bytes 2308
  1.9 19.7 %all-to-all-start = ((f32[16,2,24,128]{3,2,1,0:T(8,128)}), f32[16,2,24,128]{3,2,1,0:T(8,128)S(1)}, u32[]{:S(2)}, u32[]{:S(2)}) async-start(f32[16,2,24,128]{3,2,1,0:T(8,128)} %pieces.1), calls=%async_computation | async-start | bytes 786432 | tf_op jit(solution)/shard_map/all_to_all | solution.py:219
  23.5 15.7 %all-to-all-start.1 = ((f32[16,48,128]{2,1,0:T(8,128)}), f32[16,48,128]{2,1,0:T(8,128)S(1)}, u32[]{:S(2)}, u32[]{:S(2)}) async-start(f32[16,48,128]{2,1,0:T(8,128)} %channels.1), calls=%async_computation.1 | async-start | bytes 786432 | tf_op jit(solution)/shard_map/all_to_all | solution.py:255
  27.1 1.9 %copy-start.3 = (f32[1,8,2,192,192]{4,3,2,1,0:T(8,128)S(1)}, f32[1,8,2,192,192]{4,3,2,1,0:T(8,128)}, u32[]{:S(2)}) copy-start(f32[1,8,2,192,192]{4,3,2,1,0:T(8,128)} %param.10) | copy-start | bytes 7077892
  34.7 1.4 %copy-start.1 = (bf16[8,384,384]{2,1,0:T(8,128)(2,1)}, bf16[8,384,384]{2,1,0:T(8,128)(2,1)S(1)}, u32[]{:S(2)}) copy-start(bf16[8,384,384]{2,1,0:T(8,128)(2,1)S(1)} %weights.1.w_ref) | copy-start | bytes 7077892
  39.2 1.7 %copy-start.2 = (bf16[8,384,384]{2,1,0:T(8,128)(2,1)S(1)}, bf16[8,384,384]{2,1,0:T(8,128)(2,1)}, u32[]{:S(2)}) copy-start(bf16[8,384,384]{2,1,0:T(8,128)(2,1)} %copy-done.1) | copy-start | bytes 7077892

commit v4 on v3

--- a/solution.py
+++ b/solution.py
@@ -30,55 +30,69 @@
     return high, (value - high.astype(F32)).astype(BF16)
 
 
-def share_row(part, dish):
-    return part * 8 + dish if dish < 8 else 16 + part * 4 + dish - 8
-
-
-def pieces_kernel(x_ref, out_ref):
+CHUNKS = (8, 4)
+
+
+def eight_kernel(x_ref, out_ref, sems):
+    devices, frames_dev = out_ref.shape[:2]
+    tiles = x_ref.reshape(2, x_ref.shape[1] // 8, 8, x_ref.shape[2])
+    copies = []
+    for frame in range(frames_dev):
+        for part in range(2):
+            lanes = slice(frame * LANES, (frame + 1) * LANES)
+            copies.append(
+                pltpu.make_async_copy(
+                    tiles.at[part, 0:devices, :, lanes],
+                    out_ref.at[:, frame, part * 8 : part * 8 + 8, :],
+                    sems.at[frame, part],
+                )
+            )
+    for copy in copies:
+        copy.start()
+    for copy in copies:
+        copy.wait()
+
+
+def four_kernel(x_ref, out_ref):
     devices, frames_dev = out_ref.shape[:2]
     low = lax.broadcasted_iota(jnp.int32, (8, LANES), 0) < 4
     for frame in range(frames_dev):
         lanes = slice(frame * LANES, (frame + 1) * LANES)
         for dev in range(0, devices, 2):
-            for one in (dev, dev + 1):
-                for part in range(2):
-                    out_ref[one, frame, part * 8 : part * 8 + 8, :] = x_ref[
-                        part, one * 8 : one * 8 + 8, lanes
-                    ]
-            start = devices * 8 + dev * 4
-            real = x_ref[0, start : start + 8, lanes]
-            imag = x_ref[1, start : start + 8, lanes]
-            out_ref[dev, frame, 16:24, :] = jnp.where(low, real, pltpu.roll(imag, 4, 0))
-            out_ref[dev + 1, frame, 16:24, :] = jnp.where(low, pltpu.roll(real, 4, 0), imag)
-
-
-def weights_kernel(w_ref, order_ref, slot_ref, out_ref):
-    order = order_ref[...]
+            real = x_ref[0, dev * 4 : dev * 4 + 8, lanes]
+            imag = x_ref[1, dev * 4 : dev * 4 + 8, lanes]
+            out_ref[dev, frame] = jnp.where(low, real, pltpu.roll(imag, 4, 0))
+            out_ref[dev + 1, frame] = jnp.where(low, pltpu.roll(real, 4, 0), imag)
+
+
+def weights_kernel(w_ref, order_ref, slot_ref, *out_refs):
+    hot = (slot_ref[...] == order_ref[...]).astype(F32).T.astype(BF16)
     beams = w_ref.shape[3]
-    for half in range(2):
-        hot = (slot_ref[:, half : half + 1] == order).astype(F32).T.astype(BF16)
-        for part in range(2):
-            turned = w_ref[0, part].T
-            value = split(turned)[half]
-            product = jnp.dot(value, hot, preferred_element_type=F32)
-            rows = slice(part * beams, (part + 1) * beams)
-            if half == 0:
-                out_ref[0, rows, :] = product.astype(BF16)
-            else:
-                out_ref[0, rows, :] += product.astype(BF16)
-
-
-def channel_kernel(x_ref, proto_ref, table_ref, taps_ref, out_ref, poly, spec, filt):
-    frames = x_ref.shape[0]
+    for part in range(2):
+        halves = [
+            jnp.dot(half, hot, preferred_element_type=F32).astype(BF16)
+            for half in split(w_ref[0, part].T)
+        ]
+        begin = 0
+        for out_ref in out_refs:
+            width = out_ref.shape[2] // 2
+            both = [half[:, begin : begin + width] for half in halves]
+            out_ref[0, part * beams : (part + 1) * beams, :] = jnp.concatenate(both, axis=1)
+            begin += width
+
+
+def channel_kernel(after_ref, x_ref, proto_ref, table_ref, taps_ref, out_ref, poly, spec, filt):
+    frames, height = x_ref.shape[:2]
+    count = height // 2
     pfb_count = proto_ref.shape[0]
     fir_count = taps_ref.shape[0]
     group = 8
     low = lax.broadcasted_iota(jnp.int32, (group, 8, LANES), 1) < 4
 
-    spec[0 : fir_count - 1] = jnp.zeros((fir_count - 1, 24, 2 * LANES), F32)
+    spec[0 : fir_count - 1] = jnp.zeros((fir_count - 1, height, 2 * LANES), F32)
     for first in range(0, frames, group):
         found = []
-        for rows in range(0, 24, 8):
+        for rows in range(0, height, 8):
             total = None
             for tap in range(pfb_count):
                 begin = first - tap
@@ -91,22 +105,25 @@
                     term = jnp.concatenate([jnp.zeros((lost, 8, LANES), F32), term], axis=0)
                 total = term if total is None else total + term
             found.append(total)
-        turned = pltpu.roll(found[2], 4, 1)
-        other = [found[1], -found[0], jnp.where(low, turned, -turned)]
-        for index in range(3):
+        if count == 8:
+            other = [found[1], -found[0]]
+        else:
+            turned = pltpu.roll(found[0], 4, 1)
+            other = [jnp.where(low, turned, -turned)]
+        for index in range(height // 8):
             rows = slice(index * 8, index * 8 + 8)
             poly[first : first + group, rows, 0:LANES] = found[index]
             poly[first : first + group, rows, LANES : 2 * LANES] = other[index]
 
     for first in range(0, frames, group):
-        value = poly[first : first + group].reshape(group * 24, 2 * LANES)
+        value = poly[first : first + group].reshape(group * height, 2 * LANES)
         high, rest = split(value)
         stacked = jnp.concatenate([high, rest, high], axis=1)
         product = jnp.dot(stacked, table_ref[...], preferred_element_type=F32)
         begin = first + fir_count - 1
-        spec[begin : begin + group] = product.reshape(group, 24, 2 * LANES)
-
-    for rows in range(0, 24, 8):
+        spec[begin : begin + group] = product.reshape(group, height, 2 * LANES)
+
+    for rows in range(0, height, 8):
         for first in range(0, frames, group):
             total = None
             for tap in range(fir_count):
@@ -117,13 +134,13 @@
                 term = term + taps_ref[tap, 1, rows : rows + 8, :][None] * cross
                 total = term if total is None else total + term
             for frame in range(group):
-                begin = (first + frame) * 24 + rows
+                begin = (first + frame) * height + rows
                 filt[begin : begin + 8, :] = total[frame]
 
-    per_band = out_ref.shape[1] // 6
-    for pair in range(6):
+    per_band = out_ref.shape[1] // (count // 2)
+    for pair in range(count // 2):
         rows = [
-            filt[pl.ds(share_row(part, pair * 2 + odd), frames, stride=24), :]
+            filt[pl.ds(part * count + pair * 2 + odd, frames, stride=height), :]
             for part in range(2)
             for odd in range(2)
         ]
@@ -134,33 +151,49 @@
             ]
 
 
-def beams_kernel(x_ref, w_ref, out_ref):
+def pair_beams(x_ref, w_ref, step):
     rows = x_ref.shape[0] // 8
     beams = w_ref.shape[1] // 2
     lane = lax.broadcasted_iota(jnp.int32, (rows, LANES), 1)
     even = lane % 64 < 32
     wide = lax.broadcasted_iota(jnp.int32, (beams, LANES), 1)
     even_wide = wide % 64 < 32
+    one = x_ref[pl.ds(2 * step, rows, stride=8), :]
+    two = x_ref[pl.ds(2 * step + 1, rows, stride=8), :]
+    first = jnp.where(even, one, pltpu.roll(two, 32, 1))
+    second = jnp.where(even, pltpu.roll(one, LANES - 32, 1), two)
+    field = jnp.concatenate([first, second], axis=0)
+    high, rest = split(field)
+    both = jnp.concatenate([high, rest], axis=1)
+    both = jnp.concatenate([both, both], axis=0)
+    sums = []
+    for index in range(2):
+        product = jnp.dot(w_ref[2 * step + index], both, preferred_element_type=F32)
+        sums.append(product[:, 0:LANES] + product[:, LANES : 2 * LANES])
+    by_real = jnp.where(even_wide, sums[0][:beams], sums[1][:beams])
+    by_imag = jnp.where(even_wide, sums[0][beams:], sums[1][beams:])
+    crossed = pltpu.roll(by_imag, 64, 1)
+    return by_real + jnp.where(wide < 64, -crossed, crossed)
+
+
+def beams_kernel(*refs):
+    x_ref, w_ref, out_ref = refs[0], refs[1], refs[-1]
+    for step in range(w_ref.shape[0] // 2):
+        beam = pair_beams(x_ref, w_ref, step)
+        if len(refs) == 4:
+            beam = beam + refs[2][step]
+        out_ref[step] = beam
+
+
+def power_kernel(*refs):
+    x_ref, w_ref, out_ref = refs[0], refs[1], refs[-1]
     row = lax.broadcasted_iota(jnp.int32, (16, 2 * LANES), 0)
     column = lax.broadcasted_iota(jnp.int32, (16, 2 * LANES), 1)
     pool = jnp.where(row == column % 64 // INTEG, 1.0 / INTEG, 0.0).astype(BF16)
     for step in range(w_ref.shape[0] // 2):
-        one = x_ref[pl.ds(2 * step, rows, stride=8), :]
-        two = x_ref[pl.ds(2 * step + 1, rows, stride=8), :]
-        first = jnp.where(even, one, pltpu.roll(two, 32, 1))
-        second = jnp.where(even, pltpu.roll(one, LANES - 32, 1), two)
-        field = jnp.concatenate([first, second], axis=0)
-        high, rest = split(field)
-        both = jnp.concatenate([high, rest], axis=1)
-        both = jnp.concatenate([both, both], axis=0)
-        sums = []
-        for index in range(2):
-            product = jnp.dot(w_ref[2 * step + index], both, preferred_element_type=F32)
-            sums.append(product[:, 0:LANES] + product[:, LANES : 2 * LANES])
-        by_real = jnp.where(even_wide, sums[0][:beams], sums[1][:beams])
-        by_imag = jnp.where(even_wide, sums[0][beams:], sums[1][beams:])
-        crossed = pltpu.roll(by_imag, 64, 1)
-        beam = by_real + jnp.where(wide < 64, -crossed, crossed)
+        beam = pair_beams(x_ref, w_ref, step)
+        if len(refs) == 4:
+            beam = beam + refs[2][step]
         high, rest = split(beam * beam)
         power = lax.dot_general(
             pool,
@@ -173,17 +206,12 @@
 
 
 def slots_of(devices):
-    dishes = np.zeros((2, devices, 6), np.int32)
-    for odd in range(2):
-        for dev in range(devices):
-            for pair in range(6):
-                own = pair * 2 + odd
-                dishes[odd, dev, pair] = (
-                    dev * 8 + own if own < 8 else devices * 8 + dev * 4 + own - 8
-                )
-    flat = dishes.reshape(-1)
-    none = np.full_like(flat, -1)
-    return np.stack([np.concatenate([flat, none]), np.concatenate([none, flat])], axis=1)
+    found, base = [], 0
+    for count in CHUNKS:
+        dishes = base + np.arange(count * devices, dtype=np.int32)
+        found.append(dishes.reshape(devices, count // 2, 2).transpose(2, 0, 1).reshape(-1))
+        base += count * devices
+    return np.concatenate(found)[:, None]
 
 
 def dft_parts(channels):
@@ -208,30 +236,50 @@
     frames_dev = samples.shape[2] // channels
     frames = frames_dev * devices
 
-    pieces = pl.pallas_call(
-        pieces_kernel,
-        out_shape=jax.ShapeDtypeStruct((devices, frames_dev, 24, channels), F32),
-        in_specs=[VMEM],
-        out_specs=VMEM,
-        name="pieces",
+    def exchange(value):
+        return lax.all_to_all(value, "band", split_axis=0, concat_axis=0, tiled=True)
+
+    eight = pl.pallas_call(
+        eight_kernel,
+        out_shape=jax.ShapeDtypeStruct((devices, frames_dev, 16, channels), F32),
+        in_specs=[pl.BlockSpec(memory_space=pl.ANY)],
+        out_specs=pl.BlockSpec(memory_space=pl.ANY),
+        scratch_shapes=[pltpu.SemaphoreType.DMA((frames_dev, 2))],
+        name="eight",
         compiler_params=GRANT,
     )(samples)
-    arrived = lax.all_to_all(pieces, "band", split_axis=0, concat_axis=0, tiled=True)
-
-    eight = lax.dynamic_slice_in_dim(dish_filter, position * 8, 8, 2)
-    four = lax.dynamic_slice_in_dim(dish_filter, devices * 8 + position * 4, 4, 2)
-    taps = jnp.concatenate([eight, eight, four, four], axis=2)
-    taps = jnp.transpose(taps, (1, 0, 2, 3))
+    eight = exchange(eight)
+    rest = dishes - devices * 8
+    four = pl.pallas_call(
+        four_kernel,
+        grid=(1,),
+        out_shape=jax.ShapeDtypeStruct((devices, frames_dev, 8, channels), F32),
+        in_specs=[
+            pl.BlockSpec((2, rest, samples.shape[2]), lambda i: (0, devices * 8 // rest, 0))
+        ],
+        out_specs=pl.BlockSpec((devices, frames_dev, 8, channels), lambda i: (0, 0, 0, 0)),
+        name="four",
+        compiler_params=GRANT,
+    )(samples)
+    four = exchange(four)
+    arrived = [eight, four]
+
     weights = pl.pallas_call(
         weights_kernel,
         grid=(band_chans,),
-        out_shape=jax.ShapeDtypeStruct((band_chans, 2 * beams, 2 * dishes), BF16),
+        out_shape=[
+            jax.ShapeDtypeStruct((band_chans, 2 * beams, 2 * count * devices), BF16)
+            for count in CHUNKS
+        ],
         in_specs=[
             pl.BlockSpec((1, 2, dishes, beams), lambda i: (i, 0, 0, 0)),
             pl.BlockSpec((1, dishes), lambda i: (0, 0)),
-            pl.BlockSpec((2 * dishes, 2), lambda i: (0, 0)),
+            pl.BlockSpec((dishes, 1), lambda i: (0, 0)),
         ],
-        out_specs=pl.BlockSpec((1, 2 * beams, 2 * dishes), lambda i: (i, 0, 0)),
+        out_specs=[
+            pl.BlockSpec((1, 2 * beams, 2 * count * devices), lambda i: (i, 0, 0))
+            for count in CHUNKS
+        ],
         name="weights",
         compiler_params=GRANT,
         cost_estimate=pl.CostEstimate(
@@ -239,31 +287,45 @@
         ),
     )(beam_weights[0], dish_order.reshape(1, dishes), slots_of(devices))
 
-    filtered = pl.pallas_call(
-        channel_kernel,
-        out_shape=jax.ShapeDtypeStruct((devices, 6 * band_chans, channels), F32),
-        in_specs=[VMEM] * 4,
-        out_specs=VMEM,
-        scratch_shapes=[
-            pltpu.VMEM((frames, 24, 2 * LANES), F32),
-            pltpu.VMEM((frames + fir_count - 1, 24, 2 * LANES), F32),
-            pltpu.VMEM((frames * 24, LANES), F32),
-        ],
-        name="channels",
-        compiler_params=GRANT,
-    )(arrived.reshape(frames, 24, channels), prototype, dft_parts(channels), taps)
-    field = lax.all_to_all(filtered, "band", split_axis=0, concat_axis=0, tiled=True)
-    field = field.reshape(devices * 6 * band_chans, channels)
-
-    power = pl.pallas_call(
-        beams_kernel,
-        out_shape=jax.ShapeDtypeStruct((band_chans, frames // INTEG, beams), F32),
-        in_specs=[VMEM] * 2,
-        out_specs=VMEM,
-        name="beams",
-        compiler_params=GRANT,
-    )(field, weights)
-    return jnp.transpose(power, (0, 2, 1))[None]
+    table = dft_parts(channels)
+    fields, base = [], 0
+    for count, value in zip(CHUNKS, arrived):
+        height = 2 * count
+        taps = lax.dynamic_slice_in_dim(dish_filter, base + position * count, count, 2)
+        taps = jnp.transpose(jnp.concatenate([taps, taps], axis=2), (1, 0, 2, 3))
+        base += count * devices
+        filtered = pl.pallas_call(
+            channel_kernel,
+            out_shape=jax.ShapeDtypeStruct(
+                (devices, count // 2 * band_chans, channels), F32
+            ),
+            in_specs=[pl.BlockSpec(memory_space=pl.ANY)] + [VMEM] * 4,
+            out_specs=VMEM,
+            scratch_shapes=[
+                pltpu.VMEM((frames, height, 2 * LANES), F32),
+                pltpu.VMEM((frames + fir_count - 1, height, 2 * LANES), F32),
+                pltpu.VMEM((frames * height, LANES), F32),
+            ],
+            name=f"channels_of_{count}",
+            compiler_params=GRANT,
+        )(weights[-1], value.reshape(frames, height, channels), prototype, table, taps)
+        fields.append(exchange(filtered))
+
+    partial = []
+    for index, count in enumerate(CHUNKS):
+        last = index + 1 == len(CHUNKS)
+        shape = (band_chans, frames // INTEG, beams) if last else (band_chans // 2, beams, LANES)
+        partial = [
+            pl.pallas_call(
+                power_kernel if last else beams_kernel,
+                out_shape=jax.ShapeDtypeStruct(shape, F32),
+                in_specs=[VMEM] * (2 + len(partial)),
+                out_specs=VMEM,
+                name="power" if last else f"beams_{index}",
+                compiler_params=GRANT,
+            )(fields[index].reshape(-1, channels), weights[index], *partial)
+        ]
+    return jnp.transpose(partial[0], (0, 2, 1))[None]
 
 
 def detect(weights, field_real, field_imag):

time: 43.9 us -> 62 us (1.41)
  starting transfers between devices: 11.1 us -> 20.4 us
  waiting for transfers between devices: 15.2 us -> 22.9 us
    all_to_all x2 -> x4, starting transfers between devices: 11.1 us -> 20.4 us  [exchange(): lax.all_to_all(value, 'band', split_axis=0, concat_axis=0, tiled=True)]
    all_to_all x2 -> x4, waiting for transfers between devices: 15.2 us -> 22.9 us  [exchange(): lax.all_to_all(value, 'band', split_axis=0, concat_axis=0, tiled=True)]
    unnamed x18 -> x20, local copies, waits for them, and re-layouts: 6.1 us -> 6.57 us
    pallas_call x4 -> x7, Pallas kernels: 10.9 us -> 11.3 us  [the longest x1 4.39 us: close_body(): pl.pallas_call(weights_kernel, grid=(band_chans,), out_shape=[jax.ShapeDt...]
  transfers between devices with their start and end apart: 2 -> 4, of which waited for: 2 -> 3; matrix products, arithmetic and copies ran while one was open for 0% -> 0% of each run, Pallas kernels for 13% -> 14%
where the time goes in v4:
time: 62 us; the launch traced here: 61.4 us
  waiting for transfers between devices  22.9 us (37%)
  starting transfers between devices  20.4 us (33%)
  Pallas kernels  11.3 us (18%)
  local copies, waits for them, and re-layouts  6.6 us (11%)
    all_to_all x4, waiting for transfers between devices, exchange(): lax.all_to_all(value, 'band', split_axis=0, concat_axis=0, tiled=True)  22.9 us
    all_to_all x4, starting transfers between devices, exchange(): lax.all_to_all(value, 'band', split_axis=0, concat_axis=0, tiled=True)  20.4 us
    unnamed x20, local copies, waits for them, and re-layouts  6.57 us
    pallas_call x1, Pallas kernels, close_body(): pl.pallas_call(weights_kernel, grid=(band_chans,), out_shape=[jax.ShapeDt...  4.39 us
    pallas_call x2, Pallas kernels, close_body(): pl.pallas_call(power_kernel if last else beams_kernel, out_shape=jax.Shap...  2.82 us
    pallas_call x2, Pallas kernels, close_body(): pl.pallas_call(channel_kernel, out_shape=jax.ShapeDtypeStruct((devices, c...  2.65 us
  transfers between devices with their start and end apart: 4, of which 3 were waited for; matrix products, arithmetic and copies ran while one was open for 0% of the time, Pallas kernels for 14%

profile of v4, /device:TPU:0, one launch (start us, length us, event | category | flops | bytes accessed | tf_op | source)
XLA Modules:
  0.0 61.4 jit_solution(5272487165891723496)
XLA Ops:
  0.0 0.0 copy-start
  0.0 0.0 copy-start.1
  0.0 1.1 %copy-done.1 = f32[2,192,256]{2,1,0:T(8,128)S(1)} copy-done((f32[2,192,256]{2,1,0:T(8,128)S(1)}, f32[2,192,256]{2,1,0:T(8,128)}, u32[]{:S(2)}) %copy-start.1) | copy-done | bytes 393240
  1.1 0.0 copy-start.8
  1.1 0.0 copy-start.9
  1.1 0.8 %eight.1 = f32[16,2,16,128]{3,2,1,0:T(8,128)} custom-call(f32[2,192,256]{2,1,0:T(8,128)S(1)} %copy-done.1), custom_call_target="tpu_custom_call" | custom-call | tf_op jit(solution)/shard_map/eight/pallas_call | solution.py:242
  1.9 7.4 %all-to-all-start.2 = ((f32[16,2,16,128]{3,2,1,0:T(8,128)}), f32[16,2,16,128]{3,2,1,0:T(8,128)S(1)}, u32[]{:S(2)}, u32[]{:S(2)}) async-start(f32[16,2,16,128]{3,2,1,0:T(8,128)} %eight.1), calls=%async_computation.2 | async-start | bytes 524288 | tf_op jit(solution)/shard_map/all_to_all | solution.py:240
  9.3 0.0 copy-start.2
  9.3 1.0 %copy-done.2 = f32[2,192,256]{2,1,0:T(8,128)S(1)} copy-done((f32[2,192,256]{2,1,0:T(8,128)S(1)}, f32[2,192,256]{2,1,0:T(8,128)}, u32[]{:S(2)}) %copy-start.2) | copy-done | bytes 393240
  10.3 0.7 %four.1 = f32[16,2,8,128]{3,2,1,0:T(8,128)} custom-call(f32[2,192,256]{2,1,0:T(8,128)S(1)} %copy-done.2), custom_call_target="tpu_custom_call" | custom-call | tf_op jit(solution)/shard_map/four/pallas_call | solution.py:253
  11.0 8.4 %all-to-all-done.2 = f32[16,2,16,128]{3,2,1,0:T(8,128)S(1)} async-done(((f32[16,2,16,128]{3,2,1,0:T(8,128)}), f32[16,2,16,128]{3,2,1,0:T(8,128)S(1)}, u32[]{:S(2)}, u32[]{:S(2)}) %all-to-all-start.2) | async-done | bytes 262176 | tf_op jit(solution)/shard_map/all_to_all | solution.py:240
  19.3 3.5 %all-to-all-start = ((f32[16,2,8,128]{3,2,1,0:T(8,128)}), f32[16,2,8,128]{3,2,1,0:T(8,128)S(1)}, u32[]{:S(2)}, u32[]{:S(2)}) async-start(f32[16,2,8,128]{3,2,1,0:T(8,128)} %four.1), calls=%async_computation | async-start | bytes 262144 | tf_op jit(solution)/shard_map/all_to_all | solution.py:240
  22.9 0.0 copy-done.8
  22.9 0.0 copy-done.9
  22.9 0.0 copy-start.7
  22.9 1.9 %copy-done.7 = f32[1,8,2,192,192]{4,3,2,1,0:T(8,128)S(1)} copy-done((f32[1,8,2,192,192]{4,3,2,1,0:T(8,128)S(1)}, f32[1,8,2,192,192]{4,3,2,1,0:T(8,128)}, u32[]{:S(2)}) %copy-start.7) | copy-done | bytes 2359320
  24.8 0.0 copy-start.3
  24.8 0.0 copy-start.6
  24.8 4.4 %weights.1 = (bf16[8,384,256]{2,1,0:T(8,128)(2,1)S(1)}, bf16[8,384,128]{2,1,0:T(8,128)(2,1)S(1)}) custom-call(f32[8,2,192,192]{3,2,1,0:T(8,128)S(1)} %bitcast.17, s32[1,192]{1,0:T(1,128)S(1)} %bitcast.18, s32[192,1]{1,0:T(8,128)S(1)} %copy-done.9), custom_call_target="tpu_custom_call" | custom-call | flops 905969664 | bytes 5242880 | tf_op jit(solution)/shard_map/weights/pallas_call | solution.py:267
  29.2 0.0 copy-start.4
  29.2 1.2 %copy-done.4 = bf16[8,384,256]{2,1,0:T(8,128)(2,1)} copy-done((bf16[8,384,256]{2,1,0:T(8,128)(2,1)}, bf16[8,384,256]{2,1,0:T(8,128)(2,1)S(1)}, u32[]{:S(2)}) %copy-start.4) | copy-done | bytes 1572888
  30.3 0.0 copy-done
  30.4 0.0 copy-done.3
  30.4 0.0 copy-done.6
  30.4 1.4 %channels_of_8.1 = f32[16,32,128]{2,1,0:T(8,128)} custom-call(bf16[8,384,128]{2,1,0:T(8,128)(2,1)S(1)} %get-tuple-element.7.after_ref.refs_1_, f32[32,16,128]{2,1,0:T(8,128)S(1)} %bitcast.13, f32[16,128]{1,0:T(8,128)S(1)} %copy-done.6, bf16[768,256]{1,0:T(8,128)(2,1)S(1)} %copy-done.3, f32[8,2,16,128]{3,2,1,0:T(8,128)S(1)} %copy_bitcast_fusion.taps_ref), custom_call_target="tpu_custom_call" | custom-call | tf_op jit(solution)/shard_map/channels_of_8/pallas_call | solution.py:297
  31.8 0.0 all-to-all-done
  31.8 6.0 %all-to-all-start.3 = ((f32[16,32,128]{2,1,0:T(8,128)}), f32[16,32,128]{2,1,0:T(8,128)S(1)}, u32[]{:S(2)}, u32[]{:S(2)}) async-start(f32[16,32,128]{2,1,0:T(8,128)} %channels_of_8.1), calls=%async_computation.3 | async-start | bytes 524288 | tf_op jit(solution)/shard_map/all_to_all | solution.py:240
  37.9 1.2 %channels_of_4.1 = f32[16,16,128]{2,1,0:T(8,128)} custom-call(bf16[8,384,128]{2,1,0:T(8,128)(2,1)S(1)} %get-tuple-element.7.after_ref.refs_1_, f32[32,8,128]{2,1,0:T(8,128)S(1)} %bitcast.15, f32[16,128]{1,0:T(8,128)S(1)} %copy-done.6, bf16[768,256]{1,0:T(8,128)(2,1)S(1)} %copy-done.3, f32[8,2,8,128]{3,2,1,0:T(8,128)S(1)} %copy_bitcast_fusion.1.taps_ref), custom_call_target="tpu_custom_call" | custom-call | tf_op jit(solution)/shard_map/channels_of_4/pallas_call | solution.py:297
  39.1 8.8 %all-to-all-done.3 = f32[16,32,128]{2,1,0:T(8,128)S(1)} async-done(((f32[16,32,128]{2,1,0:T(8,128)}), f32[16,32,128]{2,1,0:T(8,128)S(1)}, u32[]{:S(2)}, u32[]{:S(2)}) %all-to-all-start.3) | async-done | bytes 262176 | tf_op jit(solution)/shard_map/all_to_all | solution.py:240
  47.9 3.5 %all-to-all-start.1 = ((f32[16,16,128]{2,1,0:T(8,128)}), f32[16,16,128]{2,1,0:T(8,128)S(1)}, u32[]{:S(2)}, u32[]{:S(2)}) async-start(f32[16,16,128]{2,1,0:T(8,128)} %channels_of_4.1), calls=%async_computation.1 | async-start | bytes 262144 | tf_op jit(solution)/shard_map/all_to_all | solution.py:240
  51.4 0.0 copy-start.5
  51.4 1.4 %copy-done.5 = bf16[8,384,256]{2,1,0:T(8,128)(2,1)S(1)} copy-done((bf16[8,384,256]{2,1,0:T(8,128)(2,1)S(1)}, bf16[8,384,256]{2,1,0:T(8,128)(2,1)}, u32[]{:S(2)}) %copy-start.5) | copy-done | bytes 1572888
  52.8 0.7 %beams_0.1.refs_2_ = f32[4,192,128]{2,1,0:T(8,128)S(1)} custom-call(f32[512,128]{1,0:T(8,128)S(1)} %bitcast.14, bf16[8,384,256]{2,1,0:T(8,128)(2,1)S(1)} %copy-done.5), custom_call_target="tpu_custom_call" | custom-call | tf_op jit(solution)/shard_map/beams_0/pallas_call | solution.py:319
  53.5 5.8 %all-to-all-done.1 = f32[16,16,128]{2,1,0:T(8,128)S(1)} async-done(((f32[16,16,128]{2,1,0:T(8,128)}), f32[16,16,128]{2,1,0:T(8,128)S(1)}, u32[]{:S(2)}, u32[]{:S(2)}) %all-to-all-start.1) | async-done | bytes 131104 | tf_op jit(solution)/shard_map/all_to_all | solution.py:240
  59.3 2.1 %power.1 = f32[8,8,192]{2,1,0:T(8,128)} custom-call(f32[256,128]{1,0:T(8,128)S(1)} %bitcast.16, bf16[8,384,128]{2,1,0:T(8,128)(2,1)S(1)} %get-tuple-element.7.after_ref.refs_1_, f32[4,192,128]{2,1,0:T(8,128)S(1)} %beams_0.1.refs_2_), custom_call_target="tpu_custom_call" | custom-call | tf_op jit(solution)/shard_map/power/pallas_call | solution.py:319
  (4 shorter events, 0.1 us)
Async XLA Ops:
  0.0 30.4 %copy-start = (f32[2,8,192,128]{3,2,1,0:T(8,128)S(1)}, f32[2,8,192,128]{3,2,1,0:T(8,128)}, u32[]{:S(2)}) copy-start(f32[2,8,192,128]{3,2,1,0:T(8,128)} %param.9) | copy-start | bytes 4718596
  0.0 1.1 %copy-start.1 = (f32[2,192,256]{2,1,0:T(8,128)S(1)}, f32[2,192,256]{2,1,0:T(8,128)}, u32[]{:S(2)}) copy-start(f32[2,192,256]{2,1,0:T(8,128)} %x_ref.3) | copy-start | bytes 1179652
  1.1 21.7 %copy-start.8 = (s32[192]{0:T(256)S(1)}, s32[192]{0:T(256)}, u32[]{:S(2)}) copy-start(s32[192]{0:T(256)} %param.11) | copy-start | bytes 2308
  1.1 21.7 %copy-start.9 = (s32[192,1]{1,0:T(8,128)S(1)}, s32[192,1]{1,0:T(8,128)}, u32[]{:S(2)}) copy-start(s32[192,1]{1,0:T(8,128)} %constant.20.clone.slot_ref) | copy-start | bytes 2308
  1.9 17.5 %all-to-all-start.2 = ((f32[16,2,16,128]{3,2,1,0:T(8,128)}), f32[16,2,16,128]{3,2,1,0:T(8,128)S(1)}, u32[]{:S(2)}, u32[]{:S(2)}) async-start(f32[16,2,16,128]{3,2,1,0:T(8,128)} %eight.1), calls=%async_computation.2 | async-start | bytes 524288 | tf_op jit(solution)/shard_map/all_to_all | solution.py:240
  9.3 1.0 %copy-start.2 = (f32[2,192,256]{2,1,0:T(8,128)S(1)}, f32[2,192,256]{2,1,0:T(8,128)}, u32[]{:S(2)}) copy-start(f32[2,192,256]{2,1,0:T(8,128)} %x_ref.3) | copy-start | bytes 1179652
  19.3 12.5 %all-to-all-start = ((f32[16,2,8,128]{3,2,1,0:T(8,128)}), f32[16,2,8,128]{3,2,1,0:T(8,128)S(1)}, u32[]{:S(2)}, u32[]{:S(2)}) async-start(f32[16,2,8,128]{3,2,1,0:T(8,128)} %four.1), calls=%async_computation | async-start | bytes 262144 | tf_op jit(solution)/shard_map/all_to_all | solution.py:240
  22.9 1.9 %copy-start.7 = (f32[1,8,2,192,192]{4,3,2,1,0:T(8,128)S(1)}, f32[1,8,2,192,192]{4,3,2,1,0:T(8,128)}, u32[]{:S(2)}) copy-start(f32[1,8,2,192,192]{4,3,2,1,0:T(8,128)} %param.10) | copy-start | bytes 7077892
  24.8 5.6 %copy-start.3 = (bf16[768,256]{1,0:T(8,128)(2,1)S(1)}, bf16[768,256]{1,0:T(8,128)(2,1)}, u32[]{:S(2)}) copy-start(bf16[768,256]{1,0:T(8,128)(2,1)} %constant.21.clone.table_ref) | copy-start | bytes 1179652
  24.8 5.6 %copy-start.6 = (f32[16,128]{1,0:T(8,128)S(1)}, f32[16,128]{1,0:T(8,128)}, u32[]{:S(2)}) copy-start(f32[16,128]{1,0:T(8,128)} %proto_ref.3) | copy-start | bytes 24580
  29.2 1.2 %copy-start.4 = (bf16[8,384,256]{2,1,0:T(8,128)(2,1)}, bf16[8,384,256]{2,1,0:T(8,128)(2,1)S(1)}, u32[]{:S(2)}) copy-start(bf16[8,384,256]{2,1,0:T(8,128)(2,1)S(1)} %get-tuple-element.8.refs_1_) | copy-start | bytes 4718596
  31.8 16.0 %all-to-all-start.3 = ((f32[16,32,128]{2,1,0:T(8,128)}), f32[16,32,128]{2,1,0:T(8,128)S(1)}, u32[]{:S(2)}, u32[]{:S(2)}) async-start(f32[16,32,128]{2,1,0:T(8,128)} %channels_of_8.1), calls=%async_computation.3 | async-start | bytes 524288 | tf_op jit(solution)/shard_map/all_to_all | solution.py:240
  47.9 11.4 %all-to-all-start.1 = ((f32[16,16,128]{2,1,0:T(8,128)}), f32[16,16,128]{2,1,0:T(8,128)S(1)}, u32[]{:S(2)}, u32[]{:S(2)}) async-start(f32[16,16,128]{2,1,0:T(8,128)} %channels_of_4.1), calls=%async_computation.1 | async-start | bytes 262144 | tf_op jit(solution)/shard_map/all_to_all | solution.py:240
  51.4 1.4 %copy-start.5 = (bf16[8,384,256]{2,1,0:T(8,128)(2,1)S(1)}, bf16[8,384,256]{2,1,0:T(8,128)(2,1)}, u32[]{:S(2)}) copy-start(bf16[8,384,256]{2,1,0:T(8,128)(2,1)} %copy-done.4) | copy-start | bytes 4718596

commit v5 on v3

--- a/solution.py
+++ b/solution.py
@@ -14,6 +14,7 @@
 BF16 = jnp.bfloat16
 LANES = 128
 VMEM = pl.BlockSpec(memory_space=pltpu.VMEM)
+HBM = pl.BlockSpec(memory_space=pltpu.HBM)
 GRANT = pltpu.CompilerParams(vmem_limit_bytes=16 << 20)
 
 
@@ -34,22 +35,38 @@
     return part * 8 + dish if dish < 8 else 16 + part * 4 + dish - 8
 
 
-def pieces_kernel(x_ref, out_ref):
+def pieces_kernel(x_ref, out_ref, rest, four, tile_sems, rest_sem, four_sem):
     devices, frames_dev = out_ref.shape[:2]
     low = lax.broadcasted_iota(jnp.int32, (8, LANES), 0) < 4
+    load = pltpu.make_async_copy(x_ref.at[:, devices * 8 :, :], rest, rest_sem)
+    load.start()
+    tiles = x_ref.reshape(2, x_ref.shape[1] // 8, 8, x_ref.shape[2])
+    moves = []
+    for frame in range(frames_dev):
+        lanes = slice(frame * LANES, (frame + 1) * LANES)
+        for part in range(2):
+            moves.append(
+                pltpu.make_async_copy(
+                    tiles.at[part, 0:devices, :, lanes],
+                    out_ref.at[:, frame, part * 8 : part * 8 + 8, :],
+                    tile_sems.at[frame, part],
+                )
+            )
+    for move in moves:
+        move.start()
+    load.wait()
     for frame in range(frames_dev):
         lanes = slice(frame * LANES, (frame + 1) * LANES)
         for dev in range(0, devices, 2):
-            for one in (dev, dev + 1):
-                for part in range(2):
-                    out_ref[one, frame, part * 8 : part * 8 + 8, :] = x_ref[
-                        part, one * 8 : one * 8 + 8, lanes
-                    ]
-            start = devices * 8 + dev * 4
-            real = x_ref[0, start : start + 8, lanes]
-            imag = x_ref[1, start : start + 8, lanes]
-            out_ref[dev, frame, 16:24, :] = jnp.where(low, real, pltpu.roll(imag, 4, 0))
-            out_ref[dev + 1, frame, 16:24, :] = jnp.where(low, pltpu.roll(real, 4, 0), imag)
+            real = rest[0, dev * 4 : dev * 4 + 8, lanes]
+            imag = rest[1, dev * 4 : dev * 4 + 8, lanes]
+            four[dev, frame] = jnp.where(low, real, pltpu.roll(imag, 4, 0))
+            four[dev + 1, frame] = jnp.where(low, pltpu.roll(real, 4, 0), imag)
+    store = pltpu.make_async_copy(four, out_ref.at[:, :, 16:24, :], four_sem)
+    store.start()
+    for move in moves:
+        move.wait()
+    store.wait()
 
 
 def weights_kernel(w_ref, order_ref, slot_ref, out_ref):
@@ -134,7 +151,15 @@
             ]
 
 
-def beams_kernel(x_ref, w_ref, out_ref):
+def beams_kernel(x_ref, w_hbm, out_ref, w_ref, sems):
+    loads = [
+        pltpu.make_async_copy(
+            w_hbm.at[2 * step : 2 * step + 2], w_ref.at[2 * step : 2 * step + 2], sems.at[step]
+        )
+        for step in range(w_hbm.shape[0] // 2)
+    ]
+    for load in loads:
+        load.start()
     rows = x_ref.shape[0] // 8
     beams = w_ref.shape[1] // 2
     lane = lax.broadcasted_iota(jnp.int32, (rows, LANES), 1)
@@ -153,6 +178,7 @@
         high, rest = split(field)
         both = jnp.concatenate([high, rest], axis=1)
         both = jnp.concatenate([both, both], axis=0)
+        loads[step].wait()
         sums = []
         for index in range(2):
             product = jnp.dot(w_ref[2 * step + index], both, preferred_element_type=F32)
@@ -211,8 +237,15 @@
     pieces = pl.pallas_call(
         pieces_kernel,
         out_shape=jax.ShapeDtypeStruct((devices, frames_dev, 24, channels), F32),
-        in_specs=[VMEM],
-        out_specs=VMEM,
+        in_specs=[HBM],
+        out_specs=HBM,
+        scratch_shapes=[
+            pltpu.VMEM((2, dishes - devices * 8, frames_dev * channels), F32),
+            pltpu.VMEM((devices, frames_dev, 8, channels), F32),
+            pltpu.SemaphoreType.DMA((frames_dev, 2)),
+            pltpu.SemaphoreType.DMA(()),
+            pltpu.SemaphoreType.DMA(()),
+        ],
         name="pieces",
         compiler_params=GRANT,
     )(samples)
@@ -258,8 +291,12 @@
     power = pl.pallas_call(
         beams_kernel,
         out_shape=jax.ShapeDtypeStruct((band_chans, frames // INTEG, beams), F32),
-        in_specs=[VMEM] * 2,
+        in_specs=[VMEM, HBM],
         out_specs=VMEM,
+        scratch_shapes=[
+            pltpu.VMEM(weights.shape, BF16),
+            pltpu.SemaphoreType.DMA((band_chans // 2,)),
+        ],
         name="beams",
         compiler_params=GRANT,
     )(field, weights)

time: 43.9 us -> 44.9 us (1.023)
  Pallas kernels: 10.9 us -> 11.9 us
    pallas_call x1, Pallas kernels: 2.6 us -> 3.49 us  [close_body(): pl.pallas_call(beams_kernel, out_shape=jax.ShapeDtypeStruct((band_chans,...]
where the time goes in v5:
time: 44.9 us; the launch traced here: 44.5 us
  waiting for transfers between devices  15.2 us (34%)
  Pallas kernels  11.9 us (27%)
  starting transfers between devices  11.1 us (25%)
  local copies, waits for them, and re-layouts  6.14 us (14%)
    all_to_all x1, waiting for transfers between devices, close_body(): lax.all_to_all(pieces, 'band', split_axis=0, concat_axis=0, tiled=True)  12.1 us
    all_to_all x1, starting transfers between devices, close_body(): lax.all_to_all(pieces, 'band', split_axis=0, concat_axis=0, tiled=True)  7.53 us
    unnamed x18, local copies, waits for them, and re-layouts  6.1 us
    pallas_call x1, Pallas kernels, close_body(): pl.pallas_call(weights_kernel, grid=(band_chans,), out_shape=jax.ShapeDty...  5.69 us
    all_to_all x1, starting transfers between devices, close_body(): lax.all_to_all(filtered, 'band', split_axis=0, concat_axis=0, tiled=True)  3.55 us
    pallas_call x1, Pallas kernels, close_body(): pl.pallas_call(beams_kernel, out_shape=jax.ShapeDtypeStruct((band_chans,...  3.49 us
    all_to_all x1, waiting for transfers between devices, close_body(): lax.all_to_all(filtered, 'band', split_axis=0, concat_axis=0, tiled=True)  3.14 us
    pallas_call x1, Pallas kernels, close_body(): pl.pallas_call(channel_kernel, out_shape=jax.ShapeDtypeStruct((devices, 6...  1.86 us
  transfers between devices with their start and end apart: 2, of which 2 were waited for; matrix products, arithmetic and copies ran while one was open for 0% of the time, Pallas kernels for 13%

profile of v5, /device:TPU:0, one launch (start us, length us, event | category | flops | bytes accessed | tf_op | source)
XLA Modules:
  0.0 44.5 jit_solution(1109306859485300534)
XLA Ops:
  0.0 0.0 copy-start
  0.0 0.0 copy-start.4
  0.0 1.1 %copy-done.4 = f32[2,192,256]{2,1,0:T(8,128)S(1)} copy-done((f32[2,192,256]{2,1,0:T(8,128)S(1)}, f32[2,192,256]{2,1,0:T(8,128)}, u32[]{:S(2)}) %copy-start.4) | copy-done | bytes 393240
  1.1 0.0 copy-start.5
  1.1 0.0 copy-start.7
  1.1 0.9 %pieces.1 = f32[16,2,24,128]{3,2,1,0:T(8,128)} custom-call(f32[2,192,256]{2,1,0:T(8,128)S(1)} %copy-done.4), custom_call_target="tpu_custom_call" | custom-call | tf_op jit(solution)/shard_map/pieces/pallas_call | solution.py:237
  2.0 0.0 copy-start.6
  2.0 0.0 copy-start.8
  2.0 7.5 %all-to-all-start = ((f32[16,2,24,128]{3,2,1,0:T(8,128)}), f32[16,2,24,128]{3,2,1,0:T(8,128)S(1)}, u32[]{:S(2)}, u32[]{:S(2)}) async-start(f32[16,2,24,128]{3,2,1,0:T(8,128)} %pieces.1), calls=%async_computation | async-start | bytes 786432 | tf_op jit(solution)/shard_map/all_to_all | solution.py:252
  9.6 0.0 copy-done
  9.7 12.1 %all-to-all-done = f32[16,2,24,128]{3,2,1,0:T(8,128)S(1)} async-done(((f32[16,2,24,128]{3,2,1,0:T(8,128)}), f32[16,2,24,128]{3,2,1,0:T(8,128)S(1)}, u32[]{:S(2)}, u32[]{:S(2)}) %all-to-all-start) | async-done | bytes 393248 | tf_op jit(solution)/shard_map/all_to_all | solution.py:252
  21.8 0.0 copy-done.5
  21.8 0.0 copy-done.7
  21.8 1.9 %channels.1 = f32[16,48,128]{2,1,0:T(8,128)} custom-call(f32[32,24,128]{2,1,0:T(8,128)S(1)} %bitcast.10, f32[16,128]{1,0:T(8,128)S(1)} %copy-done.7, bf16[768,256]{1,0:T(8,128)(2,1)S(1)} %copy-done.5, f32[8,2,24,128]{3,2,1,0:T(8,128)S(1)} %copy_bitcast_fusion.taps_ref), custom_call_target="tpu_custom_call" | custom-call | tf_op jit(solution)/shard_map/channels/pallas_call | solution.py:275
  23.6 3.6 %all-to-all-start.1 = ((f32[16,48,128]{2,1,0:T(8,128)}), f32[16,48,128]{2,1,0:T(8,128)S(1)}, u32[]{:S(2)}, u32[]{:S(2)}) async-start(f32[16,48,128]{2,1,0:T(8,128)} %channels.1), calls=%async_computation.1 | async-start | bytes 786432 | tf_op jit(solution)/shard_map/all_to_all | solution.py:288
  27.2 0.0 copy-done.6
  27.2 0.0 copy-done.8
  27.2 0.0 copy-start.3
  27.2 1.9 %copy-done.3 = f32[1,8,2,192,192]{4,3,2,1,0:T(8,128)S(1)} copy-done((f32[1,8,2,192,192]{4,3,2,1,0:T(8,128)S(1)}, f32[1,8,2,192,192]{4,3,2,1,0:T(8,128)}, u32[]{:S(2)}) %copy-start.3) | copy-done | bytes 2359320
  29.1 5.7 %weights.1.w_hbm = bf16[8,384,384]{2,1,0:T(8,128)(2,1)S(1)} custom-call(f32[8,2,192,192]{3,2,1,0:T(8,128)S(1)} %bitcast.9, s32[1,192]{1,0:T(1,128)S(1)} %bitcast.12, s32[384,2]{1,0:T(8,128)S(1)} %copy-done.6), custom_call_target="tpu_custom_call" | custom-call | flops 905969664 | bytes 5242880 | tf_op jit(solution)/shard_map/weights/pallas_call | solution.py:258
  34.8 0.0 copy-start.1
  34.8 1.4 %copy-done.1 = bf16[8,384,384]{2,1,0:T(8,128)(2,1)} copy-done((bf16[8,384,384]{2,1,0:T(8,128)(2,1)}, bf16[8,384,384]{2,1,0:T(8,128)(2,1)S(1)}, u32[]{:S(2)}) %copy-start.1) | copy-done | bytes 2359320
  36.2 3.1 %all-to-all-done.1 = f32[16,48,128]{2,1,0:T(8,128)S(1)} async-done(((f32[16,48,128]{2,1,0:T(8,128)}), f32[16,48,128]{2,1,0:T(8,128)S(1)}, u32[]{:S(2)}, u32[]{:S(2)}) %all-to-all-start.1) | async-done | bytes 393248 | tf_op jit(solution)/shard_map/all_to_all | solution.py:288
  39.4 0.0 copy-start.2
  39.4 1.7 %copy-done.2 = bf16[8,384,384]{2,1,0:T(8,128)(2,1)S(1)} copy-done((bf16[8,384,384]{2,1,0:T(8,128)(2,1)S(1)}, bf16[8,384,384]{2,1,0:T(8,128)(2,1)}, u32[]{:S(2)}) %copy-start.2) | copy-done | bytes 2359320
  41.0 3.5 %beams.1 = f32[8,8,192]{2,1,0:T(8,128)} custom-call(f32[768,128]{1,0:T(8,128)S(1)} %bitcast.11, bf16[8,384,384]{2,1,0:T(8,128)(2,1)S(1)} %copy-done.2), custom_call_target="tpu_custom_call" | custom-call | tf_op jit(solution)/shard_map/beams/pallas_call | solution.py:291
  (3 shorter events, 0.1 us)
Async XLA Ops:
  0.0 9.6 %copy-start = (f32[2,8,192,128]{3,2,1,0:T(8,128)S(1)}, f32[2,8,192,128]{3,2,1,0:T(8,128)}, u32[]{:S(2)}) copy-start(f32[2,8,192,128]{3,2,1,0:T(8,128)} %param.9) | copy-start | bytes 4718596
  0.0 1.1 %copy-start.4 = (f32[2,192,256]{2,1,0:T(8,128)S(1)}, f32[2,192,256]{2,1,0:T(8,128)}, u32[]{:S(2)}) copy-start(f32[2,192,256]{2,1,0:T(8,128)} %x_ref.1) | copy-start | bytes 1179652
  1.1 20.7 %copy-start.5 = (bf16[768,256]{1,0:T(8,128)(2,1)S(1)}, bf16[768,256]{1,0:T(8,128)(2,1)}, u32[]{:S(2)}) copy-start(bf16[768,256]{1,0:T(8,128)(2,1)} %constant.21.clone.table_ref) | copy-start | bytes 1179652
  1.1 20.7 %copy-start.7 = (f32[16,128]{1,0:T(8,128)S(1)}, f32[16,128]{1,0:T(8,128)}, u32[]{:S(2)}) copy-start(f32[16,128]{1,0:T(8,128)} %proto_ref.1) | copy-start | bytes 24580
  2.0 25.2 %copy-start.6 = (s32[384,2]{1,0:T(8,128)S(1)}, s32[384,2]{1,0:T(8,128)}, u32[]{:S(2)}) copy-start(s32[384,2]{1,0:T(8,128)} %constant.20.clone.slot_ref) | copy-start | bytes 9220
  2.0 25.2 %copy-start.8 = (s32[192]{0:T(256)S(1)}, s32[192]{0:T(256)}, u32[]{:S(2)}) copy-start(s32[192]{0:T(256)} %param.11) | copy-start | bytes 2308
  2.0 19.7 %all-to-all-start = ((f32[16,2,24,128]{3,2,1,0:T(8,128)}), f32[16,2,24,128]{3,2,1,0:T(8,128)S(1)}, u32[]{:S(2)}, u32[]{:S(2)}) async-start(f32[16,2,24,128]{3,2,1,0:T(8,128)} %pieces.1), calls=%async_computation | async-start | bytes 786432 | tf_op jit(solution)/shard_map/all_to_all | solution.py:252
  23.6 15.7 %all-to-all-start.1 = ((f32[16,48,128]{2,1,0:T(8,128)}), f32[16,48,128]{2,1,0:T(8,128)S(1)}, u32[]{:S(2)}, u32[]{:S(2)}) async-start(f32[16,48,128]{2,1,0:T(8,128)} %channels.1), calls=%async_computation.1 | async-start | bytes 786432 | tf_op jit(solution)/shard_map/all_to_all | solution.py:288
  27.2 1.9 %copy-start.3 = (f32[1,8,2,192,192]{4,3,2,1,0:T(8,128)S(1)}, f32[1,8,2,192,192]{4,3,2,1,0:T(8,128)}, u32[]{:S(2)}) copy-start(f32[1,8,2,192,192]{4,3,2,1,0:T(8,128)} %param.10) | copy-start | bytes 7077892
  34.8 1.4 %copy-start.1 = (bf16[8,384,384]{2,1,0:T(8,128)(2,1)}, bf16[8,384,384]{2,1,0:T(8,128)(2,1)S(1)}, u32[]{:S(2)}) copy-start(bf16[8,384,384]{2,1,0:T(8,128)(2,1)S(1)} %weights.1.w_hbm) | copy-start | bytes 7077892
  39.4 1.7 %copy-start.2 = (bf16[8,384,384]{2,1,0:T(8,128)(2,1)S(1)}, bf16[8,384,384]{2,1,0:T(8,128)(2,1)}, u32[]{:S(2)}) copy-start(bf16[8,384,384]{2,1,0:T(8,128)(2,1)} %copy-done.1) | copy-start | bytes 7077892

commit v6 on v5

--- a/solution.py
+++ b/solution.py
@@ -16,6 +16,7 @@
 VMEM = pl.BlockSpec(memory_space=pltpu.VMEM)
 HBM = pl.BlockSpec(memory_space=pltpu.HBM)
 GRANT = pltpu.CompilerParams(vmem_limit_bytes=16 << 20)
+LARGE_GRANT = pltpu.CompilerParams(vmem_limit_bytes=62_800_000)
 
 
 def fourier_tables(length):
@@ -247,7 +248,6 @@
             pltpu.SemaphoreType.DMA(()),
         ],
         name="pieces",
-        compiler_params=GRANT,
     )(samples)
     arrived = lax.all_to_all(pieces, "band", split_axis=0, concat_axis=0, tiled=True)
 
@@ -298,7 +298,7 @@
             pltpu.SemaphoreType.DMA((band_chans // 2,)),
         ],
         name="beams",
-        compiler_params=GRANT,
+        compiler_params=LARGE_GRANT,
     )(field, weights)
     return jnp.transpose(power, (0, 2, 1))[None]
 

time: 44.9 us -> 52.7 us (1.17)
  Pallas kernels: 11.9 us -> 21.7 us
  local copies, waits for them, and re-layouts: 6.14 us -> 4.09 us
    pallas_call x1, Pallas kernels: 0.89 us -> 9.1 us  [close_body(): pl.pallas_call(pieces_kernel, out_shape=jax.ShapeDtypeStruct((devices, fr...]
    unnamed x18 -> x16, local copies, waits for them, and re-layouts: 6.1 us -> 4.05 us
    pallas_call x1, Pallas kernels: 3.49 us -> 4.99 us  [close_body(): pl.pallas_call(beams_kernel, out_shape=jax.ShapeDtypeStruct((band_chans,...]
  transfers between devices with their start and end apart: 2 -> 2, of which waited for: 2 -> 2; matrix products, arithmetic and copies ran while one was open for 0% -> 0% of each run, Pallas kernels for 13% -> 11%
where the time goes in v6:
time: 52.7 us; the launch traced here: 52.3 us
  Pallas kernels  21.7 us (41%)
  waiting for transfers between devices  15.2 us (29%)
  starting transfers between devices  11.1 us (21%)
  local copies, waits for them, and re-layouts  4.09 us (8%)
    all_to_all x1, waiting for transfers between devices, close_body(): lax.all_to_all(pieces, 'band', split_axis=0, concat_axis=0, tiled=True)  12.1 us
    pallas_call x1, Pallas kernels, close_body(): pl.pallas_call(pieces_kernel, out_shape=jax.ShapeDtypeStruct((devices, fr...  9.1 us
    all_to_all x1, starting transfers between devices, close_body(): lax.all_to_all(pieces, 'band', split_axis=0, concat_axis=0, tiled=True)  7.54 us
    pallas_call x1, Pallas kernels, close_body(): pl.pallas_call(weights_kernel, grid=(band_chans,), out_shape=jax.ShapeDty...  5.69 us
    pallas_call x1, Pallas kernels, close_body(): pl.pallas_call(beams_kernel, out_shape=jax.ShapeDtypeStruct((band_chans,...  4.99 us
    unnamed x16, local copies, waits for them, and re-layouts  4.05 us
    all_to_all x1, starting transfers between devices, close_body(): lax.all_to_all(filtered, 'band', split_axis=0, concat_axis=0, tiled=True)  3.55 us
    all_to_all x1, waiting for transfers between devices, close_body(): lax.all_to_all(filtered, 'band', split_axis=0, concat_axis=0, tiled=True)  3.14 us
  transfers between devices with their start and end apart: 2, of which 2 were waited for; matrix products, arithmetic and copies ran while one was open for 0% of the time, Pallas kernels for 11%

profile of v6, /device:TPU:0, one launch (start us, length us, event | category | flops | bytes accessed | tf_op | source)
XLA Modules:
  0.0 52.3 jit_solution(11006220081004117120)
XLA Ops:
  0.0 0.0 copy-start
  0.0 0.0 copy-start.3
  0.0 0.0 copy-start.5
  0.0 9.1 %pieces.1 = f32[16,2,24,128]{3,2,1,0:T(8,128)} custom-call(f32[2,192,256]{2,1,0:T(8,128)} %x_ref.1), custom_call_target="tpu_custom_call" | custom-call | tf_op jit(solution)/shard_map/pieces/pallas_call | solution.py:238
  9.1 0.0 copy-start.4
  9.1 0.0 copy-start.6
  9.1 7.5 %all-to-all-start = ((f32[16,2,24,128]{3,2,1,0:T(8,128)}), f32[16,2,24,128]{3,2,1,0:T(8,128)S(1)}, u32[]{:S(2)}, u32[]{:S(2)}) async-start(f32[16,2,24,128]{3,2,1,0:T(8,128)} %pieces.1), calls=%async_computation | async-start | bytes 786432 | tf_op jit(solution)/shard_map/all_to_all | solution.py:252
  16.7 0.0 copy-done
  16.8 12.1 %all-to-all-done = f32[16,2,24,128]{3,2,1,0:T(8,128)S(1)} async-done(((f32[16,2,24,128]{3,2,1,0:T(8,128)}), f32[16,2,24,128]{3,2,1,0:T(8,128)S(1)}, u32[]{:S(2)}, u32[]{:S(2)}) %all-to-all-start) | async-done | bytes 393248 | tf_op jit(solution)/shard_map/all_to_all | solution.py:252
  28.9 0.0 copy-done.3
  28.9 0.0 copy-done.5
  28.9 1.9 %channels.1 = f32[16,48,128]{2,1,0:T(8,128)} custom-call(f32[32,24,128]{2,1,0:T(8,128)S(1)} %bitcast.10, f32[16,128]{1,0:T(8,128)S(1)} %copy-done.5, bf16[768,256]{1,0:T(8,128)(2,1)S(1)} %copy-done.3, f32[8,2,24,128]{3,2,1,0:T(8,128)S(1)} %copy_bitcast_fusion.taps_ref), custom_call_target="tpu_custom_call" | custom-call | tf_op jit(solution)/shard_map/channels/pallas_call | solution.py:275
  30.8 3.6 %all-to-all-start.1 = ((f32[16,48,128]{2,1,0:T(8,128)}), f32[16,48,128]{2,1,0:T(8,128)S(1)}, u32[]{:S(2)}, u32[]{:S(2)}) async-start(f32[16,48,128]{2,1,0:T(8,128)} %channels.1), calls=%async_computation.1 | async-start | bytes 786432 | tf_op jit(solution)/shard_map/all_to_all | solution.py:288
  34.4 0.0 copy-done.4
  34.4 0.0 copy-done.6
  34.4 0.0 copy-start.2
  34.4 1.9 %copy-done.2 = f32[1,8,2,192,192]{4,3,2,1,0:T(8,128)S(1)} copy-done((f32[1,8,2,192,192]{4,3,2,1,0:T(8,128)S(1)}, f32[1,8,2,192,192]{4,3,2,1,0:T(8,128)}, u32[]{:S(2)}) %copy-start.2) | copy-done | bytes 2359320
  36.3 5.7 %weights.1.w_hbm = bf16[8,384,384]{2,1,0:T(8,128)(2,1)S(1)} custom-call(f32[8,2,192,192]{3,2,1,0:T(8,128)S(1)} %bitcast.9, s32[1,192]{1,0:T(1,128)S(1)} %bitcast.11, s32[384,2]{1,0:T(8,128)S(1)} %copy-done.4), custom_call_target="tpu_custom_call" | custom-call | flops 905969664 | bytes 5242880 | tf_op jit(solution)/shard_map/weights/pallas_call | solution.py:258
  42.0 0.0 copy-start.1
  42.0 1.4 %copy-done.1 = bf16[8,384,384]{2,1,0:T(8,128)(2,1)} copy-done((bf16[8,384,384]{2,1,0:T(8,128)(2,1)}, bf16[8,384,384]{2,1,0:T(8,128)(2,1)S(1)}, u32[]{:S(2)}) %copy-start.1) | copy-done | bytes 2359320
  43.4 3.1 %all-to-all-done.1 = f32[16,48,128]{2,1,0:T(8,128)S(1)} async-done(((f32[16,48,128]{2,1,0:T(8,128)}), f32[16,48,128]{2,1,0:T(8,128)S(1)}, u32[]{:S(2)}, u32[]{:S(2)}) %all-to-all-start.1) | async-done | bytes 393248 | tf_op jit(solution)/shard_map/all_to_all | solution.py:288
  46.5 0.0 copy-start.7
  46.5 0.7 %copy-done.7 = f32[16,48,128]{2,1,0:T(8,128)} copy-done((f32[16,48,128]{2,1,0:T(8,128)}, f32[16,48,128]{2,1,0:T(8,128)S(1)}, u32[]{:S(2)}) %copy-start.7) | copy-done | bytes 393240
  47.3 5.0 %beams.1 = f32[8,8,192]{2,1,0:T(8,128)} custom-call(f32[768,128]{1,0:T(8,128)} %bitcast.12, bf16[8,384,384]{2,1,0:T(8,128)(2,1)} %copy-done.1), custom_call_target="tpu_custom_call" | custom-call | tf_op jit(solution)/shard_map/beams/pallas_call | solution.py:291
  (3 shorter events, 0.1 us)
Async XLA Ops:
  0.0 16.7 %copy-start = (f32[2,8,192,128]{3,2,1,0:T(8,128)S(1)}, f32[2,8,192,128]{3,2,1,0:T(8,128)}, u32[]{:S(2)}) copy-start(f32[2,8,192,128]{3,2,1,0:T(8,128)} %param.9) | copy-start | bytes 4718596
  0.0 28.9 %copy-start.3 = (bf16[768,256]{1,0:T(8,128)(2,1)S(1)}, bf16[768,256]{1,0:T(8,128)(2,1)}, u32[]{:S(2)}) copy-start(bf16[768,256]{1,0:T(8,128)(2,1)} %constant.21.clone.table_ref) | copy-start | bytes 1179652
  0.0 28.9 %copy-start.5 = (f32[16,128]{1,0:T(8,128)S(1)}, f32[16,128]{1,0:T(8,128)}, u32[]{:S(2)}) copy-start(f32[16,128]{1,0:T(8,128)} %proto_ref.1) | copy-start | bytes 24580
  9.1 25.3 %copy-start.4 = (s32[384,2]{1,0:T(8,128)S(1)}, s32[384,2]{1,0:T(8,128)}, u32[]{:S(2)}) copy-start(s32[384,2]{1,0:T(8,128)} %constant.20.clone.slot_ref) | copy-start | bytes 9220
  9.1 25.3 %copy-start.6 = (s32[192]{0:T(256)S(1)}, s32[192]{0:T(256)}, u32[]{:S(2)}) copy-start(s32[192]{0:T(256)} %param.11) | copy-start | bytes 2308
  9.1 19.7 %all-to-all-start = ((f32[16,2,24,128]{3,2,1,0:T(8,128)}), f32[16,2,24,128]{3,2,1,0:T(8,128)S(1)}, u32[]{:S(2)}, u32[]{:S(2)}) async-start(f32[16,2,24,128]{3,2,1,0:T(8,128)} %pieces.1), calls=%async_computation | async-start | bytes 786432 | tf_op jit(solution)/shard_map/all_to_all | solution.py:252
  30.8 15.7 %all-to-all-start.1 = ((f32[16,48,128]{2,1,0:T(8,128)}), f32[16,48,128]{2,1,0:T(8,128)S(1)}, u32[]{:S(2)}, u32[]{:S(2)}) async-start(f32[16,48,128]{2,1,0:T(8,128)} %channels.1), calls=%async_computation.1 | async-start | bytes 786432 | tf_op jit(solution)/shard_map/all_to_all | solution.py:288
  34.4 1.9 %copy-start.2 = (f32[1,8,2,192,192]{4,3,2,1,0:T(8,128)S(1)}, f32[1,8,2,192,192]{4,3,2,1,0:T(8,128)}, u32[]{:S(2)}) copy-start(f32[1,8,2,192,192]{4,3,2,1,0:T(8,128)} %param.10) | copy-start | bytes 7077892
  42.0 1.4 %copy-start.1 = (bf16[8,384,384]{2,1,0:T(8,128)(2,1)}, bf16[8,384,384]{2,1,0:T(8,128)(2,1)S(1)}, u32[]{:S(2)}) copy-start(bf16[8,384,384]{2,1,0:T(8,128)(2,1)S(1)} %weights.1.w_hbm) | copy-start | bytes 7077892
  46.5 0.7 %copy-start.7 = (f32[16,48,128]{2,1,0:T(8,128)}, f32[16,48,128]{2,1,0:T(8,128)S(1)}, u32[]{:S(2)}) copy-start(f32[16,48,128]{2,1,0:T(8,128)S(1)} %all-to-all-done.1) | copy-start | bytes 1179652

commit v7 on v5

--- a/solution.py
+++ b/solution.py
@@ -26,6 +26,9 @@
     return (jnp.cos(angles) * factor, jnp.sin(angles) * factor)
 
 
+held = pltpu.with_memory_space_constraint
+
+
 def split(value):
     high = value.astype(BF16)
     return high, (value - high.astype(F32)).astype(BF16)
@@ -35,26 +38,21 @@
     return part * 8 + dish if dish < 8 else 16 + part * 4 + dish - 8
 
 
-def pieces_kernel(x_ref, out_ref, rest, four, tile_sems, rest_sem, four_sem):
+def pieces_kernel(x_ref, out_ref, main, rest, four, in_sems, out_sems, four_sem):
     devices, frames_dev = out_ref.shape[:2]
     low = lax.broadcasted_iota(jnp.int32, (8, LANES), 0) < 4
-    load = pltpu.make_async_copy(x_ref.at[:, devices * 8 :, :], rest, rest_sem)
-    load.start()
-    tiles = x_ref.reshape(2, x_ref.shape[1] // 8, 8, x_ref.shape[2])
-    moves = []
-    for frame in range(frames_dev):
-        lanes = slice(frame * LANES, (frame + 1) * LANES)
-        for part in range(2):
-            moves.append(
-                pltpu.make_async_copy(
-                    tiles.at[part, 0:devices, :, lanes],
-                    out_ref.at[:, frame, part * 8 : part * 8 + 8, :],
-                    tile_sems.at[frame, part],
-                )
-            )
-    for move in moves:
-        move.start()
-    load.wait()
+    rests = [
+        pltpu.make_async_copy(x_ref.at[part, devices * 8 :], rest.at[part], in_sems.at[1, part])
+        for part in range(2)
+    ]
+    mains = [
+        pltpu.make_async_copy(x_ref.at[part, 0 : devices * 8], main.at[part], in_sems.at[0, part])
+        for part in range(2)
+    ]
+    for load in rests + mains:
+        load.start()
+    for load in rests:
+        load.wait()
     for frame in range(frames_dev):
         lanes = slice(frame * LANES, (frame + 1) * LANES)
         for dev in range(0, devices, 2):
@@ -62,11 +60,23 @@
             imag = rest[1, dev * 4 : dev * 4 + 8, lanes]
             four[dev, frame] = jnp.where(low, real, pltpu.roll(imag, 4, 0))
             four[dev + 1, frame] = jnp.where(low, pltpu.roll(real, 4, 0), imag)
-    store = pltpu.make_async_copy(four, out_ref.at[:, :, 16:24, :], four_sem)
-    store.start()
+    moves = [pltpu.make_async_copy(four, out_ref.at[:, :, 16:24, :], four_sem)]
+    moves[0].start()
+    tiles = main.reshape(2, devices, 8, main.shape[2])
+    for part in range(2):
+        mains[part].wait()
+        for frame in range(frames_dev):
+            lanes = slice(frame * LANES, (frame + 1) * LANES)
+            moves.append(
+                pltpu.make_async_copy(
+                    tiles.at[part, :, :, lanes],
+                    out_ref.at[:, frame, part * 8 : part * 8 + 8, :],
+                    out_sems.at[frame, part],
+                )
+            )
+            moves[-1].start()
     for move in moves:
         move.wait()
-    store.wait()
 
 
 def weights_kernel(w_ref, order_ref, slot_ref, out_ref):
@@ -240,15 +250,16 @@
         in_specs=[HBM],
         out_specs=HBM,
         scratch_shapes=[
+            pltpu.VMEM((2, devices * 8, frames_dev * channels), F32),
             pltpu.VMEM((2, dishes - devices * 8, frames_dev * channels), F32),
             pltpu.VMEM((devices, frames_dev, 8, channels), F32),
+            pltpu.SemaphoreType.DMA((2, 2)),
             pltpu.SemaphoreType.DMA((frames_dev, 2)),
-            pltpu.SemaphoreType.DMA(()),
             pltpu.SemaphoreType.DMA(()),
         ],
         name="pieces",
         compiler_params=GRANT,
-    )(samples)
+    )(held(samples, pltpu.HBM))
     arrived = lax.all_to_all(pieces, "band", split_axis=0, concat_axis=0, tiled=True)
 
     eight = lax.dynamic_slice_in_dim(dish_filter, position * 8, 8, 2)
@@ -284,7 +295,7 @@
         ],
         name="channels",
         compiler_params=GRANT,
-    )(arrived.reshape(frames, 24, channels), prototype, dft_parts(channels), taps)
+    )(held(arrived.reshape(frames, 24, channels), pltpu.VMEM), prototype, dft_parts(channels), taps)
     field = lax.all_to_all(filtered, "band", split_axis=0, concat_axis=0, tiled=True)
     field = field.reshape(devices * 6 * band_chans, channels)
 
@@ -299,7 +310,7 @@
         ],
         name="beams",
         compiler_params=GRANT,
-    )(field, weights)
+    )(held(field, pltpu.VMEM), held(weights, pltpu.HBM))
     return jnp.transpose(power, (0, 2, 1))[None]
 
 

time: 44.9 us -> 43.7 us (0.973)
  local copies, waits for them, and re-layouts: 6.14 us -> 3.35 us
  Pallas kernels: 11.9 us -> 13.5 us
    unnamed x18 -> x14, local copies, waits for them, and re-layouts: 6.1 us -> 3.31 us
    pallas_call x1, Pallas kernels: 0.89 us -> 1.91 us  [close_body(): pl.pallas_call(pieces_kernel, out_shape=jax.ShapeDtypeStruct((devices, fr...]
    pallas_call x1, Pallas kernels: 3.49 us -> 3.99 us  [close_body(): pl.pallas_call(beams_kernel, out_shape=jax.ShapeDtypeStruct((band_chans,...]
where the time goes in v7:
time: 43.7 us; the launch traced here: 43.3 us
  waiting for transfers between devices  15.3 us (35%)
  Pallas kernels  13.5 us (31%)
  starting transfers between devices  11.1 us (25%)
  local copies, waits for them, and re-layouts  3.35 us (8%)
    all_to_all x1, waiting for transfers between devices, close_body(): lax.all_to_all(pieces, 'band', split_axis=0, concat_axis=0, tiled=True)  12.1 us
    all_to_all x1, starting transfers between devices, close_body(): lax.all_to_all(pieces, 'band', split_axis=0, concat_axis=0, tiled=True)  7.53 us
    pallas_call x1, Pallas kernels, close_body(): pl.pallas_call(weights_kernel, grid=(band_chans,), out_shape=jax.ShapeDty...  5.69 us
    pallas_call x1, Pallas kernels, close_body(): pl.pallas_call(beams_kernel, out_shape=jax.ShapeDtypeStruct((band_chans,...  3.99 us
    all_to_all x1, starting transfers between devices, close_body(): lax.all_to_all(filtered, 'band', split_axis=0, concat_axis=0, tiled=True)  3.55 us
    unnamed x14, local copies, waits for them, and re-layouts  3.31 us
    all_to_all x1, waiting for transfers between devices, close_body(): lax.all_to_all(filtered, 'band', split_axis=0, concat_axis=0, tiled=True)  3.15 us
    pallas_call x1, Pallas kernels, close_body(): pl.pallas_call(pieces_kernel, out_shape=jax.ShapeDtypeStruct((devices, fr...  1.91 us
  transfers between devices with their start and end apart: 2, of which 2 were waited for; matrix products, arithmetic and copies ran while one was open for 0% of the time, Pallas kernels for 13%

profile of v7, /device:TPU:0, one launch (start us, length us, event | category | flops | bytes accessed | tf_op | source)
XLA Modules:
  0.0 43.3 jit_solution(3742915556907320321)
XLA Ops:
  0.0 0.0 copy-start
  0.0 0.0 copy-start.3
  0.0 0.0 copy-start.5
  0.0 1.9 %pieces.1 = f32[16,2,24,128]{3,2,1,0:T(8,128)} custom-call(f32[2,192,256]{2,1,0:T(8,128)} %x_ref.1), custom_call_target="tpu_custom_call" | custom-call | tf_op jit(solution)/shard_map/pieces/pallas_call | solution.py:247
  1.9 0.0 copy-start.4
  1.9 0.0 copy-start.6
  1.9 7.5 %all-to-all-start = ((f32[16,2,24,128]{3,2,1,0:T(8,128)}), f32[16,2,24,128]{3,2,1,0:T(8,128)S(1)}, u32[]{:S(2)}, u32[]{:S(2)}) async-start(f32[16,2,24,128]{3,2,1,0:T(8,128)} %pieces.1), calls=%async_computation | async-start | bytes 786432 | tf_op jit(solution)/shard_map/all_to_all | solution.py:263
  9.5 0.0 copy-done
  9.6 12.1 %all-to-all-done = f32[16,2,24,128]{3,2,1,0:T(8,128)S(1)} async-done(((f32[16,2,24,128]{3,2,1,0:T(8,128)}), f32[16,2,24,128]{3,2,1,0:T(8,128)S(1)}, u32[]{:S(2)}, u32[]{:S(2)}) %all-to-all-start) | async-done | bytes 393248 | tf_op jit(solution)/shard_map/all_to_all | solution.py:263
  21.7 0.0 copy-done.3
  21.7 0.0 copy-done.5
  21.7 1.9 %channels.1 = f32[16,48,128]{2,1,0:T(8,128)} custom-call(f32[32,24,128]{2,1,0:T(8,128)S(1)} %bitcast.10, f32[16,128]{1,0:T(8,128)S(1)} %copy-done.5, bf16[768,256]{1,0:T(8,128)(2,1)S(1)} %copy-done.3, f32[8,2,24,128]{3,2,1,0:T(8,128)S(1)} %copy_bitcast_fusion.taps_ref), custom_call_target="tpu_custom_call" | custom-call | tf_op jit(solution)/shard_map/channels/pallas_call | solution.py:286
  23.6 3.6 %all-to-all-start.1 = ((f32[16,48,128]{2,1,0:T(8,128)}), f32[16,48,128]{2,1,0:T(8,128)S(1)}, u32[]{:S(2)}, u32[]{:S(2)}) async-start(f32[16,48,128]{2,1,0:T(8,128)} %channels.1), calls=%async_computation.1 | async-start | bytes 786432 | tf_op jit(solution)/shard_map/all_to_all | solution.py:299
  27.1 0.0 copy-done.4
  27.1 0.0 copy-done.6
  27.1 0.0 copy-start.2
  27.2 1.9 %copy-done.2 = f32[1,8,2,192,192]{4,3,2,1,0:T(8,128)S(1)} copy-done((f32[1,8,2,192,192]{4,3,2,1,0:T(8,128)S(1)}, f32[1,8,2,192,192]{4,3,2,1,0:T(8,128)}, u32[]{:S(2)}) %copy-start.2) | copy-done | bytes 2359320
  29.0 5.7 %weights.1.w_hbm = bf16[8,384,384]{2,1,0:T(8,128)(2,1)S(1)} custom-call(f32[8,2,192,192]{3,2,1,0:T(8,128)S(1)} %bitcast.9, s32[1,192]{1,0:T(1,128)S(1)} %bitcast.12, s32[384,2]{1,0:T(8,128)S(1)} %copy-done.4), custom_call_target="tpu_custom_call" | custom-call | flops 905969664 | bytes 5242880 | tf_op jit(solution)/shard_map/weights/pallas_call | solution.py:269
  34.7 0.0 copy-start.1
  34.7 1.4 %copy-done.1 = bf16[8,384,384]{2,1,0:T(8,128)(2,1)} copy-done((bf16[8,384,384]{2,1,0:T(8,128)(2,1)}, bf16[8,384,384]{2,1,0:T(8,128)(2,1)S(1)}, u32[]{:S(2)}) %copy-start.1) | copy-done | bytes 2359320
  36.1 3.1 %all-to-all-done.1 = f32[16,48,128]{2,1,0:T(8,128)S(1)} async-done(((f32[16,48,128]{2,1,0:T(8,128)}), f32[16,48,128]{2,1,0:T(8,128)S(1)}, u32[]{:S(2)}, u32[]{:S(2)}) %all-to-all-start.1) | async-done | bytes 393248 | tf_op jit(solution)/shard_map/all_to_all | solution.py:299
  39.3 4.0 %beams.1 = f32[8,8,192]{2,1,0:T(8,128)} custom-call(f32[768,128]{1,0:T(8,128)S(1)} %bitcast.11, bf16[8,384,384]{2,1,0:T(8,128)(2,1)} %copy-done.1), custom_call_target="tpu_custom_call" | custom-call | tf_op jit(solution)/shard_map/beams/pallas_call | solution.py:302
  (3 shorter events, 0.1 us)
Async XLA Ops:
  0.0 9.5 %copy-start = (f32[2,8,192,128]{3,2,1,0:T(8,128)S(1)}, f32[2,8,192,128]{3,2,1,0:T(8,128)}, u32[]{:S(2)}) copy-start(f32[2,8,192,128]{3,2,1,0:T(8,128)} %param.9) | copy-start | bytes 4718596
  0.0 21.7 %copy-start.3 = (bf16[768,256]{1,0:T(8,128)(2,1)S(1)}, bf16[768,256]{1,0:T(8,128)(2,1)}, u32[]{:S(2)}) copy-start(bf16[768,256]{1,0:T(8,128)(2,1)} %constant.21.clone.table_ref) | copy-start | bytes 1179652
  0.0 21.7 %copy-start.5 = (f32[16,128]{1,0:T(8,128)S(1)}, f32[16,128]{1,0:T(8,128)}, u32[]{:S(2)}) copy-start(f32[16,128]{1,0:T(8,128)} %proto_ref.1) | copy-start | bytes 24580
  1.9 25.2 %copy-start.4 = (s32[384,2]{1,0:T(8,128)S(1)}, s32[384,2]{1,0:T(8,128)}, u32[]{:S(2)}) copy-start(s32[384,2]{1,0:T(8,128)} %constant.20.clone.slot_ref) | copy-start | bytes 9220
  1.9 25.2 %copy-start.6 = (s32[192]{0:T(256)S(1)}, s32[192]{0:T(256)}, u32[]{:S(2)}) copy-start(s32[192]{0:T(256)} %param.11) | copy-start | bytes 2308
  1.9 19.7 %all-to-all-start = ((f32[16,2,24,128]{3,2,1,0:T(8,128)}), f32[16,2,24,128]{3,2,1,0:T(8,128)S(1)}, u32[]{:S(2)}, u32[]{:S(2)}) async-start(f32[16,2,24,128]{3,2,1,0:T(8,128)} %pieces.1), calls=%async_computation | async-start | bytes 786432 | tf_op jit(solution)/shard_map/all_to_all | solution.py:263
  23.6 15.7 %all-to-all-start.1 = ((f32[16,48,128]{2,1,0:T(8,128)}), f32[16,48,128]{2,1,0:T(8,128)S(1)}, u32[]{:S(2)}, u32[]{:S(2)}) async-start(f32[16,48,128]{2,1,0:T(8,128)} %channels.1), calls=%async_computation.1 | async-start | bytes 786432 | tf_op jit(solution)/shard_map/all_to_all | solution.py:299
  27.1 1.9 %copy-start.2 = (f32[1,8,2,192,192]{4,3,2,1,0:T(8,128)S(1)}, f32[1,8,2,192,192]{4,3,2,1,0:T(8,128)}, u32[]{:S(2)}) copy-start(f32[1,8,2,192,192]{4,3,2,1,0:T(8,128)} %param.10) | copy-start | bytes 7077892
  34.7 1.4 %copy-start.1 = (bf16[8,384,384]{2,1,0:T(8,128)(2,1)}, bf16[8,384,384]{2,1,0:T(8,128)(2,1)S(1)}, u32[]{:S(2)}) copy-start(bf16[8,384,384]{2,1,0:T(8,128)(2,1)S(1)} %weights.1.w_hbm) | copy-start | bytes 7077892

commit v8 on v7

--- a/solution.py
+++ b/solution.py
@@ -9,6 +9,8 @@
 from jax.sharding import PartitionSpec as P
 
 INTEG = 4
+EARLY = 2
+SIDE = 4
 HIGHEST = lax.Precision.HIGHEST
 F32 = jnp.float32
 BF16 = jnp.bfloat16
@@ -79,23 +81,37 @@
         move.wait()
 
 
-def weights_kernel(w_ref, order_ref, slot_ref, out_ref):
+def weights_kernel(w_ref, order_ref, slot_ref, first_ref, later_ref):
+    step = pl.program_id(0)
     order = order_ref[...]
     beams = w_ref.shape[3]
-    for half in range(2):
-        hot = (slot_ref[:, half : half + 1] == order).astype(F32).T.astype(BF16)
-        for part in range(2):
-            turned = w_ref[0, part].T
-            value = split(turned)[half]
-            product = jnp.dot(value, hot, preferred_element_type=F32)
-            rows = slice(part * beams, (part + 1) * beams)
-            if half == 0:
-                out_ref[0, rows, :] = product.astype(BF16)
-            else:
-                out_ref[0, rows, :] += product.astype(BF16)
-
-
-def channel_kernel(x_ref, proto_ref, table_ref, taps_ref, out_ref, poly, spec, filt):
+
+    def make(out_ref):
+        for half in range(2):
+            hot = (slot_ref[:, half : half + 1] == order).astype(F32).T.astype(BF16)
+            for part in range(2):
+                value = split(w_ref[0, part].T)[half]
+                product = jnp.dot(value, hot, preferred_element_type=F32).astype(BF16)
+                rows = slice(part * beams, (part + 1) * beams)
+                if half == 0:
+                    out_ref[0, rows, :] = product
+                else:
+                    out_ref[0, rows, :] += product
+
+    @pl.when(step < EARLY)
+    def _():
+        make(first_ref)
+
+    @pl.when(step >= EARLY)
+    def _():
+        make(later_ref)
+
+
+def channel_kernel(
+    place_ref, x_ref, proto_ref, table_ref, taps_ref, *refs
+):
+    out_refs, (poly, spec, filt, ready) = refs[:SIDE], refs[SIDE:]
+    place = place_ref[0]
     frames = x_ref.shape[0]
     pfb_count = proto_ref.shape[0]
     fir_count = taps_ref.shape[0]
@@ -147,7 +163,7 @@
                 begin = (first + frame) * 24 + rows
                 filt[begin : begin + 8, :] = total[frame]
 
-    per_band = out_ref.shape[1] // 6
+    per_band = ready.shape[1] // 6
     for pair in range(6):
         rows = [
             filt[pl.ds(share_row(part, pair * 2 + odd), frames, stride=24), :]
@@ -155,23 +171,39 @@
             for odd in range(2)
         ]
         turned = jnp.concatenate(rows, axis=0).T
-        for dev in range(out_ref.shape[0]):
-            out_ref[dev, pair * per_band : (pair + 1) * per_band, :] = turned[
+        for dev in range(SIDE * SIDE):
+            ready[dev ^ place, pair * per_band : (pair + 1) * per_band, :] = turned[
                 dev * per_band : (dev + 1) * per_band
             ]
-
-
-def beams_kernel(x_ref, w_hbm, out_ref, w_ref, sems):
-    loads = [
-        pltpu.make_async_copy(
-            w_hbm.at[2 * step : 2 * step + 2], w_ref.at[2 * step : 2 * step + 2], sems.at[step]
+    for outer in range(SIDE):
+        out_refs[outer][...] = ready[outer * SIDE : (outer + 1) * SIDE]
+
+
+def regroup_kernel(*refs):
+    arrived, out_refs = refs[:SIDE], refs[SIDE:]
+    for outer in range(SIDE):
+        for inner in range(1, SIDE):
+            out_refs[inner - 1][outer] = arrived[outer][inner]
+
+
+def beams_kernel(*refs):
+    near, far = refs[:SIDE], refs[SIDE : 2 * SIDE - 1]
+    early_ref, late_hbm, out_ref, x_ref, late_ref, sems = refs[2 * SIDE - 1 :]
+    loads = []
+    for step in range(late_ref.shape[0] // 2):
+        pair = slice(2 * step, 2 * step + 2)
+        loads.append(
+            pltpu.make_async_copy(late_hbm.at[pair], late_ref.at[pair], sems.at[step])
         )
-        for step in range(w_hbm.shape[0] // 2)
-    ]
-    for load in loads:
-        load.start()
+        loads[-1].start()
+    height = near[0].shape[1]
+    for outer in range(SIDE):
+        for inner in range(SIDE):
+            begin = (outer * SIDE + inner) * height
+            block = near[outer][0] if inner == 0 else far[inner - 1][outer]
+            x_ref[begin : begin + height, :] = block
     rows = x_ref.shape[0] // 8
-    beams = w_ref.shape[1] // 2
+    beams = early_ref.shape[1] // 2
     lane = lax.broadcasted_iota(jnp.int32, (rows, LANES), 1)
     even = lane % 64 < 32
     wide = lax.broadcasted_iota(jnp.int32, (beams, LANES), 1)
@@ -179,7 +211,7 @@
     row = lax.broadcasted_iota(jnp.int32, (16, 2 * LANES), 0)
     column = lax.broadcasted_iota(jnp.int32, (16, 2 * LANES), 1)
     pool = jnp.where(row == column % 64 // INTEG, 1.0 / INTEG, 0.0).astype(BF16)
-    for step in range(w_ref.shape[0] // 2):
+    for step in range(out_ref.shape[0] // 2):
         one = x_ref[pl.ds(2 * step, rows, stride=8), :]
         two = x_ref[pl.ds(2 * step + 1, rows, stride=8), :]
         first = jnp.where(even, one, pltpu.roll(two, 32, 1))
@@ -188,10 +220,14 @@
         high, rest = split(field)
         both = jnp.concatenate([high, rest], axis=1)
         both = jnp.concatenate([both, both], axis=0)
-        loads[step].wait()
+        if 2 * step < EARLY:
+            w_ref, begin = early_ref, 2 * step
+        else:
+            w_ref, begin = late_ref, 2 * step - EARLY
+            loads[begin // 2].wait()
         sums = []
         for index in range(2):
-            product = jnp.dot(w_ref[2 * step + index], both, preferred_element_type=F32)
+            product = jnp.dot(w_ref[begin + index], both, preferred_element_type=F32)
             sums.append(product[:, 0:LANES] + product[:, LANES : 2 * LANES])
         by_real = jnp.where(even_wide, sums[0][:beams], sums[1][:beams])
         by_imag = jnp.where(even_wide, sums[0][beams:], sums[1][beams:])
@@ -208,18 +244,19 @@
         out_ref[2 * step + 1] = power[8:16]
 
 
-def slots_of(devices):
-    dishes = np.zeros((2, devices, 6), np.int32)
-    for odd in range(2):
-        for dev in range(devices):
-            for pair in range(6):
-                own = pair * 2 + odd
-                dishes[odd, dev, pair] = (
-                    dev * 8 + own if own < 8 else devices * 8 + dev * 4 + own - 8
-                )
-    flat = dishes.reshape(-1)
-    none = np.full_like(flat, -1)
-    return np.stack([np.concatenate([flat, none]), np.concatenate([none, flat])], axis=1)
+def slots_of(devices, place):
+    index = np.arange(devices * 12)
+    odd, other, pair = index // (devices * 6), index // 6 % devices, index % 6
+    own = jnp.asarray(pair * 2 + odd, jnp.int32)
+    source = jnp.asarray(other, jnp.int32) ^ place
+    dishes = jnp.where(own < 8, source * 8 + own, devices * 8 + source * 4 + own - 8)
+    none = jnp.full_like(dishes, -1)
+    return jnp.stack([jnp.concatenate([dishes, none]), jnp.concatenate([none, dishes])], axis=1)
+
+
+def moved(value, step):
+    devices = lax.axis_size("band")
+    return lax.ppermute(value, "band", [(dev, dev ^ step) for dev in range(devices)])
 
 
 def dft_parts(channels):
@@ -266,51 +303,81 @@
     four = lax.dynamic_slice_in_dim(dish_filter, devices * 8 + position * 4, 4, 2)
     taps = jnp.concatenate([eight, eight, four, four], axis=2)
     taps = jnp.transpose(taps, (1, 0, 2, 3))
-    weights = pl.pallas_call(
+    def weight_shape(count):
+        return jax.ShapeDtypeStruct((count, 2 * beams, 2 * dishes), BF16)
+
+    early, late = pl.pallas_call(
         weights_kernel,
         grid=(band_chans,),
-        out_shape=jax.ShapeDtypeStruct((band_chans, 2 * beams, 2 * dishes), BF16),
+        out_shape=[weight_shape(EARLY), weight_shape(band_chans - EARLY)],
         in_specs=[
             pl.BlockSpec((1, 2, dishes, beams), lambda i: (i, 0, 0, 0)),
             pl.BlockSpec((1, dishes), lambda i: (0, 0)),
             pl.BlockSpec((2 * dishes, 2), lambda i: (0, 0)),
         ],
-        out_specs=pl.BlockSpec((1, 2 * beams, 2 * dishes), lambda i: (i, 0, 0)),
+        out_specs=[
+            pl.BlockSpec(
+                (1, 2 * beams, 2 * dishes), lambda i: (jnp.minimum(i, EARLY - 1), 0, 0)
+            ),
+            pl.BlockSpec((1, 2 * beams, 2 * dishes), lambda i: (jnp.maximum(i - EARLY, 0), 0, 0)),
+        ],
         name="weights",
         compiler_params=GRANT,
         cost_estimate=pl.CostEstimate(
             flops=8 * 4 * 2 * 192 * 192 * 384, bytes_accessed=5 << 20, transcendentals=0
         ),
-    )(beam_weights[0], dish_order.reshape(1, dishes), slots_of(devices))
-
+    )(beam_weights[0], dish_order.reshape(1, dishes), slots_of(devices, position))
+    arrived, early, late = lax.optimization_barrier((arrived, early, late))
+
+    block = (6 * band_chans, channels)
     filtered = pl.pallas_call(
         channel_kernel,
-        out_shape=jax.ShapeDtypeStruct((devices, 6 * band_chans, channels), F32),
-        in_specs=[VMEM] * 4,
-        out_specs=VMEM,
+        out_shape=[jax.ShapeDtypeStruct((SIDE,) + block, F32)] * SIDE,
+        in_specs=[pl.BlockSpec(memory_space=pltpu.SMEM)] + [VMEM] * 4,
+        out_specs=[VMEM] * SIDE,
         scratch_shapes=[
             pltpu.VMEM((frames, 24, 2 * LANES), F32),
             pltpu.VMEM((frames + fir_count - 1, 24, 2 * LANES), F32),
             pltpu.VMEM((frames * 24, LANES), F32),
+            pltpu.VMEM((devices,) + block, F32),
         ],
         name="channels",
         compiler_params=GRANT,
-    )(held(arrived.reshape(frames, 24, channels), pltpu.VMEM), prototype, dft_parts(channels), taps)
-    field = lax.all_to_all(filtered, "band", split_axis=0, concat_axis=0, tiled=True)
-    field = field.reshape(devices * 6 * band_chans, channels)
+    )(
+        position.reshape(1),
+        held(arrived.reshape(frames, 24, channels), pltpu.VMEM),
+        prototype,
+        dft_parts(channels),
+        taps,
+    )
+    near = [filtered[0]] + [None] * (SIDE - 1)
+    for outer in range(SIDE - 1, 0, -1):
+        near[outer] = moved(filtered[outer], outer * SIDE)
+    grouped = pl.pallas_call(
+        regroup_kernel,
+        out_shape=[jax.ShapeDtypeStruct((SIDE,) + block, F32)] * (SIDE - 1),
+        in_specs=[VMEM] * SIDE,
+        out_specs=[VMEM] * (SIDE - 1),
+        name="regroup",
+        compiler_params=GRANT,
+    )(*near)
+    far = [None] * (SIDE - 1)
+    for inner in range(SIDE - 1, 0, -1):
+        far[inner - 1] = moved(grouped[inner - 1], inner)
 
     power = pl.pallas_call(
         beams_kernel,
         out_shape=jax.ShapeDtypeStruct((band_chans, frames // INTEG, beams), F32),
-        in_specs=[VMEM, HBM],
+        in_specs=[VMEM] * (2 * SIDE) + [HBM],
         out_specs=VMEM,
         scratch_shapes=[
-            pltpu.VMEM(weights.shape, BF16),
-            pltpu.SemaphoreType.DMA((band_chans // 2,)),
+            pltpu.VMEM((devices * 6 * band_chans, channels), F32),
+            pltpu.VMEM(late.shape, BF16),
+            pltpu.SemaphoreType.DMA((band_chans // 2 - 1,)),
         ],
         name="beams",
         compiler_params=GRANT,
-    )(held(field, pltpu.VMEM), held(weights, pltpu.HBM))
+    )(*near, *far, held(early, pltpu.VMEM), held(late, pltpu.HBM))
     return jnp.transpose(power, (0, 2, 1))[None]
 
 
@@ -397,6 +464,7 @@
             channels == LANES
             and beam_weights.shape[1] == 8
             and devices * 8 == channels
+            and devices == SIDE * SIDE
             and dish_filter.shape[2] == 12 * devices
             and samples.shape[2] * devices == 32 * channels
         )

time: 43.7 us -> 44.7 us (1.023)
  starting transfers between devices: 11.1 us -> 13.8 us
  Pallas kernels: 13.5 us -> 12.3 us
  waiting for transfers between devices: 15.3 us -> 14.8 us
    ppermute x0 -> x6, waiting for transfers between devices: none -> 11.9 us  [moved(): lax.ppermute(value, 'band', [(dev, dev ^ step) for dev in range(devices)])]
    all_to_all x1, waiting for transfers between devices: 12.1 us -> 2.9 us  [close_body(): lax.all_to_all(pieces, 'band', split_axis=0, concat_axis=0, tiled=True)]
    ppermute x0 -> x6, starting transfers between devices: none -> 6.38 us  [moved(): lax.ppermute(value, 'band', [(dev, dev ^ step) for dev in range(devices)])]
    all_to_all x1 -> x0, starting transfers between devices: 3.55 us -> none  [close_body(): lax.all_to_all(filtered, 'band', split_axis=0, concat_axis=0, tiled=True)]
    all_to_all x1 -> x0, waiting for transfers between devices: 3.15 us -> none  [close_body(): lax.all_to_all(filtered, 'band', split_axis=0, concat_axis=0, tiled=True)]
    pallas_call x2 -> x3, Pallas kernels: 7.56 us -> 6.93 us  [the longest x1 5.76 us: close_body(): pl.pallas_call(weights_kernel, grid=(band_chans,), out_shape=[weight_shap...]
    pallas_call x1, Pallas kernels: 3.99 us -> 3.46 us  [close_body(): pl.pallas_call(beams_kernel, out_shape=jax.ShapeDtypeStruct((band_chans,...]
    unnamed x14 -> x18, local copies, waits for them, and re-layouts: 3.31 us -> 3.15 us
  transfers between devices with their start and end apart: 2 -> 7, of which waited for: 2 -> 5; matrix products, arithmetic and copies ran while one was open for 0% -> 1% of each run, Pallas kernels for 13% -> 13%
where the time goes in v8:
time: 44.7 us; the launch traced here: 44.5 us
  waiting for transfers between devices  14.8 us (33%)
  starting transfers between devices  13.8 us (31%)
  Pallas kernels  12.3 us (28%)
  local copies, waits for them, and re-layouts  3.41 us (8%)
    ppermute x6, waiting for transfers between devices, moved(): lax.ppermute(value, 'band', [(dev, dev ^ step) for dev in range(devices)])  11.9 us
    all_to_all x1, starting transfers between devices, close_body(): lax.all_to_all(pieces, 'band', split_axis=0, concat_axis=0, tiled=True)  7.41 us
    ppermute x6, starting transfers between devices, moved(): lax.ppermute(value, 'band', [(dev, dev ^ step) for dev in range(devices)])  6.38 us
    pallas_call x1, Pallas kernels, close_body(): pl.pallas_call(weights_kernel, grid=(band_chans,), out_shape=[weight_shap...  5.76 us
    pallas_call x1, Pallas kernels, close_body(): pl.pallas_call(beams_kernel, out_shape=jax.ShapeDtypeStruct((band_chans,...  3.46 us
    unnamed x18, local copies, waits for them, and re-layouts  3.15 us
    all_to_all x1, waiting for transfers between devices, close_body(): lax.all_to_all(pieces, 'band', split_axis=0, concat_axis=0, tiled=True)  2.9 us
    pallas_call x1, Pallas kernels, close_body(): pl.pallas_call(pieces_kernel, out_shape=jax.ShapeDtypeStruct((devices, fr...  1.89 us
  transfers between devices with their start and end apart: 7, of which 5 were waited for; matrix products, arithmetic and copies ran while one was open for 1% of the time, Pallas kernels for 13%

profile of v8, /device:TPU:0, one launch (start us, length us, event | category | flops | bytes accessed | tf_op | source)
XLA Modules:
  0.0 44.5 jit_solution(2543601489908431050)
XLA Ops:
  0.0 0.0 copy-start
  0.0 0.0 copy-start.8
  0.0 0.0 copy-start.6
  0.0 0.0 copy-start.7
  0.0 0.0 copy-start.5
  0.0 1.9 %pieces.1 = f32[16,2,24,128]{3,2,1,0:T(8,128)} custom-call(f32[2,192,256]{2,1,0:T(8,128)} %x_ref.1), custom_call_target="tpu_custom_call" | custom-call | tf_op jit(solution)/shard_map/pieces/pallas_call | solution.py:284
  1.9 7.4 %all-to-all-start = ((f32[16,2,24,128]{3,2,1,0:T(8,128)}), f32[16,2,24,128]{3,2,1,0:T(8,128)S(1)}, u32[]{:S(2)}, u32[]{:S(2)}) async-start(f32[16,2,24,128]{3,2,1,0:T(8,128)} %pieces.1), calls=%async_computation | async-start | bytes 786432 | tf_op jit(solution)/shard_map/all_to_all | solution.py:300
  9.3 0.0 copy-done.8
  9.3 0.0 copy-done.6
  9.4 0.0 copy-done.7
  9.4 0.1 fusion.5
  9.5 0.1 copy.15.slot_ref
  9.6 0.0 copy-done.5
  9.6 0.0 copy-start.4
  9.6 1.9 %copy-done.4 = f32[1,8,2,192,192]{4,3,2,1,0:T(8,128)S(1)} copy-done((f32[1,8,2,192,192]{4,3,2,1,0:T(8,128)S(1)}, f32[1,8,2,192,192]{4,3,2,1,0:T(8,128)}, u32[]{:S(2)}) %copy-start.4) | copy-done | bytes 2359320
  11.5 0.0 copy-start.2
  11.5 0.0 copy-start.3
  11.5 5.8 %weights.1 = (bf16[2,384,384]{2,1,0:T(8,128)(2,1)S(1)}, bf16[6,384,384]{2,1,0:T(8,128)(2,1)S(1)}) custom-call(f32[8,2,192,192]{3,2,1,0:T(8,128)S(1)} %bitcast.10, s32[1,192]{1,0:T(1,128)S(1)} %bitcast.11, s32[384,2]{1,0:T(8,128)S(1)} %copy.15.slot_ref), custom_call_target="tpu_custom_call" | custom-call | flops 905969664 | bytes 5242880 | tf_op jit(solution)/shard_map/weights/pallas_call | solution.py:309
  17.3 0.0 copy-start.1
  17.3 1.2 %copy-done.1 = bf16[6,384,384]{2,1,0:T(8,128)(2,1)} copy-done((bf16[6,384,384]{2,1,0:T(8,128)(2,1)}, bf16[6,384,384]{2,1,0:T(8,128)(2,1)S(1)}, u32[]{:S(2)}) %copy-start.1) | copy-done | bytes 1769496
  18.6 0.0 copy-done
  18.6 2.9 %all-to-all-done = f32[16,2,24,128]{3,2,1,0:T(8,128)S(1)} async-done(((f32[16,2,24,128]{3,2,1,0:T(8,128)}), f32[16,2,24,128]{3,2,1,0:T(8,128)S(1)}, u32[]{:S(2)}, u32[]{:S(2)}) %all-to-all-start) | async-done | bytes 393248 | tf_op jit(solution)/shard_map/all_to_all | solution.py:300
  21.5 0.0 copy-done.2
  21.5 0.0 copy-done.3
  21.5 1.2 %channels.1 = (f32[4,48,128]{2,1,0:T(8,128)S(1)}, f32[4,48,128]{2,1,0:T(8,128)S(1)}, f32[4,48,128]{2,1,0:T(8,128)S(1)}, f32[4,48,128]{2,1,0:T(8,128)S(1)}) custom-call(s32[1]{0:T(128)} %bitcast.place_ref, f32[32,24,128]{2,1,0:T(8,128)S(1)} %bitcast.9, f32[16,128]{1,0:T(8,128)S(1)} %copy-done.3, bf16[768,256]{1,0:T(8,128)(2,1)S(1)} %copy-done.2, ...), custom_call_target="tpu_custom_call" | custom-call | tf_op jit(solution)/shard_map/channels/pallas_call | solution.py:333
  22.7 0.8 %collective-permute-start = (f32[4,48,128]{2,1,0:T(8,128)S(1)}, f32[4,48,128]{2,1,0:T(8,128)S(1)}, u32[]{:S(2)}, u32[]{:S(2)}) collective-permute-start(f32[4,48,128]{2,1,0:T(8,128)S(1)} %get-tuple-element.21), channel_id=1, source_target_pairs={{0,4},{1,5},{2,6},{3,7},{4,0},{5,1},{6,2},{7,3},{8,12},{9,13},{10,... | collective-permute-start | bytes 294920 | tf_op jit(solution)/shard_map/ppermute | solution.py:259
  23.5 1.1 %collective-permute-start.1 = (f32[4,48,128]{2,1,0:T(8,128)S(1)}, f32[4,48,128]{2,1,0:T(8,128)S(1)}, u32[]{:S(2)}, u32[]{:S(2)}) collective-permute-start(f32[4,48,128]{2,1,0:T(8,128)S(1)} %get-tuple-element.22), channel_id=1, source_target_pairs={{0,8},{1,9},{2,10},{3,11},{4,12},{5,13},{6,14},{7,15},{8,0},{9,1},... | collective-permute-start | bytes 294920 | tf_op jit(solution)/shard_map/ppermute | solution.py:259
  24.6 2.6 %collective-permute-start.2 = (f32[4,48,128]{2,1,0:T(8,128)S(1)}, f32[4,48,128]{2,1,0:T(8,128)S(1)}, u32[]{:S(2)}, u32[]{:S(2)}) collective-permute-start(f32[4,48,128]{2,1,0:T(8,128)S(1)} %get-tuple-element.23), channel_id=1, source_target_pairs={{0,12},{1,13},{2,14},{3,15},{4,8},{5,9},{6,10},{7,11},{8,4},{9,5},... | collective-permute-start | bytes 294920 | tf_op jit(solution)/shard_map/ppermute | solution.py:259
  27.2 1.0 %collective-permute-done.refs_1_ = f32[4,48,128]{2,1,0:T(8,128)S(1)} collective-permute-done((f32[4,48,128]{2,1,0:T(8,128)S(1)}, f32[4,48,128]{2,1,0:T(8,128)S(1)}, u32[]{:S(2)}, u32[]{:S(2)}) %collective-permute-start) | collective-permute-done | bytes 98336 | tf_op jit(solution)/shard_map/ppermute | solution.py:259
  28.2 5.8 %collective-permute-done.1.refs_2_ = f32[4,48,128]{2,1,0:T(8,128)S(1)} collective-permute-done((f32[4,48,128]{2,1,0:T(8,128)S(1)}, f32[4,48,128]{2,1,0:T(8,128)S(1)}, u32[]{:S(2)}, u32[]{:S(2)}) %collective-permute-start.1) | collective-permute-done | bytes 98336 | tf_op jit(solution)/shard_map/ppermute | solution.py:259
  34.0 0.0 collective-permute-done.2.refs_3_
  34.0 0.1 collective-permute-start.3
  34.1 1.1 %collective-permute-start.4 = (f32[4,48,128]{2,1,0:T(8,128)S(1)}, f32[4,48,128]{2,1,0:T(8,128)S(1)}, u32[]{:S(2)}, u32[]{:S(2)}) collective-permute-start(f32[4,48,128]{2,1,0:T(8,128)S(1)} %get-tuple-element.25), channel_id=1, source_target_pairs={{0,2},{1,3},{2,0},{3,1},{4,6},{5,7},{6,4},{7,5},{8,10},{9,11},{10,... | collective-permute-start | bytes 294920 | tf_op jit(solution)/shard_map/ppermute | solution.py:259
  35.2 0.8 %collective-permute-start.5 = (f32[4,48,128]{2,1,0:T(8,128)S(1)}, f32[4,48,128]{2,1,0:T(8,128)S(1)}, u32[]{:S(2)}, u32[]{:S(2)}) collective-permute-start(f32[4,48,128]{2,1,0:T(8,128)S(1)} %get-tuple-element.26), channel_id=1, source_target_pairs={{0,3},{1,2},{2,1},{3,0},{4,7},{5,6},{6,5},{7,4},{8,11},{9,10},{10,... | collective-permute-start | bytes 294920 | tf_op jit(solution)/shard_map/ppermute | solution.py:259
  36.0 0.0 collective-permute-done.3.refs_4_
  36.0 3.8 %collective-permute-done.4.refs_5_ = f32[4,48,128]{2,1,0:T(8,128)S(1)} collective-permute-done((f32[4,48,128]{2,1,0:T(8,128)S(1)}, f32[4,48,128]{2,1,0:T(8,128)S(1)}, u32[]{:S(2)}, u32[]{:S(2)}) %collective-permute-start.4) | collective-permute-done | bytes 98336 | tf_op jit(solution)/shard_map/ppermute | solution.py:259
  39.8 1.2 %collective-permute-done.5.refs_6_ = f32[4,48,128]{2,1,0:T(8,128)S(1)} collective-permute-done((f32[4,48,128]{2,1,0:T(8,128)S(1)}, f32[4,48,128]{2,1,0:T(8,128)S(1)}, u32[]{:S(2)}, u32[]{:S(2)}) %collective-permute-start.5) | collective-permute-done | bytes 98336 | tf_op jit(solution)/shard_map/ppermute | solution.py:259
  41.0 3.5 %beams.1 = f32[8,8,192]{2,1,0:T(8,128)} custom-call(f32[4,48,128]{2,1,0:T(8,128)S(1)} %get-tuple-element.20.refs_0_, f32[4,48,128]{2,1,0:T(8,128)S(1)} %collective-permute-done.refs_1_, f32[4,48,128]{2,1,0:T(8,128)S(1)} %collective-permute-done.1.refs_2_, f32[4,48,128]{2,1,0:T(8,128)S(1)} %collective-permute-done.2.refs_3_, ...), custom_call_target="tpu_custom_call" | custom-call | tf_op jit(solution)/shard_map/beams/pallas_call | solution.py:368
  (8 shorter events, 0.1 us)
Async XLA Ops:
  0.0 18.6 %copy-start = (f32[2,8,192,128]{3,2,1,0:T(8,128)S(1)}, f32[2,8,192,128]{3,2,1,0:T(8,128)}, u32[]{:S(2)}) copy-start(f32[2,8,192,128]{3,2,1,0:T(8,128)} %param.10) | copy-start | bytes 4718596
  0.0 9.3 %copy-start.8 = (pred[192]{0:T(512)(128)(4,1)S(1)}, pred[192]{0:T(512)(128)(4,1)}, u32[]{:S(2)}) copy-start(pred[192]{0:T(512)(128)(4,1)} %constant.37) | copy-start | bytes 580
  0.0 9.3 %copy-start.6 = (s32[192]{0:T(256)S(1)}, s32[192]{0:T(256)}, u32[]{:S(2)}) copy-start(s32[192]{0:T(256)} %constant.30.clone) | copy-start | bytes 2308
  0.0 9.4 %copy-start.7 = (s32[192]{0:T(256)S(1)}, s32[192]{0:T(256)}, u32[]{:S(2)}) copy-start(s32[192]{0:T(256)} %constant.29.clone) | copy-start | bytes 2308
  0.0 9.6 %copy-start.5 = (s32[192]{0:T(256)S(1)}, s32[192]{0:T(256)}, u32[]{:S(2)}) copy-start(s32[192]{0:T(256)} %param.12) | copy-start | bytes 2308
  1.9 19.6 %all-to-all-start = ((f32[16,2,24,128]{3,2,1,0:T(8,128)}), f32[16,2,24,128]{3,2,1,0:T(8,128)S(1)}, u32[]{:S(2)}, u32[]{:S(2)}) async-start(f32[16,2,24,128]{3,2,1,0:T(8,128)} %pieces.1), calls=%async_computation | async-start | bytes 786432 | tf_op jit(solution)/shard_map/all_to_all | solution.py:300
  9.6 1.9 %copy-start.4 = (f32[1,8,2,192,192]{4,3,2,1,0:T(8,128)S(1)}, f32[1,8,2,192,192]{4,3,2,1,0:T(8,128)}, u32[]{:S(2)}) copy-start(f32[1,8,2,192,192]{4,3,2,1,0:T(8,128)} %param.11) | copy-start | bytes 7077892
  11.5 10.0 %copy-start.2 = (bf16[768,256]{1,0:T(8,128)(2,1)S(1)}, bf16[768,256]{1,0:T(8,128)(2,1)}, u32[]{:S(2)}) copy-start(bf16[768,256]{1,0:T(8,128)(2,1)} %constant.31.clone.table_ref) | copy-start | bytes 1179652
  11.5 10.0 %copy-start.3 = (f32[16,128]{1,0:T(8,128)S(1)}, f32[16,128]{1,0:T(8,128)}, u32[]{:S(2)}) copy-start(f32[16,128]{1,0:T(8,128)} %proto_ref.1) | copy-start | bytes 24580
  17.3 1.2 %copy-start.1 = (bf16[6,384,384]{2,1,0:T(8,128)(2,1)}, bf16[6,384,384]{2,1,0:T(8,128)(2,1)S(1)}, u32[]{:S(2)}) copy-start(bf16[6,384,384]{2,1,0:T(8,128)(2,1)S(1)} %get-tuple-element.28.refs_8_) | copy-start | bytes 5308420
  22.7 5.5 %collective-permute-start = (f32[4,48,128]{2,1,0:T(8,128)S(1)}, f32[4,48,128]{2,1,0:T(8,128)S(1)}, u32[]{:S(2)}, u32[]{:S(2)}) collective-permute-start(f32[4,48,128]{2,1,0:T(8,128)S(1)} %get-tuple-element.21), channel_id=1, source_target_pairs={{0,4},{1,5},{2,6},{3,7},{4,0},{5,1},{6,2},{7,3},{8,12},{9,13},{10,... | collective-permute-start | bytes 294920 | tf_op jit(solution)/shard_map/ppermute | solution.py:259
  23.5 10.5 %collective-permute-start.1 = (f32[4,48,128]{2,1,0:T(8,128)S(1)}, f32[4,48,128]{2,1,0:T(8,128)S(1)}, u32[]{:S(2)}, u32[]{:S(2)}) collective-permute-start(f32[4,48,128]{2,1,0:T(8,128)S(1)} %get-tuple-element.22), channel_id=1, source_target_pairs={{0,8},{1,9},{2,10},{3,11},{4,12},{5,13},{6,14},{7,15},{8,0},{9,1},... | collective-permute-start | bytes 294920 | tf_op jit(solution)/shard_map/ppermute | solution.py:259
  24.6 9.4 %collective-permute-start.2 = (f32[4,48,128]{2,1,0:T(8,128)S(1)}, f32[4,48,128]{2,1,0:T(8,128)S(1)}, u32[]{:S(2)}, u32[]{:S(2)}) collective-permute-start(f32[4,48,128]{2,1,0:T(8,128)S(1)} %get-tuple-element.23), channel_id=1, source_target_pairs={{0,12},{1,13},{2,14},{3,15},{4,8},{5,9},{6,10},{7,11},{8,4},{9,5},... | collective-permute-start | bytes 294920 | tf_op jit(solution)/shard_map/ppermute | solution.py:259
  34.0 1.9 %collective-permute-start.3 = (f32[4,48,128]{2,1,0:T(8,128)S(1)}, f32[4,48,128]{2,1,0:T(8,128)S(1)}, u32[]{:S(2)}, u32[]{:S(2)}) collective-permute-start(f32[4,48,128]{2,1,0:T(8,128)S(1)} %get-tuple-element.24), channel_id=1, source_target_pairs={{0,1},{1,0},{2,3},{3,2},{4,5},{5,4},{6,7},{7,6},{8,9},{9,8},{10,11... | collective-permute-start | bytes 294920 | tf_op jit(solution)/shard_map/ppermute | solution.py:259
  34.1 5.7 %collective-permute-start.4 = (f32[4,48,128]{2,1,0:T(8,128)S(1)}, f32[4,48,128]{2,1,0:T(8,128)S(1)}, u32[]{:S(2)}, u32[]{:S(2)}) collective-permute-start(f32[4,48,128]{2,1,0:T(8,128)S(1)} %get-tuple-element.25), channel_id=1, source_target_pairs={{0,2},{1,3},{2,0},{3,1},{4,6},{5,7},{6,4},{7,5},{8,10},{9,11},{10,... | collective-permute-start | bytes 294920 | tf_op jit(solution)/shard_map/ppermute | solution.py:259
  35.2 5.8 %collective-permute-start.5 = (f32[4,48,128]{2,1,0:T(8,128)S(1)}, f32[4,48,128]{2,1,0:T(8,128)S(1)}, u32[]{:S(2)}, u32[]{:S(2)}) collective-permute-start(f32[4,48,128]{2,1,0:T(8,128)S(1)} %get-tuple-element.26), channel_id=1, source_target_pairs={{0,3},{1,2},{2,1},{3,0},{4,7},{5,6},{6,5},{7,4},{8,11},{9,10},{10,... | collective-permute-start | bytes 294920 | tf_op jit(solution)/shard_map/ppermute | solution.py:259

commit v9 on v3

--- a/solution.py
+++ b/solution.py
@@ -9,6 +9,8 @@
 from jax.sharding import PartitionSpec as P
 
 INTEG = 4
+ORDERS = ((6, 2, 5, 1, 7, 3, 4), (2, 7, 1, 4, 3, 6, 5))
+STEPS = len(ORDERS[0])
 HIGHEST = lax.Precision.HIGHEST
 F32 = jnp.float32
 BF16 = jnp.bfloat16
@@ -34,46 +36,80 @@
     return part * 8 + dish if dish < 8 else 16 + part * 4 + dish - 8
 
 
-def pieces_kernel(x_ref, out_ref):
-    devices, frames_dev = out_ref.shape[:2]
+def chip_at(place, step):
+    return jnp.where(place % 2 == 0, ORDERS[0][step], ORDERS[1][step])
+
+
+def pieces_kernel(x_ref, own_ref, other_ref):
+    place = lax.axis_index("band")
+    chips, frames_dev = own_ref.shape[:2]
+    first_rest = chips * 16
     low = lax.broadcasted_iota(jnp.int32, (8, LANES), 0) < 4
-    for frame in range(frames_dev):
-        lanes = slice(frame * LANES, (frame + 1) * LANES)
-        for dev in range(0, devices, 2):
-            for one in (dev, dev + 1):
+    for chip in range(chips):
+        for core, out_ref in enumerate((own_ref, other_ref)):
+            dest = place ^ (2 * chip + core)
+            rows = pl.ds(pl.multiple_of(dest * 8, 8), 8)
+            for frame in range(frames_dev):
+                lanes = slice(frame * LANES, (frame + 1) * LANES)
                 for part in range(2):
-                    out_ref[one, frame, part * 8 : part * 8 + 8, :] = x_ref[
-                        part, one * 8 : one * 8 + 8, lanes
-                    ]
-            start = devices * 8 + dev * 4
-            real = x_ref[0, start : start + 8, lanes]
-            imag = x_ref[1, start : start + 8, lanes]
-            out_ref[dev, frame, 16:24, :] = jnp.where(low, real, pltpu.roll(imag, 4, 0))
-            out_ref[dev + 1, frame, 16:24, :] = jnp.where(low, pltpu.roll(real, 4, 0), imag)
+                    out_ref[chip, frame, part * 8 : part * 8 + 8, :] = x_ref[part, rows, lanes]
+        pair = (place ^ (2 * chip)) // 2
+        rows = pl.ds(pl.multiple_of(first_rest + pair * 8, 8), 8)
+        for frame in range(frames_dev):
+            lanes = slice(frame * LANES, (frame + 1) * LANES)
+            real, imag = x_ref[0, rows, lanes], x_ref[1, rows, lanes]
+            even = jnp.where(low, real, pltpu.roll(imag, 4, 0))
+            odd = jnp.where(low, pltpu.roll(real, 4, 0), imag)
+            is_even = place % 2 == 0
+            own_ref[chip, frame, 16:24, :] = jnp.where(is_even, even, odd)
+            other_ref[chip, frame, 16:24, :] = jnp.where(is_even, odd, even)
+
+
+def regroup_kernel(own_ref, came_ref, *out_refs):
+    place = lax.axis_index("band")
+    for step, out_ref in enumerate(out_refs):
+        chip = chip_at(place, step)
+        out_ref[0] = own_ref[chip]
+        out_ref[1] = came_ref[chip]
+
+
+def sources(place, own_ref, came_ref, far_refs):
+    yield 0, own_ref[0]
+    yield 1, came_ref[0]
+    for step, far_ref in enumerate(far_refs):
+        for core in range(2):
+            yield 2 * chip_at(place, step) + core, far_ref[core]
 
 
 def weights_kernel(w_ref, order_ref, slot_ref, out_ref):
-    order = order_ref[...]
+    hot = (slot_ref[...] == order_ref[...]).astype(F32).T.astype(BF16)
     beams = w_ref.shape[3]
-    for half in range(2):
-        hot = (slot_ref[:, half : half + 1] == order).astype(F32).T.astype(BF16)
+    for chan in range(w_ref.shape[0]):
         for part in range(2):
-            turned = w_ref[0, part].T
-            value = split(turned)[half]
-            product = jnp.dot(value, hot, preferred_element_type=F32)
+            halves = [
+                jnp.dot(half, hot, preferred_element_type=F32).astype(BF16)
+                for half in split(w_ref[chan, part].T)
+            ]
             rows = slice(part * beams, (part + 1) * beams)
-            if half == 0:
-                out_ref[0, rows, :] = product.astype(BF16)
-            else:
-                out_ref[0, rows, :] += product.astype(BF16)
-
-
-def channel_kernel(x_ref, proto_ref, table_ref, taps_ref, out_ref, poly, spec, filt):
-    frames = x_ref.shape[0]
+            out_ref[chan, rows, :] = jnp.concatenate(halves, axis=1)
+
+
+def channel_kernel(*refs):
+    came, refs = refs[: 2 + STEPS], refs[2 + STEPS :]
+    proto_ref, table_ref, taps_ref, own_ref, other_ref = refs[:5]
+    past, poly, spec, filt, ready = refs[5:]
+    place = lax.axis_index("band")
     pfb_count = proto_ref.shape[0]
     fir_count = taps_ref.shape[0]
+    frames_dev = came[0].shape[1]
+    frames = poly.shape[0]
     group = 8
     low = lax.broadcasted_iota(jnp.int32, (group, 8, LANES), 1) < 4
+
+    past[0 : pfb_count - 1] = jnp.zeros((pfb_count - 1, 24, LANES), F32)
+    for other, block in sources(place, came[0], came[1], came[2:]):
+        begin = pfb_count - 1 + (place ^ other) * frames_dev
+        past[pl.ds(begin, frames_dev)] = block
 
     spec[0 : fir_count - 1] = jnp.zeros((fir_count - 1, 24, 2 * LANES), F32)
     for first in range(0, frames, group):
@@ -81,14 +117,9 @@
         for rows in range(0, 24, 8):
             total = None
             for tap in range(pfb_count):
-                begin = first - tap
-                lost = max(0, -begin)
-                if lost >= group:
-                    continue
-                block = x_ref[begin + lost : begin + group, rows : rows + 8, :]
+                begin = first + pfb_count - 1 - tap
+                block = past[begin : begin + group, rows : rows + 8, :]
                 term = block * proto_ref[tap : tap + 1, :][None]
-                if lost:
-                    term = jnp.concatenate([jnp.zeros((lost, 8, LANES), F32), term], axis=0)
                 total = term if total is None else total + term
             found.append(total)
         turned = pltpu.roll(found[2], 4, 1)
@@ -120,7 +151,7 @@
                 begin = (first + frame) * 24 + rows
                 filt[begin : begin + 8, :] = total[frame]
 
-    per_band = out_ref.shape[1] // 6
+    per_band = ready.shape[1] // 6
     for pair in range(6):
         rows = [
             filt[pl.ds(share_row(part, pair * 2 + odd), frames, stride=24), :]
@@ -128,13 +159,21 @@
             for odd in range(2)
         ]
         turned = jnp.concatenate(rows, axis=0).T
-        for dev in range(out_ref.shape[0]):
-            out_ref[dev, pair * per_band : (pair + 1) * per_band, :] = turned[
+        for dev in range(ready.shape[0]):
+            ready[dev ^ place, pair * per_band : (pair + 1) * per_band, :] = turned[
                 dev * per_band : (dev + 1) * per_band
             ]
-
-
-def beams_kernel(x_ref, w_ref, out_ref):
+    for chip in range(ready.shape[0] // 2):
+        own_ref[chip] = ready[2 * chip]
+        other_ref[chip] = ready[2 * chip + 1]
+
+
+def beams_kernel(*refs):
+    came, (w_ref, out_ref, x_ref) = refs[: 2 + STEPS], refs[2 + STEPS :]
+    place = lax.axis_index("band")
+    height = came[0].shape[1]
+    for other, block in sources(place, came[0], came[1], came[2:]):
+        x_ref[pl.ds(pl.multiple_of(other * height, 8), height), :] = block
     rows = x_ref.shape[0] // 8
     beams = w_ref.shape[1] // 2
     lane = lax.broadcasted_iota(jnp.int32, (rows, LANES), 1)
@@ -144,7 +183,7 @@
     row = lax.broadcasted_iota(jnp.int32, (16, 2 * LANES), 0)
     column = lax.broadcasted_iota(jnp.int32, (16, 2 * LANES), 1)
     pool = jnp.where(row == column % 64 // INTEG, 1.0 / INTEG, 0.0).astype(BF16)
-    for step in range(w_ref.shape[0] // 2):
+    for step in range(out_ref.shape[0] // 2):
         one = x_ref[pl.ds(2 * step, rows, stride=8), :]
         two = x_ref[pl.ds(2 * step + 1, rows, stride=8), :]
         first = jnp.where(even, one, pltpu.roll(two, 32, 1))
@@ -172,18 +211,35 @@
         out_ref[2 * step + 1] = power[8:16]
 
 
-def slots_of(devices):
-    dishes = np.zeros((2, devices, 6), np.int32)
-    for odd in range(2):
-        for dev in range(devices):
-            for pair in range(6):
-                own = pair * 2 + odd
-                dishes[odd, dev, pair] = (
-                    dev * 8 + own if own < 8 else devices * 8 + dev * 4 + own - 8
-                )
-    flat = dishes.reshape(-1)
-    none = np.full_like(flat, -1)
-    return np.stack([np.concatenate([flat, none]), np.concatenate([none, flat])], axis=1)
+def slots_of(devices, place):
+    index = np.arange(devices * 12)
+    odd, other, pair = index // (devices * 6), index // 6 % devices, index % 6
+    own = jnp.asarray(pair * 2 + odd, jnp.int32)
+    source = jnp.asarray(other, jnp.int32) ^ place
+    dishes = jnp.where(own < 8, source * 8 + own, devices * 8 + source * 4 + own - 8)
+    return dishes[:, None]
+
+
+def exchange(own, other):
+    devices = lax.axis_size("band")
+
+    def moved(value, steps):
+        pairs = [(dev, dev ^ steps[dev % 2]) for dev in range(devices)]
+        return lax.ppermute(value, "band", pairs)
+
+    came = moved(other, (1, 1))
+    grouped = pl.pallas_call(
+        regroup_kernel,
+        out_shape=[jax.ShapeDtypeStruct((2,) + own.shape[1:], F32)] * STEPS,
+        in_specs=[VMEM] * 2,
+        out_specs=[VMEM] * STEPS,
+        name="regroup",
+        compiler_params=GRANT,
+    )(own, came)
+    far = [
+        moved(grouped[step], (2 * ORDERS[0][step], 2 * ORDERS[1][step])) for step in range(STEPS)
+    ]
+    return [own, came] + far
 
 
 def dft_parts(channels):
@@ -208,15 +264,16 @@
     frames_dev = samples.shape[2] // channels
     frames = frames_dev * devices
 
+    chips = devices // 2
     pieces = pl.pallas_call(
         pieces_kernel,
-        out_shape=jax.ShapeDtypeStruct((devices, frames_dev, 24, channels), F32),
+        out_shape=[jax.ShapeDtypeStruct((chips, frames_dev, 24, channels), F32)] * 2,
         in_specs=[VMEM],
-        out_specs=VMEM,
+        out_specs=[VMEM] * 2,
         name="pieces",
         compiler_params=GRANT,
     )(samples)
-    arrived = lax.all_to_all(pieces, "band", split_axis=0, concat_axis=0, tiled=True)
+    arrived = exchange(*pieces)
 
     eight = lax.dynamic_slice_in_dim(dish_filter, position * 8, 8, 2)
     four = lax.dynamic_slice_in_dim(dish_filter, devices * 8 + position * 4, 4, 2)
@@ -224,45 +281,43 @@
     taps = jnp.transpose(taps, (1, 0, 2, 3))
     weights = pl.pallas_call(
         weights_kernel,
-        grid=(band_chans,),
         out_shape=jax.ShapeDtypeStruct((band_chans, 2 * beams, 2 * dishes), BF16),
-        in_specs=[
-            pl.BlockSpec((1, 2, dishes, beams), lambda i: (i, 0, 0, 0)),
-            pl.BlockSpec((1, dishes), lambda i: (0, 0)),
-            pl.BlockSpec((2 * dishes, 2), lambda i: (0, 0)),
-        ],
-        out_specs=pl.BlockSpec((1, 2 * beams, 2 * dishes), lambda i: (i, 0, 0)),
+        in_specs=[VMEM] * 3,
+        out_specs=VMEM,
         name="weights",
         compiler_params=GRANT,
         cost_estimate=pl.CostEstimate(
             flops=8 * 4 * 2 * 192 * 192 * 384, bytes_accessed=5 << 20, transcendentals=0
         ),
-    )(beam_weights[0], dish_order.reshape(1, dishes), slots_of(devices))
-
+    )(beam_weights[0], dish_order.reshape(1, dishes), slots_of(devices, position))
+
+    block = (6 * band_chans, channels)
     filtered = pl.pallas_call(
         channel_kernel,
-        out_shape=jax.ShapeDtypeStruct((devices, 6 * band_chans, channels), F32),
-        in_specs=[VMEM] * 4,
-        out_specs=VMEM,
+        out_shape=[jax.ShapeDtypeStruct((chips,) + block, F32)] * 2,
+        in_specs=[VMEM] * (5 + STEPS),
+        out_specs=[VMEM] * 2,
         scratch_shapes=[
+            pltpu.VMEM((frames + prototype.shape[0] - 1, 24, LANES), F32),
             pltpu.VMEM((frames, 24, 2 * LANES), F32),
             pltpu.VMEM((frames + fir_count - 1, 24, 2 * LANES), F32),
             pltpu.VMEM((frames * 24, LANES), F32),
+            pltpu.VMEM((devices,) + block, F32),
         ],
         name="channels",
         compiler_params=GRANT,
-    )(arrived.reshape(frames, 24, channels), prototype, dft_parts(channels), taps)
-    field = lax.all_to_all(filtered, "band", split_axis=0, concat_axis=0, tiled=True)
-    field = field.reshape(devices * 6 * band_chans, channels)
+    )(*arrived, prototype, dft_parts(channels), taps)
+    field = exchange(*filtered)
 
     power = pl.pallas_call(
         beams_kernel,
         out_shape=jax.ShapeDtypeStruct((band_chans, frames // INTEG, beams), F32),
-        in_specs=[VMEM] * 2,
+        in_specs=[VMEM] * (3 + STEPS),
         out_specs=VMEM,
+        scratch_shapes=[pltpu.VMEM((devices * 6 * band_chans, channels), F32)],
         name="beams",
         compiler_params=GRANT,
-    )(field, weights)
+    )(*field, weights)
     return jnp.transpose(power, (0, 2, 1))[None]
 
 
@@ -349,6 +404,7 @@
             channels == LANES
             and beam_weights.shape[1] == 8
             and devices * 8 == channels
+            and devices == 2 * (STEPS + 1)
             and dish_filter.shape[2] == 12 * devices
             and samples.shape[2] * devices == 32 * channels
         )

time: 43.9 us -> 41.8 us (0.952)
  starting transfers between devices: 11.1 us -> 24.3 us
  waiting for transfers between devices: 15.2 us -> 7.39 us
  Pallas kernels: 10.9 us -> 5.85 us
  local copies, waits for them, and re-layouts: 6.14 us -> 3.86 us
    ppermute x0 -> x16, starting transfers between devices: none -> 24.3 us  [moved(): return lax.ppermute(value, 'band', pairs)]
    all_to_all x2 -> x0, waiting for transfers between devices: 15.2 us -> none  [the longest x1 12.1 us: close_body(): lax.all_to_all(pieces, 'band', split_axis=0, concat_axis=0, tiled=True)]
    all_to_all x2 -> x0, starting transfers between devices: 11.1 us -> none  [the longest x1 7.52 us: close_body(): lax.all_to_all(pieces, 'band', split_axis=0, concat_axis=0, tiled=True)]
    ppermute x0 -> x16, waiting for transfers between devices: none -> 7.39 us  [moved(): return lax.ppermute(value, 'band', pairs)]
    pallas_call x3 -> x5, Pallas kernels: 8.32 us -> 3.21 us  [the longest x1 1.83 us: close_body(): pl.pallas_call(weights_kernel, out_shape=jax.ShapeDtypeStruct((band_chans...]
    unnamed x18, local copies, waits for them, and re-layouts: 6.1 us -> 3.72 us
  transfers between devices with their start and end apart: 2 -> 16, of which waited for: 2 -> 4; matrix products, arithmetic and copies ran while one was open for 0% -> 0% of each run, Pallas kernels for 13% -> 4%
where the time goes in v9:
time: 41.8 us; the launch traced here: 41.6 us
  starting transfers between devices  24.3 us (58%)
  waiting for transfers between devices  7.39 us (18%)
  Pallas kernels  5.85 us (14%)
  local copies, waits for them, and re-layouts  3.86 us (9%)
    ppermute x16, starting transfers between devices, moved(): return lax.ppermute(value, 'band', pairs)  24.3 us
    ppermute x16, waiting for transfers between devices, moved(): return lax.ppermute(value, 'band', pairs)  7.39 us
    unnamed x18, local copies, waits for them, and re-layouts  3.72 us
    pallas_call x1, Pallas kernels, close_body(): pl.pallas_call(beams_kernel, out_shape=jax.ShapeDtypeStruct((band_chans,...  2.64 us
    pallas_call x1, Pallas kernels, close_body(): pl.pallas_call(weights_kernel, out_shape=jax.ShapeDtypeStruct((band_chans...  1.83 us
    pallas_call x1, Pallas kernels, close_body(): pl.pallas_call(channel_kernel, out_shape=[jax.ShapeDtypeStruct((chips,) +...  1.26 us
  transfers between devices with their start and end apart: 16, of which 4 were waited for; matrix products, arithmetic and copies ran while one was open for 0% of the time, Pallas kernels for 4%

profile of v9, /device:TPU:0, one launch (start us, length us, event | category | flops | bytes accessed | tf_op | source)
XLA Modules:
  0.0 41.6 jit_solution(6855324329651573157)
XLA Ops:
  0.0 0.0 copy-start
  0.0 0.0 copy-start.8
  0.0 0.0 copy-start.6
  0.0 0.0 copy-start.2
  0.0 1.1 %copy-done.2 = f32[2,192,256]{2,1,0:T(8,128)S(1)} copy-done((f32[2,192,256]{2,1,0:T(8,128)S(1)}, f32[2,192,256]{2,1,0:T(8,128)}, u32[]{:S(2)}) %copy-start.2) | copy-done | bytes 393240
  1.1 0.0 copy-start.3
  1.1 0.0 copy-start.7
  1.1 0.0 copy-start.5
  1.1 0.1 pieces.1
  1.2 0.5 %collective-permute-start = (f32[8,2,24,128]{3,2,1,0:T(8,128)S(1)}, f32[8,2,24,128]{3,2,1,0:T(8,128)S(1)}, u32[]{:S(2)}, u32[]{:S(2)}) collective-permute-start(f32[8,2,24,128]{3,2,1,0:T(8,128)S(1)} %get-tuple-element.24), channel_id=1, source_target_pairs={{0,1},{1,0},{2,3},{3,2},{4,5},{5,4},{6,7},{7,6},{8,9},{9,8},{10,11... | collective-permute-start | bytes 589832 | tf_op jit(solution)/shard_map/ppermute | solution.py:228
  1.7 0.0 copy-done
  1.8 1.1 %collective-permute-done.came_ref.refs_1_ = f32[8,2,24,128]{3,2,1,0:T(8,128)S(1)} collective-permute-done((f32[8,2,24,128]{3,2,1,0:T(8,128)S(1)}, f32[8,2,24,128]{3,2,1,0:T(8,128)S(1)}, u32[]{:S(2)}, u32[]{:S(2)}) %collective-permute-start) | collective-permute-done | bytes 196640 | tf_op jit(solution)/shard_map/ppermute | solution.py:228
  2.8 5.0 %collective-permute-start.1 = (f32[2,2,24,128]{3,2,1,0:T(8,128)S(1)}, f32[2,2,24,128]{3,2,1,0:T(8,128)S(1)}, u32[]{:S(2)}, u32[]{:S(2)}) collective-permute-start(f32[2,2,24,128]{3,2,1,0:T(8,128)S(1)} %get-tuple-element.25), channel_id=1, source_target_pairs={{0,12},{1,5},{2,14},{3,7},{4,8},{5,1},{6,10},{7,3},{8,4},{9,13},{1... | collective-permute-start | bytes 147464 | tf_op jit(solution)/shard_map/ppermute | solution.py:228
  7.9 0.0 collective-permute-start.2
  7.9 1.8 %collective-permute-start.3 = (f32[2,2,24,128]{3,2,1,0:T(8,128)S(1)}, f32[2,2,24,128]{3,2,1,0:T(8,128)S(1)}, u32[]{:S(2)}, u32[]{:S(2)}) collective-permute-start(f32[2,2,24,128]{3,2,1,0:T(8,128)S(1)} %get-tuple-element.27), channel_id=1, source_target_pairs={{0,10},{1,3},{2,8},{3,1},{4,14},{5,7},{6,12},{7,5},{8,2},{9,11},{1... | collective-permute-start | bytes 147464 | tf_op jit(solution)/shard_map/ppermute | solution.py:228
  9.7 0.4 collective-permute-start.4
  10.1 4.7 %collective-permute-start.5 = (f32[2,2,24,128]{3,2,1,0:T(8,128)S(1)}, f32[2,2,24,128]{3,2,1,0:T(8,128)S(1)}, u32[]{:S(2)}, u32[]{:S(2)}) collective-permute-start(f32[2,2,24,128]{3,2,1,0:T(8,128)S(1)} %get-tuple-element.29), channel_id=1, source_target_pairs={{0,14},{1,7},{2,12},{3,5},{4,10},{5,3},{6,8},{7,1},{8,6},{9,15},{1... | collective-permute-start | bytes 147464 | tf_op jit(solution)/shard_map/ppermute | solution.py:228
  14.8 0.0 collective-permute-done.1.refs_2_
  14.8 0.0 collective-permute-start.6
  14.8 0.0 collective-permute-done.2.refs_3_
  14.8 0.6 %collective-permute-start.7 = (f32[2,2,24,128]{3,2,1,0:T(8,128)S(1)}, f32[2,2,24,128]{3,2,1,0:T(8,128)S(1)}, u32[]{:S(2)}, u32[]{:S(2)}) collective-permute-start(f32[2,2,24,128]{3,2,1,0:T(8,128)S(1)} %get-tuple-element.31), channel_id=1, source_target_pairs={{0,8},{1,11},{2,10},{3,9},{4,12},{5,15},{6,14},{7,13},{8,0},{9,3},... | collective-permute-start | bytes 147464 | tf_op jit(solution)/shard_map/ppermute | solution.py:228
  15.4 0.0 collective-permute-done.3.refs_4_
  15.4 0.0 collective-permute-done.4.refs_5_
  15.4 1.5 %collective-permute-done.5.refs_6_ = f32[2,2,24,128]{3,2,1,0:T(8,128)S(1)} collective-permute-done((f32[2,2,24,128]{3,2,1,0:T(8,128)S(1)}, f32[2,2,24,128]{3,2,1,0:T(8,128)S(1)}, u32[]{:S(2)}, u32[]{:S(2)}) %collective-permute-start.5) | collective-permute-done | bytes 49184 | tf_op jit(solution)/shard_map/ppermute | solution.py:228
  16.9 3.4 %collective-permute-done.6.refs_7_ = f32[2,2,24,128]{3,2,1,0:T(8,128)S(1)} collective-permute-done((f32[2,2,24,128]{3,2,1,0:T(8,128)S(1)}, f32[2,2,24,128]{3,2,1,0:T(8,128)S(1)}, u32[]{:S(2)}, u32[]{:S(2)}) %collective-permute-start.6) | collective-permute-done | bytes 49184 | tf_op jit(solution)/shard_map/ppermute | solution.py:228
  20.3 0.0 collective-permute-done.7.refs_8_
  20.3 0.0 copy-done.3
  20.3 0.0 copy-start.4
  20.3 0.7 %copy-done.4 = f32[16,128]{1,0:T(8,128)S(1)} copy-done((f32[16,128]{1,0:T(8,128)S(1)}, f32[16,128]{1,0:T(8,128)}, u32[]{:S(2)}) %copy-start.4) | copy-done | bytes 8216
  21.0 1.3 %channels.1 = (f32[8,48,128]{2,1,0:T(8,128)S(1)}, f32[8,48,128]{2,1,0:T(8,128)S(1)}) custom-call(f32[8,2,24,128]{3,2,1,0:T(8,128)S(1)} %get-tuple-element.23.own_ref.refs_0_, f32[8,2,24,128]{3,2,1,0:T(8,128)S(1)} %collective-permute-done.came_ref.refs_1_, f32[2,2,24,128]{3,2,1,0:T(8,128)S(1)} %collective-permute-done.1.refs_2_, ...), custom_call_target="tpu_custom_call" | custom-call | tf_op jit(solution)/shard_map/channels/pallas_call | solution.py:295
  22.2 0.1 collective-permute-start.8
  22.3 1.4 %collective-permute-done.8.came_ref.refs_1_ = f32[8,48,128]{2,1,0:T(8,128)S(1)} collective-permute-done((f32[8,48,128]{2,1,0:T(8,128)S(1)}, f32[8,48,128]{2,1,0:T(8,128)S(1)}, u32[]{:S(2)}, u32[]{:S(2)}) %collective-permute-start.8) | collective-permute-done | bytes 196640 | tf_op jit(solution)/shard_map/ppermute | solution.py:228
  23.8 1.0 %collective-permute-start.9 = (f32[2,48,128]{2,1,0:T(8,128)S(1)}, f32[2,48,128]{2,1,0:T(8,128)S(1)}, u32[]{:S(2)}, u32[]{:S(2)}) collective-permute-start(f32[2,48,128]{2,1,0:T(8,128)S(1)} %get-tuple-element.34), channel_id=1, source_target_pairs={{0,12},{1,5},{2,14},{3,7},{4,8},{5,1},{6,10},{7,3},{8,4},{9,13},{1... | collective-permute-start | bytes 147464 | tf_op jit(solution)/shard_map/ppermute | solution.py:228
  24.7 0.6 %collective-permute-start.10 = (f32[2,48,128]{2,1,0:T(8,128)S(1)}, f32[2,48,128]{2,1,0:T(8,128)S(1)}, u32[]{:S(2)}, u32[]{:S(2)}) collective-permute-start(f32[2,48,128]{2,1,0:T(8,128)S(1)} %get-tuple-element.35), channel_id=1, source_target_pairs={{0,4},{1,15},{2,6},{3,13},{4,0},{5,11},{6,2},{7,9},{8,12},{9,7},{1... | collective-permute-start | bytes 147464 | tf_op jit(solution)/shard_map/ppermute | solution.py:228
  25.4 0.0 copy-done.8
  25.4 0.0 copy-done.6
  25.4 0.0 copy-done.7
  25.4 0.1 copy.13.slot_ref
  25.5 2.5 %collective-permute-start.11 = (f32[2,48,128]{2,1,0:T(8,128)S(1)}, f32[2,48,128]{2,1,0:T(8,128)S(1)}, u32[]{:S(2)}, u32[]{:S(2)}) collective-permute-start(f32[2,48,128]{2,1,0:T(8,128)S(1)} %get-tuple-element.36), channel_id=1, source_target_pairs={{0,10},{1,3},{2,8},{3,1},{4,14},{5,7},{6,12},{7,5},{8,2},{9,11},{1... | collective-permute-start | bytes 147464 | tf_op jit(solution)/shard_map/ppermute | solution.py:228
  28.0 1.9 %collective-permute-start.12 = (f32[2,48,128]{2,1,0:T(8,128)S(1)}, f32[2,48,128]{2,1,0:T(8,128)S(1)}, u32[]{:S(2)}, u32[]{:S(2)}) collective-permute-start(f32[2,48,128]{2,1,0:T(8,128)S(1)} %get-tuple-element.37), channel_id=1, source_target_pairs={{0,2},{1,9},{2,0},{3,11},{4,6},{5,13},{6,4},{7,15},{8,10},{9,1},{1... | collective-permute-start | bytes 147464 | tf_op jit(solution)/shard_map/ppermute | solution.py:228
  29.9 2.4 %collective-permute-start.13 = (f32[2,48,128]{2,1,0:T(8,128)S(1)}, f32[2,48,128]{2,1,0:T(8,128)S(1)}, u32[]{:S(2)}, u32[]{:S(2)}) collective-permute-start(f32[2,48,128]{2,1,0:T(8,128)S(1)} %get-tuple-element.38), channel_id=1, source_target_pairs={{0,14},{1,7},{2,12},{3,5},{4,10},{5,3},{6,8},{7,1},{8,6},{9,15},{1... | collective-permute-start | bytes 147464 | tf_op jit(solution)/shard_map/ppermute | solution.py:228
  32.3 0.0 collective-permute-done.9.refs_2_
  32.3 0.0 collective-permute-start.14
  32.3 0.0 collective-permute-done.10.refs_3_
  32.3 2.9 %collective-permute-start.15 = (f32[2,48,128]{2,1,0:T(8,128)S(1)}, f32[2,48,128]{2,1,0:T(8,128)S(1)}, u32[]{:S(2)}, u32[]{:S(2)}) collective-permute-start(f32[2,48,128]{2,1,0:T(8,128)S(1)} %get-tuple-element.40), channel_id=1, source_target_pairs={{0,8},{1,11},{2,10},{3,9},{4,12},{5,15},{6,14},{7,13},{8,0},{9,3},... | collective-permute-start | bytes 147464 | tf_op jit(solution)/shard_map/ppermute | solution.py:228
  35.2 0.0 copy-done.5
  35.2 0.0 copy-start.1
  35.2 1.9 %copy-done.1 = f32[1,8,2,192,192]{4,3,2,1,0:T(8,128)S(1)} copy-done((f32[1,8,2,192,192]{4,3,2,1,0:T(8,128)S(1)}, f32[1,8,2,192,192]{4,3,2,1,0:T(8,128)}, u32[]{:S(2)}) %copy-start.1) | copy-done | bytes 2359320
  37.1 1.8 %weights.1.refs_9_ = bf16[8,384,384]{2,1,0:T(8,128)(2,1)S(1)} custom-call(f32[8,2,192,192]{3,2,1,0:T(8,128)S(1)} %bitcast.8, s32[1,192]{1,0:T(1,128)S(1)} %bitcast.9, s32[192,1]{1,0:T(8,128)S(1)} %copy.13.slot_ref), custom_call_target="tpu_custom_call" | custom-call | flops 905969664 | bytes 5242880 | tf_op jit(solution)/shard_map/weights/pallas_call | solution.py:282
  38.9 0.0 collective-permute-done.11.refs_4_
  38.9 0.0 collective-permute-done.12.refs_5_
  39.0 0.0 collective-permute-done.13.refs_6_
  39.0 0.0 collective-permute-done.14.refs_7_
  39.0 0.0 collective-permute-done.15.refs_8_
  39.0 2.6 %beams.1 = f32[8,8,192]{2,1,0:T(8,128)} custom-call(f32[8,48,128]{2,1,0:T(8,128)S(1)} %get-tuple-element.32.own_ref.refs_0_, f32[8,48,128]{2,1,0:T(8,128)S(1)} %collective-permute-done.8.came_ref.refs_1_, f32[2,48,128]{2,1,0:T(8,128)S(1)} %collective-permute-done.9.refs_2_, f32[2,48,128]{2,1,0:T(8,128)S(1)} %collective-permute-done.10.refs_3_, ...), custom_call_target="tpu_custom_call" | custom-call | tf_op jit(solution)/shard_map/beams/pallas_call | solution.py:312
  (6 shorter events, 0.1 us)
Async XLA Ops:
  0.0 1.7 %copy-start = (f32[2,8,192,128]{3,2,1,0:T(8,128)S(1)}, f32[2,8,192,128]{3,2,1,0:T(8,128)}, u32[]{:S(2)}) copy-start(f32[2,8,192,128]{3,2,1,0:T(8,128)} %param.10) | copy-start | bytes 4718596
  0.0 25.4 %copy-start.8 = (pred[192]{0:T(512)(128)(4,1)S(1)}, pred[192]{0:T(512)(128)(4,1)}, u32[]{:S(2)}) copy-start(pred[192]{0:T(512)(128)(4,1)} %constant.31) | copy-start | bytes 580
  0.0 25.4 %copy-start.6 = (s32[192]{0:T(256)S(1)}, s32[192]{0:T(256)}, u32[]{:S(2)}) copy-start(s32[192]{0:T(256)} %constant.28.clone) | copy-start | bytes 2308
  0.0 1.1 %copy-start.2 = (f32[2,192,256]{2,1,0:T(8,128)S(1)}, f32[2,192,256]{2,1,0:T(8,128)}, u32[]{:S(2)}) copy-start(f32[2,192,256]{2,1,0:T(8,128)} %x_ref.1) | copy-start | bytes 1179652
  1.1 19.2 %copy-start.3 = (bf16[768,256]{1,0:T(8,128)(2,1)S(1)}, bf16[768,256]{1,0:T(8,128)(2,1)}, u32[]{:S(2)}) copy-start(bf16[768,256]{1,0:T(8,128)(2,1)} %constant.29.clone.refs_10_) | copy-start | bytes 1179652
  1.1 24.3 %copy-start.7 = (s32[192]{0:T(256)S(1)}, s32[192]{0:T(256)}, u32[]{:S(2)}) copy-start(s32[192]{0:T(256)} %constant.27.clone) | copy-start | bytes 2308
  1.1 34.1 %copy-start.5 = (s32[192]{0:T(256)S(1)}, s32[192]{0:T(256)}, u32[]{:S(2)}) copy-start(s32[192]{0:T(256)} %param.12) | copy-start | bytes 2308
  1.2 1.6 %collective-permute-start = (f32[8,2,24,128]{3,2,1,0:T(8,128)S(1)}, f32[8,2,24,128]{3,2,1,0:T(8,128)S(1)}, u32[]{:S(2)}, u32[]{:S(2)}) collective-permute-start(f32[8,2,24,128]{3,2,1,0:T(8,128)S(1)} %get-tuple-element.24), channel_id=1, source_target_pairs={{0,1},{1,0},{2,3},{3,2},{4,5},{5,4},{6,7},{7,6},{8,9},{9,8},{10,11... | collective-permute-start | bytes 589832 | tf_op jit(solution)/shard_map/ppermute | solution.py:228
  2.8 11.9 %collective-permute-start.1 = (f32[2,2,24,128]{3,2,1,0:T(8,128)S(1)}, f32[2,2,24,128]{3,2,1,0:T(8,128)S(1)}, u32[]{:S(2)}, u32[]{:S(2)}) collective-permute-start(f32[2,2,24,128]{3,2,1,0:T(8,128)S(1)} %get-tuple-element.25), channel_id=1, source_target_pairs={{0,12},{1,5},{2,14},{3,7},{4,8},{5,1},{6,10},{7,3},{8,4},{9,13},{1... | collective-permute-start | bytes 147464 | tf_op jit(solution)/shard_map/ppermute | solution.py:228
  7.9 6.9 %collective-permute-start.2 = (f32[2,2,24,128]{3,2,1,0:T(8,128)S(1)}, f32[2,2,24,128]{3,2,1,0:T(8,128)S(1)}, u32[]{:S(2)}, u32[]{:S(2)}) collective-permute-start(f32[2,2,24,128]{3,2,1,0:T(8,128)S(1)} %get-tuple-element.26), channel_id=1, source_target_pairs={{0,4},{1,15},{2,6},{3,13},{4,0},{5,11},{6,2},{7,9},{8,12},{9,7},{1... | collective-permute-start | bytes 147464 | tf_op jit(solution)/shard_map/ppermute | solution.py:228
  7.9 7.5 %collective-permute-start.3 = (f32[2,2,24,128]{3,2,1,0:T(8,128)S(1)}, f32[2,2,24,128]{3,2,1,0:T(8,128)S(1)}, u32[]{:S(2)}, u32[]{:S(2)}) collective-permute-start(f32[2,2,24,128]{3,2,1,0:T(8,128)S(1)} %get-tuple-element.27), channel_id=1, source_target_pairs={{0,10},{1,3},{2,8},{3,1},{4,14},{5,7},{6,12},{7,5},{8,2},{9,11},{1... | collective-permute-start | bytes 147464 | tf_op jit(solution)/shard_map/ppermute | solution.py:228
  9.7 5.7 %collective-permute-start.4 = (f32[2,2,24,128]{3,2,1,0:T(8,128)S(1)}, f32[2,2,24,128]{3,2,1,0:T(8,128)S(1)}, u32[]{:S(2)}, u32[]{:S(2)}) collective-permute-start(f32[2,2,24,128]{3,2,1,0:T(8,128)S(1)} %get-tuple-element.28), channel_id=1, source_target_pairs={{0,2},{1,9},{2,0},{3,11},{4,6},{5,13},{6,4},{7,15},{8,10},{9,1},{1... | collective-permute-start | bytes 147464 | tf_op jit(solution)/shard_map/ppermute | solution.py:228
  10.1 6.8 %collective-permute-start.5 = (f32[2,2,24,128]{3,2,1,0:T(8,128)S(1)}, f32[2,2,24,128]{3,2,1,0:T(8,128)S(1)}, u32[]{:S(2)}, u32[]{:S(2)}) collective-permute-start(f32[2,2,24,128]{3,2,1,0:T(8,128)S(1)} %get-tuple-element.29), channel_id=1, source_target_pairs={{0,14},{1,7},{2,12},{3,5},{4,10},{5,3},{6,8},{7,1},{8,6},{9,15},{1... | collective-permute-start | bytes 147464 | tf_op jit(solution)/shard_map/ppermute | solution.py:228
  14.8 5.5 %collective-permute-start.6 = (f32[2,2,24,128]{3,2,1,0:T(8,128)S(1)}, f32[2,2,24,128]{3,2,1,0:T(8,128)S(1)}, u32[]{:S(2)}, u32[]{:S(2)}) collective-permute-start(f32[2,2,24,128]{3,2,1,0:T(8,128)S(1)} %get-tuple-element.30), channel_id=1, source_target_pairs={{0,6},{1,13},{2,4},{3,15},{4,2},{5,9},{6,0},{7,11},{8,14},{9,5},{1... | collective-permute-start | bytes 147464 | tf_op jit(solution)/shard_map/ppermute | solution.py:228
  14.8 5.5 %collective-permute-start.7 = (f32[2,2,24,128]{3,2,1,0:T(8,128)S(1)}, f32[2,2,24,128]{3,2,1,0:T(8,128)S(1)}, u32[]{:S(2)}, u32[]{:S(2)}) collective-permute-start(f32[2,2,24,128]{3,2,1,0:T(8,128)S(1)} %get-tuple-element.31), channel_id=1, source_target_pairs={{0,8},{1,11},{2,10},{3,9},{4,12},{5,15},{6,14},{7,13},{8,0},{9,3},... | collective-permute-start | bytes 147464 | tf_op jit(solution)/shard_map/ppermute | solution.py:228
  20.3 0.7 %copy-start.4 = (f32[16,128]{1,0:T(8,128)S(1)}, f32[16,128]{1,0:T(8,128)}, u32[]{:S(2)}) copy-start(f32[16,128]{1,0:T(8,128)} %refs_9_.1) | copy-start | bytes 24580
  22.2 1.5 %collective-permute-start.8 = (f32[8,48,128]{2,1,0:T(8,128)S(1)}, f32[8,48,128]{2,1,0:T(8,128)S(1)}, u32[]{:S(2)}, u32[]{:S(2)}) collective-permute-start(f32[8,48,128]{2,1,0:T(8,128)S(1)} %get-tuple-element.33), channel_id=1, source_target_pairs={{0,1},{1,0},{2,3},{3,2},{4,5},{5,4},{6,7},{7,6},{8,9},{9,8},{10,11... | collective-permute-start | bytes 589832 | tf_op jit(solution)/shard_map/ppermute | solution.py:228
  23.8 8.5 %collective-permute-start.9 = (f32[2,48,128]{2,1,0:T(8,128)S(1)}, f32[2,48,128]{2,1,0:T(8,128)S(1)}, u32[]{:S(2)}, u32[]{:S(2)}) collective-permute-start(f32[2,48,128]{2,1,0:T(8,128)S(1)} %get-tuple-element.34), channel_id=1, source_target_pairs={{0,12},{1,5},{2,14},{3,7},{4,8},{5,1},{6,10},{7,3},{8,4},{9,13},{1... | collective-permute-start | bytes 147464 | tf_op jit(solution)/shard_map/ppermute | solution.py:228
  24.7 7.5 %collective-permute-start.10 = (f32[2,48,128]{2,1,0:T(8,128)S(1)}, f32[2,48,128]{2,1,0:T(8,128)S(1)}, u32[]{:S(2)}, u32[]{:S(2)}) collective-permute-start(f32[2,48,128]{2,1,0:T(8,128)S(1)} %get-tuple-element.35), channel_id=1, source_target_pairs={{0,4},{1,15},{2,6},{3,13},{4,0},{5,11},{6,2},{7,9},{8,12},{9,7},{1... | collective-permute-start | bytes 147464 | tf_op jit(solution)/shard_map/ppermute | solution.py:228
  25.5 13.4 %collective-permute-start.11 = (f32[2,48,128]{2,1,0:T(8,128)S(1)}, f32[2,48,128]{2,1,0:T(8,128)S(1)}, u32[]{:S(2)}, u32[]{:S(2)}) collective-permute-start(f32[2,48,128]{2,1,0:T(8,128)S(1)} %get-tuple-element.36), channel_id=1, source_target_pairs={{0,10},{1,3},{2,8},{3,1},{4,14},{5,7},{6,12},{7,5},{8,2},{9,11},{1... | collective-permute-start | bytes 147464 | tf_op jit(solution)/shard_map/ppermute | solution.py:228
  28.0 10.9 %collective-permute-start.12 = (f32[2,48,128]{2,1,0:T(8,128)S(1)}, f32[2,48,128]{2,1,0:T(8,128)S(1)}, u32[]{:S(2)}, u32[]{:S(2)}) collective-permute-start(f32[2,48,128]{2,1,0:T(8,128)S(1)} %get-tuple-element.37), channel_id=1, source_target_pairs={{0,2},{1,9},{2,0},{3,11},{4,6},{5,13},{6,4},{7,15},{8,10},{9,1},{1... | collective-permute-start | bytes 147464 | tf_op jit(solution)/shard_map/ppermute | solution.py:228
  29.9 9.0 %collective-permute-start.13 = (f32[2,48,128]{2,1,0:T(8,128)S(1)}, f32[2,48,128]{2,1,0:T(8,128)S(1)}, u32[]{:S(2)}, u32[]{:S(2)}) collective-permute-start(f32[2,48,128]{2,1,0:T(8,128)S(1)} %get-tuple-element.38), channel_id=1, source_target_pairs={{0,14},{1,7},{2,12},{3,5},{4,10},{5,3},{6,8},{7,1},{8,6},{9,15},{1... | collective-permute-start | bytes 147464 | tf_op jit(solution)/shard_map/ppermute | solution.py:228
  32.3 6.7 %collective-permute-start.14 = (f32[2,48,128]{2,1,0:T(8,128)S(1)}, f32[2,48,128]{2,1,0:T(8,128)S(1)}, u32[]{:S(2)}, u32[]{:S(2)}) collective-permute-start(f32[2,48,128]{2,1,0:T(8,128)S(1)} %get-tuple-element.39), channel_id=1, source_target_pairs={{0,6},{1,13},{2,4},{3,15},{4,2},{5,9},{6,0},{7,11},{8,14},{9,5},{1... | collective-permute-start | bytes 147464 | tf_op jit(solution)/shard_map/ppermute | solution.py:228
  32.3 6.7 %collective-permute-start.15 = (f32[2,48,128]{2,1,0:T(8,128)S(1)}, f32[2,48,128]{2,1,0:T(8,128)S(1)}, u32[]{:S(2)}, u32[]{:S(2)}) collective-permute-start(f32[2,48,128]{2,1,0:T(8,128)S(1)} %get-tuple-element.40), channel_id=1, source_target_pairs={{0,8},{1,11},{2,10},{3,9},{4,12},{5,15},{6,14},{7,13},{8,0},{9,3},... | collective-permute-start | bytes 147464 | tf_op jit(solution)/shard_map/ppermute | solution.py:228
  35.2 1.9 %copy-start.1 = (f32[1,8,2,192,192]{4,3,2,1,0:T(8,128)S(1)}, f32[1,8,2,192,192]{4,3,2,1,0:T(8,128)}, u32[]{:S(2)}) copy-start(f32[1,8,2,192,192]{4,3,2,1,0:T(8,128)} %param.11) | copy-start | bytes 7077892

commit v10 on v9

--- a/solution.py
+++ b/solution.py
@@ -16,6 +16,7 @@
 BF16 = jnp.bfloat16
 LANES = 128
 VMEM = pl.BlockSpec(memory_space=pltpu.VMEM)
+HBM = pl.BlockSpec(memory_space=pltpu.HBM)
 GRANT = pltpu.CompilerParams(vmem_limit_bytes=16 << 20)
 
 
@@ -25,6 +26,9 @@
     angles = product.astype(jnp.float32) * (2.0 * math.pi / length)
     factor = 1.0 / math.sqrt(length)
     return (jnp.cos(angles) * factor, jnp.sin(angles) * factor)
+
+
+held = pltpu.with_memory_space_constraint
 
 
 def split(value):
@@ -81,17 +85,33 @@
             yield 2 * chip_at(place, step) + core, far_ref[core]
 
 
-def weights_kernel(w_ref, order_ref, slot_ref, out_ref):
+def weights_kernel(
+    w_ref, order_ref, slot_ref, table_ref, out_ref, table_out_ref, buffer, sems, table_sem
+):
+    table_copy = pltpu.make_async_copy(table_ref, table_out_ref, table_sem)
+    loads = [
+        pltpu.make_async_copy(w_ref.at[chan], buffer.at[chan], sems.at[chan])
+        for chan in range(w_ref.shape[0])
+    ]
+    ahead = 3
+    for load in loads[:ahead]:
+        load.start()
     hot = (slot_ref[...] == order_ref[...]).astype(F32).T.astype(BF16)
     beams = w_ref.shape[3]
-    for chan in range(w_ref.shape[0]):
+    for chan, load in enumerate(loads):
+        load.wait()
+        if chan + ahead < len(loads):
+            loads[chan + ahead].start()
+        elif chan + ahead == len(loads):
+            table_copy.start()
         for part in range(2):
             halves = [
                 jnp.dot(half, hot, preferred_element_type=F32).astype(BF16)
-                for half in split(w_ref[chan, part].T)
+                for half in split(buffer[chan, part].T)
             ]
             rows = slice(part * beams, (part + 1) * beams)
             out_ref[chan, rows, :] = jnp.concatenate(halves, axis=1)
+    table_copy.wait()
 
 
 def channel_kernel(*refs):
@@ -183,27 +203,29 @@
     row = lax.broadcasted_iota(jnp.int32, (16, 2 * LANES), 0)
     column = lax.broadcasted_iota(jnp.int32, (16, 2 * LANES), 1)
     pool = jnp.where(row == column % 64 // INTEG, 1.0 / INTEG, 0.0).astype(BF16)
-    for step in range(out_ref.shape[0] // 2):
+    steps = range(out_ref.shape[0] // 2)
+    fields = []
+    for step in steps:
         one = x_ref[pl.ds(2 * step, rows, stride=8), :]
         two = x_ref[pl.ds(2 * step + 1, rows, stride=8), :]
         first = jnp.where(even, one, pltpu.roll(two, 32, 1))
         second = jnp.where(even, pltpu.roll(one, LANES - 32, 1), two)
-        field = jnp.concatenate([first, second], axis=0)
-        high, rest = split(field)
-        both = jnp.concatenate([high, rest], axis=1)
-        both = jnp.concatenate([both, both], axis=0)
+        both = jnp.concatenate(split(jnp.concatenate([first, second], axis=0)), axis=1)
+        fields.append(jnp.concatenate([both, both], axis=0))
+    beam_of = []
+    for step in steps:
         sums = []
         for index in range(2):
-            product = jnp.dot(w_ref[2 * step + index], both, preferred_element_type=F32)
+            product = jnp.dot(w_ref[2 * step + index], fields[step], preferred_element_type=F32)
             sums.append(product[:, 0:LANES] + product[:, LANES : 2 * LANES])
         by_real = jnp.where(even_wide, sums[0][:beams], sums[1][:beams])
         by_imag = jnp.where(even_wide, sums[0][beams:], sums[1][beams:])
         crossed = pltpu.roll(by_imag, 64, 1)
-        beam = by_real + jnp.where(wide < 64, -crossed, crossed)
-        high, rest = split(beam * beam)
+        beam_of.append(by_real + jnp.where(wide < 64, -crossed, crossed))
+    for step in steps:
         power = lax.dot_general(
             pool,
-            jnp.concatenate([high, rest], axis=1),
+            jnp.concatenate(split(beam_of[step] * beam_of[step]), axis=1),
             (((1,), (1,)), ((), ())),
             preferred_element_type=F32,
         )
@@ -279,17 +301,32 @@
     four = lax.dynamic_slice_in_dim(dish_filter, devices * 8 + position * 4, 4, 2)
     taps = jnp.concatenate([eight, eight, four, four], axis=2)
     taps = jnp.transpose(taps, (1, 0, 2, 3))
-    weights = pl.pallas_call(
+    table = dft_parts(channels)
+    weights, table = pl.pallas_call(
         weights_kernel,
-        out_shape=jax.ShapeDtypeStruct((band_chans, 2 * beams, 2 * dishes), BF16),
-        in_specs=[VMEM] * 3,
-        out_specs=VMEM,
+        out_shape=[
+            jax.ShapeDtypeStruct((band_chans, 2 * beams, 2 * dishes), BF16),
+            jax.ShapeDtypeStruct(table.shape, BF16),
+        ],
+        in_specs=[HBM, VMEM, VMEM, HBM],
+        out_specs=[VMEM] * 2,
+        scratch_shapes=[
+            pltpu.VMEM((band_chans, 2, dishes, beams), F32),
+            pltpu.SemaphoreType.DMA((band_chans,)),
+            pltpu.SemaphoreType.DMA(()),
+        ],
         name="weights",
         compiler_params=GRANT,
         cost_estimate=pl.CostEstimate(
             flops=8 * 4 * 2 * 192 * 192 * 384, bytes_accessed=5 << 20, transcendentals=0
         ),
-    )(beam_weights[0], dish_order.reshape(1, dishes), slots_of(devices, position))
+    )(
+        held(beam_weights[0], pltpu.HBM),
+        dish_order.reshape(1, dishes),
+        slots_of(devices, position),
+        held(jnp.asarray(table), pltpu.HBM),
+    )
+    *arrived, weights, table = lax.optimization_barrier((*arrived, weights, table))
 
     block = (6 * band_chans, channels)
     filtered = pl.pallas_call(
@@ -306,7 +343,7 @@
         ],
         name="channels",
         compiler_params=GRANT,
-    )(*arrived, prototype, dft_parts(channels), taps)
+    )(*arrived, prototype, table, taps)
     field = exchange(*filtered)
 
     power = pl.pallas_call(

time: 41.8 us -> 41.9 us (level)
  Pallas kernels: 5.85 us -> 7.92 us
  local copies, waits for them, and re-layouts: 3.86 us -> 1.95 us
  waiting for transfers between devices: 7.39 us -> 6.46 us
  other arithmetic: 0.03 us -> 0.74 us
    pallas_call x1, Pallas kernels: 1.83 us -> 4.58 us  [close_body(): pl.pallas_call(weights_kernel, out_shape=[jax.ShapeDtypeStruct((band_chan...]
    unnamed x18 -> x8, local copies, waits for them, and re-layouts: 3.72 us -> 1.8 us
    ppermute x16, waiting for transfers between devices: 7.39 us -> 6.46 us  [moved(): return lax.ppermute(value, 'band', pairs)]
    select_n x1, other arithmetic: 0.01 us -> 0.72 us  [slots_of(): jnp.where(own < 8, source * 8 + own, devices * 8 + source * 4 + own - 8)]
    pallas_call x1, Pallas kernels: 2.64 us -> 1.93 us  [close_body(): pl.pallas_call(beams_kernel, out_shape=jax.ShapeDtypeStruct((band_chans,...]
  transfers between devices with their start and end apart: 16 -> 16, of which waited for: 4 -> 4; matrix products, arithmetic and copies ran while one was open for 0% -> 2% of each run, Pallas kernels for 4% -> 11%
where the time goes in v10:
time: 41.9 us; the launch traced here: 41.7 us
  starting transfers between devices  24.5 us (58%)
  Pallas kernels  7.92 us (19%)
  waiting for transfers between devices  6.46 us (15%)
  local copies, waits for them, and re-layouts  1.95 us (5%)
  other arithmetic  0.74 us (2%)
    ppermute x16, starting transfers between devices, moved(): return lax.ppermute(value, 'band', pairs)  24.5 us
    ppermute x16, waiting for transfers between devices, moved(): return lax.ppermute(value, 'band', pairs)  6.46 us
    pallas_call x1, Pallas kernels, close_body(): pl.pallas_call(weights_kernel, out_shape=[jax.ShapeDtypeStruct((band_chan...  4.58 us
    pallas_call x1, Pallas kernels, close_body(): pl.pallas_call(beams_kernel, out_shape=jax.ShapeDtypeStruct((band_chans,...  1.93 us
    unnamed x8, local copies, waits for them, and re-layouts  1.8 us
    pallas_call x1, Pallas kernels, close_body(): pl.pallas_call(channel_kernel, out_shape=[jax.ShapeDtypeStruct((chips,) +...  1.31 us
  transfers between devices with their start and end apart: 16, of which 4 were waited for; matrix products, arithmetic and copies ran while one was open for 2% of the time, Pallas kernels for 11%

profile of v10, /device:TPU:0, one launch (start us, length us, event | category | flops | bytes accessed | tf_op | source)
XLA Modules:
  0.0 41.7 jit_solution(2668148482204404306)
XLA Ops:
  0.0 0.0 copy-start
  0.0 0.0 copy-start.1
  0.0 1.1 %copy-done.1 = f32[2,192,256]{2,1,0:T(8,128)S(1)} copy-done((f32[2,192,256]{2,1,0:T(8,128)S(1)}, f32[2,192,256]{2,1,0:T(8,128)}, u32[]{:S(2)}) %copy-start.1) | copy-done | bytes 393240
  1.1 0.1 pieces.1
  1.2 0.5 %collective-permute-start = (f32[8,2,24,128]{3,2,1,0:T(8,128)S(1)}, f32[8,2,24,128]{3,2,1,0:T(8,128)S(1)}, u32[]{:S(2)}, u32[]{:S(2)}) collective-permute-start(f32[8,2,24,128]{3,2,1,0:T(8,128)S(1)} %get-tuple-element.37), channel_id=1, source_target_pairs={{0,1},{1,0},{2,3},{3,2},{4,5},{5,4},{6,7},{7,6},{8,9},{9,8},{10,11... | collective-permute-start | bytes 589832 | tf_op jit(solution)/shard_map/ppermute | solution.py:250
  1.7 0.0 copy-done
  1.8 0.7 %fusion.1 = s32[192]{0:T(256)S(1)} fusion(pred[192]{0:T(512)(128)(4,1)} %constant.31, s32[192]{0:T(256)} %constant.27.clone, s32[192]{0:T(256)} %constant.28.clone, s32[]{:T(128)S(6)} %axis_index.12), kind=kLoop, calls=%fused_computation.5 | loop fusion | flops 1536 | bytes 2500 | tf_op jit(solution)/shard_map/jit(_where)/select_n | solution.py:241
  2.5 0.3 collective-permute-done.came_ref.refs_1_
  2.8 5.0 %collective-permute-start.1 = (f32[2,2,24,128]{3,2,1,0:T(8,128)S(1)}, f32[2,2,24,128]{3,2,1,0:T(8,128)S(1)}, u32[]{:S(2)}, u32[]{:S(2)}) collective-permute-start(f32[2,2,24,128]{3,2,1,0:T(8,128)S(1)} %get-tuple-element.38), channel_id=1, source_target_pairs={{0,12},{1,5},{2,14},{3,7},{4,8},{5,1},{6,10},{7,3},{8,4},{9,13},{1... | collective-permute-start | bytes 147464 | tf_op jit(solution)/shard_map/ppermute | solution.py:250
  7.8 0.0 collective-permute-start.2
  7.9 0.1 copy.11.slot_ref
  8.0 1.8 %collective-permute-start.3 = (f32[2,2,24,128]{3,2,1,0:T(8,128)S(1)}, f32[2,2,24,128]{3,2,1,0:T(8,128)S(1)}, u32[]{:S(2)}, u32[]{:S(2)}) collective-permute-start(f32[2,2,24,128]{3,2,1,0:T(8,128)S(1)} %get-tuple-element.40), channel_id=1, source_target_pairs={{0,10},{1,3},{2,8},{3,1},{4,14},{5,7},{6,12},{7,5},{8,2},{9,11},{1... | collective-permute-start | bytes 147464 | tf_op jit(solution)/shard_map/ppermute | solution.py:250
  9.8 0.4 collective-permute-start.4
  10.2 4.7 %collective-permute-start.5 = (f32[2,2,24,128]{3,2,1,0:T(8,128)S(1)}, f32[2,2,24,128]{3,2,1,0:T(8,128)S(1)}, u32[]{:S(2)}, u32[]{:S(2)}) collective-permute-start(f32[2,2,24,128]{3,2,1,0:T(8,128)S(1)} %get-tuple-element.42), channel_id=1, source_target_pairs={{0,14},{1,7},{2,12},{3,5},{4,10},{5,3},{6,8},{7,1},{8,6},{9,15},{1... | collective-permute-start | bytes 147464 | tf_op jit(solution)/shard_map/ppermute | solution.py:250
  14.9 0.0 collective-permute-done.1.refs_2_
  14.9 0.0 collective-permute-start.6
  14.9 0.0 collective-permute-done.2.refs_3_
  14.9 0.6 %collective-permute-start.7 = (f32[2,2,24,128]{3,2,1,0:T(8,128)S(1)}, f32[2,2,24,128]{3,2,1,0:T(8,128)S(1)}, u32[]{:S(2)}, u32[]{:S(2)}) collective-permute-start(f32[2,2,24,128]{3,2,1,0:T(8,128)S(1)} %get-tuple-element.44), channel_id=1, source_target_pairs={{0,8},{1,11},{2,10},{3,9},{4,12},{5,15},{6,14},{7,13},{8,0},{9,3},... | collective-permute-start | bytes 147464 | tf_op jit(solution)/shard_map/ppermute | solution.py:250
  15.5 0.0 copy-start.3
  15.5 0.7 %copy-done.3 = s32[192]{0:T(256)S(1)} copy-done((s32[192]{0:T(256)S(1)}, s32[192]{0:T(256)}, u32[]{:S(2)}) %copy-start.3) | copy-done | bytes 792
  16.1 0.0 copy-start.2
  16.1 4.6 %weights.1 = (bf16[8,384,384]{2,1,0:T(8,128)(2,1)S(1)}, bf16[768,256]{1,0:T(8,128)(2,1)S(1)}) custom-call(f32[8,2,192,192]{3,2,1,0:T(8,128)} %bitcast.9, s32[1,192]{1,0:T(1,128)S(1)} %bitcast.8, s32[192,1]{1,0:T(8,128)S(1)} %copy.11.slot_ref, bf16[768,256]{1,0:T(8,128)(2,1)} %constant.29.clone.table_ref), custom_call_target="tpu_custom_call" | custom-call | flops 905969664 | bytes 5242880 | tf_op jit(solution)/shard_map/weights/pallas_call | solution.py:305
  20.7 0.0 collective-permute-done.3.refs_4_
  20.7 0.0 collective-permute-done.4.refs_5_
  20.7 0.0 collective-permute-done.5.refs_6_
  20.8 0.0 collective-permute-done.6.refs_7_
  20.8 0.0 collective-permute-done.7.refs_8_
  20.8 0.0 copy-done.2
  20.8 1.3 %channels.1 = (f32[8,48,128]{2,1,0:T(8,128)S(1)}, f32[8,48,128]{2,1,0:T(8,128)S(1)}) custom-call(f32[8,2,24,128]{3,2,1,0:T(8,128)S(1)} %get-tuple-element.47.own_ref.refs_0_, f32[8,2,24,128]{3,2,1,0:T(8,128)S(1)} %collective-permute-done.came_ref.refs_1_, f32[2,2,24,128]{3,2,1,0:T(8,128)S(1)} %collective-permute-done.1.refs_2_, ...), custom_call_target="tpu_custom_call" | custom-call | tf_op jit(solution)/shard_map/channels/pallas_call | solution.py:332
  22.1 0.1 collective-permute-start.8
  22.2 1.4 %collective-permute-done.8.came_ref.refs_1_ = f32[8,48,128]{2,1,0:T(8,128)S(1)} collective-permute-done((f32[8,48,128]{2,1,0:T(8,128)S(1)}, f32[8,48,128]{2,1,0:T(8,128)S(1)}, u32[]{:S(2)}, u32[]{:S(2)}) %collective-permute-start.8) | collective-permute-done | bytes 196640 | tf_op jit(solution)/shard_map/ppermute | solution.py:250
  23.6 3.8 %collective-permute-start.9 = (f32[2,48,128]{2,1,0:T(8,128)S(1)}, f32[2,48,128]{2,1,0:T(8,128)S(1)}, u32[]{:S(2)}, u32[]{:S(2)}) collective-permute-start(f32[2,48,128]{2,1,0:T(8,128)S(1)} %get-tuple-element.59), channel_id=1, source_target_pairs={{0,12},{1,5},{2,14},{3,7},{4,8},{5,1},{6,10},{7,3},{8,4},{9,13},{1... | collective-permute-start | bytes 147464 | tf_op jit(solution)/shard_map/ppermute | solution.py:250
  27.4 0.0 collective-permute-start.10
  27.4 1.7 %collective-permute-start.11 = (f32[2,48,128]{2,1,0:T(8,128)S(1)}, f32[2,48,128]{2,1,0:T(8,128)S(1)}, u32[]{:S(2)}, u32[]{:S(2)}) collective-permute-start(f32[2,48,128]{2,1,0:T(8,128)S(1)} %get-tuple-element.61), channel_id=1, source_target_pairs={{0,10},{1,3},{2,8},{3,1},{4,14},{5,7},{6,12},{7,5},{8,2},{9,11},{1... | collective-permute-start | bytes 147464 | tf_op jit(solution)/shard_map/ppermute | solution.py:250
  29.2 0.4 collective-permute-start.12
  29.6 4.7 %collective-permute-start.13 = (f32[2,48,128]{2,1,0:T(8,128)S(1)}, f32[2,48,128]{2,1,0:T(8,128)S(1)}, u32[]{:S(2)}, u32[]{:S(2)}) collective-permute-start(f32[2,48,128]{2,1,0:T(8,128)S(1)} %get-tuple-element.63), channel_id=1, source_target_pairs={{0,14},{1,7},{2,12},{3,5},{4,10},{5,3},{6,8},{7,1},{8,6},{9,15},{1... | collective-permute-start | bytes 147464 | tf_op jit(solution)/shard_map/ppermute | solution.py:250
  34.3 0.0 collective-permute-done.9.refs_2_
  34.3 0.0 collective-permute-start.14
  34.3 0.0 collective-permute-done.10.refs_3_
  34.3 0.8 %collective-permute-start.15 = (f32[2,48,128]{2,1,0:T(8,128)S(1)}, f32[2,48,128]{2,1,0:T(8,128)S(1)}, u32[]{:S(2)}, u32[]{:S(2)}) collective-permute-start(f32[2,48,128]{2,1,0:T(8,128)S(1)} %get-tuple-element.65), channel_id=1, source_target_pairs={{0,8},{1,11},{2,10},{3,9},{4,12},{5,15},{6,14},{7,13},{8,0},{9,3},... | collective-permute-start | bytes 147464 | tf_op jit(solution)/shard_map/ppermute | solution.py:250
  35.1 0.0 collective-permute-done.11.refs_4_
  35.1 0.0 collective-permute-done.12.refs_5_
  35.1 1.3 %collective-permute-done.13.refs_6_ = f32[2,48,128]{2,1,0:T(8,128)S(1)} collective-permute-done((f32[2,48,128]{2,1,0:T(8,128)S(1)}, f32[2,48,128]{2,1,0:T(8,128)S(1)}, u32[]{:S(2)}, u32[]{:S(2)}) %collective-permute-start.13) | collective-permute-done | bytes 49184 | tf_op jit(solution)/shard_map/ppermute | solution.py:250
  36.3 3.4 %collective-permute-done.14.refs_7_ = f32[2,48,128]{2,1,0:T(8,128)S(1)} collective-permute-done((f32[2,48,128]{2,1,0:T(8,128)S(1)}, f32[2,48,128]{2,1,0:T(8,128)S(1)}, u32[]{:S(2)}, u32[]{:S(2)}) %collective-permute-start.14) | collective-permute-done | bytes 49184 | tf_op jit(solution)/shard_map/ppermute | solution.py:250
  39.8 0.0 collective-permute-done.15.refs_8_
  39.8 1.9 %beams.1 = f32[8,8,192]{2,1,0:T(8,128)} custom-call(f32[8,48,128]{2,1,0:T(8,128)S(1)} %get-tuple-element.57.own_ref.refs_0_, f32[8,48,128]{2,1,0:T(8,128)S(1)} %collective-permute-done.8.came_ref.refs_1_, f32[2,48,128]{2,1,0:T(8,128)S(1)} %collective-permute-done.9.refs_2_, f32[2,48,128]{2,1,0:T(8,128)S(1)} %collective-permute-done.10.refs_3_, ...), custom_call_target="tpu_custom_call" | custom-call | tf_op jit(solution)/shard_map/beams/pallas_call | solution.py:349
  (5 shorter events, 0.1 us)
Async XLA Ops:
  0.0 1.7 %copy-start = (f32[2,8,192,128]{3,2,1,0:T(8,128)S(1)}, f32[2,8,192,128]{3,2,1,0:T(8,128)}, u32[]{:S(2)}) copy-start(f32[2,8,192,128]{3,2,1,0:T(8,128)} %param.10) | copy-start | bytes 4718596
  0.0 1.1 %copy-start.1 = (f32[2,192,256]{2,1,0:T(8,128)S(1)}, f32[2,192,256]{2,1,0:T(8,128)}, u32[]{:S(2)}) copy-start(f32[2,192,256]{2,1,0:T(8,128)} %x_ref.1) | copy-start | bytes 1179652
  1.2 1.6 %collective-permute-start = (f32[8,2,24,128]{3,2,1,0:T(8,128)S(1)}, f32[8,2,24,128]{3,2,1,0:T(8,128)S(1)}, u32[]{:S(2)}, u32[]{:S(2)}) collective-permute-start(f32[8,2,24,128]{3,2,1,0:T(8,128)S(1)} %get-tuple-element.37), channel_id=1, source_target_pairs={{0,1},{1,0},{2,3},{3,2},{4,5},{5,4},{6,7},{7,6},{8,9},{9,8},{10,11... | collective-permute-start | bytes 589832 | tf_op jit(solution)/shard_map/ppermute | solution.py:250
  2.8 12.1 %collective-permute-start.1 = (f32[2,2,24,128]{3,2,1,0:T(8,128)S(1)}, f32[2,2,24,128]{3,2,1,0:T(8,128)S(1)}, u32[]{:S(2)}, u32[]{:S(2)}) collective-permute-start(f32[2,2,24,128]{3,2,1,0:T(8,128)S(1)} %get-tuple-element.38), channel_id=1, source_target_pairs={{0,12},{1,5},{2,14},{3,7},{4,8},{5,1},{6,10},{7,3},{8,4},{9,13},{1... | collective-permute-start | bytes 147464 | tf_op jit(solution)/shard_map/ppermute | solution.py:250
  7.8 7.0 %collective-permute-start.2 = (f32[2,2,24,128]{3,2,1,0:T(8,128)S(1)}, f32[2,2,24,128]{3,2,1,0:T(8,128)S(1)}, u32[]{:S(2)}, u32[]{:S(2)}) collective-permute-start(f32[2,2,24,128]{3,2,1,0:T(8,128)S(1)} %get-tuple-element.39), channel_id=1, source_target_pairs={{0,4},{1,15},{2,6},{3,13},{4,0},{5,11},{6,2},{7,9},{8,12},{9,7},{1... | collective-permute-start | bytes 147464 | tf_op jit(solution)/shard_map/ppermute | solution.py:250
  8.0 12.7 %collective-permute-start.3 = (f32[2,2,24,128]{3,2,1,0:T(8,128)S(1)}, f32[2,2,24,128]{3,2,1,0:T(8,128)S(1)}, u32[]{:S(2)}, u32[]{:S(2)}) collective-permute-start(f32[2,2,24,128]{3,2,1,0:T(8,128)S(1)} %get-tuple-element.40), channel_id=1, source_target_pairs={{0,10},{1,3},{2,8},{3,1},{4,14},{5,7},{6,12},{7,5},{8,2},{9,11},{1... | collective-permute-start | bytes 147464 | tf_op jit(solution)/shard_map/ppermute | solution.py:250
  9.8 10.9 %collective-permute-start.4 = (f32[2,2,24,128]{3,2,1,0:T(8,128)S(1)}, f32[2,2,24,128]{3,2,1,0:T(8,128)S(1)}, u32[]{:S(2)}, u32[]{:S(2)}) collective-permute-start(f32[2,2,24,128]{3,2,1,0:T(8,128)S(1)} %get-tuple-element.41), channel_id=1, source_target_pairs={{0,2},{1,9},{2,0},{3,11},{4,6},{5,13},{6,4},{7,15},{8,10},{9,1},{1... | collective-permute-start | bytes 147464 | tf_op jit(solution)/shard_map/ppermute | solution.py:250
  10.2 10.6 %collective-permute-start.5 = (f32[2,2,24,128]{3,2,1,0:T(8,128)S(1)}, f32[2,2,24,128]{3,2,1,0:T(8,128)S(1)}, u32[]{:S(2)}, u32[]{:S(2)}) collective-permute-start(f32[2,2,24,128]{3,2,1,0:T(8,128)S(1)} %get-tuple-element.42), channel_id=1, source_target_pairs={{0,14},{1,7},{2,12},{3,5},{4,10},{5,3},{6,8},{7,1},{8,6},{9,15},{1... | collective-permute-start | bytes 147464 | tf_op jit(solution)/shard_map/ppermute | solution.py:250
  14.9 5.9 %collective-permute-start.6 = (f32[2,2,24,128]{3,2,1,0:T(8,128)S(1)}, f32[2,2,24,128]{3,2,1,0:T(8,128)S(1)}, u32[]{:S(2)}, u32[]{:S(2)}) collective-permute-start(f32[2,2,24,128]{3,2,1,0:T(8,128)S(1)} %get-tuple-element.43), channel_id=1, source_target_pairs={{0,6},{1,13},{2,4},{3,15},{4,2},{5,9},{6,0},{7,11},{8,14},{9,5},{1... | collective-permute-start | bytes 147464 | tf_op jit(solution)/shard_map/ppermute | solution.py:250
  14.9 5.9 %collective-permute-start.7 = (f32[2,2,24,128]{3,2,1,0:T(8,128)S(1)}, f32[2,2,24,128]{3,2,1,0:T(8,128)S(1)}, u32[]{:S(2)}, u32[]{:S(2)}) collective-permute-start(f32[2,2,24,128]{3,2,1,0:T(8,128)S(1)} %get-tuple-element.44), channel_id=1, source_target_pairs={{0,8},{1,11},{2,10},{3,9},{4,12},{5,15},{6,14},{7,13},{8,0},{9,3},... | collective-permute-start | bytes 147464 | tf_op jit(solution)/shard_map/ppermute | solution.py:250
  15.5 0.7 %copy-start.3 = (s32[192]{0:T(256)S(1)}, s32[192]{0:T(256)}, u32[]{:S(2)}) copy-start(s32[192]{0:T(256)} %param.12) | copy-start | bytes 2308
  16.1 4.6 %copy-start.2 = (f32[16,128]{1,0:T(8,128)S(1)}, f32[16,128]{1,0:T(8,128)}, u32[]{:S(2)}) copy-start(f32[16,128]{1,0:T(8,128)} %refs_9_.1) | copy-start | bytes 24580
  22.1 1.5 %collective-permute-start.8 = (f32[8,48,128]{2,1,0:T(8,128)S(1)}, f32[8,48,128]{2,1,0:T(8,128)S(1)}, u32[]{:S(2)}, u32[]{:S(2)}) collective-permute-start(f32[8,48,128]{2,1,0:T(8,128)S(1)} %get-tuple-element.58), channel_id=1, source_target_pairs={{0,1},{1,0},{2,3},{3,2},{4,5},{5,4},{6,7},{7,6},{8,9},{9,8},{10,11... | collective-permute-start | bytes 589832 | tf_op jit(solution)/shard_map/ppermute | solution.py:250
  23.6 10.6 %collective-permute-start.9 = (f32[2,48,128]{2,1,0:T(8,128)S(1)}, f32[2,48,128]{2,1,0:T(8,128)S(1)}, u32[]{:S(2)}, u32[]{:S(2)}) collective-permute-start(f32[2,48,128]{2,1,0:T(8,128)S(1)} %get-tuple-element.59), channel_id=1, source_target_pairs={{0,12},{1,5},{2,14},{3,7},{4,8},{5,1},{6,10},{7,3},{8,4},{9,13},{1... | collective-permute-start | bytes 147464 | tf_op jit(solution)/shard_map/ppermute | solution.py:250
  27.4 6.8 %collective-permute-start.10 = (f32[2,48,128]{2,1,0:T(8,128)S(1)}, f32[2,48,128]{2,1,0:T(8,128)S(1)}, u32[]{:S(2)}, u32[]{:S(2)}) collective-permute-start(f32[2,48,128]{2,1,0:T(8,128)S(1)} %get-tuple-element.60), channel_id=1, source_target_pairs={{0,4},{1,15},{2,6},{3,13},{4,0},{5,11},{6,2},{7,9},{8,12},{9,7},{1... | collective-permute-start | bytes 147464 | tf_op jit(solution)/shard_map/ppermute | solution.py:250
  27.4 7.6 %collective-permute-start.11 = (f32[2,48,128]{2,1,0:T(8,128)S(1)}, f32[2,48,128]{2,1,0:T(8,128)S(1)}, u32[]{:S(2)}, u32[]{:S(2)}) collective-permute-start(f32[2,48,128]{2,1,0:T(8,128)S(1)} %get-tuple-element.61), channel_id=1, source_target_pairs={{0,10},{1,3},{2,8},{3,1},{4,14},{5,7},{6,12},{7,5},{8,2},{9,11},{1... | collective-permute-start | bytes 147464 | tf_op jit(solution)/shard_map/ppermute | solution.py:250
  29.2 5.9 %collective-permute-start.12 = (f32[2,48,128]{2,1,0:T(8,128)S(1)}, f32[2,48,128]{2,1,0:T(8,128)S(1)}, u32[]{:S(2)}, u32[]{:S(2)}) collective-permute-start(f32[2,48,128]{2,1,0:T(8,128)S(1)} %get-tuple-element.62), channel_id=1, source_target_pairs={{0,2},{1,9},{2,0},{3,11},{4,6},{5,13},{6,4},{7,15},{8,10},{9,1},{1... | collective-permute-start | bytes 147464 | tf_op jit(solution)/shard_map/ppermute | solution.py:250
  29.6 6.8 %collective-permute-start.13 = (f32[2,48,128]{2,1,0:T(8,128)S(1)}, f32[2,48,128]{2,1,0:T(8,128)S(1)}, u32[]{:S(2)}, u32[]{:S(2)}) collective-permute-start(f32[2,48,128]{2,1,0:T(8,128)S(1)} %get-tuple-element.63), channel_id=1, source_target_pairs={{0,14},{1,7},{2,12},{3,5},{4,10},{5,3},{6,8},{7,1},{8,6},{9,15},{1... | collective-permute-start | bytes 147464 | tf_op jit(solution)/shard_map/ppermute | solution.py:250
  34.3 5.5 %collective-permute-start.14 = (f32[2,48,128]{2,1,0:T(8,128)S(1)}, f32[2,48,128]{2,1,0:T(8,128)S(1)}, u32[]{:S(2)}, u32[]{:S(2)}) collective-permute-start(f32[2,48,128]{2,1,0:T(8,128)S(1)} %get-tuple-element.64), channel_id=1, source_target_pairs={{0,6},{1,13},{2,4},{3,15},{4,2},{5,9},{6,0},{7,11},{8,14},{9,5},{1... | collective-permute-start | bytes 147464 | tf_op jit(solution)/shard_map/ppermute | solution.py:250
  34.3 5.5 %collective-permute-start.15 = (f32[2,48,128]{2,1,0:T(8,128)S(1)}, f32[2,48,128]{2,1,0:T(8,128)S(1)}, u32[]{:S(2)}, u32[]{:S(2)}) collective-permute-start(f32[2,48,128]{2,1,0:T(8,128)S(1)} %get-tuple-element.65), channel_id=1, source_target_pairs={{0,8},{1,11},{2,10},{3,9},{4,12},{5,15},{6,14},{7,13},{8,0},{9,3},... | collective-permute-start | bytes 147464 | tf_op jit(solution)/shard_map/ppermute | solution.py:250

commit v11 on v10

--- a/solution.py
+++ b/solution.py
@@ -9,8 +9,6 @@
 from jax.sharding import PartitionSpec as P
 
 INTEG = 4
-ORDERS = ((6, 2, 5, 1, 7, 3, 4), (2, 7, 1, 4, 3, 6, 5))
-STEPS = len(ORDERS[0])
 HIGHEST = lax.Precision.HIGHEST
 F32 = jnp.float32
 BF16 = jnp.bfloat16
@@ -40,57 +38,50 @@
     return part * 8 + dish if dish < 8 else 16 + part * 4 + dish - 8
 
 
-def chip_at(place, step):
-    return jnp.where(place % 2 == 0, ORDERS[0][step], ORDERS[1][step])
-
-
 def pieces_kernel(x_ref, own_ref, other_ref):
-    place = lax.axis_index("band")
+    core = lax.axis_index("band") % 2
     chips, frames_dev = own_ref.shape[:2]
     first_rest = chips * 16
     low = lax.broadcasted_iota(jnp.int32, (8, LANES), 0) < 4
     for chip in range(chips):
-        for core, out_ref in enumerate((own_ref, other_ref)):
-            dest = place ^ (2 * chip + core)
+        for other, out_ref in enumerate((own_ref, other_ref)):
+            dest = 2 * chip + (core ^ other)
             rows = pl.ds(pl.multiple_of(dest * 8, 8), 8)
             for frame in range(frames_dev):
                 lanes = slice(frame * LANES, (frame + 1) * LANES)
                 for part in range(2):
                     out_ref[chip, frame, part * 8 : part * 8 + 8, :] = x_ref[part, rows, lanes]
-        pair = (place ^ (2 * chip)) // 2
-        rows = pl.ds(pl.multiple_of(first_rest + pair * 8, 8), 8)
+        rows = slice(first_rest + chip * 8, first_rest + chip * 8 + 8)
         for frame in range(frames_dev):
             lanes = slice(frame * LANES, (frame + 1) * LANES)
             real, imag = x_ref[0, rows, lanes], x_ref[1, rows, lanes]
             even = jnp.where(low, real, pltpu.roll(imag, 4, 0))
             odd = jnp.where(low, pltpu.roll(real, 4, 0), imag)
-            is_even = place % 2 == 0
-            own_ref[chip, frame, 16:24, :] = jnp.where(is_even, even, odd)
-            other_ref[chip, frame, 16:24, :] = jnp.where(is_even, odd, even)
-
-
-def regroup_kernel(own_ref, came_ref, *out_refs):
-    place = lax.axis_index("band")
-    for step, out_ref in enumerate(out_refs):
-        chip = chip_at(place, step)
-        out_ref[0] = own_ref[chip]
-        out_ref[1] = came_ref[chip]
-
-
-def sources(place, own_ref, came_ref, far_refs):
-    yield 0, own_ref[0]
-    yield 1, came_ref[0]
-    for step, far_ref in enumerate(far_refs):
-        for core in range(2):
-            yield 2 * chip_at(place, step) + core, far_ref[core]
+            own_ref[chip, frame, 16:24, :] = jnp.where(core == 0, even, odd)
+            other_ref[chip, frame, 16:24, :] = jnp.where(core == 0, odd, even)
+
+
+def join_kernel(own_ref, came_ref, out_ref, sems):
+    copies = [
+        pltpu.make_async_copy(ref, out_ref.at[:, other], sems.at[other])
+        for other, ref in enumerate((own_ref, came_ref))
+    ]
+    for copy in copies:
+        copy.start()
+    for copy in copies:
+        copy.wait()
 
 
 def weights_kernel(
-    w_ref, order_ref, slot_ref, table_ref, out_ref, table_out_ref, buffer, sems, table_sem
+    w_ref, order_ref, slot_ref, table_ref, out_ref, table_out_ref, buffer, made, sems, table_sem
 ):
     table_copy = pltpu.make_async_copy(table_ref, table_out_ref, table_sem)
     loads = [
-        pltpu.make_async_copy(w_ref.at[chan], buffer.at[chan], sems.at[chan])
+        pltpu.make_async_copy(w_ref.at[chan], buffer.at[chan], sems.at[0, chan])
+        for chan in range(w_ref.shape[0])
+    ]
+    stores = [
+        pltpu.make_async_copy(made.at[chan], out_ref.at[chan], sems.at[1, chan])
         for chan in range(w_ref.shape[0])
     ]
     ahead = 3
@@ -110,26 +101,29 @@
                 for half in split(buffer[chan, part].T)
             ]
             rows = slice(part * beams, (part + 1) * beams)
-            out_ref[chan, rows, :] = jnp.concatenate(halves, axis=1)
+            made[chan, rows, :] = jnp.concatenate(halves, axis=1)
+        stores[chan].start()
+    for store in stores:
+        store.wait()
     table_copy.wait()
 
 
-def channel_kernel(*refs):
-    came, refs = refs[: 2 + STEPS], refs[2 + STEPS :]
-    proto_ref, table_ref, taps_ref, own_ref, other_ref = refs[:5]
-    past, poly, spec, filt, ready = refs[5:]
-    place = lax.axis_index("band")
+def channel_kernel(
+    x_ref, proto_ref, table_ref, taps_ref, own_ref, other_ref, past, poly, spec, filt, ready
+):
+    core = lax.axis_index("band") % 2
     pfb_count = proto_ref.shape[0]
     fir_count = taps_ref.shape[0]
-    frames_dev = came[0].shape[1]
+    chips, _, frames_dev = x_ref.shape[:3]
     frames = poly.shape[0]
     group = 8
     low = lax.broadcasted_iota(jnp.int32, (group, 8, LANES), 1) < 4
 
     past[0 : pfb_count - 1] = jnp.zeros((pfb_count - 1, 24, LANES), F32)
-    for other, block in sources(place, came[0], came[1], came[2:]):
-        begin = pfb_count - 1 + (place ^ other) * frames_dev
-        past[pl.ds(begin, frames_dev)] = block
+    for chip in range(chips):
+        for other in range(2):
+            begin = pfb_count - 1 + (2 * chip + (core ^ other)) * frames_dev
+            past[pl.ds(begin, frames_dev)] = x_ref[chip, other]
 
     spec[0 : fir_count - 1] = jnp.zeros((fir_count - 1, 24, 2 * LANES), F32)
     for first in range(0, frames, group):
@@ -171,7 +165,7 @@
                 begin = (first + frame) * 24 + rows
                 filt[begin : begin + 8, :] = total[frame]
 
-    per_band = ready.shape[1] // 6
+    per_band = ready.shape[2] // 6
     for pair in range(6):
         rows = [
             filt[pl.ds(share_row(part, pair * 2 + odd), frames, stride=24), :]
@@ -179,21 +173,22 @@
             for odd in range(2)
         ]
         turned = jnp.concatenate(rows, axis=0).T
-        for dev in range(ready.shape[0]):
-            ready[dev ^ place, pair * per_band : (pair + 1) * per_band, :] = turned[
+        for dev in range(2 * chips):
+            ready[(dev % 2) ^ core, dev // 2, pair * per_band : (pair + 1) * per_band, :] = turned[
                 dev * per_band : (dev + 1) * per_band
             ]
-    for chip in range(ready.shape[0] // 2):
-        own_ref[chip] = ready[2 * chip]
-        other_ref[chip] = ready[2 * chip + 1]
-
-
-def beams_kernel(*refs):
-    came, (w_ref, out_ref, x_ref) = refs[: 2 + STEPS], refs[2 + STEPS :]
-    place = lax.axis_index("band")
-    height = came[0].shape[1]
-    for other, block in sources(place, came[0], came[1], came[2:]):
-        x_ref[pl.ds(pl.multiple_of(other * height, 8), height), :] = block
+    own_ref[...] = ready[0]
+    other_ref[...] = ready[1]
+
+
+def beams_kernel(x_ref, w_hbm, out_ref, w_ref, sems):
+    loads = [
+        pltpu.make_async_copy(w_hbm.at[chan], w_ref.at[chan], sems.at[chan])
+        for chan in range(w_hbm.shape[0])
+    ]
+    ahead = 3
+    for load in loads[:ahead]:
+        load.start()
     rows = x_ref.shape[0] // 8
     beams = w_ref.shape[1] // 2
     lane = lax.broadcasted_iota(jnp.int32, (rows, LANES), 1)
@@ -216,7 +211,11 @@
     for step in steps:
         sums = []
         for index in range(2):
-            product = jnp.dot(w_ref[2 * step + index], fields[step], preferred_element_type=F32)
+            chan = 2 * step + index
+            loads[chan].wait()
+            if chan + ahead < len(loads):
+                loads[chan + ahead].start()
+            product = jnp.dot(w_ref[chan], fields[step], preferred_element_type=F32)
             sums.append(product[:, 0:LANES] + product[:, LANES : 2 * LANES])
         by_real = jnp.where(even_wide, sums[0][:beams], sums[1][:beams])
         by_imag = jnp.where(even_wide, sums[0][beams:], sums[1][beams:])
@@ -233,35 +232,31 @@
         out_ref[2 * step + 1] = power[8:16]
 
 
-def slots_of(devices, place):
+def slots_of(devices, core):
     index = np.arange(devices * 12)
     odd, other, pair = index // (devices * 6), index // 6 % devices, index % 6
     own = jnp.asarray(pair * 2 + odd, jnp.int32)
-    source = jnp.asarray(other, jnp.int32) ^ place
+    source = jnp.asarray(other, jnp.int32) ^ core
     dishes = jnp.where(own < 8, source * 8 + own, devices * 8 + source * 4 + own - 8)
     return dishes[:, None]
 
 
 def exchange(own, other):
     devices = lax.axis_size("band")
-
-    def moved(value, steps):
-        pairs = [(dev, dev ^ steps[dev % 2]) for dev in range(devices)]
-        return lax.ppermute(value, "band", pairs)
-
-    came = moved(other, (1, 1))
-    grouped = pl.pallas_call(
-        regroup_kernel,
-        out_shape=[jax.ShapeDtypeStruct((2,) + own.shape[1:], F32)] * STEPS,
+    came = lax.ppermute(other, "band", [(dev, dev ^ 1) for dev in range(devices)])
+    joined = pl.pallas_call(
+        join_kernel,
+        out_shape=jax.ShapeDtypeStruct((own.shape[0], 2) + own.shape[1:], F32),
         in_specs=[VMEM] * 2,
-        out_specs=[VMEM] * STEPS,
-        name="regroup",
+        out_specs=HBM,
+        scratch_shapes=[pltpu.SemaphoreType.DMA((2,))],
+        name="join",
         compiler_params=GRANT,
-    )(own, came)
-    far = [
-        moved(grouped[step], (2 * ORDERS[0][step], 2 * ORDERS[1][step])) for step in range(STEPS)
-    ]
-    return [own, came] + far
+    )(held(own, pltpu.VMEM), held(came, pltpu.VMEM))
+    groups = [list(range(core, devices, 2)) for core in range(2)]
+    return lax.all_to_all(
+        joined, "band", split_axis=0, concat_axis=0, tiled=True, axis_index_groups=groups
+    )
 
 
 def dft_parts(channels):
@@ -309,10 +304,11 @@
             jax.ShapeDtypeStruct(table.shape, BF16),
         ],
         in_specs=[HBM, VMEM, VMEM, HBM],
-        out_specs=[VMEM] * 2,
+        out_specs=[HBM, VMEM],
         scratch_shapes=[
             pltpu.VMEM((band_chans, 2, dishes, beams), F32),
-            pltpu.SemaphoreType.DMA((band_chans,)),
+            pltpu.VMEM((band_chans, 2 * beams, 2 * dishes), BF16),
+            pltpu.SemaphoreType.DMA((2, band_chans)),
             pltpu.SemaphoreType.DMA(()),
         ],
         name="weights",
@@ -323,38 +319,41 @@
     )(
         held(beam_weights[0], pltpu.HBM),
         dish_order.reshape(1, dishes),
-        slots_of(devices, position),
+        slots_of(devices, position % 2),
         held(jnp.asarray(table), pltpu.HBM),
     )
-    *arrived, weights, table = lax.optimization_barrier((*arrived, weights, table))
+    arrived, weights, table = lax.optimization_barrier((arrived, weights, table))
 
     block = (6 * band_chans, channels)
     filtered = pl.pallas_call(
         channel_kernel,
         out_shape=[jax.ShapeDtypeStruct((chips,) + block, F32)] * 2,
-        in_specs=[VMEM] * (5 + STEPS),
+        in_specs=[VMEM] * 4,
         out_specs=[VMEM] * 2,
         scratch_shapes=[
             pltpu.VMEM((frames + prototype.shape[0] - 1, 24, LANES), F32),
             pltpu.VMEM((frames, 24, 2 * LANES), F32),
             pltpu.VMEM((frames + fir_count - 1, 24, 2 * LANES), F32),
             pltpu.VMEM((frames * 24, LANES), F32),
-            pltpu.VMEM((devices,) + block, F32),
+            pltpu.VMEM((2, chips) + block, F32),
         ],
         name="channels",
         compiler_params=GRANT,
-    )(*arrived, prototype, table, taps)
-    field = exchange(*filtered)
+    )(held(arrived, pltpu.VMEM), prototype, held(table, pltpu.VMEM), taps)
+    field = exchange(*filtered).reshape(devices * 6 * band_chans, channels)
 
     power = pl.pallas_call(
         beams_kernel,
         out_shape=jax.ShapeDtypeStruct((band_chans, frames // INTEG, beams), F32),
-        in_specs=[VMEM] * (3 + STEPS),
+        in_specs=[VMEM, HBM],
         out_specs=VMEM,
-        scratch_shapes=[pltpu.VMEM((devices * 6 * band_chans, channels), F32)],
+        scratch_shapes=[
+            pltpu.VMEM(weights.shape, BF16),
+            pltpu.SemaphoreType.DMA((band_chans,)),
+        ],
         name="beams",
         compiler_params=GRANT,
-    )(*field, weights)
+    )(held(field, pltpu.VMEM), held(weights, pltpu.HBM))
     return jnp.transpose(power, (0, 2, 1))[None]
 
 
@@ -441,7 +440,7 @@
             channels == LANES
             and beam_weights.shape[1] == 8
             and devices * 8 == channels
-            and devices == 2 * (STEPS + 1)
+            and devices % 2 == 0
             and dish_filter.shape[2] == 12 * devices
             and samples.shape[2] * devices == 32 * channels
         )

time: 41.9 us -> 46.7 us (1.11)
  starting transfers between devices: 24.5 us -> 7.81 us
  blocking collectives: 0 us -> 15.8 us
  Pallas kernels: 7.92 us -> 12.2 us
  waiting for transfers between devices: 6.46 us -> 7.68 us
  local copies, waits for them, and re-layouts: 1.95 us -> 2.7 us
  other arithmetic: 0.74 us -> 0.03 us
    ppermute x16 -> x2, starting transfers between devices: 24.5 us -> 0.6 us  [exchange(): lax.ppermute(other, 'band', [(dev, dev ^ 1) for dev in range(devices)])]
    all_to_all x0 -> x1, blocking collectives: none -> 15.8 us  [exchange(): lax.all_to_all(joined, 'band', split_axis=0, concat_axis=0, tiled=True, a...]
    all_to_all x0 -> x1, starting transfers between devices: none -> 7.21 us  [exchange(): lax.all_to_all(joined, 'band', split_axis=0, concat_axis=0, tiled=True, a...]
    all_to_all x0 -> x1, waiting for transfers between devices: none -> 5.19 us  [exchange(): lax.all_to_all(joined, 'band', split_axis=0, concat_axis=0, tiled=True, a...]
    ppermute x16 -> x2, waiting for transfers between devices: 6.46 us -> 2.5 us  [exchange(): lax.ppermute(other, 'band', [(dev, dev ^ 1) for dev in range(devices)])]
    pallas_call x1, Pallas kernels: 1.93 us -> 4.97 us  [close_body(): pl.pallas_call(beams_kernel, out_shape=jax.ShapeDtypeStruct((band_chans,...]
    pallas_call x2, Pallas kernels: 0.05 us -> 0.86 us  [exchange(): pl.pallas_call(join_kernel, out_shape=jax.ShapeDtypeStruct((own.shape[0],...]
    unnamed x8 -> x16, local copies, waits for them, and re-layouts: 1.8 us -> 2.55 us
  transfers between devices with their start and end apart: 16 -> 3, of which waited for: 4 -> 3; matrix products, arithmetic and copies ran while one was open for 2% -> 0% of each run, Pallas kernels for 11% -> 11%
where the time goes in v11:
time: 46.7 us; the launch traced here: 46.4 us
  blocking collectives  15.8 us (34%)
  Pallas kernels  12.2 us (26%)
  starting transfers between devices  7.81 us (17%)
  waiting for transfers between devices  7.68 us (16%)
  local copies, waits for them, and re-layouts  2.7 us (6%)
    all_to_all x1, blocking collectives, exchange(): lax.all_to_all(joined, 'band', split_axis=0, concat_axis=0, tiled=True, a...  15.8 us
    all_to_all x1, starting transfers between devices, exchange(): lax.all_to_all(joined, 'band', split_axis=0, concat_axis=0, tiled=True, a...  7.21 us
    all_to_all x1, waiting for transfers between devices, exchange(): lax.all_to_all(joined, 'band', split_axis=0, concat_axis=0, tiled=True, a...  5.19 us
    pallas_call x1, Pallas kernels, close_body(): pl.pallas_call(weights_kernel, out_shape=[jax.ShapeDtypeStruct((band_chan...  5.09 us
    pallas_call x1, Pallas kernels, close_body(): pl.pallas_call(beams_kernel, out_shape=jax.ShapeDtypeStruct((band_chans,...  4.97 us
    unnamed x16, local copies, waits for them, and re-layouts  2.55 us
    ppermute x2, waiting for transfers between devices, exchange(): lax.ppermute(other, 'band', [(dev, dev ^ 1) for dev in range(devices)])  2.5 us
    pallas_call x1, Pallas kernels, close_body(): pl.pallas_call(channel_kernel, out_shape=[jax.ShapeDtypeStruct((chips,) +...  1.26 us
  transfers between devices with their start and end apart: 3, of which 3 were waited for; matrix products, arithmetic and copies ran while one was open for 0% of the time, Pallas kernels for 11%

profile of v11, /device:TPU:0, one launch (start us, length us, event | category | flops | bytes accessed | tf_op | source)
XLA Modules:
  0.0 46.4 jit_solution(13704370697132353244)
XLA Ops:
  0.0 0.0 copy-start
  0.0 0.0 copy-start.7
  0.0 0.0 copy-start.5
  0.0 0.0 copy-start.6
  0.0 0.0 copy-start.2
  0.0 1.1 %copy-done.2 = f32[2,192,256]{2,1,0:T(8,128)S(1)} copy-done((f32[2,192,256]{2,1,0:T(8,128)S(1)}, f32[2,192,256]{2,1,0:T(8,128)}, u32[]{:S(2)}) %copy-start.2) | copy-done | bytes 393240
  1.1 0.0 copy-start.4
  1.2 0.5 %collective-permute-start = (f32[8,2,24,128]{3,2,1,0:T(8,128)S(1)}, f32[8,2,24,128]{3,2,1,0:T(8,128)S(1)}, u32[]{:S(2)}, u32[]{:S(2)}) collective-permute-start(f32[8,2,24,128]{3,2,1,0:T(8,128)S(1)} %get-tuple-element.15), channel_id=1, source_target_pairs={{0,1},{1,0},{2,3},{3,2},{4,5},{5,4},{6,7},{7,6},{8,9},{9,8},{10,11... | collective-permute-start | bytes 589832 | tf_op jit(solution)/shard_map/ppermute | solution.py:246
  1.7 1.1 %collective-permute-done.came_ref = f32[8,2,24,128]{3,2,1,0:T(8,128)S(1)} collective-permute-done((f32[8,2,24,128]{3,2,1,0:T(8,128)S(1)}, f32[8,2,24,128]{3,2,1,0:T(8,128)S(1)}, u32[]{:S(2)}, u32[]{:S(2)}) %collective-permute-start) | collective-permute-done | bytes 196640 | tf_op jit(solution)/shard_map/ppermute | solution.py:246
  2.8 0.8 %join.2 = f32[8,2,2,24,128]{4,3,2,1,0:T(8,128)} custom-call(f32[8,2,24,128]{3,2,1,0:T(8,128)S(1)} %get-tuple-element.14.own_ref, f32[8,2,24,128]{3,2,1,0:T(8,128)S(1)} %collective-permute-done.came_ref), custom_call_target="tpu_custom_call" | custom-call | tf_op jit(solution)/shard_map/join/pallas_call | solution.py:247
  3.6 7.2 %all-to-all-start = ((f32[8,2,2,24,128]{4,3,2,1,0:T(8,128)}), f32[8,2,2,24,128]{4,3,2,1,0:T(8,128)S(1)}, u32[]{:S(2)}, u32[]{:S(2)}) async-start(f32[8,2,2,24,128]{4,3,2,1,0:T(8,128)} %join.2), calls=%async_computation | async-start | bytes 786432 | tf_op jit(solution)/shard_map/all_to_all | solution.py:257
  10.8 0.0 copy-done.7
  10.8 0.0 copy-done.5
  10.8 0.0 copy-done.6
  10.8 0.1 copy.11.slot_ref
  10.9 0.0 copy-done.4
  11.0 0.0 copy-start.3
  11.0 5.1 %weights.1 = (bf16[8,384,384]{2,1,0:T(8,128)(2,1)S(1)}, bf16[768,256]{1,0:T(8,128)(2,1)S(1)}) custom-call(f32[8,2,192,192]{3,2,1,0:T(8,128)} %bitcast.11, s32[1,192]{1,0:T(1,128)S(1)} %bitcast.10, s32[192,1]{1,0:T(8,128)S(1)} %copy.11.slot_ref, bf16[768,256]{1,0:T(8,128)(2,1)} %constant.41.clone.table_ref), custom_call_target="tpu_custom_call" | custom-call | flops 905969664 | bytes 5242880 | tf_op jit(solution)/shard_map/weights/pallas_call | solution.py:300
  16.1 0.0 copy-start.1
  16.1 1.4 %copy-done.1 = bf16[8,384,384]{2,1,0:T(8,128)(2,1)} copy-done((bf16[8,384,384]{2,1,0:T(8,128)(2,1)}, bf16[8,384,384]{2,1,0:T(8,128)(2,1)S(1)}, u32[]{:S(2)}) %copy-start.1) | copy-done | bytes 2359320
  17.5 0.0 copy-done
  17.6 5.2 %all-to-all-done.x_ref = f32[8,2,2,24,128]{4,3,2,1,0:T(8,128)S(1)} async-done(((f32[8,2,2,24,128]{4,3,2,1,0:T(8,128)}), f32[8,2,2,24,128]{4,3,2,1,0:T(8,128)S(1)}, u32[]{:S(2)}, u32[]{:S(2)}) %all-to-all-start) | async-done | bytes 393248 | tf_op jit(solution)/shard_map/all_to_all | solution.py:257
  22.8 0.0 copy-done.3
  22.8 1.3 %channels.1 = (f32[8,48,128]{2,1,0:T(8,128)S(1)}, f32[8,48,128]{2,1,0:T(8,128)S(1)}) custom-call(f32[8,2,2,24,128]{4,3,2,1,0:T(8,128)S(1)} %all-to-all-done.x_ref, f32[16,128]{1,0:T(8,128)S(1)} %copy-done.3, bf16[768,256]{1,0:T(8,128)(2,1)S(1)} %get-tuple-element.19.table_ref, f32[8,2,24,128]{3,2,1,0:T(8,128)S(1)} %copy_bitcast_fusion.taps_ref), custom_call_target="tpu_custom_call" | custom-call | tf_op jit(solution)/shard_map/channels/pallas_call | solution.py:328
  24.0 0.1 collective-permute-start.1
  24.1 1.4 %collective-permute-done.1.came_ref = f32[8,48,128]{2,1,0:T(8,128)S(1)} collective-permute-done((f32[8,48,128]{2,1,0:T(8,128)S(1)}, f32[8,48,128]{2,1,0:T(8,128)S(1)}, u32[]{:S(2)}, u32[]{:S(2)}) %collective-permute-start.1) | collective-permute-done | bytes 196640 | tf_op jit(solution)/shard_map/ppermute | solution.py:246
  25.5 0.1 join.3
  25.6 15.8 %all_to_all.10 = f32[8,2,48,128]{3,2,1,0:T(8,128)S(1)} all-to-all(f32[8,2,48,128]{3,2,1,0:T(8,128)S(1)} %join.3), channel_id=1, replica_groups={{0,2,4,6,8,10,12,14},{1,3,5,7,9,11,13,15},{16,18,20,22,24,26,28,30},{17..., dimensions={0} | all-to-all | bytes 786432 | tf_op jit(solution)/shard_map/all_to_all | solution.py:257
  41.4 5.0 %beams.1 = f32[8,8,192]{2,1,0:T(8,128)} custom-call(f32[768,128]{1,0:T(8,128)S(1)} %bitcast.9, bf16[8,384,384]{2,1,0:T(8,128)(2,1)} %copy-done.1), custom_call_target="tpu_custom_call" | custom-call | tf_op jit(solution)/shard_map/beams/pallas_call | solution.py:345
  (5 shorter events, 0.1 us)
Async XLA Ops:
  0.0 17.5 %copy-start = (f32[2,8,192,128]{3,2,1,0:T(8,128)S(1)}, f32[2,8,192,128]{3,2,1,0:T(8,128)}, u32[]{:S(2)}) copy-start(f32[2,8,192,128]{3,2,1,0:T(8,128)} %param.10) | copy-start | bytes 4718596
  0.0 10.8 %copy-start.7 = (pred[192]{0:T(512)(128)(4,1)S(1)}, pred[192]{0:T(512)(128)(4,1)}, u32[]{:S(2)}) copy-start(pred[192]{0:T(512)(128)(4,1)} %constant.43) | copy-start | bytes 580
  0.0 10.8 %copy-start.5 = (s32[192]{0:T(256)S(1)}, s32[192]{0:T(256)}, u32[]{:S(2)}) copy-start(s32[192]{0:T(256)} %constant.40.clone) | copy-start | bytes 2308
  0.0 10.8 %copy-start.6 = (s32[192]{0:T(256)S(1)}, s32[192]{0:T(256)}, u32[]{:S(2)}) copy-start(s32[192]{0:T(256)} %constant.39.clone) | copy-start | bytes 2308
  0.0 1.1 %copy-start.2 = (f32[2,192,256]{2,1,0:T(8,128)S(1)}, f32[2,192,256]{2,1,0:T(8,128)}, u32[]{:S(2)}) copy-start(f32[2,192,256]{2,1,0:T(8,128)} %x_ref.1) | copy-start | bytes 1179652
  1.1 9.8 %copy-start.4 = (s32[192]{0:T(256)S(1)}, s32[192]{0:T(256)}, u32[]{:S(2)}) copy-start(s32[192]{0:T(256)} %param.12) | copy-start | bytes 2308
  1.2 1.6 %collective-permute-start = (f32[8,2,24,128]{3,2,1,0:T(8,128)S(1)}, f32[8,2,24,128]{3,2,1,0:T(8,128)S(1)}, u32[]{:S(2)}, u32[]{:S(2)}) collective-permute-start(f32[8,2,24,128]{3,2,1,0:T(8,128)S(1)} %get-tuple-element.15), channel_id=1, source_target_pairs={{0,1},{1,0},{2,3},{3,2},{4,5},{5,4},{6,7},{7,6},{8,9},{9,8},{10,11... | collective-permute-start | bytes 589832 | tf_op jit(solution)/shard_map/ppermute | solution.py:246
  3.6 19.2 %all-to-all-start = ((f32[8,2,2,24,128]{4,3,2,1,0:T(8,128)}), f32[8,2,2,24,128]{4,3,2,1,0:T(8,128)S(1)}, u32[]{:S(2)}, u32[]{:S(2)}) async-start(f32[8,2,2,24,128]{4,3,2,1,0:T(8,128)} %join.2), calls=%async_computation | async-start | bytes 786432 | tf_op jit(solution)/shard_map/all_to_all | solution.py:257
  11.0 11.8 %copy-start.3 = (f32[16,128]{1,0:T(8,128)S(1)}, f32[16,128]{1,0:T(8,128)}, u32[]{:S(2)}) copy-start(f32[16,128]{1,0:T(8,128)} %proto_ref.1) | copy-start | bytes 24580
  16.1 1.4 %copy-start.1 = (bf16[8,384,384]{2,1,0:T(8,128)(2,1)}, bf16[8,384,384]{2,1,0:T(8,128)(2,1)S(1)}, u32[]{:S(2)}) copy-start(bf16[8,384,384]{2,1,0:T(8,128)(2,1)S(1)} %get-tuple-element.22.w_hbm) | copy-start | bytes 7077892
  24.0 1.5 %collective-permute-start.1 = (f32[8,48,128]{2,1,0:T(8,128)S(1)}, f32[8,48,128]{2,1,0:T(8,128)S(1)}, u32[]{:S(2)}, u32[]{:S(2)}) collective-permute-start(f32[8,48,128]{2,1,0:T(8,128)S(1)} %get-tuple-element.21), channel_id=1, source_target_pairs={{0,1},{1,0},{2,3},{3,2},{4,5},{5,4},{6,7},{7,6},{8,9},{9,8},{10,11... | collective-permute-start | bytes 589832 | tf_op jit(solution)/shard_map/ppermute | solution.py:246

commit v12 on v3

--- a/solution.py
+++ b/solution.py
@@ -9,11 +9,13 @@
 from jax.sharding import PartitionSpec as P
 
 INTEG = 4
+EARLY = 2
 HIGHEST = lax.Precision.HIGHEST
 F32 = jnp.float32
 BF16 = jnp.bfloat16
 LANES = 128
 VMEM = pl.BlockSpec(memory_space=pltpu.VMEM)
+HBM = pl.BlockSpec(memory_space=pltpu.HBM)
 GRANT = pltpu.CompilerParams(vmem_limit_bytes=16 << 20)
 
 
@@ -23,6 +25,9 @@
     angles = product.astype(jnp.float32) * (2.0 * math.pi / length)
     factor = 1.0 / math.sqrt(length)
     return (jnp.cos(angles) * factor, jnp.sin(angles) * factor)
+
+
+held = pltpu.with_memory_space_constraint
 
 
 def split(value):
@@ -52,28 +57,59 @@
             out_ref[dev + 1, frame, 16:24, :] = jnp.where(low, pltpu.roll(real, 4, 0), imag)
 
 
-def weights_kernel(w_ref, order_ref, slot_ref, out_ref):
-    order = order_ref[...]
+def weights_kernel(
+    w_ref, order_ref, slot_ref, table_ref, early_ref, late_ref, table_out_ref, *scratch
+):
+    buffer, made, sems, table_sem = scratch
+    table_copy = pltpu.make_async_copy(table_ref, table_out_ref, table_sem)
+    loads = [
+        pltpu.make_async_copy(w_ref.at[chan], buffer.at[chan], sems.at[0, chan])
+        for chan in range(w_ref.shape[0])
+    ]
+    stores = [
+        pltpu.make_async_copy(made.at[chan], late_ref.at[chan], sems.at[1, chan])
+        for chan in range(late_ref.shape[0])
+    ]
+    ahead = 3
+    for load in loads[:ahead]:
+        load.start()
+    hot = (slot_ref[...] == order_ref[...]).astype(F32).T.astype(BF16)
     beams = w_ref.shape[3]
-    for half in range(2):
-        hot = (slot_ref[:, half : half + 1] == order).astype(F32).T.astype(BF16)
+    for chan, load in enumerate(loads):
+        load.wait()
+        if chan + ahead < len(loads):
+            loads[chan + ahead].start()
+        elif chan + ahead == len(loads):
+            table_copy.start()
         for part in range(2):
-            turned = w_ref[0, part].T
-            value = split(turned)[half]
-            product = jnp.dot(value, hot, preferred_element_type=F32)
+            halves = [
+                jnp.dot(half, hot, preferred_element_type=F32).astype(BF16)
+                for half in split(buffer[chan, part].T)
+            ]
             rows = slice(part * beams, (part + 1) * beams)
-            if half == 0:
-                out_ref[0, rows, :] = product.astype(BF16)
+            both = jnp.concatenate(halves, axis=1)
+            if chan < EARLY:
+                early_ref[chan, rows, :] = both
             else:
-                out_ref[0, rows, :] += product.astype(BF16)
-
-
-def channel_kernel(x_ref, proto_ref, table_ref, taps_ref, out_ref, poly, spec, filt):
-    frames = x_ref.shape[0]
+                made[chan - EARLY, rows, :] = both
+        if chan >= EARLY:
+            stores[chan - EARLY].start()
+    for store in stores:
+        store.wait()
+    table_copy.wait()
+
+
+def channel_kernel(
+    x_ref, proto_ref, table_ref, taps_ref, out_ref, past, poly, spec, filt
+):
     pfb_count = proto_ref.shape[0]
     fir_count = taps_ref.shape[0]
+    frames = poly.shape[0]
     group = 8
     low = lax.broadcasted_iota(jnp.int32, (group, 8, LANES), 1) < 4
+
+    past[0 : pfb_count - 1] = jnp.zeros((pfb_count - 1, 24, LANES), F32)
+    past[pfb_count - 1 :] = x_ref[...]
 
     spec[0 : fir_count - 1] = jnp.zeros((fir_count - 1, 24, 2 * LANES), F32)
     for first in range(0, frames, group):
@@ -81,14 +117,9 @@
         for rows in range(0, 24, 8):
             total = None
             for tap in range(pfb_count):
-                begin = first - tap
-                lost = max(0, -begin)
-                if lost >= group:
-                    continue
-                block = x_ref[begin + lost : begin + group, rows : rows + 8, :]
+                begin = first + pfb_count - 1 - tap
+                block = past[begin : begin + group, rows : rows + 8, :]
                 term = block * proto_ref[tap : tap + 1, :][None]
-                if lost:
-                    term = jnp.concatenate([jnp.zeros((lost, 8, LANES), F32), term], axis=0)
                 total = term if total is None else total + term
             found.append(total)
         turned = pltpu.roll(found[2], 4, 1)
@@ -134,9 +165,16 @@
             ]
 
 
-def beams_kernel(x_ref, w_ref, out_ref):
+def beams_kernel(x_ref, early_ref, late_hbm, out_ref, late_ref, sems):
+    loads = []
+    for step in range(late_hbm.shape[0] // 2):
+        pair = slice(2 * step, 2 * step + 2)
+        loads.append(
+            pltpu.make_async_copy(late_hbm.at[pair], late_ref.at[pair], sems.at[step])
+        )
+        loads[-1].start()
     rows = x_ref.shape[0] // 8
-    beams = w_ref.shape[1] // 2
+    beams = early_ref.shape[1] // 2
     lane = lax.broadcasted_iota(jnp.int32, (rows, LANES), 1)
     even = lane % 64 < 32
     wide = lax.broadcasted_iota(jnp.int32, (beams, LANES), 1)
@@ -144,27 +182,35 @@
     row = lax.broadcasted_iota(jnp.int32, (16, 2 * LANES), 0)
     column = lax.broadcasted_iota(jnp.int32, (16, 2 * LANES), 1)
     pool = jnp.where(row == column % 64 // INTEG, 1.0 / INTEG, 0.0).astype(BF16)
-    for step in range(w_ref.shape[0] // 2):
+    steps = range(out_ref.shape[0] // 2)
+    fields = []
+    for step in steps:
         one = x_ref[pl.ds(2 * step, rows, stride=8), :]
         two = x_ref[pl.ds(2 * step + 1, rows, stride=8), :]
         first = jnp.where(even, one, pltpu.roll(two, 32, 1))
         second = jnp.where(even, pltpu.roll(one, LANES - 32, 1), two)
-        field = jnp.concatenate([first, second], axis=0)
-        high, rest = split(field)
-        both = jnp.concatenate([high, rest], axis=1)
-        both = jnp.concatenate([both, both], axis=0)
+        both = jnp.concatenate(split(jnp.concatenate([first, second], axis=0)), axis=1)
+        fields.append(jnp.concatenate([both, both], axis=0))
+    beam_of = []
+    for step in steps:
+        if 2 * step < EARLY:
+            w_ref, begin = early_ref, 2 * step
+        else:
+            w_ref, begin = late_ref, 2 * step - EARLY
+            loads[begin // 2].wait()
         sums = []
         for index in range(2):
-            product = jnp.dot(w_ref[2 * step + index], both, preferred_element_type=F32)
+            weights = w_ref[begin + index]
+            product = jnp.dot(weights, fields[step], preferred_element_type=F32)
             sums.append(product[:, 0:LANES] + product[:, LANES : 2 * LANES])
         by_real = jnp.where(even_wide, sums[0][:beams], sums[1][:beams])
         by_imag = jnp.where(even_wide, sums[0][beams:], sums[1][beams:])
         crossed = pltpu.roll(by_imag, 64, 1)
-        beam = by_real + jnp.where(wide < 64, -crossed, crossed)
-        high, rest = split(beam * beam)
+        beam_of.append(by_real + jnp.where(wide < 64, -crossed, crossed))
+    for step in steps:
         power = lax.dot_general(
             pool,
-            jnp.concatenate([high, rest], axis=1),
+            jnp.concatenate(split(beam_of[step] * beam_of[step]), axis=1),
             (((1,), (1,)), ((), ())),
             preferred_element_type=F32,
         )
@@ -173,17 +219,11 @@
 
 
 def slots_of(devices):
-    dishes = np.zeros((2, devices, 6), np.int32)
-    for odd in range(2):
-        for dev in range(devices):
-            for pair in range(6):
-                own = pair * 2 + odd
-                dishes[odd, dev, pair] = (
-                    dev * 8 + own if own < 8 else devices * 8 + dev * 4 + own - 8
-                )
-    flat = dishes.reshape(-1)
-    none = np.full_like(flat, -1)
-    return np.stack([np.concatenate([flat, none]), np.concatenate([none, flat])], axis=1)
+    index = np.arange(devices * 12, dtype=np.int32)
+    own = index % 6 * 2 + index // (devices * 6)
+    source = index // 6 % devices
+    dishes = np.where(own < 8, source * 8 + own, devices * 8 + source * 4 + own - 8)
+    return dishes.astype(np.int32)[:, None]
 
 
 def dft_parts(channels):
@@ -208,6 +248,9 @@
     frames_dev = samples.shape[2] // channels
     frames = frames_dev * devices
 
+    def exchange(value):
+        return lax.all_to_all(value, "band", split_axis=0, concat_axis=0, tiled=True)
+
     pieces = pl.pallas_call(
         pieces_kernel,
         out_shape=jax.ShapeDtypeStruct((devices, frames_dev, 24, channels), F32),
@@ -216,53 +259,70 @@
         name="pieces",
         compiler_params=GRANT,
     )(samples)
-    arrived = lax.all_to_all(pieces, "band", split_axis=0, concat_axis=0, tiled=True)
+    arrived = exchange(pieces).reshape(frames, 24, channels)
 
     eight = lax.dynamic_slice_in_dim(dish_filter, position * 8, 8, 2)
     four = lax.dynamic_slice_in_dim(dish_filter, devices * 8 + position * 4, 4, 2)
     taps = jnp.concatenate([eight, eight, four, four], axis=2)
     taps = jnp.transpose(taps, (1, 0, 2, 3))
-    weights = pl.pallas_call(
+    table = dft_parts(channels)
+    early, late, table = pl.pallas_call(
         weights_kernel,
-        grid=(band_chans,),
-        out_shape=jax.ShapeDtypeStruct((band_chans, 2 * beams, 2 * dishes), BF16),
-        in_specs=[
-            pl.BlockSpec((1, 2, dishes, beams), lambda i: (i, 0, 0, 0)),
-            pl.BlockSpec((1, dishes), lambda i: (0, 0)),
-            pl.BlockSpec((2 * dishes, 2), lambda i: (0, 0)),
+        out_shape=[
+            jax.ShapeDtypeStruct((EARLY, 2 * beams, 2 * dishes), BF16),
+            pltpu.HBM((band_chans - EARLY, 2 * beams, 2 * dishes), BF16),
+            jax.ShapeDtypeStruct(table.shape, BF16),
         ],
-        out_specs=pl.BlockSpec((1, 2 * beams, 2 * dishes), lambda i: (i, 0, 0)),
+        in_specs=[HBM, VMEM, VMEM, HBM],
+        out_specs=[VMEM, HBM, VMEM],
+        scratch_shapes=[
+            pltpu.VMEM((band_chans, 2, dishes, beams), F32),
+            pltpu.VMEM((band_chans - EARLY, 2 * beams, 2 * dishes), BF16),
+            pltpu.SemaphoreType.DMA((2, band_chans)),
+            pltpu.SemaphoreType.DMA(()),
+        ],
         name="weights",
         compiler_params=GRANT,
         cost_estimate=pl.CostEstimate(
             flops=8 * 4 * 2 * 192 * 192 * 384, bytes_accessed=5 << 20, transcendentals=0
         ),
-    )(beam_weights[0], dish_order.reshape(1, dishes), slots_of(devices))
-
+    )(
+        held(beam_weights[0], pltpu.HBM),
+        dish_order.reshape(1, dishes),
+        slots_of(devices),
+        held(jnp.asarray(table), pltpu.HBM),
+    )
+    arrived, early, late, table = lax.optimization_barrier((arrived, early, late, table))
+
+    block = (6 * band_chans, channels)
     filtered = pl.pallas_call(
         channel_kernel,
-        out_shape=jax.ShapeDtypeStruct((devices, 6 * band_chans, channels), F32),
+        out_shape=jax.ShapeDtypeStruct((devices,) + block, F32),
         in_specs=[VMEM] * 4,
         out_specs=VMEM,
         scratch_shapes=[
+            pltpu.VMEM((frames + prototype.shape[0] - 1, 24, LANES), F32),
             pltpu.VMEM((frames, 24, 2 * LANES), F32),
             pltpu.VMEM((frames + fir_count - 1, 24, 2 * LANES), F32),
             pltpu.VMEM((frames * 24, LANES), F32),
         ],
         name="channels",
         compiler_params=GRANT,
-    )(arrived.reshape(frames, 24, channels), prototype, dft_parts(channels), taps)
-    field = lax.all_to_all(filtered, "band", split_axis=0, concat_axis=0, tiled=True)
-    field = field.reshape(devices * 6 * band_chans, channels)
+    )(held(arrived, pltpu.VMEM), prototype, held(table, pltpu.VMEM), taps)
+    field = exchange(filtered).reshape(devices * 6 * band_chans, channels)
 
     power = pl.pallas_call(
         beams_kernel,
         out_shape=jax.ShapeDtypeStruct((band_chans, frames // INTEG, beams), F32),
-        in_specs=[VMEM] * 2,
+        in_specs=[VMEM, VMEM, HBM],
         out_specs=VMEM,
+        scratch_shapes=[
+            pltpu.VMEM(late.shape, BF16),
+            pltpu.SemaphoreType.DMA((late.shape[0] // 2,)),
+        ],
         name="beams",
         compiler_params=GRANT,
-    )(field, weights)
+    )(held(field, pltpu.VMEM), held(early, pltpu.VMEM), held(late, pltpu.HBM))
     return jnp.transpose(power, (0, 2, 1))[None]
 
 

time: 43.9 us -> 42 us (0.957)
  blocking collectives: 0 us -> 15.5 us
  waiting for transfers between devices: 15.2 us -> 6.7 us
  local copies, waits for them, and re-layouts: 6.14 us -> 1.17 us
  starting transfers between devices: 11.1 us -> 7.39 us
    all_to_all x0 -> x1, blocking collectives: none -> 15.5 us  [exchange(): lax.all_to_all(value, 'band', split_axis=0, concat_axis=0, tiled=True)]
    all_to_all x2 -> x1, waiting for transfers between devices: 15.2 us -> 6.7 us  [exchange(): lax.all_to_all(value, 'band', split_axis=0, concat_axis=0, tiled=True)]
    unnamed x18 -> x10, local copies, waits for them, and re-layouts: 6.1 us -> 1.13 us
    all_to_all x2 -> x1, starting transfers between devices: 11.1 us -> 7.39 us  [exchange(): lax.all_to_all(value, 'band', split_axis=0, concat_axis=0, tiled=True)]
    pallas_call x2, Pallas kernels: 7.55 us -> 6.55 us  [the longest x1 5.36 us: close_body(): pl.pallas_call(weights_kernel, out_shape=[jax.ShapeDtypeStruct((EARLY, 2...]
    pallas_call x1, Pallas kernels: 2.6 us -> 3.49 us  [close_body(): pl.pallas_call(beams_kernel, out_shape=jax.ShapeDtypeStruct((band_chans,...]
  transfers between devices with their start and end apart: 2 -> 1, of which waited for: 2 -> 1; matrix products, arithmetic and copies ran while one was open for 0% -> 0% of each run, Pallas kernels for 13% -> 13%
where the time goes in v12:
time: 42 us; the launch traced here: 41.7 us
  blocking collectives  15.5 us (37%)
  Pallas kernels  10.8 us (26%)
  starting transfers between devices  7.39 us (18%)
  waiting for transfers between devices  6.7 us (16%)
  local copies, waits for them, and re-layouts  1.17 us (3%)
    all_to_all x1, blocking collectives, exchange(): lax.all_to_all(value, 'band', split_axis=0, concat_axis=0, tiled=True)  15.5 us
    all_to_all x1, starting transfers between devices, exchange(): lax.all_to_all(value, 'band', split_axis=0, concat_axis=0, tiled=True)  7.39 us
    all_to_all x1, waiting for transfers between devices, exchange(): lax.all_to_all(value, 'band', split_axis=0, concat_axis=0, tiled=True)  6.7 us
    pallas_call x1, Pallas kernels, close_body(): pl.pallas_call(weights_kernel, out_shape=[jax.ShapeDtypeStruct((EARLY, 2...  5.36 us
    pallas_call x1, Pallas kernels, close_body(): pl.pallas_call(beams_kernel, out_shape=jax.ShapeDtypeStruct((band_chans,...  3.49 us
    pallas_call x1, Pallas kernels, close_body(): pl.pallas_call(channel_kernel, out_shape=jax.ShapeDtypeStruct((devices,)...  1.19 us
    unnamed x10, local copies, waits for them, and re-layouts  1.13 us
  transfers between devices with their start and end apart: 1, of which 1 were waited for; matrix products, arithmetic and copies ran while one was open for 0% of the time, Pallas kernels for 13%

profile of v12, /device:TPU:0, one launch (start us, length us, event | category | flops | bytes accessed | tf_op | source)
XLA Modules:
  0.0 41.7 jit_solution(17374521209114107385)
XLA Ops:
  0.0 0.0 copy-start
  0.0 0.0 copy-start.1
  0.0 1.1 %copy-done.1 = f32[2,192,256]{2,1,0:T(8,128)S(1)} copy-done((f32[2,192,256]{2,1,0:T(8,128)S(1)}, f32[2,192,256]{2,1,0:T(8,128)}, u32[]{:S(2)}) %copy-start.1) | copy-done | bytes 393240
  1.1 0.0 copy-start.2
  1.1 0.0 copy-start.4
  1.1 0.8 %pieces.1 = f32[16,2,24,128]{3,2,1,0:T(8,128)} custom-call(f32[2,192,256]{2,1,0:T(8,128)S(1)} %copy-done.1), custom_call_target="tpu_custom_call" | custom-call | tf_op jit(solution)/shard_map/pieces/pallas_call | solution.py:254
  1.9 7.4 %all-to-all-start = ((f32[16,2,24,128]{3,2,1,0:T(8,128)}), f32[16,2,24,128]{3,2,1,0:T(8,128)S(1)}, u32[]{:S(2)}, u32[]{:S(2)}) async-start(f32[16,2,24,128]{3,2,1,0:T(8,128)} %pieces.1), calls=%async_computation | async-start | bytes 786432 | tf_op jit(solution)/shard_map/all_to_all | solution.py:252
  9.3 0.0 copy-done.2
  9.3 0.0 copy-done.4
  9.3 0.0 copy-start.3
  9.3 5.4 %weights.1 = (bf16[2,384,384]{2,1,0:T(8,128)(2,1)S(1)}, bf16[6,384,384]{2,1,0:T(8,128)(2,1)}, bf16[768,256]{1,0:T(8,128)(2,1)S(1)}) custom-call(f32[8,2,192,192]{3,2,1,0:T(8,128)} %bitcast.12, s32[1,192]{1,0:T(1,128)S(1)} %bitcast.11, s32[192,1]{1,0:T(8,128)S(1)} %copy-done.2, bf16[768,256]{1,0:T(8,128)(2,1)} %constant.20.clone.table_ref), custom_call_target="tpu_custom_call" | custom-call | flops 905969664 | bytes 5242880 | tf_op jit(solution)/shard_map/weights/pallas_call | solution.py:269
  14.7 0.0 copy-done
  14.8 6.7 %all-to-all-done = f32[16,2,24,128]{3,2,1,0:T(8,128)S(1)} async-done(((f32[16,2,24,128]{3,2,1,0:T(8,128)}), f32[16,2,24,128]{3,2,1,0:T(8,128)S(1)}, u32[]{:S(2)}, u32[]{:S(2)}) %all-to-all-start) | async-done | bytes 393248 | tf_op jit(solution)/shard_map/all_to_all | solution.py:252
  21.5 0.0 copy-done.3
  21.5 1.2 %channels.1 = f32[16,48,128]{2,1,0:T(8,128)S(1)} custom-call(f32[32,24,128]{2,1,0:T(8,128)S(1)} %bitcast.9, f32[16,128]{1,0:T(8,128)S(1)} %copy-done.3, bf16[768,256]{1,0:T(8,128)(2,1)S(1)} %get-tuple-element.16.table_ref, f32[8,2,24,128]{3,2,1,0:T(8,128)S(1)} %copy_bitcast_fusion.taps_ref), custom_call_target="tpu_custom_call" | custom-call | tf_op jit(solution)/shard_map/channels/pallas_call | solution.py:298
  22.7 15.5 %all_to_all.10 = f32[16,48,128]{2,1,0:T(8,128)S(1)} all-to-all(f32[16,48,128]{2,1,0:T(8,128)S(1)} %channels.1), channel_id=1, replica_groups=mesh['grp'=2,'band'=16] {'band'}, dimensions={0} | all-to-all | bytes 786432 | tf_op jit(solution)/shard_map/all_to_all | solution.py:252
  38.2 3.5 %beams.1 = f32[8,8,192]{2,1,0:T(8,128)} custom-call(f32[768,128]{1,0:T(8,128)S(1)} %bitcast.10, bf16[2,384,384]{2,1,0:T(8,128)(2,1)S(1)} %get-tuple-element.17.early_ref, bf16[6,384,384]{2,1,0:T(8,128)(2,1)} %get-tuple-element.18.late_hbm), custom_call_target="tpu_custom_call" | custom-call | tf_op jit(solution)/shard_map/beams/pallas_call | solution.py:314
  (3 shorter events, 0.1 us)
Async XLA Ops:
  0.0 14.7 %copy-start = (f32[2,8,192,128]{3,2,1,0:T(8,128)S(1)}, f32[2,8,192,128]{3,2,1,0:T(8,128)}, u32[]{:S(2)}) copy-start(f32[2,8,192,128]{3,2,1,0:T(8,128)} %param.9) | copy-start | bytes 4718596
  0.0 1.1 %copy-start.1 = (f32[2,192,256]{2,1,0:T(8,128)S(1)}, f32[2,192,256]{2,1,0:T(8,128)}, u32[]{:S(2)}) copy-start(f32[2,192,256]{2,1,0:T(8,128)} %x_ref.1) | copy-start | bytes 1179652
  1.1 8.2 %copy-start.2 = (s32[192,1]{1,0:T(8,128)S(1)}, s32[192,1]{1,0:T(8,128)}, u32[]{:S(2)}) copy-start(s32[192,1]{1,0:T(8,128)} %constant.21.clone.slot_ref) | copy-start | bytes 2308
  1.1 8.2 %copy-start.4 = (s32[192]{0:T(256)S(1)}, s32[192]{0:T(256)}, u32[]{:S(2)}) copy-start(s32[192]{0:T(256)} %param.11) | copy-start | bytes 2308
  1.9 19.6 %all-to-all-start = ((f32[16,2,24,128]{3,2,1,0:T(8,128)}), f32[16,2,24,128]{3,2,1,0:T(8,128)S(1)}, u32[]{:S(2)}, u32[]{:S(2)}) async-start(f32[16,2,24,128]{3,2,1,0:T(8,128)} %pieces.1), calls=%async_computation | async-start | bytes 786432 | tf_op jit(solution)/shard_map/all_to_all | solution.py:252
  9.3 12.2 %copy-start.3 = (f32[16,128]{1,0:T(8,128)S(1)}, f32[16,128]{1,0:T(8,128)}, u32[]{:S(2)}) copy-start(f32[16,128]{1,0:T(8,128)} %proto_ref.1) | copy-start | bytes 24580

commit v13 on v12

--- a/solution.py
+++ b/solution.py
@@ -39,22 +39,47 @@
     return part * 8 + dish if dish < 8 else 16 + part * 4 + dish - 8
 
 
-def pieces_kernel(x_ref, out_ref):
+def pieces_kernel(x_hbm, out_hbm, x_ref, out_ref, in_sems, out_sems):
     devices, frames_dev = out_ref.shape[:2]
     low = lax.broadcasted_iota(jnp.int32, (8, LANES), 0) < 4
-    for frame in range(frames_dev):
-        lanes = slice(frame * LANES, (frame + 1) * LANES)
-        for dev in range(0, devices, 2):
-            for one in (dev, dev + 1):
-                for part in range(2):
-                    out_ref[one, frame, part * 8 : part * 8 + 8, :] = x_ref[
-                        part, one * 8 : one * 8 + 8, lanes
-                    ]
-            start = devices * 8 + dev * 4
-            real = x_ref[0, start : start + 8, lanes]
-            imag = x_ref[1, start : start + 8, lanes]
-            out_ref[dev, frame, 16:24, :] = jnp.where(low, real, pltpu.roll(imag, 4, 0))
-            out_ref[dev + 1, frame, 16:24, :] = jnp.where(low, pltpu.roll(real, 4, 0), imag)
+    half = devices // 2
+    loads, stores = [], []
+    for part_of in range(2):
+        begin = part_of * half
+        ranges = [(begin * 8, half * 8), (devices * 8 + begin * 4, half * 4)]
+        loads.append([])
+        for index, (first, count) in enumerate(ranges):
+            rows = slice(first, first + count)
+            loads[-1].append(
+                pltpu.make_async_copy(
+                    x_hbm.at[:, rows], x_ref.at[:, rows], in_sems.at[part_of, index]
+                )
+            )
+        devs = slice(begin, begin + half)
+        stores.append(
+            pltpu.make_async_copy(out_ref.at[devs], out_hbm.at[devs], out_sems.at[part_of])
+        )
+    for load in loads[0] + loads[1]:
+        load.start()
+    for part_of in range(2):
+        for load in loads[part_of]:
+            load.wait()
+        for dev in range(part_of * half, (part_of + 1) * half, 2):
+            rest = devices * 8 + dev * 4
+            for frame in range(frames_dev):
+                lanes = slice(frame * LANES, (frame + 1) * LANES)
+                for one in (dev, dev + 1):
+                    for part in range(2):
+                        out_ref[one, frame, part * 8 : part * 8 + 8, :] = x_ref[
+                            part, one * 8 : one * 8 + 8, lanes
+                        ]
+                real = x_ref[0, rest : rest + 8, lanes]
+                imag = x_ref[1, rest : rest + 8, lanes]
+                out_ref[dev, frame, 16:24, :] = jnp.where(low, real, pltpu.roll(imag, 4, 0))
+                out_ref[dev + 1, frame, 16:24, :] = jnp.where(low, pltpu.roll(real, 4, 0), imag)
+        stores[part_of].start()
+    for store in stores:
+        store.wait()
 
 
 def weights_kernel(
@@ -165,14 +190,7 @@
             ]
 
 
-def beams_kernel(x_ref, early_ref, late_hbm, out_ref, late_ref, sems):
-    loads = []
-    for step in range(late_hbm.shape[0] // 2):
-        pair = slice(2 * step, 2 * step + 2)
-        loads.append(
-            pltpu.make_async_copy(late_hbm.at[pair], late_ref.at[pair], sems.at[step])
-        )
-        loads[-1].start()
+def beams_kernel(x_ref, early_ref, late_ref, out_ref):
     rows = x_ref.shape[0] // 8
     beams = early_ref.shape[1] // 2
     lane = lax.broadcasted_iota(jnp.int32, (rows, LANES), 1)
@@ -197,7 +215,6 @@
             w_ref, begin = early_ref, 2 * step
         else:
             w_ref, begin = late_ref, 2 * step - EARLY
-            loads[begin // 2].wait()
         sums = []
         for index in range(2):
             weights = w_ref[begin + index]
@@ -253,12 +270,18 @@
 
     pieces = pl.pallas_call(
         pieces_kernel,
-        out_shape=jax.ShapeDtypeStruct((devices, frames_dev, 24, channels), F32),
-        in_specs=[VMEM],
-        out_specs=VMEM,
+        out_shape=pltpu.HBM((devices, frames_dev, 24, channels), F32),
+        in_specs=[HBM],
+        out_specs=HBM,
+        scratch_shapes=[
+            pltpu.VMEM(samples.shape, F32),
+            pltpu.VMEM((devices, frames_dev, 24, channels), F32),
+            pltpu.SemaphoreType.DMA((2, 2)),
+            pltpu.SemaphoreType.DMA((2,)),
+        ],
         name="pieces",
         compiler_params=GRANT,
-    )(samples)
+    )(held(samples, pltpu.HBM))
     arrived = exchange(pieces).reshape(frames, 24, channels)
 
     eight = lax.dynamic_slice_in_dim(dish_filter, position * 8, 8, 2)
@@ -314,15 +337,11 @@
     power = pl.pallas_call(
         beams_kernel,
         out_shape=jax.ShapeDtypeStruct((band_chans, frames // INTEG, beams), F32),
-        in_specs=[VMEM, VMEM, HBM],
+        in_specs=[VMEM] * 3,
         out_specs=VMEM,
-        scratch_shapes=[
-            pltpu.VMEM(late.shape, BF16),
-            pltpu.SemaphoreType.DMA((late.shape[0] // 2,)),
-        ],
         name="beams",
         compiler_params=GRANT,
-    )(held(field, pltpu.VMEM), held(early, pltpu.VMEM), held(late, pltpu.HBM))
+    )(held(field, pltpu.VMEM), held(early, pltpu.VMEM), late)
     return jnp.transpose(power, (0, 2, 1))[None]
 
 

time: 42 us -> 42.6 us (1.014)
  local copies, waits for them, and re-layouts: 1.17 us -> 2.67 us
  waiting for transfers between devices: 6.7 us -> 5.23 us
  Pallas kernels: 10.8 us -> 11.3 us
    pallas_call x1, Pallas kernels: 3.49 us -> 1.88 us  [close_body(): pl.pallas_call(beams_kernel, out_shape=jax.ShapeDtypeStruct((band_chans,...]
    unnamed x10 -> x18, local copies, waits for them, and re-layouts: 1.13 us -> 2.63 us
    all_to_all x1, waiting for transfers between devices: 6.7 us -> 5.23 us  [exchange(): lax.all_to_all(value, 'band', split_axis=0, concat_axis=0, tiled=True)]
    pallas_call x1, Pallas kernels: 0.78 us -> 1.87 us  [close_body(): pl.pallas_call(pieces_kernel, out_shape=pltpu.HBM((devices, frames_dev, 2...]
    pallas_call x1, Pallas kernels: 1.19 us -> 2.18 us  [close_body(): pl.pallas_call(channel_kernel, out_shape=jax.ShapeDtypeStruct((devices,)...]
where the time goes in v13:
time: 42.6 us; the launch traced here: 42.3 us
  blocking collectives  15.5 us (36%)
  Pallas kernels  11.3 us (27%)
  starting transfers between devices  7.45 us (17%)
  waiting for transfers between devices  5.23 us (12%)
  local copies, waits for them, and re-layouts  2.67 us (6%)
    all_to_all x1, blocking collectives, exchange(): lax.all_to_all(value, 'band', split_axis=0, concat_axis=0, tiled=True)  15.5 us
    all_to_all x1, starting transfers between devices, exchange(): lax.all_to_all(value, 'band', split_axis=0, concat_axis=0, tiled=True)  7.45 us
    pallas_call x1, Pallas kernels, close_body(): pl.pallas_call(weights_kernel, out_shape=[jax.ShapeDtypeStruct((EARLY, 2...  5.34 us
    all_to_all x1, waiting for transfers between devices, exchange(): lax.all_to_all(value, 'band', split_axis=0, concat_axis=0, tiled=True)  5.23 us
    unnamed x18, local copies, waits for them, and re-layouts  2.63 us
    pallas_call x1, Pallas kernels, close_body(): pl.pallas_call(channel_kernel, out_shape=jax.ShapeDtypeStruct((devices,)...  2.18 us
    pallas_call x1, Pallas kernels, close_body(): pl.pallas_call(beams_kernel, out_shape=jax.ShapeDtypeStruct((band_chans,...  1.88 us
    pallas_call x1, Pallas kernels, close_body(): pl.pallas_call(pieces_kernel, out_shape=pltpu.HBM((devices, frames_dev, 2...  1.87 us
  transfers between devices with their start and end apart: 1, of which 1 were waited for; matrix products, arithmetic and copies ran while one was open for 0% of the time, Pallas kernels for 13%

profile of v13, /device:TPU:0, one launch (start us, length us, event | category | flops | bytes accessed | tf_op | source)
XLA Modules:
  0.0 42.3 jit_solution(9413457223010646090)
XLA Ops:
  0.0 0.0 copy-start
  0.0 0.0 copy-start.6
  0.0 0.0 copy-start.8
  0.0 1.9 %pieces.1 = f32[16,2,24,128]{3,2,1,0:T(8,128)} custom-call(f32[2,192,256]{2,1,0:T(8,128)} %x_hbm.1), custom_call_target="tpu_custom_call" | custom-call | tf_op jit(solution)/shard_map/pieces/pallas_call | solution.py:271
  1.9 7.4 %all-to-all-start = ((f32[16,2,24,128]{3,2,1,0:T(8,128)}), f32[16,2,24,128]{3,2,1,0:T(8,128)}, u32[]{:S(2)}, u32[]{:S(2)}) async-start(f32[16,2,24,128]{3,2,1,0:T(8,128)} %pieces.1), calls=%async_computation | async-start | bytes 786432 | tf_op jit(solution)/shard_map/all_to_all | solution.py:269
  9.3 0.0 copy-done.6
  9.4 0.0 copy-done.8
  9.4 0.0 copy-start.7
  9.4 5.3 %weights.1 = (bf16[2,384,384]{2,1,0:T(8,128)(2,1)S(1)}, bf16[6,384,384]{2,1,0:T(8,128)(2,1)}, bf16[768,256]{1,0:T(8,128)(2,1)S(1)}) custom-call(f32[8,2,192,192]{3,2,1,0:T(8,128)} %bitcast.11, s32[1,192]{1,0:T(1,128)S(1)} %bitcast.10, s32[192,1]{1,0:T(8,128)S(1)} %copy-done.6, bf16[768,256]{1,0:T(8,128)(2,1)} %constant.20.clone.table_ref), custom_call_target="tpu_custom_call" | custom-call | flops 905969664 | bytes 5242880 | tf_op jit(solution)/shard_map/weights/pallas_call | solution.py:292
  14.7 0.0 copy-start.2
  14.7 0.8 %copy-done.2 = bf16[2,384,384]{2,1,0:T(8,128)(2,1)} copy-done((bf16[2,384,384]{2,1,0:T(8,128)(2,1)}, bf16[2,384,384]{2,1,0:T(8,128)(2,1)S(1)}, u32[]{:S(2)}) %copy-start.2) | copy-done | bytes 589848
  15.5 0.0 copy-start.4
  15.5 0.7 %copy-done.4 = bf16[768,256]{1,0:T(8,128)(2,1)} copy-done((bf16[768,256]{1,0:T(8,128)(2,1)}, bf16[768,256]{1,0:T(8,128)(2,1)S(1)}, u32[]{:S(2)}) %copy-start.4) | copy-done | bytes 393240
  16.3 0.0 copy-done
  16.3 0.0 copy-start.1
  16.4 5.2 %all-to-all-done = f32[16,2,24,128]{3,2,1,0:T(8,128)} async-done(((f32[16,2,24,128]{3,2,1,0:T(8,128)}), f32[16,2,24,128]{3,2,1,0:T(8,128)}, u32[]{:S(2)}, u32[]{:S(2)}) %all-to-all-start) | async-done | bytes 393248 | tf_op jit(solution)/shard_map/all_to_all | solution.py:269
  21.6 0.0 copy-start.3
  21.6 0.0 copy-done.7
  21.6 0.0 copy-start.5
  21.6 1.1 %copy-done.5 = bf16[768,256]{1,0:T(8,128)(2,1)S(1)} copy-done((bf16[768,256]{1,0:T(8,128)(2,1)S(1)}, bf16[768,256]{1,0:T(8,128)(2,1)}, u32[]{:S(2)}) %copy-start.5) | copy-done | bytes 393240
  22.7 2.2 %channels.1 = f32[16,48,128]{2,1,0:T(8,128)S(1)} custom-call(f32[32,24,128]{2,1,0:T(8,128)} %bitcast.x_ref, f32[16,128]{1,0:T(8,128)S(1)} %copy-done.7, bf16[768,256]{1,0:T(8,128)(2,1)S(1)} %copy-done.5, f32[8,2,24,128]{3,2,1,0:T(8,128)S(1)} %copy_bitcast_fusion.taps_ref), custom_call_target="tpu_custom_call" | custom-call | tf_op jit(solution)/shard_map/channels/pallas_call | solution.py:321
  24.9 15.5 %all_to_all.10 = f32[16,48,128]{2,1,0:T(8,128)S(1)} all-to-all(f32[16,48,128]{2,1,0:T(8,128)S(1)} %channels.1), channel_id=1, replica_groups=mesh['grp'=2,'band'=16] {'band'}, dimensions={0} | all-to-all | bytes 786432 | tf_op jit(solution)/shard_map/all_to_all | solution.py:269
  40.4 0.0 copy-done.1
  40.4 0.0 copy-done.3
  40.4 1.9 %beams.1 = f32[8,8,192]{2,1,0:T(8,128)} custom-call(f32[768,128]{1,0:T(8,128)S(1)} %bitcast.9, bf16[2,384,384]{2,1,0:T(8,128)(2,1)S(1)} %copy-done.3, bf16[6,384,384]{2,1,0:T(8,128)(2,1)S(1)} %copy-done.1), custom_call_target="tpu_custom_call" | custom-call | tf_op jit(solution)/shard_map/beams/pallas_call | solution.py:337
  (3 shorter events, 0.1 us)
Async XLA Ops:
  0.0 16.3 %copy-start = (f32[2,8,192,128]{3,2,1,0:T(8,128)S(1)}, f32[2,8,192,128]{3,2,1,0:T(8,128)}, u32[]{:S(2)}) copy-start(f32[2,8,192,128]{3,2,1,0:T(8,128)} %param.9) | copy-start | bytes 4718596
  0.0 9.3 %copy-start.6 = (s32[192,1]{1,0:T(8,128)S(1)}, s32[192,1]{1,0:T(8,128)}, u32[]{:S(2)}) copy-start(s32[192,1]{1,0:T(8,128)} %constant.21.clone.slot_ref) | copy-start | bytes 2308
  0.0 9.4 %copy-start.8 = (s32[192]{0:T(256)S(1)}, s32[192]{0:T(256)}, u32[]{:S(2)}) copy-start(s32[192]{0:T(256)} %param.11) | copy-start | bytes 2308
  1.9 19.7 %all-to-all-start = ((f32[16,2,24,128]{3,2,1,0:T(8,128)}), f32[16,2,24,128]{3,2,1,0:T(8,128)}, u32[]{:S(2)}, u32[]{:S(2)}) async-start(f32[16,2,24,128]{3,2,1,0:T(8,128)} %pieces.1), calls=%async_computation | async-start | bytes 786432 | tf_op jit(solution)/shard_map/all_to_all | solution.py:269
  9.4 12.2 %copy-start.7 = (f32[16,128]{1,0:T(8,128)S(1)}, f32[16,128]{1,0:T(8,128)}, u32[]{:S(2)}) copy-start(f32[16,128]{1,0:T(8,128)} %proto_ref.1) | copy-start | bytes 24580
  14.7 0.8 %copy-start.2 = (bf16[2,384,384]{2,1,0:T(8,128)(2,1)}, bf16[2,384,384]{2,1,0:T(8,128)(2,1)S(1)}, u32[]{:S(2)}) copy-start(bf16[2,384,384]{2,1,0:T(8,128)(2,1)S(1)} %get-tuple-element.17.early_ref) | copy-start | bytes 1769476
  15.5 0.7 %copy-start.4 = (bf16[768,256]{1,0:T(8,128)(2,1)}, bf16[768,256]{1,0:T(8,128)(2,1)S(1)}, u32[]{:S(2)}) copy-start(bf16[768,256]{1,0:T(8,128)(2,1)S(1)} %get-tuple-element.16.table_ref) | copy-start | bytes 1179652
  16.3 24.1 %copy-start.1 = (bf16[6,384,384]{2,1,0:T(8,128)(2,1)S(1)}, bf16[6,384,384]{2,1,0:T(8,128)(2,1)}, u32[]{:S(2)}) copy-start(bf16[6,384,384]{2,1,0:T(8,128)(2,1)} %get-tuple-element.18.late_ref) | copy-start | bytes 5308420
  21.6 18.8 %copy-start.3 = (bf16[2,384,384]{2,1,0:T(8,128)(2,1)S(1)}, bf16[2,384,384]{2,1,0:T(8,128)(2,1)}, u32[]{:S(2)}) copy-start(bf16[2,384,384]{2,1,0:T(8,128)(2,1)} %copy-done.2) | copy-start | bytes 1769476
  21.6 1.1 %copy-start.5 = (bf16[768,256]{1,0:T(8,128)(2,1)S(1)}, bf16[768,256]{1,0:T(8,128)(2,1)}, u32[]{:S(2)}) copy-start(bf16[768,256]{1,0:T(8,128)(2,1)} %copy-done.4) | copy-start | bytes 1179652

commit v14 on v12

--- a/solution.py
+++ b/solution.py
@@ -9,7 +9,6 @@
 from jax.sharding import PartitionSpec as P
 
 INTEG = 4
-EARLY = 2
 HIGHEST = lax.Precision.HIGHEST
 F32 = jnp.float32
 BF16 = jnp.bfloat16
@@ -58,17 +57,16 @@
 
 
 def weights_kernel(
-    w_ref, order_ref, slot_ref, table_ref, early_ref, late_ref, table_out_ref, *scratch
+    w_ref, order_ref, slot_ref, table_ref, out_ref, table_out_ref, buffer, made, sems, table_sem
 ):
-    buffer, made, sems, table_sem = scratch
     table_copy = pltpu.make_async_copy(table_ref, table_out_ref, table_sem)
     loads = [
         pltpu.make_async_copy(w_ref.at[chan], buffer.at[chan], sems.at[0, chan])
         for chan in range(w_ref.shape[0])
     ]
     stores = [
-        pltpu.make_async_copy(made.at[chan], late_ref.at[chan], sems.at[1, chan])
-        for chan in range(late_ref.shape[0])
+        pltpu.make_async_copy(made.at[chan], out_ref.at[chan], sems.at[1, chan])
+        for chan in range(w_ref.shape[0])
     ]
     ahead = 3
     for load in loads[:ahead]:
@@ -87,13 +85,8 @@
                 for half in split(buffer[chan, part].T)
             ]
             rows = slice(part * beams, (part + 1) * beams)
-            both = jnp.concatenate(halves, axis=1)
-            if chan < EARLY:
-                early_ref[chan, rows, :] = both
-            else:
-                made[chan - EARLY, rows, :] = both
-        if chan >= EARLY:
-            stores[chan - EARLY].start()
+            made[chan, rows, :] = jnp.concatenate(halves, axis=1)
+        stores[chan].start()
     for store in stores:
         store.wait()
     table_copy.wait()
@@ -165,16 +158,9 @@
             ]
 
 
-def beams_kernel(x_ref, early_ref, late_hbm, out_ref, late_ref, sems):
-    loads = []
-    for step in range(late_hbm.shape[0] // 2):
-        pair = slice(2 * step, 2 * step + 2)
-        loads.append(
-            pltpu.make_async_copy(late_hbm.at[pair], late_ref.at[pair], sems.at[step])
-        )
-        loads[-1].start()
+def beams_kernel(x_ref, w_ref, out_ref):
     rows = x_ref.shape[0] // 8
-    beams = early_ref.shape[1] // 2
+    beams = w_ref.shape[1] // 2
     lane = lax.broadcasted_iota(jnp.int32, (rows, LANES), 1)
     even = lane % 64 < 32
     wide = lax.broadcasted_iota(jnp.int32, (beams, LANES), 1)
@@ -193,15 +179,9 @@
         fields.append(jnp.concatenate([both, both], axis=0))
     beam_of = []
     for step in steps:
-        if 2 * step < EARLY:
-            w_ref, begin = early_ref, 2 * step
-        else:
-            w_ref, begin = late_ref, 2 * step - EARLY
-            loads[begin // 2].wait()
         sums = []
         for index in range(2):
-            weights = w_ref[begin + index]
-            product = jnp.dot(weights, fields[step], preferred_element_type=F32)
+            product = jnp.dot(w_ref[2 * step + index], fields[step], preferred_element_type=F32)
             sums.append(product[:, 0:LANES] + product[:, LANES : 2 * LANES])
         by_real = jnp.where(even_wide, sums[0][:beams], sums[1][:beams])
         by_imag = jnp.where(even_wide, sums[0][beams:], sums[1][beams:])
@@ -266,18 +246,17 @@
     taps = jnp.concatenate([eight, eight, four, four], axis=2)
     taps = jnp.transpose(taps, (1, 0, 2, 3))
     table = dft_parts(channels)
-    early, late, table = pl.pallas_call(
+    weights, table = pl.pallas_call(
         weights_kernel,
         out_shape=[
-            jax.ShapeDtypeStruct((EARLY, 2 * beams, 2 * dishes), BF16),
-            pltpu.HBM((band_chans - EARLY, 2 * beams, 2 * dishes), BF16),
+            pltpu.HBM((band_chans, 2 * beams, 2 * dishes), BF16),
             jax.ShapeDtypeStruct(table.shape, BF16),
         ],
         in_specs=[HBM, VMEM, VMEM, HBM],
-        out_specs=[VMEM, HBM, VMEM],
+        out_specs=[HBM, VMEM],
         scratch_shapes=[
             pltpu.VMEM((band_chans, 2, dishes, beams), F32),
-            pltpu.VMEM((band_chans - EARLY, 2 * beams, 2 * dishes), BF16),
+            pltpu.VMEM((band_chans, 2 * beams, 2 * dishes), BF16),
             pltpu.SemaphoreType.DMA((2, band_chans)),
             pltpu.SemaphoreType.DMA(()),
         ],
@@ -292,7 +271,7 @@
         slots_of(devices),
         held(jnp.asarray(table), pltpu.HBM),
     )
-    arrived, early, late, table = lax.optimization_barrier((arrived, early, late, table))
+    arrived, weights, table = lax.optimization_barrier((arrived, weights, table))
 
     block = (6 * band_chans, channels)
     filtered = pl.pallas_call(
@@ -309,20 +288,17 @@
         name="channels",
         compiler_params=GRANT,
     )(held(arrived, pltpu.VMEM), prototype, held(table, pltpu.VMEM), taps)
+    filtered, weights = lax.optimization_barrier((filtered, weights))
     field = exchange(filtered).reshape(devices * 6 * band_chans, channels)
 
     power = pl.pallas_call(
         beams_kernel,
         out_shape=jax.ShapeDtypeStruct((band_chans, frames // INTEG, beams), F32),
-        in_specs=[VMEM, VMEM, HBM],
+        in_specs=[VMEM] * 2,
         out_specs=VMEM,
-        scratch_shapes=[
-            pltpu.VMEM(late.shape, BF16),
-            pltpu.SemaphoreType.DMA((late.shape[0] // 2,)),
-        ],
         name="beams",
         compiler_params=GRANT,
-    )(held(field, pltpu.VMEM), held(early, pltpu.VMEM), held(late, pltpu.HBM))
+    )(held(field, pltpu.VMEM), weights)
     return jnp.transpose(power, (0, 2, 1))[None]
 
 

time: 42 us -> 42.1 us (level)
  local copies, waits for them, and re-layouts: 1.17 us -> 2.84 us
  Pallas kernels: 10.8 us -> 9.2 us
    unnamed x10 -> x12, local copies, waits for them, and re-layouts: 1.13 us -> 2.8 us
    pallas_call x1, Pallas kernels: 3.49 us -> 1.88 us  [close_body(): pl.pallas_call(beams_kernel, out_shape=jax.ShapeDtypeStruct((band_chans,...]
where the time goes in v14:
time: 42.1 us; the launch traced here: 41.8 us
  blocking collectives  15.5 us (37%)
  Pallas kernels  9.2 us (22%)
  starting transfers between devices  7.39 us (18%)
  waiting for transfers between devices  6.7 us (16%)
  local copies, waits for them, and re-layouts  2.84 us (7%)
    all_to_all x1, blocking collectives, exchange(): lax.all_to_all(value, 'band', split_axis=0, concat_axis=0, tiled=True)  15.5 us
    all_to_all x1, starting transfers between devices, exchange(): lax.all_to_all(value, 'band', split_axis=0, concat_axis=0, tiled=True)  7.39 us
    all_to_all x1, waiting for transfers between devices, exchange(): lax.all_to_all(value, 'band', split_axis=0, concat_axis=0, tiled=True)  6.7 us
    pallas_call x1, Pallas kernels, close_body(): pl.pallas_call(weights_kernel, out_shape=[pltpu.HBM((band_chans, 2 * beam...  5.36 us
    unnamed x12, local copies, waits for them, and re-layouts  2.8 us
    pallas_call x1, Pallas kernels, close_body(): pl.pallas_call(beams_kernel, out_shape=jax.ShapeDtypeStruct((band_chans,...  1.88 us
    pallas_call x1, Pallas kernels, close_body(): pl.pallas_call(channel_kernel, out_shape=jax.ShapeDtypeStruct((devices,)...  1.19 us
  transfers between devices with their start and end apart: 1, of which 1 were waited for; matrix products, arithmetic and copies ran while one was open for 0% of the time, Pallas kernels for 13%

profile of v14, /device:TPU:0, one launch (start us, length us, event | category | flops | bytes accessed | tf_op | source)
XLA Modules:
  0.0 41.8 jit_solution(15661103698161676747)
XLA Ops:
  0.0 0.0 copy-start
  0.0 0.0 copy-start.2
  0.0 1.1 %copy-done.2 = f32[2,192,256]{2,1,0:T(8,128)S(1)} copy-done((f32[2,192,256]{2,1,0:T(8,128)S(1)}, f32[2,192,256]{2,1,0:T(8,128)}, u32[]{:S(2)}) %copy-start.2) | copy-done | bytes 393240
  1.1 0.0 copy-start.3
  1.1 0.0 copy-start.5
  1.1 0.8 %pieces.1 = f32[16,2,24,128]{3,2,1,0:T(8,128)} custom-call(f32[2,192,256]{2,1,0:T(8,128)S(1)} %copy-done.2), custom_call_target="tpu_custom_call" | custom-call | tf_op jit(solution)/shard_map/pieces/pallas_call | solution.py:234
  1.9 7.4 %all-to-all-start = ((f32[16,2,24,128]{3,2,1,0:T(8,128)}), f32[16,2,24,128]{3,2,1,0:T(8,128)S(1)}, u32[]{:S(2)}, u32[]{:S(2)}) async-start(f32[16,2,24,128]{3,2,1,0:T(8,128)} %pieces.1), calls=%async_computation | async-start | bytes 786432 | tf_op jit(solution)/shard_map/all_to_all | solution.py:232
  9.3 0.0 copy-done.3
  9.3 0.0 copy-done.5
  9.3 0.0 copy-start.4
  9.3 5.4 %weights.1 = (bf16[8,384,384]{2,1,0:T(8,128)(2,1)}, bf16[768,256]{1,0:T(8,128)(2,1)S(1)}) custom-call(f32[8,2,192,192]{3,2,1,0:T(8,128)} %bitcast.12, s32[1,192]{1,0:T(1,128)S(1)} %bitcast.11, s32[192,1]{1,0:T(8,128)S(1)} %copy-done.3, bf16[768,256]{1,0:T(8,128)(2,1)} %constant.20.clone.table_ref), custom_call_target="tpu_custom_call" | custom-call | flops 905969664 | bytes 5242880 | tf_op jit(solution)/shard_map/weights/pallas_call | solution.py:249
  14.7 0.0 copy-done
  14.8 6.7 %all-to-all-done = f32[16,2,24,128]{3,2,1,0:T(8,128)S(1)} async-done(((f32[16,2,24,128]{3,2,1,0:T(8,128)}), f32[16,2,24,128]{3,2,1,0:T(8,128)S(1)}, u32[]{:S(2)}, u32[]{:S(2)}) %all-to-all-start) | async-done | bytes 393248 | tf_op jit(solution)/shard_map/all_to_all | solution.py:232
  21.5 0.0 copy-done.4
  21.5 1.2 %channels.1 = f32[16,48,128]{2,1,0:T(8,128)S(1)} custom-call(f32[32,24,128]{2,1,0:T(8,128)S(1)} %bitcast.9, f32[16,128]{1,0:T(8,128)S(1)} %copy-done.4, bf16[768,256]{1,0:T(8,128)(2,1)S(1)} %get-tuple-element.15.table_ref, f32[8,2,24,128]{3,2,1,0:T(8,128)S(1)} %copy_bitcast_fusion.taps_ref), custom_call_target="tpu_custom_call" | custom-call | tf_op jit(solution)/shard_map/channels/pallas_call | solution.py:277
  22.7 15.5 %all_to_all.10 = f32[16,48,128]{2,1,0:T(8,128)S(1)} all-to-all(f32[16,48,128]{2,1,0:T(8,128)S(1)} %channels.1), channel_id=1, replica_groups=mesh['grp'=2,'band'=16] {'band'}, dimensions={0} | all-to-all | bytes 786432 | tf_op jit(solution)/shard_map/all_to_all | solution.py:232
  38.2 0.0 copy-start.1
  38.2 1.7 %copy-done.1 = bf16[8,384,384]{2,1,0:T(8,128)(2,1)S(1)} copy-done((bf16[8,384,384]{2,1,0:T(8,128)(2,1)S(1)}, bf16[8,384,384]{2,1,0:T(8,128)(2,1)}, u32[]{:S(2)}) %copy-start.1) | copy-done | bytes 2359320
  39.9 1.9 %beams.1 = f32[8,8,192]{2,1,0:T(8,128)} custom-call(f32[768,128]{1,0:T(8,128)S(1)} %bitcast.10, bf16[8,384,384]{2,1,0:T(8,128)(2,1)S(1)} %copy-done.1), custom_call_target="tpu_custom_call" | custom-call | tf_op jit(solution)/shard_map/beams/pallas_call | solution.py:294
  (3 shorter events, 0.1 us)
Async XLA Ops:
  0.0 14.7 %copy-start = (f32[2,8,192,128]{3,2,1,0:T(8,128)S(1)}, f32[2,8,192,128]{3,2,1,0:T(8,128)}, u32[]{:S(2)}) copy-start(f32[2,8,192,128]{3,2,1,0:T(8,128)} %param.9) | copy-start | bytes 4718596
  0.0 1.1 %copy-start.2 = (f32[2,192,256]{2,1,0:T(8,128)S(1)}, f32[2,192,256]{2,1,0:T(8,128)}, u32[]{:S(2)}) copy-start(f32[2,192,256]{2,1,0:T(8,128)} %x_ref.1) | copy-start | bytes 1179652
  1.1 8.2 %copy-start.3 = (s32[192,1]{1,0:T(8,128)S(1)}, s32[192,1]{1,0:T(8,128)}, u32[]{:S(2)}) copy-start(s32[192,1]{1,0:T(8,128)} %constant.21.clone.slot_ref) | copy-start | bytes 2308
  1.1 8.2 %copy-start.5 = (s32[192]{0:T(256)S(1)}, s32[192]{0:T(256)}, u32[]{:S(2)}) copy-start(s32[192]{0:T(256)} %param.11) | copy-start | bytes 2308
  1.9 19.6 %all-to-all-start = ((f32[16,2,24,128]{3,2,1,0:T(8,128)}), f32[16,2,24,128]{3,2,1,0:T(8,128)S(1)}, u32[]{:S(2)}, u32[]{:S(2)}) async-start(f32[16,2,24,128]{3,2,1,0:T(8,128)} %pieces.1), calls=%async_computation | async-start | bytes 786432 | tf_op jit(solution)/shard_map/all_to_all | solution.py:232
  9.3 12.2 %copy-start.4 = (f32[16,128]{1,0:T(8,128)S(1)}, f32[16,128]{1,0:T(8,128)}, u32[]{:S(2)}) copy-start(f32[16,128]{1,0:T(8,128)} %proto_ref.1) | copy-start | bytes 24580
  38.2 1.7 %copy-start.1 = (bf16[8,384,384]{2,1,0:T(8,128)(2,1)S(1)}, bf16[8,384,384]{2,1,0:T(8,128)(2,1)}, u32[]{:S(2)}) copy-start(bf16[8,384,384]{2,1,0:T(8,128)(2,1)} %get-tuple-element.18.w_ref) | copy-start | bytes 7077892

commit v15 on v12

--- a/solution.py
+++ b/solution.py
@@ -100,8 +100,11 @@
 
 
 def channel_kernel(
-    x_ref, proto_ref, table_ref, taps_ref, out_ref, past, poly, spec, filt
+    x_ref, proto_ref, table_ref, taps_ref, late_ref, out_ref, late_out_ref, *scratch
 ):
+    past, poly, spec, filt, late_sem = scratch
+    late_copy = pltpu.make_async_copy(late_ref, late_out_ref, late_sem)
+    late_copy.start()
     pfb_count = proto_ref.shape[0]
     fir_count = taps_ref.shape[0]
     frames = poly.shape[0]
@@ -163,16 +166,10 @@
             out_ref[dev, pair * per_band : (pair + 1) * per_band, :] = turned[
                 dev * per_band : (dev + 1) * per_band
             ]
-
-
-def beams_kernel(x_ref, early_ref, late_hbm, out_ref, late_ref, sems):
-    loads = []
-    for step in range(late_hbm.shape[0] // 2):
-        pair = slice(2 * step, 2 * step + 2)
-        loads.append(
-            pltpu.make_async_copy(late_hbm.at[pair], late_ref.at[pair], sems.at[step])
-        )
-        loads[-1].start()
+    late_copy.wait()
+
+
+def beams_kernel(x_ref, early_ref, late_ref, out_ref):
     rows = x_ref.shape[0] // 8
     beams = early_ref.shape[1] // 2
     lane = lax.broadcasted_iota(jnp.int32, (rows, LANES), 1)
@@ -197,7 +194,6 @@
             w_ref, begin = early_ref, 2 * step
         else:
             w_ref, begin = late_ref, 2 * step - EARLY
-            loads[begin // 2].wait()
         sums = []
         for index in range(2):
             weights = w_ref[begin + index]
@@ -295,34 +291,40 @@
     arrived, early, late, table = lax.optimization_barrier((arrived, early, late, table))
 
     block = (6 * band_chans, channels)
-    filtered = pl.pallas_call(
+    filtered, late = pl.pallas_call(
         channel_kernel,
-        out_shape=jax.ShapeDtypeStruct((devices,) + block, F32),
-        in_specs=[VMEM] * 4,
-        out_specs=VMEM,
+        out_shape=[
+            jax.ShapeDtypeStruct((devices,) + block, F32),
+            jax.ShapeDtypeStruct(late.shape, BF16),
+        ],
+        in_specs=[VMEM] * 4 + [HBM],
+        out_specs=[VMEM] * 2,
         scratch_shapes=[
             pltpu.VMEM((frames + prototype.shape[0] - 1, 24, LANES), F32),
             pltpu.VMEM((frames, 24, 2 * LANES), F32),
             pltpu.VMEM((frames + fir_count - 1, 24, 2 * LANES), F32),
             pltpu.VMEM((frames * 24, LANES), F32),
+            pltpu.SemaphoreType.DMA(()),
         ],
         name="channels",
         compiler_params=GRANT,
-    )(held(arrived, pltpu.VMEM), prototype, held(table, pltpu.VMEM), taps)
+    )(
+        held(arrived, pltpu.VMEM),
+        prototype,
+        held(table, pltpu.VMEM),
+        taps,
+        held(late, pltpu.HBM),
+    )
     field = exchange(filtered).reshape(devices * 6 * band_chans, channels)
 
     power = pl.pallas_call(
         beams_kernel,
         out_shape=jax.ShapeDtypeStruct((band_chans, frames // INTEG, beams), F32),
-        in_specs=[VMEM, VMEM, HBM],
+        in_specs=[VMEM] * 3,
         out_specs=VMEM,
-        scratch_shapes=[
-            pltpu.VMEM(late.shape, BF16),
-            pltpu.SemaphoreType.DMA((late.shape[0] // 2,)),
-        ],
         name="beams",
         compiler_params=GRANT,
-    )(held(field, pltpu.VMEM), held(early, pltpu.VMEM), held(late, pltpu.HBM))
+    )(held(field, pltpu.VMEM), held(early, pltpu.VMEM), held(late, pltpu.VMEM))
     return jnp.transpose(power, (0, 2, 1))[None]
 
 

time: 42 us -> 40.8 us (0.971)
  local copies, waits for them, and re-layouts: 1.17 us -> 2.73 us
  waiting for transfers between devices: 6.7 us -> 5.15 us
  Pallas kernels: 10.8 us -> 9.52 us
    pallas_call x1, Pallas kernels: 3.49 us -> 1.88 us  [close_body(): pl.pallas_call(beams_kernel, out_shape=jax.ShapeDtypeStruct((band_chans,...]
    unnamed x10, local copies, waits for them, and re-layouts: 1.13 us -> 2.69 us
    all_to_all x1, waiting for transfers between devices: 6.7 us -> 5.15 us  [exchange(): lax.all_to_all(value, 'band', split_axis=0, concat_axis=0, tiled=True)]
where the time goes in v15:
time: 40.8 us; the launch traced here: 40.4 us
  blocking collectives  15.5 us (38%)
  Pallas kernels  9.52 us (23%)
  starting transfers between devices  7.39 us (18%)
  waiting for transfers between devices  5.15 us (13%)
  local copies, waits for them, and re-layouts  2.73 us (7%)
    all_to_all x1, blocking collectives, exchange(): lax.all_to_all(value, 'band', split_axis=0, concat_axis=0, tiled=True)  15.5 us
    all_to_all x1, starting transfers between devices, exchange(): lax.all_to_all(value, 'band', split_axis=0, concat_axis=0, tiled=True)  7.39 us
    pallas_call x1, Pallas kernels, close_body(): pl.pallas_call(weights_kernel, out_shape=[jax.ShapeDtypeStruct((EARLY, 2...  5.36 us
    all_to_all x1, waiting for transfers between devices, exchange(): lax.all_to_all(value, 'band', split_axis=0, concat_axis=0, tiled=True)  5.15 us
    unnamed x10, local copies, waits for them, and re-layouts  2.69 us
    pallas_call x1, Pallas kernels, close_body(): pl.pallas_call(beams_kernel, out_shape=jax.ShapeDtypeStruct((band_chans,...  1.88 us
    pallas_call x1, Pallas kernels, close_body(): pl.pallas_call(channel_kernel, out_shape=[jax.ShapeDtypeStruct((devices,)...  1.49 us
  transfers between devices with their start and end apart: 1, of which 1 were waited for; matrix products, arithmetic and copies ran while one was open for 0% of the time, Pallas kernels for 13%

profile of v15, /device:TPU:0, one launch (start us, length us, event | category | flops | bytes accessed | tf_op | source)
XLA Modules:
  0.0 40.4 jit_solution(4576442880182108065)
XLA Ops:
  0.0 0.0 copy-start
  0.0 0.0 copy-start.1
  0.0 1.1 %copy-done.1 = f32[2,192,256]{2,1,0:T(8,128)S(1)} copy-done((f32[2,192,256]{2,1,0:T(8,128)S(1)}, f32[2,192,256]{2,1,0:T(8,128)}, u32[]{:S(2)}) %copy-start.1) | copy-done | bytes 393240
  1.1 0.8 %pieces.1 = f32[16,2,24,128]{3,2,1,0:T(8,128)} custom-call(f32[2,192,256]{2,1,0:T(8,128)S(1)} %copy-done.1), custom_call_target="tpu_custom_call" | custom-call | tf_op jit(solution)/shard_map/pieces/pallas_call | solution.py:250
  1.9 7.4 %all-to-all-start = ((f32[16,2,24,128]{3,2,1,0:T(8,128)}), f32[16,2,24,128]{3,2,1,0:T(8,128)S(1)}, u32[]{:S(2)}, u32[]{:S(2)}) async-start(f32[16,2,24,128]{3,2,1,0:T(8,128)} %pieces.1), calls=%async_computation | async-start | bytes 786432 | tf_op jit(solution)/shard_map/all_to_all | solution.py:248
  9.3 0.0 copy-start.2
  9.3 0.9 %copy-done.2 = s32[192,1]{1,0:T(8,128)S(1)} copy-done((s32[192,1]{1,0:T(8,128)S(1)}, s32[192,1]{1,0:T(8,128)}, u32[]{:S(2)}) %copy-start.2) | copy-done | bytes 792
  10.2 0.0 copy-start.4
  10.2 0.7 %copy-done.4 = s32[192]{0:T(256)S(1)} copy-done((s32[192]{0:T(256)S(1)}, s32[192]{0:T(256)}, u32[]{:S(2)}) %copy-start.4) | copy-done | bytes 792
  10.9 0.0 copy-start.3
  10.9 5.4 %weights.1 = (bf16[2,384,384]{2,1,0:T(8,128)(2,1)S(1)}, bf16[6,384,384]{2,1,0:T(8,128)(2,1)}, bf16[768,256]{1,0:T(8,128)(2,1)S(1)}) custom-call(f32[8,2,192,192]{3,2,1,0:T(8,128)} %bitcast.12, s32[1,192]{1,0:T(1,128)S(1)} %bitcast.11, s32[192,1]{1,0:T(8,128)S(1)} %copy-done.2, bf16[768,256]{1,0:T(8,128)(2,1)} %constant.20.clone.table_ref), custom_call_target="tpu_custom_call" | custom-call | flops 905969664 | bytes 5242880 | tf_op jit(solution)/shard_map/weights/pallas_call | solution.py:265
  16.3 0.0 copy-done
  16.4 5.2 %all-to-all-done = f32[16,2,24,128]{3,2,1,0:T(8,128)S(1)} async-done(((f32[16,2,24,128]{3,2,1,0:T(8,128)}), f32[16,2,24,128]{3,2,1,0:T(8,128)S(1)}, u32[]{:S(2)}, u32[]{:S(2)}) %all-to-all-start) | async-done | bytes 393248 | tf_op jit(solution)/shard_map/all_to_all | solution.py:248
  21.5 0.0 copy-done.3
  21.5 1.5 %channels.1 = (f32[16,48,128]{2,1,0:T(8,128)S(1)}, bf16[6,384,384]{2,1,0:T(8,128)(2,1)S(1)}) custom-call(f32[32,24,128]{2,1,0:T(8,128)S(1)} %bitcast.9, f32[16,128]{1,0:T(8,128)S(1)} %copy-done.3, bf16[768,256]{1,0:T(8,128)(2,1)S(1)} %get-tuple-element.18.table_ref, f32[8,2,24,128]{3,2,1,0:T(8,128)S(1)} %copy_bitcast_fusion.taps_ref, ...), custom_call_target="tpu_custom_call" | custom-call | tf_op jit(solution)/shard_map/channels/pallas_call | solution.py:294
  23.0 15.5 %all_to_all.10 = f32[16,48,128]{2,1,0:T(8,128)S(1)} all-to-all(f32[16,48,128]{2,1,0:T(8,128)S(1)} %get-tuple-element.20), channel_id=1, replica_groups=mesh['grp'=2,'band'=16] {'band'}, dimensions={0} | all-to-all | bytes 786432 | tf_op jit(solution)/shard_map/all_to_all | solution.py:248
  38.5 1.9 %beams.1 = f32[8,8,192]{2,1,0:T(8,128)} custom-call(f32[768,128]{1,0:T(8,128)S(1)} %bitcast.10, bf16[2,384,384]{2,1,0:T(8,128)(2,1)S(1)} %get-tuple-element.21.early_ref, bf16[6,384,384]{2,1,0:T(8,128)(2,1)S(1)} %get-tuple-element.22.late_ref), custom_call_target="tpu_custom_call" | custom-call | tf_op jit(solution)/shard_map/beams/pallas_call | solution.py:320
  (3 shorter events, 0.1 us)
Async XLA Ops:
  0.0 16.3 %copy-start = (f32[2,8,192,128]{3,2,1,0:T(8,128)S(1)}, f32[2,8,192,128]{3,2,1,0:T(8,128)}, u32[]{:S(2)}) copy-start(f32[2,8,192,128]{3,2,1,0:T(8,128)} %param.9) | copy-start | bytes 4718596
  0.0 1.1 %copy-start.1 = (f32[2,192,256]{2,1,0:T(8,128)S(1)}, f32[2,192,256]{2,1,0:T(8,128)}, u32[]{:S(2)}) copy-start(f32[2,192,256]{2,1,0:T(8,128)} %x_ref.1) | copy-start | bytes 1179652
  1.9 19.6 %all-to-all-start = ((f32[16,2,24,128]{3,2,1,0:T(8,128)}), f32[16,2,24,128]{3,2,1,0:T(8,128)S(1)}, u32[]{:S(2)}, u32[]{:S(2)}) async-start(f32[16,2,24,128]{3,2,1,0:T(8,128)} %pieces.1), calls=%async_computation | async-start | bytes 786432 | tf_op jit(solution)/shard_map/all_to_all | solution.py:248
  9.3 0.9 %copy-start.2 = (s32[192,1]{1,0:T(8,128)S(1)}, s32[192,1]{1,0:T(8,128)}, u32[]{:S(2)}) copy-start(s32[192,1]{1,0:T(8,128)} %constant.21.clone.slot_ref) | copy-start | bytes 2308
  10.2 0.7 %copy-start.4 = (s32[192]{0:T(256)S(1)}, s32[192]{0:T(256)}, u32[]{:S(2)}) copy-start(s32[192]{0:T(256)} %param.11) | copy-start | bytes 2308
  10.9 10.6 %copy-start.3 = (f32[16,128]{1,0:T(8,128)S(1)}, f32[16,128]{1,0:T(8,128)}, u32[]{:S(2)}) copy-start(f32[16,128]{1,0:T(8,128)} %proto_ref.1) | copy-start | bytes 24580

commit v16 on v15

--- a/solution.py
+++ b/solution.py
@@ -58,10 +58,8 @@
 
 
 def weights_kernel(
-    w_ref, order_ref, slot_ref, table_ref, early_ref, late_ref, table_out_ref, *scratch
+    w_ref, order_ref, slot_ref, early_ref, late_ref, buffer, made, sems
 ):
-    buffer, made, sems, table_sem = scratch
-    table_copy = pltpu.make_async_copy(table_ref, table_out_ref, table_sem)
     loads = [
         pltpu.make_async_copy(w_ref.at[chan], buffer.at[chan], sems.at[0, chan])
         for chan in range(w_ref.shape[0])
@@ -79,8 +77,6 @@
         load.wait()
         if chan + ahead < len(loads):
             loads[chan + ahead].start()
-        elif chan + ahead == len(loads):
-            table_copy.start()
         for part in range(2):
             halves = [
                 jnp.dot(half, hot, preferred_element_type=F32).astype(BF16)
@@ -96,17 +92,27 @@
             stores[chan - EARLY].start()
     for store in stores:
         store.wait()
-    table_copy.wait()
 
 
 def channel_kernel(
-    x_ref, proto_ref, table_ref, taps_ref, late_ref, out_ref, late_out_ref, *scratch
+    x_ref, proto_ref, table_hbm, taps_hbm, late_ref, out_ref, late_out_ref, *scratch
 ):
-    past, poly, spec, filt, late_sem = scratch
-    late_copy = pltpu.make_async_copy(late_ref, late_out_ref, late_sem)
+    past, poly, spec, filt, table_ref, taps_ref, sems = scratch
+    place = lax.axis_index("band")
+    devices = out_ref.shape[0]
+    eight = pl.ds(pl.multiple_of(place * 8, 8), 8)
+    pair_rows = pl.ds(pl.multiple_of(devices * 8 + place // 2 * 8, 8), 8)
+    loads = [
+        pltpu.make_async_copy(taps_hbm.at[:, :, eight, :], taps_ref.at[:, :, 0:8], sems.at[0]),
+        pltpu.make_async_copy(taps_hbm.at[:, :, pair_rows, :], taps_ref.at[:, :, 8:16], sems.at[1]),
+        pltpu.make_async_copy(table_hbm, table_ref, sems.at[2]),
+    ]
+    for load in loads:
+        load.start()
+    late_copy = pltpu.make_async_copy(late_ref, late_out_ref, sems.at[3])
     late_copy.start()
     pfb_count = proto_ref.shape[0]
-    fir_count = taps_ref.shape[0]
+    fir_count = taps_ref.shape[1]
     frames = poly.shape[0]
     group = 8
     low = lax.broadcasted_iota(jnp.int32, (group, 8, LANES), 1) < 4
@@ -132,6 +138,9 @@
             poly[first : first + group, rows, 0:LANES] = found[index]
             poly[first : first + group, rows, LANES : 2 * LANES] = other[index]
 
+    for load in loads:
+        load.wait()
+
     for first in range(0, frames, group):
         value = poly[first : first + group].reshape(group * 24, 2 * LANES)
         high, rest = split(value)
@@ -141,14 +150,24 @@
         spec[begin : begin + group] = product.reshape(group, 24, 2 * LANES)
 
     for rows in range(0, 24, 8):
+        taps = []
+        for tap in range(fir_count):
+            for part in range(2):
+                if rows < 16:
+                    taps.append(taps_ref[part, tap, 0:8][None])
+                    continue
+                four = taps_ref[part, tap, 8:16]
+                turned = pltpu.roll(four, 4, 0)
+                even = jnp.where(low[0], four, turned)
+                odd = jnp.where(low[0], turned, four)
+                taps.append(jnp.where(place % 2 == 0, even, odd)[None])
         for first in range(0, frames, group):
             total = None
             for tap in range(fir_count):
                 begin = first + fir_count - 1 - tap
                 near = spec[begin : begin + group, rows : rows + 8, 0:LANES]
                 cross = spec[begin : begin + group, rows : rows + 8, LANES : 2 * LANES]
-                term = taps_ref[tap, 0, rows : rows + 8, :][None] * near
-                term = term + taps_ref[tap, 1, rows : rows + 8, :][None] * cross
+                term = taps[2 * tap] * near + taps[2 * tap + 1] * cross
                 total = term if total is None else total + term
             for frame in range(group):
                 begin = (first + frame) * 24 + rows
@@ -235,7 +254,6 @@
 
 def close_body(samples, prototype, dish_filter, beam_weights, dish_order):
     devices = lax.axis_size("band")
-    position = lax.axis_index("band")
     channels = prototype.shape[1]
     fir_count = dish_filter.shape[1]
     dishes = dish_filter.shape[2]
@@ -257,25 +275,19 @@
     )(samples)
     arrived = exchange(pieces).reshape(frames, 24, channels)
 
-    eight = lax.dynamic_slice_in_dim(dish_filter, position * 8, 8, 2)
-    four = lax.dynamic_slice_in_dim(dish_filter, devices * 8 + position * 4, 4, 2)
-    taps = jnp.concatenate([eight, eight, four, four], axis=2)
-    taps = jnp.transpose(taps, (1, 0, 2, 3))
     table = dft_parts(channels)
-    early, late, table = pl.pallas_call(
+    early, late = pl.pallas_call(
         weights_kernel,
         out_shape=[
             jax.ShapeDtypeStruct((EARLY, 2 * beams, 2 * dishes), BF16),
             pltpu.HBM((band_chans - EARLY, 2 * beams, 2 * dishes), BF16),
-            jax.ShapeDtypeStruct(table.shape, BF16),
         ],
-        in_specs=[HBM, VMEM, VMEM, HBM],
-        out_specs=[VMEM, HBM, VMEM],
+        in_specs=[HBM, VMEM, VMEM],
+        out_specs=[VMEM, HBM],
         scratch_shapes=[
             pltpu.VMEM((band_chans, 2, dishes, beams), F32),
             pltpu.VMEM((band_chans - EARLY, 2 * beams, 2 * dishes), BF16),
             pltpu.SemaphoreType.DMA((2, band_chans)),
-            pltpu.SemaphoreType.DMA(()),
         ],
         name="weights",
         compiler_params=GRANT,
@@ -286,9 +298,8 @@
         held(beam_weights[0], pltpu.HBM),
         dish_order.reshape(1, dishes),
         slots_of(devices),
-        held(jnp.asarray(table), pltpu.HBM),
     )
-    arrived, early, late, table = lax.optimization_barrier((arrived, early, late, table))
+    arrived, early, late = lax.optimization_barrier((arrived, early, late))
 
     block = (6 * band_chans, channels)
     filtered, late = pl.pallas_call(
@@ -297,22 +308,24 @@
             jax.ShapeDtypeStruct((devices,) + block, F32),
             jax.ShapeDtypeStruct(late.shape, BF16),
         ],
-        in_specs=[VMEM] * 4 + [HBM],
+        in_specs=[VMEM] * 2 + [HBM] * 3,
         out_specs=[VMEM] * 2,
         scratch_shapes=[
             pltpu.VMEM((frames + prototype.shape[0] - 1, 24, LANES), F32),
             pltpu.VMEM((frames, 24, 2 * LANES), F32),
             pltpu.VMEM((frames + fir_count - 1, 24, 2 * LANES), F32),
             pltpu.VMEM((frames * 24, LANES), F32),
-            pltpu.SemaphoreType.DMA(()),
+            pltpu.VMEM(table.shape, BF16),
+            pltpu.VMEM((2, fir_count, 16, LANES), F32),
+            pltpu.SemaphoreType.DMA((4,)),
         ],
         name="channels",
         compiler_params=GRANT,
     )(
         held(arrived, pltpu.VMEM),
         prototype,
-        held(table, pltpu.VMEM),
-        taps,
+        held(jnp.asarray(table), pltpu.HBM),
+        held(dish_filter, pltpu.HBM),
         held(late, pltpu.HBM),
     )
     field = exchange(filtered).reshape(devices * 6 * band_chans, channels)

time: 40.8 us -> 41.2 us (level)
  Pallas kernels: 9.52 us -> 10.1 us
    pallas_call x1, Pallas kernels: 1.49 us -> 2.08 us  [close_body(): pl.pallas_call(channel_kernel, out_shape=[jax.ShapeDtypeStruct((devices,)...]
    unnamed x10 -> x8, local copies, waits for them, and re-layouts: 2.69 us -> 2.57 us
where the time goes in v16:
time: 41.2 us; the launch traced here: 40.9 us
  blocking collectives  15.5 us (38%)
  Pallas kernels  10.1 us (25%)
  starting transfers between devices  7.39 us (18%)
  waiting for transfers between devices  5.25 us (13%)
  local copies, waits for them, and re-layouts  2.57 us (6%)
    all_to_all x1, blocking collectives, exchange(): lax.all_to_all(value, 'band', split_axis=0, concat_axis=0, tiled=True)  15.5 us
    all_to_all x1, starting transfers between devices, exchange(): lax.all_to_all(value, 'band', split_axis=0, concat_axis=0, tiled=True)  7.39 us
    pallas_call x1, Pallas kernels, close_body(): pl.pallas_call(weights_kernel, out_shape=[jax.ShapeDtypeStruct((EARLY, 2...  5.35 us
    all_to_all x1, waiting for transfers between devices, exchange(): lax.all_to_all(value, 'band', split_axis=0, concat_axis=0, tiled=True)  5.25 us
    unnamed x8, local copies, waits for them, and re-layouts  2.57 us
    pallas_call x1, Pallas kernels, close_body(): pl.pallas_call(channel_kernel, out_shape=[jax.ShapeDtypeStruct((devices,)...  2.08 us
    pallas_call x1, Pallas kernels, close_body(): pl.pallas_call(beams_kernel, out_shape=jax.ShapeDtypeStruct((band_chans,...  1.88 us
  transfers between devices with their start and end apart: 1, of which 1 were waited for; matrix products, arithmetic and copies ran while one was open for 0% of the time, Pallas kernels for 13%

profile of v16, /device:TPU:0, one launch (start us, length us, event | category | flops | bytes accessed | tf_op | source)
XLA Modules:
  0.0 40.9 jit_solution(16330389390281417851)
XLA Ops:
  0.0 0.0 copy-start
  0.0 1.0 %copy-done = f32[2,192,256]{2,1,0:T(8,128)S(1)} copy-done((f32[2,192,256]{2,1,0:T(8,128)S(1)}, f32[2,192,256]{2,1,0:T(8,128)}, u32[]{:S(2)}) %copy-start) | copy-done | bytes 393240
  1.0 0.8 %pieces.1 = f32[16,2,24,128]{3,2,1,0:T(8,128)} custom-call(f32[2,192,256]{2,1,0:T(8,128)S(1)} %copy-done), custom_call_target="tpu_custom_call" | custom-call | tf_op jit(solution)/shard_map/pieces/pallas_call | solution.py:268
  1.8 7.4 %all-to-all-start = ((f32[16,2,24,128]{3,2,1,0:T(8,128)}), f32[16,2,24,128]{3,2,1,0:T(8,128)S(1)}, u32[]{:S(2)}, u32[]{:S(2)}) async-start(f32[16,2,24,128]{3,2,1,0:T(8,128)} %pieces.1), calls=%async_computation | async-start | bytes 786432 | tf_op jit(solution)/shard_map/all_to_all | solution.py:266
  9.2 0.0 copy-start.1
  9.2 0.0 copy-start.2
  9.2 0.7 %copy-done.2 = s32[192]{0:T(256)S(1)} copy-done((s32[192]{0:T(256)S(1)}, s32[192]{0:T(256)}, u32[]{:S(2)}) %copy-start.2) | copy-done | bytes 792
  9.9 0.0 copy-start.3
  9.9 0.9 %copy-done.3 = s32[192,1]{1,0:T(8,128)S(1)} copy-done((s32[192,1]{1,0:T(8,128)S(1)}, s32[192,1]{1,0:T(8,128)}, u32[]{:S(2)}) %copy-start.3) | copy-done | bytes 792
  10.8 5.3 %weights.1 = (bf16[2,384,384]{2,1,0:T(8,128)(2,1)S(1)}, bf16[6,384,384]{2,1,0:T(8,128)(2,1)}) custom-call(f32[8,2,192,192]{3,2,1,0:T(8,128)} %bitcast.10, s32[1,192]{1,0:T(1,128)S(1)} %bitcast.9, s32[192,1]{1,0:T(8,128)S(1)} %copy-done.3), custom_call_target="tpu_custom_call" | custom-call | flops 905969664 | bytes 5242880 | tf_op jit(solution)/shard_map/weights/pallas_call | solution.py:279
  16.1 5.3 %all-to-all-done = f32[16,2,24,128]{3,2,1,0:T(8,128)S(1)} async-done(((f32[16,2,24,128]{3,2,1,0:T(8,128)}), f32[16,2,24,128]{3,2,1,0:T(8,128)S(1)}, u32[]{:S(2)}, u32[]{:S(2)}) %all-to-all-start) | async-done | bytes 393248 | tf_op jit(solution)/shard_map/all_to_all | solution.py:266
  21.4 0.0 copy-done.1
  21.4 2.1 %channels.1 = (f32[16,48,128]{2,1,0:T(8,128)S(1)}, bf16[6,384,384]{2,1,0:T(8,128)(2,1)S(1)}) custom-call(f32[32,24,128]{2,1,0:T(8,128)S(1)} %bitcast.8, f32[16,128]{1,0:T(8,128)S(1)} %copy-done.1, bf16[768,256]{1,0:T(8,128)(2,1)} %constant.5.clone.table_hbm, f32[2,8,192,128]{3,2,1,0:T(8,128)} %taps_hbm.1, bf16[6,384,384]{2,1,0:T(8,128)(2,1)} %get-tuple-element.15.late_ref), custom_call_target="tpu_custom_call" | custom-call | tf_op jit(solution)/shard_map/channels/pallas_call | solution.py:305
  23.5 15.5 %all_to_all.10 = f32[16,48,128]{2,1,0:T(8,128)S(1)} all-to-all(f32[16,48,128]{2,1,0:T(8,128)S(1)} %get-tuple-element.16), channel_id=1, replica_groups=mesh['grp'=2,'band'=16] {'band'}, dimensions={0} | all-to-all | bytes 786432 | tf_op jit(solution)/shard_map/all_to_all | solution.py:266
  39.0 1.9 %beams.1 = f32[8,8,192]{2,1,0:T(8,128)} custom-call(f32[768,128]{1,0:T(8,128)S(1)} %bitcast.7, bf16[2,384,384]{2,1,0:T(8,128)(2,1)S(1)} %get-tuple-element.17.early_ref, bf16[6,384,384]{2,1,0:T(8,128)(2,1)S(1)} %get-tuple-element.18.late_ref), custom_call_target="tpu_custom_call" | custom-call | tf_op jit(solution)/shard_map/beams/pallas_call | solution.py:333
Async XLA Ops:
  0.0 1.0 %copy-start = (f32[2,192,256]{2,1,0:T(8,128)S(1)}, f32[2,192,256]{2,1,0:T(8,128)}, u32[]{:S(2)}) copy-start(f32[2,192,256]{2,1,0:T(8,128)} %x_ref.1) | copy-start | bytes 1179652
  1.8 19.6 %all-to-all-start = ((f32[16,2,24,128]{3,2,1,0:T(8,128)}), f32[16,2,24,128]{3,2,1,0:T(8,128)S(1)}, u32[]{:S(2)}, u32[]{:S(2)}) async-start(f32[16,2,24,128]{3,2,1,0:T(8,128)} %pieces.1), calls=%async_computation | async-start | bytes 786432 | tf_op jit(solution)/shard_map/all_to_all | solution.py:266
  9.2 12.2 %copy-start.1 = (f32[16,128]{1,0:T(8,128)S(1)}, f32[16,128]{1,0:T(8,128)}, u32[]{:S(2)}) copy-start(f32[16,128]{1,0:T(8,128)} %proto_ref.1) | copy-start | bytes 24580
  9.2 0.7 %copy-start.2 = (s32[192]{0:T(256)S(1)}, s32[192]{0:T(256)}, u32[]{:S(2)}) copy-start(s32[192]{0:T(256)} %param.11) | copy-start | bytes 2308
  9.9 0.9 %copy-start.3 = (s32[192,1]{1,0:T(8,128)S(1)}, s32[192,1]{1,0:T(8,128)}, u32[]{:S(2)}) copy-start(s32[192,1]{1,0:T(8,128)} %constant.4.clone.slot_ref) | copy-start | bytes 2308

commit v17 on v16

--- a/solution.py
+++ b/solution.py
@@ -9,7 +9,6 @@
 from jax.sharding import PartitionSpec as P
 
 INTEG = 4
-EARLY = 2
 HIGHEST = lax.Precision.HIGHEST
 F32 = jnp.float32
 BF16 = jnp.bfloat16
@@ -57,45 +56,19 @@
             out_ref[dev + 1, frame, 16:24, :] = jnp.where(low, pltpu.roll(real, 4, 0), imag)
 
 
-def weights_kernel(
-    w_ref, order_ref, slot_ref, early_ref, late_ref, buffer, made, sems
-):
-    loads = [
-        pltpu.make_async_copy(w_ref.at[chan], buffer.at[chan], sems.at[0, chan])
-        for chan in range(w_ref.shape[0])
-    ]
-    stores = [
-        pltpu.make_async_copy(made.at[chan], late_ref.at[chan], sems.at[1, chan])
-        for chan in range(late_ref.shape[0])
-    ]
-    ahead = 3
-    for load in loads[:ahead]:
-        load.start()
-    hot = (slot_ref[...] == order_ref[...]).astype(F32).T.astype(BF16)
+def make_weights(w_ref, hot, out_ref, chan):
     beams = w_ref.shape[3]
-    for chan, load in enumerate(loads):
-        load.wait()
-        if chan + ahead < len(loads):
-            loads[chan + ahead].start()
-        for part in range(2):
-            halves = [
-                jnp.dot(half, hot, preferred_element_type=F32).astype(BF16)
-                for half in split(buffer[chan, part].T)
-            ]
-            rows = slice(part * beams, (part + 1) * beams)
-            both = jnp.concatenate(halves, axis=1)
-            if chan < EARLY:
-                early_ref[chan, rows, :] = both
-            else:
-                made[chan - EARLY, rows, :] = both
-        if chan >= EARLY:
-            stores[chan - EARLY].start()
-    for store in stores:
-        store.wait()
+    for part in range(2):
+        halves = [
+            jnp.dot(half, hot, preferred_element_type=F32).astype(BF16)
+            for half in split(w_ref[chan, part].T)
+        ]
+        rows = slice(part * beams, (part + 1) * beams)
+        out_ref[chan, rows, :] = jnp.concatenate(halves, axis=1)
 
 
 def channel_kernel(
-    x_ref, proto_ref, table_hbm, taps_hbm, late_ref, out_ref, late_out_ref, *scratch
+    x_ref, proto_ref, w_ref, order_ref, slot_ref, table_hbm, taps_hbm, out_ref, w_out_ref, *scratch
 ):
     past, poly, spec, filt, table_ref, taps_ref, sems = scratch
     place = lax.axis_index("band")
@@ -109,8 +82,8 @@
     ]
     for load in loads:
         load.start()
-    late_copy = pltpu.make_async_copy(late_ref, late_out_ref, sems.at[3])
-    late_copy.start()
+    hot = (slot_ref[...] == order_ref[...]).astype(F32).T.astype(BF16)
+    chans = w_ref.shape[0]
     pfb_count = proto_ref.shape[0]
     fir_count = taps_ref.shape[1]
     frames = poly.shape[0]
@@ -137,6 +110,8 @@
             rows = slice(index * 8, index * 8 + 8)
             poly[first : first + group, rows, 0:LANES] = found[index]
             poly[first : first + group, rows, LANES : 2 * LANES] = other[index]
+        for chan in range(first * chans // frames, (first + group) * chans // frames):
+            make_weights(w_ref, hot, w_out_ref, chan)
 
     for load in loads:
         load.wait()
@@ -185,12 +160,11 @@
             out_ref[dev, pair * per_band : (pair + 1) * per_band, :] = turned[
                 dev * per_band : (dev + 1) * per_band
             ]
-    late_copy.wait()
-
-
-def beams_kernel(x_ref, early_ref, late_ref, out_ref):
+
+
+def beams_kernel(x_ref, w_ref, out_ref):
     rows = x_ref.shape[0] // 8
-    beams = early_ref.shape[1] // 2
+    beams = w_ref.shape[1] // 2
     lane = lax.broadcasted_iota(jnp.int32, (rows, LANES), 1)
     even = lane % 64 < 32
     wide = lax.broadcasted_iota(jnp.int32, (beams, LANES), 1)
@@ -209,14 +183,9 @@
         fields.append(jnp.concatenate([both, both], axis=0))
     beam_of = []
     for step in steps:
-        if 2 * step < EARLY:
-            w_ref, begin = early_ref, 2 * step
-        else:
-            w_ref, begin = late_ref, 2 * step - EARLY
         sums = []
         for index in range(2):
-            weights = w_ref[begin + index]
-            product = jnp.dot(weights, fields[step], preferred_element_type=F32)
+            product = jnp.dot(w_ref[2 * step + index], fields[step], preferred_element_type=F32)
             sums.append(product[:, 0:LANES] + product[:, LANES : 2 * LANES])
         by_real = jnp.where(even_wide, sums[0][:beams], sums[1][:beams])
         by_imag = jnp.where(even_wide, sums[0][beams:], sums[1][beams:])
@@ -276,39 +245,14 @@
     arrived = exchange(pieces).reshape(frames, 24, channels)
 
     table = dft_parts(channels)
-    early, late = pl.pallas_call(
-        weights_kernel,
-        out_shape=[
-            jax.ShapeDtypeStruct((EARLY, 2 * beams, 2 * dishes), BF16),
-            pltpu.HBM((band_chans - EARLY, 2 * beams, 2 * dishes), BF16),
-        ],
-        in_specs=[HBM, VMEM, VMEM],
-        out_specs=[VMEM, HBM],
-        scratch_shapes=[
-            pltpu.VMEM((band_chans, 2, dishes, beams), F32),
-            pltpu.VMEM((band_chans - EARLY, 2 * beams, 2 * dishes), BF16),
-            pltpu.SemaphoreType.DMA((2, band_chans)),
-        ],
-        name="weights",
-        compiler_params=GRANT,
-        cost_estimate=pl.CostEstimate(
-            flops=8 * 4 * 2 * 192 * 192 * 384, bytes_accessed=5 << 20, transcendentals=0
-        ),
-    )(
-        held(beam_weights[0], pltpu.HBM),
-        dish_order.reshape(1, dishes),
-        slots_of(devices),
-    )
-    arrived, early, late = lax.optimization_barrier((arrived, early, late))
-
     block = (6 * band_chans, channels)
-    filtered, late = pl.pallas_call(
+    filtered, weights = pl.pallas_call(
         channel_kernel,
         out_shape=[
             jax.ShapeDtypeStruct((devices,) + block, F32),
-            jax.ShapeDtypeStruct(late.shape, BF16),
+            jax.ShapeDtypeStruct((band_chans, 2 * beams, 2 * dishes), BF16),
         ],
-        in_specs=[VMEM] * 2 + [HBM] * 3,
+        in_specs=[VMEM] * 5 + [HBM] * 2,
         out_specs=[VMEM] * 2,
         scratch_shapes=[
             pltpu.VMEM((frames + prototype.shape[0] - 1, 24, LANES), F32),
@@ -317,27 +261,29 @@
             pltpu.VMEM((frames * 24, LANES), F32),
             pltpu.VMEM(table.shape, BF16),
             pltpu.VMEM((2, fir_count, 16, LANES), F32),
-            pltpu.SemaphoreType.DMA((4,)),
+            pltpu.SemaphoreType.DMA((3,)),
         ],
         name="channels",
         compiler_params=GRANT,
     )(
         held(arrived, pltpu.VMEM),
         prototype,
+        beam_weights[0],
+        dish_order.reshape(1, dishes),
+        slots_of(devices),
         held(jnp.asarray(table), pltpu.HBM),
         held(dish_filter, pltpu.HBM),
-        held(late, pltpu.HBM),
     )
     field = exchange(filtered).reshape(devices * 6 * band_chans, channels)
 
     power = pl.pallas_call(
         beams_kernel,
         out_shape=jax.ShapeDtypeStruct((band_chans, frames // INTEG, beams), F32),
-        in_specs=[VMEM] * 3,
+        in_specs=[VMEM] * 2,
         out_specs=VMEM,
         name="beams",
         compiler_params=GRANT,
-    )(held(field, pltpu.VMEM), held(early, pltpu.VMEM), held(late, pltpu.VMEM))
+    )(held(field, pltpu.VMEM), held(weights, pltpu.VMEM))
     return jnp.transpose(power, (0, 2, 1))[None]
 
 

time: 41.2 us -> 46.2 us (1.12)
  blocking collectives: 15.5 us -> 34.9 us
  starting transfers between devices: 7.39 us -> 0 us
  waiting for transfers between devices: 5.25 us -> 0 us
  Pallas kernels: 10.1 us -> 5.7 us
  local copies, waits for them, and re-layouts: 2.57 us -> 5.15 us
    all_to_all x1 -> x2, blocking collectives: 15.5 us -> 34.9 us  [exchange(): lax.all_to_all(value, 'band', split_axis=0, concat_axis=0, tiled=True)]
    all_to_all x1 -> x0, starting transfers between devices: 7.39 us -> none  [exchange(): lax.all_to_all(value, 'band', split_axis=0, concat_axis=0, tiled=True)]
    pallas_call x1 -> x0, Pallas kernels: 5.35 us -> none  [close_body(): pl.pallas_call(weights_kernel, out_shape=[jax.ShapeDtypeStruct((EARLY, 2...]
    all_to_all x1 -> x0, waiting for transfers between devices: 5.25 us -> none  [exchange(): lax.all_to_all(value, 'band', split_axis=0, concat_axis=0, tiled=True)]
    unnamed x8 -> x10, local copies, waits for them, and re-layouts: 2.57 us -> 5.15 us
    pallas_call x1, Pallas kernels: 2.08 us -> 3.8 us  [close_body(): pl.pallas_call(channel_kernel, out_shape=[jax.ShapeDtypeStruct((devices,)...]
    pallas_call x1, Pallas kernels: 0.78 us -> 0.03 us  [close_body(): pl.pallas_call(pieces_kernel, out_shape=jax.ShapeDtypeStruct((devices, fr...]
  transfers between devices with their start and end apart: 1 -> 0, of which waited for: 1 -> 0; matrix products, arithmetic and copies ran while one was open for 0% -> 0% of each run, Pallas kernels for 13% -> 0%
where the time goes in v17:
time: 46.2 us; the launch traced here: 45.8 us
  blocking collectives  34.9 us (76%)
  Pallas kernels  5.7 us (12%)
  local copies, waits for them, and re-layouts  5.15 us (11%)
    all_to_all x2, blocking collectives, exchange(): lax.all_to_all(value, 'band', split_axis=0, concat_axis=0, tiled=True)  34.9 us
    unnamed x10, local copies, waits for them, and re-layouts  5.15 us
    pallas_call x1, Pallas kernels, close_body(): pl.pallas_call(channel_kernel, out_shape=[jax.ShapeDtypeStruct((devices,)...  3.8 us
    pallas_call x1, Pallas kernels, close_body(): pl.pallas_call(beams_kernel, out_shape=jax.ShapeDtypeStruct((band_chans,...  1.88 us

profile of v17, /device:TPU:0, one launch (start us, length us, event | category | flops | bytes accessed | tf_op | source)
XLA Modules:
  0.0 45.8 jit_solution(2285799954452561788)
XLA Ops:
  0.0 0.0 copy-start.1
  0.0 1.0 %copy-done.1 = f32[2,192,256]{2,1,0:T(8,128)S(1)} copy-done((f32[2,192,256]{2,1,0:T(8,128)S(1)}, f32[2,192,256]{2,1,0:T(8,128)}, u32[]{:S(2)}) %copy-start.1) | copy-done | bytes 393240
  1.0 19.4 %all_to_all.10 = f32[16,2,24,128]{3,2,1,0:T(8,128)S(1)} all-to-all(f32[16,2,24,128]{3,2,1,0:T(8,128)S(1)} %pieces.1), channel_id=1, replica_groups=mesh['grp'=2,'band'=16] {'band'}, dimensions={0} | all-to-all | bytes 786432 | tf_op jit(solution)/shard_map/all_to_all | solution.py:235
  20.4 0.0 copy-start
  20.4 1.9 %copy-done = f32[1,8,2,192,192]{4,3,2,1,0:T(8,128)S(1)} copy-done((f32[1,8,2,192,192]{4,3,2,1,0:T(8,128)S(1)}, f32[1,8,2,192,192]{4,3,2,1,0:T(8,128)}, u32[]{:S(2)}) %copy-start) | copy-done | bytes 2359320
  22.3 0.0 copy-start.2
  22.3 0.9 %copy-done.2 = s32[192,1]{1,0:T(8,128)S(1)} copy-done((s32[192,1]{1,0:T(8,128)S(1)}, s32[192,1]{1,0:T(8,128)}, u32[]{:S(2)}) %copy-start.2) | copy-done | bytes 792
  23.2 0.0 copy-start.3
  23.2 0.7 %copy-done.3 = f32[16,128]{1,0:T(8,128)S(1)} copy-done((f32[16,128]{1,0:T(8,128)S(1)}, f32[16,128]{1,0:T(8,128)}, u32[]{:S(2)}) %copy-start.3) | copy-done | bytes 8216
  23.9 0.0 copy-start.4
  23.9 0.7 %copy-done.4 = s32[192]{0:T(256)S(1)} copy-done((s32[192]{0:T(256)S(1)}, s32[192]{0:T(256)}, u32[]{:S(2)}) %copy-start.4) | copy-done | bytes 792
  24.6 3.8 %channels.1 = (f32[16,48,128]{2,1,0:T(8,128)S(1)}, bf16[8,384,384]{2,1,0:T(8,128)(2,1)S(1)}) custom-call(f32[32,24,128]{2,1,0:T(8,128)S(1)} %bitcast.8, f32[16,128]{1,0:T(8,128)S(1)} %copy-done.3, f32[8,2,192,192]{3,2,1,0:T(8,128)S(1)} %bitcast.7, s32[1,192]{1,0:T(1,128)S(1)} %bitcast.10, s32[192,1]{1,0:T(8,128)S(1)} %copy-done.2, ...), custom_call_target="tpu_custom_call" | custom-call | tf_op jit(solution)/shard_map/channels/pallas_call | solution.py:249
  28.4 15.5 %all_to_all.11 = f32[16,48,128]{2,1,0:T(8,128)S(1)} all-to-all(f32[16,48,128]{2,1,0:T(8,128)S(1)} %get-tuple-element.7), channel_id=1, replica_groups=mesh['grp'=2,'band'=16] {'band'}, dimensions={0} | all-to-all | bytes 786432 | tf_op jit(solution)/shard_map/all_to_all | solution.py:235
  43.9 1.9 %beams.1 = f32[8,8,192]{2,1,0:T(8,128)} custom-call(f32[768,128]{1,0:T(8,128)S(1)} %bitcast.9, bf16[8,384,384]{2,1,0:T(8,128)(2,1)S(1)} %get-tuple-element.8.w_ref), custom_call_target="tpu_custom_call" | custom-call | tf_op jit(solution)/shard_map/beams/pallas_call | solution.py:279
  (1 shorter events, 0.0 us)
Async XLA Ops:
  0.0 1.0 %copy-start.1 = (f32[2,192,256]{2,1,0:T(8,128)S(1)}, f32[2,192,256]{2,1,0:T(8,128)}, u32[]{:S(2)}) copy-start(f32[2,192,256]{2,1,0:T(8,128)} %x_ref.1) | copy-start | bytes 1179652
  20.4 1.9 %copy-start = (f32[1,8,2,192,192]{4,3,2,1,0:T(8,128)S(1)}, f32[1,8,2,192,192]{4,3,2,1,0:T(8,128)}, u32[]{:S(2)}) copy-start(f32[1,8,2,192,192]{4,3,2,1,0:T(8,128)} %param.10) | copy-start | bytes 7077892
  22.3 0.9 %copy-start.2 = (s32[192,1]{1,0:T(8,128)S(1)}, s32[192,1]{1,0:T(8,128)}, u32[]{:S(2)}) copy-start(s32[192,1]{1,0:T(8,128)} %constant.5.clone.slot_ref) | copy-start | bytes 2308
  23.2 0.7 %copy-start.3 = (f32[16,128]{1,0:T(8,128)S(1)}, f32[16,128]{1,0:T(8,128)}, u32[]{:S(2)}) copy-start(f32[16,128]{1,0:T(8,128)} %proto_ref.1) | copy-start | bytes 24580
  23.9 0.7 %copy-start.4 = (s32[192]{0:T(256)S(1)}, s32[192]{0:T(256)}, u32[]{:S(2)}) copy-start(s32[192]{0:T(256)} %param.11) | copy-start | bytes 2308

commit v18 on v15

--- a/solution.py
+++ b/solution.py
@@ -10,6 +10,7 @@
 
 INTEG = 4
 EARLY = 2
+LAST = 2
 HIGHEST = lax.Precision.HIGHEST
 F32 = jnp.float32
 BF16 = jnp.bfloat16
@@ -103,7 +104,8 @@
     x_ref, proto_ref, table_ref, taps_ref, late_ref, out_ref, late_out_ref, *scratch
 ):
     past, poly, spec, filt, late_sem = scratch
-    late_copy = pltpu.make_async_copy(late_ref, late_out_ref, late_sem)
+    count = late_out_ref.shape[0]
+    late_copy = pltpu.make_async_copy(late_ref.at[0:count], late_out_ref, late_sem)
     late_copy.start()
     pfb_count = proto_ref.shape[0]
     fir_count = taps_ref.shape[0]
@@ -169,7 +171,10 @@
     late_copy.wait()
 
 
-def beams_kernel(x_ref, early_ref, late_ref, out_ref):
+def beams_kernel(x_ref, early_ref, middle_ref, late_hbm, out_hbm, last_ref, out_ref, sems):
+    chans = out_ref.shape[0]
+    last_load = pltpu.make_async_copy(late_hbm.at[middle_ref.shape[0] :], last_ref, sems.at[0])
+    last_load.start()
     rows = x_ref.shape[0] // 8
     beams = early_ref.shape[1] // 2
     lane = lax.broadcasted_iota(jnp.int32, (rows, LANES), 1)
@@ -192,8 +197,12 @@
     for step in steps:
         if 2 * step < EARLY:
             w_ref, begin = early_ref, 2 * step
+        elif 2 * step < chans - LAST:
+            w_ref, begin = middle_ref, 2 * step - EARLY
         else:
-            w_ref, begin = late_ref, 2 * step - EARLY
+            w_ref, begin = last_ref, 2 * step - (chans - LAST)
+            if begin == 0:
+                last_load.wait()
         sums = []
         for index in range(2):
             weights = w_ref[begin + index]
@@ -203,6 +212,7 @@
         by_imag = jnp.where(even_wide, sums[0][beams:], sums[1][beams:])
         crossed = pltpu.roll(by_imag, 64, 1)
         beam_of.append(by_real + jnp.where(wide < 64, -crossed, crossed))
+    stores = []
     for step in steps:
         power = lax.dot_general(
             pool,
@@ -212,6 +222,13 @@
         )
         out_ref[2 * step] = power[0:8]
         out_ref[2 * step + 1] = power[8:16]
+        pair = slice(2 * step, 2 * step + 2)
+        stores.append(
+            pltpu.make_async_copy(out_ref.at[pair], out_hbm.at[pair], sems.at[1 + step])
+        )
+        stores[-1].start()
+    for store in stores:
+        store.wait()
 
 
 def slots_of(devices):
@@ -291,11 +308,11 @@
     arrived, early, late, table = lax.optimization_barrier((arrived, early, late, table))
 
     block = (6 * band_chans, channels)
-    filtered, late = pl.pallas_call(
+    filtered, middle = pl.pallas_call(
         channel_kernel,
         out_shape=[
             jax.ShapeDtypeStruct((devices,) + block, F32),
-            jax.ShapeDtypeStruct(late.shape, BF16),
+            jax.ShapeDtypeStruct((late.shape[0] - LAST,) + late.shape[1:], BF16),
         ],
         in_specs=[VMEM] * 4 + [HBM],
         out_specs=[VMEM] * 2,
@@ -317,14 +334,25 @@
     )
     field = exchange(filtered).reshape(devices * 6 * band_chans, channels)
 
+    power_shape = (band_chans, frames // INTEG, beams)
     power = pl.pallas_call(
         beams_kernel,
-        out_shape=jax.ShapeDtypeStruct((band_chans, frames // INTEG, beams), F32),
-        in_specs=[VMEM] * 3,
-        out_specs=VMEM,
+        out_shape=pltpu.HBM(power_shape, F32),
+        in_specs=[VMEM] * 3 + [HBM],
+        out_specs=HBM,
+        scratch_shapes=[
+            pltpu.VMEM((LAST,) + late.shape[1:], BF16),
+            pltpu.VMEM(power_shape, F32),
+            pltpu.SemaphoreType.DMA((1 + band_chans // 2,)),
+        ],
         name="beams",
         compiler_params=GRANT,
-    )(held(field, pltpu.VMEM), held(early, pltpu.VMEM), held(late, pltpu.VMEM))
+    )(
+        held(field, pltpu.VMEM),
+        held(early, pltpu.VMEM),
+        held(middle, pltpu.VMEM),
+        held(late, pltpu.HBM),
+    )
     return jnp.transpose(power, (0, 2, 1))[None]
 
 

time: 40.8 us -> 41.7 us (1.022)
  local copies, waits for them, and re-layouts: 2.73 us -> 1.17 us
  waiting for transfers between devices: 5.15 us -> 6.7 us
  Pallas kernels: 9.52 us -> 10.4 us
    unnamed x10, local copies, waits for them, and re-layouts: 2.69 us -> 1.13 us
    all_to_all x1, waiting for transfers between devices: 5.15 us -> 6.7 us  [exchange(): lax.all_to_all(value, 'band', split_axis=0, concat_axis=0, tiled=True)]
    pallas_call x1, Pallas kernels: 1.88 us -> 2.99 us  [close_body(): pl.pallas_call(beams_kernel, out_shape=pltpu.HBM(power_shape, F32), in_sp...]
where the time goes in v18:
time: 41.7 us; the launch traced here: 41.3 us
  blocking collectives  15.5 us (37%)
  Pallas kernels  10.4 us (25%)
  starting transfers between devices  7.39 us (18%)
  waiting for transfers between devices  6.7 us (16%)
  local copies, waits for them, and re-layouts  1.17 us (3%)
    all_to_all x1, blocking collectives, exchange(): lax.all_to_all(value, 'band', split_axis=0, concat_axis=0, tiled=True)  15.5 us
    all_to_all x1, starting transfers between devices, exchange(): lax.all_to_all(value, 'band', split_axis=0, concat_axis=0, tiled=True)  7.39 us
    all_to_all x1, waiting for transfers between devices, exchange(): lax.all_to_all(value, 'band', split_axis=0, concat_axis=0, tiled=True)  6.7 us
    pallas_call x1, Pallas kernels, close_body(): pl.pallas_call(weights_kernel, out_shape=[jax.ShapeDtypeStruct((EARLY, 2...  5.36 us
    pallas_call x1, Pallas kernels, close_body(): pl.pallas_call(beams_kernel, out_shape=pltpu.HBM(power_shape, F32), in_sp...  2.99 us
    pallas_call x1, Pallas kernels, close_body(): pl.pallas_call(channel_kernel, out_shape=[jax.ShapeDtypeStruct((devices,)...  1.29 us
    unnamed x10, local copies, waits for them, and re-layouts  1.13 us
  transfers between devices with their start and end apart: 1, of which 1 were waited for; matrix products, arithmetic and copies ran while one was open for 0% of the time, Pallas kernels for 13%

profile of v18, /device:TPU:0, one launch (start us, length us, event | category | flops | bytes accessed | tf_op | source)
XLA Modules:
  0.0 41.3 jit_solution(2561182251572247509)
XLA Ops:
  0.0 0.0 copy-start
  0.0 0.0 copy-start.1
  0.0 1.1 %copy-done.1 = f32[2,192,256]{2,1,0:T(8,128)S(1)} copy-done((f32[2,192,256]{2,1,0:T(8,128)S(1)}, f32[2,192,256]{2,1,0:T(8,128)}, u32[]{:S(2)}) %copy-start.1) | copy-done | bytes 393240
  1.1 0.0 copy-start.2
  1.1 0.0 copy-start.4
  1.1 0.8 %pieces.1 = f32[16,2,24,128]{3,2,1,0:T(8,128)} custom-call(f32[2,192,256]{2,1,0:T(8,128)S(1)} %copy-done.1), custom_call_target="tpu_custom_call" | custom-call | tf_op jit(solution)/shard_map/pieces/pallas_call | solution.py:267
  1.9 7.4 %all-to-all-start = ((f32[16,2,24,128]{3,2,1,0:T(8,128)}), f32[16,2,24,128]{3,2,1,0:T(8,128)S(1)}, u32[]{:S(2)}, u32[]{:S(2)}) async-start(f32[16,2,24,128]{3,2,1,0:T(8,128)} %pieces.1), calls=%async_computation | async-start | bytes 786432 | tf_op jit(solution)/shard_map/all_to_all | solution.py:265
  9.3 0.0 copy-done.2
  9.3 0.0 copy-done.4
  9.3 0.0 copy-start.3
  9.4 5.4 %weights.1 = (bf16[2,384,384]{2,1,0:T(8,128)(2,1)S(1)}, bf16[6,384,384]{2,1,0:T(8,128)(2,1)}, bf16[768,256]{1,0:T(8,128)(2,1)S(1)}) custom-call(f32[8,2,192,192]{3,2,1,0:T(8,128)} %bitcast.12, s32[1,192]{1,0:T(1,128)S(1)} %bitcast.11, s32[192,1]{1,0:T(8,128)S(1)} %copy-done.2, bf16[768,256]{1,0:T(8,128)(2,1)} %constant.20.clone.table_ref), custom_call_target="tpu_custom_call" | custom-call | flops 905969664 | bytes 5242880 | tf_op jit(solution)/shard_map/weights/pallas_call | solution.py:282
  14.7 0.0 copy-done
  14.8 6.7 %all-to-all-done = f32[16,2,24,128]{3,2,1,0:T(8,128)S(1)} async-done(((f32[16,2,24,128]{3,2,1,0:T(8,128)}), f32[16,2,24,128]{3,2,1,0:T(8,128)S(1)}, u32[]{:S(2)}, u32[]{:S(2)}) %all-to-all-start) | async-done | bytes 393248 | tf_op jit(solution)/shard_map/all_to_all | solution.py:265
  21.5 0.0 copy-done.3
  21.5 1.3 %channels.1 = (f32[16,48,128]{2,1,0:T(8,128)S(1)}, bf16[4,384,384]{2,1,0:T(8,128)(2,1)S(1)}) custom-call(f32[32,24,128]{2,1,0:T(8,128)S(1)} %bitcast.9, f32[16,128]{1,0:T(8,128)S(1)} %copy-done.3, bf16[768,256]{1,0:T(8,128)(2,1)S(1)} %get-tuple-element.18.table_ref, f32[8,2,24,128]{3,2,1,0:T(8,128)S(1)} %copy_bitcast_fusion.taps_ref, ...), custom_call_target="tpu_custom_call" | custom-call | tf_op jit(solution)/shard_map/channels/pallas_call | solution.py:311
  22.8 15.5 %all_to_all.10 = f32[16,48,128]{2,1,0:T(8,128)S(1)} all-to-all(f32[16,48,128]{2,1,0:T(8,128)S(1)} %get-tuple-element.20), channel_id=1, replica_groups=mesh['grp'=2,'band'=16] {'band'}, dimensions={0} | all-to-all | bytes 786432 | tf_op jit(solution)/shard_map/all_to_all | solution.py:265
  38.3 3.0 %beams.1 = f32[8,8,192]{2,1,0:T(8,128)} custom-call(f32[768,128]{1,0:T(8,128)S(1)} %bitcast.10, bf16[2,384,384]{2,1,0:T(8,128)(2,1)S(1)} %get-tuple-element.21.early_ref, bf16[4,384,384]{2,1,0:T(8,128)(2,1)S(1)} %get-tuple-element.22.middle_ref, bf16[6,384,384]{2,1,0:T(8,128)(2,1)} %get-tuple-element.19.late_ref.late_hbm), custom_call_target="tpu_custom_call" | custom-call | tf_op jit(solution)/shard_map/beams/pallas_call | solution.py:338
  (3 shorter events, 0.1 us)
Async XLA Ops:
  0.0 14.7 %copy-start = (f32[2,8,192,128]{3,2,1,0:T(8,128)S(1)}, f32[2,8,192,128]{3,2,1,0:T(8,128)}, u32[]{:S(2)}) copy-start(f32[2,8,192,128]{3,2,1,0:T(8,128)} %param.9) | copy-start | bytes 4718596
  0.0 1.1 %copy-start.1 = (f32[2,192,256]{2,1,0:T(8,128)S(1)}, f32[2,192,256]{2,1,0:T(8,128)}, u32[]{:S(2)}) copy-start(f32[2,192,256]{2,1,0:T(8,128)} %x_ref.1) | copy-start | bytes 1179652
  1.1 8.2 %copy-start.2 = (s32[192,1]{1,0:T(8,128)S(1)}, s32[192,1]{1,0:T(8,128)}, u32[]{:S(2)}) copy-start(s32[192,1]{1,0:T(8,128)} %constant.21.clone.slot_ref) | copy-start | bytes 2308
  1.1 8.2 %copy-start.4 = (s32[192]{0:T(256)S(1)}, s32[192]{0:T(256)}, u32[]{:S(2)}) copy-start(s32[192]{0:T(256)} %param.11) | copy-start | bytes 2308
  1.9 19.6 %all-to-all-start = ((f32[16,2,24,128]{3,2,1,0:T(8,128)}), f32[16,2,24,128]{3,2,1,0:T(8,128)S(1)}, u32[]{:S(2)}, u32[]{:S(2)}) async-start(f32[16,2,24,128]{3,2,1,0:T(8,128)} %pieces.1), calls=%async_computation | async-start | bytes 786432 | tf_op jit(solution)/shard_map/all_to_all | solution.py:265
  9.3 12.2 %copy-start.3 = (f32[16,128]{1,0:T(8,128)S(1)}, f32[16,128]{1,0:T(8,128)}, u32[]{:S(2)}) copy-start(f32[16,128]{1,0:T(8,128)} %proto_ref.1) | copy-start | bytes 24580

commit v19 on v15

--- a/solution.py
+++ b/solution.py
@@ -194,13 +194,11 @@
             w_ref, begin = early_ref, 2 * step
         else:
             w_ref, begin = late_ref, 2 * step - EARLY
-        sums = []
-        for index in range(2):
-            weights = w_ref[begin + index]
-            product = jnp.dot(weights, fields[step], preferred_element_type=F32)
-            sums.append(product[:, 0:LANES] + product[:, LANES : 2 * LANES])
-        by_real = jnp.where(even_wide, sums[0][:beams], sums[1][:beams])
-        by_imag = jnp.where(even_wide, sums[0][beams:], sums[1][beams:])
+        pair = w_ref[begin : begin + 2].reshape(4 * beams, w_ref.shape[2])
+        product = jnp.dot(pair, fields[step], preferred_element_type=F32)
+        sums = product[:, 0:LANES] + product[:, LANES : 2 * LANES]
+        by_real = jnp.where(even_wide, sums[:beams], sums[2 * beams : 3 * beams])
+        by_imag = jnp.where(even_wide, sums[beams : 2 * beams], sums[3 * beams :])
         crossed = pltpu.roll(by_imag, 64, 1)
         beam_of.append(by_real + jnp.where(wide < 64, -crossed, crossed))
     for step in steps:

time: 40.8 us -> 40.8 us (level)
  no operation moved by 1% of the time
where the time goes in v19:
time: 40.8 us; the launch traced here: 40.4 us
  blocking collectives  15.5 us (38%)
  Pallas kernels  9.55 us (23%)
  starting transfers between devices  7.39 us (18%)
  waiting for transfers between devices  5.15 us (13%)
  local copies, waits for them, and re-layouts  2.73 us (7%)
    all_to_all x1, blocking collectives, exchange(): lax.all_to_all(value, 'band', split_axis=0, concat_axis=0, tiled=True)  15.5 us
    all_to_all x1, starting transfers between devices, exchange(): lax.all_to_all(value, 'band', split_axis=0, concat_axis=0, tiled=True)  7.39 us
    pallas_call x1, Pallas kernels, close_body(): pl.pallas_call(weights_kernel, out_shape=[jax.ShapeDtypeStruct((EARLY, 2...  5.36 us
    all_to_all x1, waiting for transfers between devices, exchange(): lax.all_to_all(value, 'band', split_axis=0, concat_axis=0, tiled=True)  5.15 us
    unnamed x10, local copies, waits for them, and re-layouts  2.69 us
    pallas_call x1, Pallas kernels, close_body(): pl.pallas_call(beams_kernel, out_shape=jax.ShapeDtypeStruct((band_chans,...  1.91 us
    pallas_call x1, Pallas kernels, close_body(): pl.pallas_call(channel_kernel, out_shape=[jax.ShapeDtypeStruct((devices,)...  1.49 us
  transfers between devices with their start and end apart: 1, of which 1 were waited for; matrix products, arithmetic and copies ran while one was open for 0% of the time, Pallas kernels for 13%

profile of v19, /device:TPU:0, one launch (start us, length us, event | category | flops | bytes accessed | tf_op | source)
XLA Modules:
  0.0 40.4 jit_solution(4280883022529350643)
XLA Ops:
  0.0 0.0 copy-start
  0.0 0.0 copy-start.1
  0.0 1.1 %copy-done.1 = f32[2,192,256]{2,1,0:T(8,128)S(1)} copy-done((f32[2,192,256]{2,1,0:T(8,128)S(1)}, f32[2,192,256]{2,1,0:T(8,128)}, u32[]{:S(2)}) %copy-start.1) | copy-done | bytes 393240
  1.1 0.8 %pieces.1 = f32[16,2,24,128]{3,2,1,0:T(8,128)} custom-call(f32[2,192,256]{2,1,0:T(8,128)S(1)} %copy-done.1), custom_call_target="tpu_custom_call" | custom-call | tf_op jit(solution)/shard_map/pieces/pallas_call | solution.py:248
  1.9 7.4 %all-to-all-start = ((f32[16,2,24,128]{3,2,1,0:T(8,128)}), f32[16,2,24,128]{3,2,1,0:T(8,128)S(1)}, u32[]{:S(2)}, u32[]{:S(2)}) async-start(f32[16,2,24,128]{3,2,1,0:T(8,128)} %pieces.1), calls=%async_computation | async-start | bytes 786432 | tf_op jit(solution)/shard_map/all_to_all | solution.py:246
  9.3 0.0 copy-start.2
  9.3 0.9 %copy-done.2 = s32[192,1]{1,0:T(8,128)S(1)} copy-done((s32[192,1]{1,0:T(8,128)S(1)}, s32[192,1]{1,0:T(8,128)}, u32[]{:S(2)}) %copy-start.2) | copy-done | bytes 792
  10.2 0.0 copy-start.4
  10.2 0.7 %copy-done.4 = s32[192]{0:T(256)S(1)} copy-done((s32[192]{0:T(256)S(1)}, s32[192]{0:T(256)}, u32[]{:S(2)}) %copy-start.4) | copy-done | bytes 792
  10.9 0.0 copy-start.3
  10.9 5.4 %weights.1 = (bf16[2,384,384]{2,1,0:T(8,128)(2,1)S(1)}, bf16[6,384,384]{2,1,0:T(8,128)(2,1)}, bf16[768,256]{1,0:T(8,128)(2,1)S(1)}) custom-call(f32[8,2,192,192]{3,2,1,0:T(8,128)} %bitcast.12, s32[1,192]{1,0:T(1,128)S(1)} %bitcast.11, s32[192,1]{1,0:T(8,128)S(1)} %copy-done.2, bf16[768,256]{1,0:T(8,128)(2,1)} %constant.20.clone.table_ref), custom_call_target="tpu_custom_call" | custom-call | flops 905969664 | bytes 5242880 | tf_op jit(solution)/shard_map/weights/pallas_call | solution.py:263
  16.3 0.0 copy-done
  16.4 5.2 %all-to-all-done = f32[16,2,24,128]{3,2,1,0:T(8,128)S(1)} async-done(((f32[16,2,24,128]{3,2,1,0:T(8,128)}), f32[16,2,24,128]{3,2,1,0:T(8,128)S(1)}, u32[]{:S(2)}, u32[]{:S(2)}) %all-to-all-start) | async-done | bytes 393248 | tf_op jit(solution)/shard_map/all_to_all | solution.py:246
  21.5 0.0 copy-done.3
  21.5 1.5 %channels.1 = (f32[16,48,128]{2,1,0:T(8,128)S(1)}, bf16[6,384,384]{2,1,0:T(8,128)(2,1)S(1)}) custom-call(f32[32,24,128]{2,1,0:T(8,128)S(1)} %bitcast.9, f32[16,128]{1,0:T(8,128)S(1)} %copy-done.3, bf16[768,256]{1,0:T(8,128)(2,1)S(1)} %get-tuple-element.18.table_ref, f32[8,2,24,128]{3,2,1,0:T(8,128)S(1)} %copy_bitcast_fusion.taps_ref, ...), custom_call_target="tpu_custom_call" | custom-call | tf_op jit(solution)/shard_map/channels/pallas_call | solution.py:292
  23.0 15.5 %all_to_all.10 = f32[16,48,128]{2,1,0:T(8,128)S(1)} all-to-all(f32[16,48,128]{2,1,0:T(8,128)S(1)} %get-tuple-element.20), channel_id=1, replica_groups=mesh['grp'=2,'band'=16] {'band'}, dimensions={0} | all-to-all | bytes 786432 | tf_op jit(solution)/shard_map/all_to_all | solution.py:246
  38.5 1.9 %beams.1 = f32[8,8,192]{2,1,0:T(8,128)} custom-call(f32[768,128]{1,0:T(8,128)S(1)} %bitcast.10, bf16[2,384,384]{2,1,0:T(8,128)(2,1)S(1)} %get-tuple-element.21.early_ref, bf16[6,384,384]{2,1,0:T(8,128)(2,1)S(1)} %get-tuple-element.22.late_ref), custom_call_target="tpu_custom_call" | custom-call | tf_op jit(solution)/shard_map/beams/pallas_call | solution.py:318
  (3 shorter events, 0.1 us)
Async XLA Ops:
  0.0 16.3 %copy-start = (f32[2,8,192,128]{3,2,1,0:T(8,128)S(1)}, f32[2,8,192,128]{3,2,1,0:T(8,128)}, u32[]{:S(2)}) copy-start(f32[2,8,192,128]{3,2,1,0:T(8,128)} %param.9) | copy-start | bytes 4718596
  0.0 1.1 %copy-start.1 = (f32[2,192,256]{2,1,0:T(8,128)S(1)}, f32[2,192,256]{2,1,0:T(8,128)}, u32[]{:S(2)}) copy-start(f32[2,192,256]{2,1,0:T(8,128)} %x_ref.1) | copy-start | bytes 1179652
  1.9 19.6 %all-to-all-start = ((f32[16,2,24,128]{3,2,1,0:T(8,128)}), f32[16,2,24,128]{3,2,1,0:T(8,128)S(1)}, u32[]{:S(2)}, u32[]{:S(2)}) async-start(f32[16,2,24,128]{3,2,1,0:T(8,128)} %pieces.1), calls=%async_computation | async-start | bytes 786432 | tf_op jit(solution)/shard_map/all_to_all | solution.py:246
  9.3 0.9 %copy-start.2 = (s32[192,1]{1,0:T(8,128)S(1)}, s32[192,1]{1,0:T(8,128)}, u32[]{:S(2)}) copy-start(s32[192,1]{1,0:T(8,128)} %constant.21.clone.slot_ref) | copy-start | bytes 2308
  10.2 0.7 %copy-start.4 = (s32[192]{0:T(256)S(1)}, s32[192]{0:T(256)}, u32[]{:S(2)}) copy-start(s32[192]{0:T(256)} %param.11) | copy-start | bytes 2308
  10.9 10.6 %copy-start.3 = (f32[16,128]{1,0:T(8,128)S(1)}, f32[16,128]{1,0:T(8,128)}, u32[]{:S(2)}) copy-start(f32[16,128]{1,0:T(8,128)} %proto_ref.1) | copy-start | bytes 24580

commit v20 on v15

--- a/solution.py
+++ b/solution.py
@@ -102,9 +102,13 @@
 def channel_kernel(
     x_ref, proto_ref, table_ref, taps_ref, late_ref, out_ref, late_out_ref, *scratch
 ):
-    past, poly, spec, filt, late_sem = scratch
-    late_copy = pltpu.make_async_copy(late_ref, late_out_ref, late_sem)
-    late_copy.start()
+    past, poly, spec, filt, late_sems = scratch
+    late_copies = [
+        pltpu.make_async_copy(late_ref.at[chan], late_out_ref.at[chan], late_sems.at[chan])
+        for chan in range(late_ref.shape[0])
+    ]
+    for copy in late_copies:
+        copy.start()
     pfb_count = proto_ref.shape[0]
     fir_count = taps_ref.shape[0]
     frames = poly.shape[0]
@@ -166,7 +170,8 @@
             out_ref[dev, pair * per_band : (pair + 1) * per_band, :] = turned[
                 dev * per_band : (dev + 1) * per_band
             ]
-    late_copy.wait()
+    for copy in late_copies:
+        copy.wait()
 
 
 def beams_kernel(x_ref, early_ref, late_ref, out_ref):
@@ -304,7 +309,7 @@
             pltpu.VMEM((frames, 24, 2 * LANES), F32),
             pltpu.VMEM((frames + fir_count - 1, 24, 2 * LANES), F32),
             pltpu.VMEM((frames * 24, LANES), F32),
-            pltpu.SemaphoreType.DMA(()),
+            pltpu.SemaphoreType.DMA((late.shape[0],)),
         ],
         name="channels",
         compiler_params=GRANT,

time: 40.8 us -> 41.2 us (level)
  Pallas kernels: 9.52 us -> 9.98 us
    pallas_call x1, Pallas kernels: 1.49 us -> 1.95 us  [close_body(): pl.pallas_call(channel_kernel, out_shape=[jax.ShapeDtypeStruct((devices,)...]
where the time goes in v20:
time: 41.2 us; the launch traced here: 40.9 us
  blocking collectives  15.5 us (38%)
  Pallas kernels  9.98 us (24%)
  starting transfers between devices  7.39 us (18%)
  waiting for transfers between devices  5.15 us (12%)
  local copies, waits for them, and re-layouts  2.73 us (7%)
    all_to_all x1, blocking collectives, exchange(): lax.all_to_all(value, 'band', split_axis=0, concat_axis=0, tiled=True)  15.5 us
    all_to_all x1, starting transfers between devices, exchange(): lax.all_to_all(value, 'band', split_axis=0, concat_axis=0, tiled=True)  7.39 us
    pallas_call x1, Pallas kernels, close_body(): pl.pallas_call(weights_kernel, out_shape=[jax.ShapeDtypeStruct((EARLY, 2...  5.36 us
    all_to_all x1, waiting for transfers between devices, exchange(): lax.all_to_all(value, 'band', split_axis=0, concat_axis=0, tiled=True)  5.15 us
    unnamed x10, local copies, waits for them, and re-layouts  2.69 us
    pallas_call x1, Pallas kernels, close_body(): pl.pallas_call(channel_kernel, out_shape=[jax.ShapeDtypeStruct((devices,)...  1.95 us
    pallas_call x1, Pallas kernels, close_body(): pl.pallas_call(beams_kernel, out_shape=jax.ShapeDtypeStruct((band_chans,...  1.87 us
  transfers between devices with their start and end apart: 1, of which 1 were waited for; matrix products, arithmetic and copies ran while one was open for 0% of the time, Pallas kernels for 13%

profile of v20, /device:TPU:0, one launch (start us, length us, event | category | flops | bytes accessed | tf_op | source)
XLA Modules:
  0.0 40.9 jit_solution(2385520613652354503)
XLA Ops:
  0.0 0.0 copy-start
  0.0 0.0 copy-start.1
  0.0 1.1 %copy-done.1 = f32[2,192,256]{2,1,0:T(8,128)S(1)} copy-done((f32[2,192,256]{2,1,0:T(8,128)S(1)}, f32[2,192,256]{2,1,0:T(8,128)}, u32[]{:S(2)}) %copy-start.1) | copy-done | bytes 393240
  1.1 0.8 %pieces.1 = f32[16,2,24,128]{3,2,1,0:T(8,128)} custom-call(f32[2,192,256]{2,1,0:T(8,128)S(1)} %copy-done.1), custom_call_target="tpu_custom_call" | custom-call | tf_op jit(solution)/shard_map/pieces/pallas_call | solution.py:255
  1.9 7.4 %all-to-all-start = ((f32[16,2,24,128]{3,2,1,0:T(8,128)}), f32[16,2,24,128]{3,2,1,0:T(8,128)S(1)}, u32[]{:S(2)}, u32[]{:S(2)}) async-start(f32[16,2,24,128]{3,2,1,0:T(8,128)} %pieces.1), calls=%async_computation | async-start | bytes 786432 | tf_op jit(solution)/shard_map/all_to_all | solution.py:253
  9.3 0.0 copy-start.2
  9.3 0.9 %copy-done.2 = s32[192,1]{1,0:T(8,128)S(1)} copy-done((s32[192,1]{1,0:T(8,128)S(1)}, s32[192,1]{1,0:T(8,128)}, u32[]{:S(2)}) %copy-start.2) | copy-done | bytes 792
  10.2 0.0 copy-start.4
  10.2 0.7 %copy-done.4 = s32[192]{0:T(256)S(1)} copy-done((s32[192]{0:T(256)S(1)}, s32[192]{0:T(256)}, u32[]{:S(2)}) %copy-start.4) | copy-done | bytes 792
  10.9 0.0 copy-start.3
  10.9 5.4 %weights.1 = (bf16[2,384,384]{2,1,0:T(8,128)(2,1)S(1)}, bf16[6,384,384]{2,1,0:T(8,128)(2,1)}, bf16[768,256]{1,0:T(8,128)(2,1)S(1)}) custom-call(f32[8,2,192,192]{3,2,1,0:T(8,128)} %bitcast.12, s32[1,192]{1,0:T(1,128)S(1)} %bitcast.11, s32[192,1]{1,0:T(8,128)S(1)} %copy-done.2, bf16[768,256]{1,0:T(8,128)(2,1)} %constant.20.clone.table_ref), custom_call_target="tpu_custom_call" | custom-call | flops 905969664 | bytes 5242880 | tf_op jit(solution)/shard_map/weights/pallas_call | solution.py:270
  16.3 0.0 copy-done
  16.4 5.2 %all-to-all-done = f32[16,2,24,128]{3,2,1,0:T(8,128)S(1)} async-done(((f32[16,2,24,128]{3,2,1,0:T(8,128)}), f32[16,2,24,128]{3,2,1,0:T(8,128)S(1)}, u32[]{:S(2)}, u32[]{:S(2)}) %all-to-all-start) | async-done | bytes 393248 | tf_op jit(solution)/shard_map/all_to_all | solution.py:253
  21.5 0.0 copy-done.3
  21.5 1.9 %channels.1 = (f32[16,48,128]{2,1,0:T(8,128)S(1)}, bf16[6,384,384]{2,1,0:T(8,128)(2,1)S(1)}) custom-call(f32[32,24,128]{2,1,0:T(8,128)S(1)} %bitcast.9, f32[16,128]{1,0:T(8,128)S(1)} %copy-done.3, bf16[768,256]{1,0:T(8,128)(2,1)S(1)} %get-tuple-element.18.table_ref, f32[8,2,24,128]{3,2,1,0:T(8,128)S(1)} %copy_bitcast_fusion.taps_ref, ...), custom_call_target="tpu_custom_call" | custom-call | tf_op jit(solution)/shard_map/channels/pallas_call | solution.py:299
  23.5 15.5 %all_to_all.10 = f32[16,48,128]{2,1,0:T(8,128)S(1)} all-to-all(f32[16,48,128]{2,1,0:T(8,128)S(1)} %get-tuple-element.20), channel_id=1, replica_groups=mesh['grp'=2,'band'=16] {'band'}, dimensions={0} | all-to-all | bytes 786432 | tf_op jit(solution)/shard_map/all_to_all | solution.py:253
  39.0 1.9 %beams.1 = f32[8,8,192]{2,1,0:T(8,128)} custom-call(f32[768,128]{1,0:T(8,128)S(1)} %bitcast.10, bf16[2,384,384]{2,1,0:T(8,128)(2,1)S(1)} %get-tuple-element.21.early_ref, bf16[6,384,384]{2,1,0:T(8,128)(2,1)S(1)} %get-tuple-element.22.late_ref), custom_call_target="tpu_custom_call" | custom-call | tf_op jit(solution)/shard_map/beams/pallas_call | solution.py:325
  (3 shorter events, 0.1 us)
Async XLA Ops:
  0.0 16.3 %copy-start = (f32[2,8,192,128]{3,2,1,0:T(8,128)S(1)}, f32[2,8,192,128]{3,2,1,0:T(8,128)}, u32[]{:S(2)}) copy-start(f32[2,8,192,128]{3,2,1,0:T(8,128)} %param.9) | copy-start | bytes 4718596
  0.0 1.1 %copy-start.1 = (f32[2,192,256]{2,1,0:T(8,128)S(1)}, f32[2,192,256]{2,1,0:T(8,128)}, u32[]{:S(2)}) copy-start(f32[2,192,256]{2,1,0:T(8,128)} %x_ref.1) | copy-start | bytes 1179652
  1.9 19.6 %all-to-all-start = ((f32[16,2,24,128]{3,2,1,0:T(8,128)}), f32[16,2,24,128]{3,2,1,0:T(8,128)S(1)}, u32[]{:S(2)}, u32[]{:S(2)}) async-start(f32[16,2,24,128]{3,2,1,0:T(8,128)} %pieces.1), calls=%async_computation | async-start | bytes 786432 | tf_op jit(solution)/shard_map/all_to_all | solution.py:253
  9.3 0.9 %copy-start.2 = (s32[192,1]{1,0:T(8,128)S(1)}, s32[192,1]{1,0:T(8,128)}, u32[]{:S(2)}) copy-start(s32[192,1]{1,0:T(8,128)} %constant.21.clone.slot_ref) | copy-start | bytes 2308
  10.2 0.7 %copy-start.4 = (s32[192]{0:T(256)S(1)}, s32[192]{0:T(256)}, u32[]{:S(2)}) copy-start(s32[192]{0:T(256)} %param.11) | copy-start | bytes 2308
  10.9 10.6 %copy-start.3 = (f32[16,128]{1,0:T(8,128)S(1)}, f32[16,128]{1,0:T(8,128)}, u32[]{:S(2)}) copy-start(f32[16,128]{1,0:T(8,128)} %proto_ref.1) | copy-start | bytes 24580

commit v21 on v15

--- a/solution.py
+++ b/solution.py
@@ -39,7 +39,10 @@
     return part * 8 + dish if dish < 8 else 16 + part * 4 + dish - 8
 
 
-def pieces_kernel(x_ref, out_ref):
+def pieces_kernel(x_hbm, out_hbm, x_ref, out_ref, sems):
+    load = pltpu.make_async_copy(x_hbm, x_ref, sems.at[0])
+    load.start()
+    load.wait()
     devices, frames_dev = out_ref.shape[:2]
     low = lax.broadcasted_iota(jnp.int32, (8, LANES), 0) < 4
     for frame in range(frames_dev):
@@ -55,6 +58,9 @@
             imag = x_ref[1, start : start + 8, lanes]
             out_ref[dev, frame, 16:24, :] = jnp.where(low, real, pltpu.roll(imag, 4, 0))
             out_ref[dev + 1, frame, 16:24, :] = jnp.where(low, pltpu.roll(real, 4, 0), imag)
+    store = pltpu.make_async_copy(out_ref, out_hbm, sems.at[1])
+    store.start()
+    store.wait()
 
 
 def weights_kernel(
@@ -247,14 +253,20 @@
     def exchange(value):
         return lax.all_to_all(value, "band", split_axis=0, concat_axis=0, tiled=True)
 
+    pieces_shape = (devices, frames_dev, 24, channels)
     pieces = pl.pallas_call(
         pieces_kernel,
-        out_shape=jax.ShapeDtypeStruct((devices, frames_dev, 24, channels), F32),
-        in_specs=[VMEM],
-        out_specs=VMEM,
+        out_shape=pltpu.HBM(pieces_shape, F32),
+        in_specs=[HBM],
+        out_specs=HBM,
+        scratch_shapes=[
+            pltpu.VMEM(samples.shape, F32),
+            pltpu.VMEM(pieces_shape, F32),
+            pltpu.SemaphoreType.DMA((2,)),
+        ],
         name="pieces",
         compiler_params=GRANT,
-    )(samples)
+    )(held(samples, pltpu.HBM))
     arrived = exchange(pieces).reshape(frames, 24, channels)
 
     eight = lax.dynamic_slice_in_dim(dish_filter, position * 8, 8, 2)

time: 40.8 us -> 40.8 us (level)
  local copies, waits for them, and re-layouts: 2.73 us -> 1.61 us
  Pallas kernels: 9.52 us -> 10.6 us
    pallas_call x1, Pallas kernels: 0.8 us -> 1.91 us  [close_body(): pl.pallas_call(pieces_kernel, out_shape=pltpu.HBM(pieces_shape, F32), in_...]
    unnamed x10 -> x8, local copies, waits for them, and re-layouts: 2.69 us -> 1.57 us
where the time goes in v21:
time: 40.8 us; the launch traced here: 40.4 us
  blocking collectives  15.5 us (38%)
  Pallas kernels  10.6 us (26%)
  starting transfers between devices  7.4 us (18%)
  waiting for transfers between devices  5.14 us (13%)
  local copies, waits for them, and re-layouts  1.61 us (4%)
    all_to_all x1, blocking collectives, exchange(): lax.all_to_all(value, 'band', split_axis=0, concat_axis=0, tiled=True)  15.5 us
    all_to_all x1, starting transfers between devices, exchange(): lax.all_to_all(value, 'band', split_axis=0, concat_axis=0, tiled=True)  7.4 us
    pallas_call x1, Pallas kernels, close_body(): pl.pallas_call(weights_kernel, out_shape=[jax.ShapeDtypeStruct((EARLY, 2...  5.37 us
    all_to_all x1, waiting for transfers between devices, exchange(): lax.all_to_all(value, 'band', split_axis=0, concat_axis=0, tiled=True)  5.14 us
    pallas_call x1, Pallas kernels, close_body(): pl.pallas_call(pieces_kernel, out_shape=pltpu.HBM(pieces_shape, F32), in_...  1.91 us
    pallas_call x1, Pallas kernels, close_body(): pl.pallas_call(beams_kernel, out_shape=jax.ShapeDtypeStruct((band_chans,...  1.87 us
    unnamed x8, local copies, waits for them, and re-layouts  1.57 us
    pallas_call x1, Pallas kernels, close_body(): pl.pallas_call(channel_kernel, out_shape=[jax.ShapeDtypeStruct((devices,)...  1.49 us
  transfers between devices with their start and end apart: 1, of which 1 were waited for; matrix products, arithmetic and copies ran while one was open for 0% of the time, Pallas kernels for 13%

profile of v21, /device:TPU:0, one launch (start us, length us, event | category | flops | bytes accessed | tf_op | source)
XLA Modules:
  0.0 40.4 jit_solution(1936858415290535923)
XLA Ops:
  0.0 0.0 copy-start
  0.0 1.9 %pieces.1 = f32[16,2,24,128]{3,2,1,0:T(8,128)} custom-call(f32[2,192,256]{2,1,0:T(8,128)} %x_hbm.1), custom_call_target="tpu_custom_call" | custom-call | tf_op jit(solution)/shard_map/pieces/pallas_call | solution.py:257
  1.9 7.4 %all-to-all-start = ((f32[16,2,24,128]{3,2,1,0:T(8,128)}), f32[16,2,24,128]{3,2,1,0:T(8,128)S(1)}, u32[]{:S(2)}, u32[]{:S(2)}) async-start(f32[16,2,24,128]{3,2,1,0:T(8,128)} %pieces.1), calls=%async_computation | async-start | bytes 786432 | tf_op jit(solution)/shard_map/all_to_all | solution.py:254
  9.3 0.0 copy-start.1
  9.3 0.9 %copy-done.1 = s32[192,1]{1,0:T(8,128)S(1)} copy-done((s32[192,1]{1,0:T(8,128)S(1)}, s32[192,1]{1,0:T(8,128)}, u32[]{:S(2)}) %copy-start.1) | copy-done | bytes 792
  10.2 0.0 copy-start.3
  10.2 0.7 %copy-done.3 = s32[192]{0:T(256)S(1)} copy-done((s32[192]{0:T(256)S(1)}, s32[192]{0:T(256)}, u32[]{:S(2)}) %copy-start.3) | copy-done | bytes 792
  10.9 0.0 copy-start.2
  10.9 5.4 %weights.1 = (bf16[2,384,384]{2,1,0:T(8,128)(2,1)S(1)}, bf16[6,384,384]{2,1,0:T(8,128)(2,1)}, bf16[768,256]{1,0:T(8,128)(2,1)S(1)}) custom-call(f32[8,2,192,192]{3,2,1,0:T(8,128)} %bitcast.12, s32[1,192]{1,0:T(1,128)S(1)} %bitcast.11, s32[192,1]{1,0:T(8,128)S(1)} %copy-done.1, bf16[768,256]{1,0:T(8,128)(2,1)} %constant.20.clone.table_ref), custom_call_target="tpu_custom_call" | custom-call | flops 905969664 | bytes 5242880 | tf_op jit(solution)/shard_map/weights/pallas_call | solution.py:277
  16.3 0.0 copy-done
  16.4 5.1 %all-to-all-done = f32[16,2,24,128]{3,2,1,0:T(8,128)S(1)} async-done(((f32[16,2,24,128]{3,2,1,0:T(8,128)}), f32[16,2,24,128]{3,2,1,0:T(8,128)S(1)}, u32[]{:S(2)}, u32[]{:S(2)}) %all-to-all-start) | async-done | bytes 393248 | tf_op jit(solution)/shard_map/all_to_all | solution.py:254
  21.5 0.0 copy-done.2
  21.5 1.5 %channels.1 = (f32[16,48,128]{2,1,0:T(8,128)S(1)}, bf16[6,384,384]{2,1,0:T(8,128)(2,1)S(1)}) custom-call(f32[32,24,128]{2,1,0:T(8,128)S(1)} %bitcast.9, f32[16,128]{1,0:T(8,128)S(1)} %copy-done.2, bf16[768,256]{1,0:T(8,128)(2,1)S(1)} %get-tuple-element.18.table_ref, f32[8,2,24,128]{3,2,1,0:T(8,128)S(1)} %copy_bitcast_fusion.taps_ref, ...), custom_call_target="tpu_custom_call" | custom-call | tf_op jit(solution)/shard_map/channels/pallas_call | solution.py:306
  23.0 15.5 %all_to_all.10 = f32[16,48,128]{2,1,0:T(8,128)S(1)} all-to-all(f32[16,48,128]{2,1,0:T(8,128)S(1)} %get-tuple-element.20), channel_id=1, replica_groups=mesh['grp'=2,'band'=16] {'band'}, dimensions={0} | all-to-all | bytes 786432 | tf_op jit(solution)/shard_map/all_to_all | solution.py:254
  38.5 1.9 %beams.1 = f32[8,8,192]{2,1,0:T(8,128)} custom-call(f32[768,128]{1,0:T(8,128)S(1)} %bitcast.10, bf16[2,384,384]{2,1,0:T(8,128)(2,1)S(1)} %get-tuple-element.21.early_ref, bf16[6,384,384]{2,1,0:T(8,128)(2,1)S(1)} %get-tuple-element.22.late_ref), custom_call_target="tpu_custom_call" | custom-call | tf_op jit(solution)/shard_map/beams/pallas_call | solution.py:332
  (3 shorter events, 0.1 us)
Async XLA Ops:
  0.0 16.3 %copy-start = (f32[2,8,192,128]{3,2,1,0:T(8,128)S(1)}, f32[2,8,192,128]{3,2,1,0:T(8,128)}, u32[]{:S(2)}) copy-start(f32[2,8,192,128]{3,2,1,0:T(8,128)} %param.9) | copy-start | bytes 4718596
  1.9 19.6 %all-to-all-start = ((f32[16,2,24,128]{3,2,1,0:T(8,128)}), f32[16,2,24,128]{3,2,1,0:T(8,128)S(1)}, u32[]{:S(2)}, u32[]{:S(2)}) async-start(f32[16,2,24,128]{3,2,1,0:T(8,128)} %pieces.1), calls=%async_computation | async-start | bytes 786432 | tf_op jit(solution)/shard_map/all_to_all | solution.py:254
  9.3 0.9 %copy-start.1 = (s32[192,1]{1,0:T(8,128)S(1)}, s32[192,1]{1,0:T(8,128)}, u32[]{:S(2)}) copy-start(s32[192,1]{1,0:T(8,128)} %constant.21.clone.slot_ref) | copy-start | bytes 2308
  10.2 0.7 %copy-start.3 = (s32[192]{0:T(256)S(1)}, s32[192]{0:T(256)}, u32[]{:S(2)}) copy-start(s32[192]{0:T(256)} %param.11) | copy-start | bytes 2308
  10.9 10.6 %copy-start.2 = (f32[16,128]{1,0:T(8,128)S(1)}, f32[16,128]{1,0:T(8,128)}, u32[]{:S(2)}) copy-start(f32[16,128]{1,0:T(8,128)} %proto_ref.1) | copy-start | bytes 24580

commit v22 on v15

--- a/solution.py
+++ b/solution.py
@@ -102,7 +102,7 @@
 def channel_kernel(
     x_ref, proto_ref, table_ref, taps_ref, late_ref, out_ref, late_out_ref, *scratch
 ):
-    past, poly, spec, filt, late_sem = scratch
+    poly, spec, filt, late_sem = scratch
     late_copy = pltpu.make_async_copy(late_ref, late_out_ref, late_sem)
     late_copy.start()
     pfb_count = proto_ref.shape[0]
@@ -111,18 +111,20 @@
     group = 8
     low = lax.broadcasted_iota(jnp.int32, (group, 8, LANES), 1) < 4
 
-    past[0 : pfb_count - 1] = jnp.zeros((pfb_count - 1, 24, LANES), F32)
-    past[pfb_count - 1 :] = x_ref[...]
-
     spec[0 : fir_count - 1] = jnp.zeros((fir_count - 1, 24, 2 * LANES), F32)
     for first in range(0, frames, group):
         found = []
         for rows in range(0, 24, 8):
             total = None
             for tap in range(pfb_count):
-                begin = first + pfb_count - 1 - tap
-                block = past[begin : begin + group, rows : rows + 8, :]
+                begin = first - tap
+                lost = max(0, -begin)
+                if lost >= group:
+                    continue
+                block = x_ref[begin + lost : begin + group, rows : rows + 8, :]
                 term = block * proto_ref[tap : tap + 1, :][None]
+                if lost:
+                    term = jnp.concatenate([jnp.zeros((lost, 8, LANES), F32), term], axis=0)
                 total = term if total is None else total + term
             found.append(total)
         turned = pltpu.roll(found[2], 4, 1)
@@ -300,7 +302,6 @@
         in_specs=[VMEM] * 4 + [HBM],
         out_specs=[VMEM] * 2,
         scratch_shapes=[
-            pltpu.VMEM((frames + prototype.shape[0] - 1, 24, LANES), F32),
             pltpu.VMEM((frames, 24, 2 * LANES), F32),
             pltpu.VMEM((frames + fir_count - 1, 24, 2 * LANES), F32),
             pltpu.VMEM((frames * 24, LANES), F32),

time: 40.8 us -> 40.8 us (level)
  no operation moved by 1% of the time
where the time goes in v22:
time: 40.8 us; the launch traced here: 40.4 us
  blocking collectives  15.5 us (38%)
  Pallas kernels  9.52 us (23%)
  starting transfers between devices  7.39 us (18%)
  waiting for transfers between devices  5.15 us (13%)
  local copies, waits for them, and re-layouts  2.73 us (7%)
    all_to_all x1, blocking collectives, exchange(): lax.all_to_all(value, 'band', split_axis=0, concat_axis=0, tiled=True)  15.5 us
    all_to_all x1, starting transfers between devices, exchange(): lax.all_to_all(value, 'band', split_axis=0, concat_axis=0, tiled=True)  7.39 us
    pallas_call x1, Pallas kernels, close_body(): pl.pallas_call(weights_kernel, out_shape=[jax.ShapeDtypeStruct((EARLY, 2...  5.36 us
    all_to_all x1, waiting for transfers between devices, exchange(): lax.all_to_all(value, 'band', split_axis=0, concat_axis=0, tiled=True)  5.15 us
    unnamed x10, local copies, waits for them, and re-layouts  2.69 us
    pallas_call x1, Pallas kernels, close_body(): pl.pallas_call(beams_kernel, out_shape=jax.ShapeDtypeStruct((band_chans,...  1.88 us
    pallas_call x1, Pallas kernels, close_body(): pl.pallas_call(channel_kernel, out_shape=[jax.ShapeDtypeStruct((devices,)...  1.49 us
  transfers between devices with their start and end apart: 1, of which 1 were waited for; matrix products, arithmetic and copies ran while one was open for 0% of the time, Pallas kernels for 13%

profile of v22, /device:TPU:0, one launch (start us, length us, event | category | flops | bytes accessed | tf_op | source)
XLA Modules:
  0.0 40.4 jit_solution(6246529015953237845)
XLA Ops:
  0.0 0.0 copy-start
  0.0 0.0 copy-start.1
  0.0 1.1 %copy-done.1 = f32[2,192,256]{2,1,0:T(8,128)S(1)} copy-done((f32[2,192,256]{2,1,0:T(8,128)S(1)}, f32[2,192,256]{2,1,0:T(8,128)}, u32[]{:S(2)}) %copy-start.1) | copy-done | bytes 393240
  1.1 0.8 %pieces.1 = f32[16,2,24,128]{3,2,1,0:T(8,128)} custom-call(f32[2,192,256]{2,1,0:T(8,128)S(1)} %copy-done.1), custom_call_target="tpu_custom_call" | custom-call | tf_op jit(solution)/shard_map/pieces/pallas_call | solution.py:252
  1.9 7.4 %all-to-all-start = ((f32[16,2,24,128]{3,2,1,0:T(8,128)}), f32[16,2,24,128]{3,2,1,0:T(8,128)S(1)}, u32[]{:S(2)}, u32[]{:S(2)}) async-start(f32[16,2,24,128]{3,2,1,0:T(8,128)} %pieces.1), calls=%async_computation | async-start | bytes 786432 | tf_op jit(solution)/shard_map/all_to_all | solution.py:250
  9.3 0.0 copy-start.2
  9.3 0.9 %copy-done.2 = s32[192,1]{1,0:T(8,128)S(1)} copy-done((s32[192,1]{1,0:T(8,128)S(1)}, s32[192,1]{1,0:T(8,128)}, u32[]{:S(2)}) %copy-start.2) | copy-done | bytes 792
  10.2 0.0 copy-start.4
  10.2 0.7 %copy-done.4 = s32[192]{0:T(256)S(1)} copy-done((s32[192]{0:T(256)S(1)}, s32[192]{0:T(256)}, u32[]{:S(2)}) %copy-start.4) | copy-done | bytes 792
  10.9 0.0 copy-start.3
  10.9 5.4 %weights.1 = (bf16[2,384,384]{2,1,0:T(8,128)(2,1)S(1)}, bf16[6,384,384]{2,1,0:T(8,128)(2,1)}, bf16[768,256]{1,0:T(8,128)(2,1)S(1)}) custom-call(f32[8,2,192,192]{3,2,1,0:T(8,128)} %bitcast.12, s32[1,192]{1,0:T(1,128)S(1)} %bitcast.11, s32[192,1]{1,0:T(8,128)S(1)} %copy-done.2, bf16[768,256]{1,0:T(8,128)(2,1)} %constant.20.clone.table_ref), custom_call_target="tpu_custom_call" | custom-call | flops 905969664 | bytes 5242880 | tf_op jit(solution)/shard_map/weights/pallas_call | solution.py:267
  16.3 0.0 copy-done
  16.4 5.2 %all-to-all-done = f32[16,2,24,128]{3,2,1,0:T(8,128)S(1)} async-done(((f32[16,2,24,128]{3,2,1,0:T(8,128)}), f32[16,2,24,128]{3,2,1,0:T(8,128)S(1)}, u32[]{:S(2)}, u32[]{:S(2)}) %all-to-all-start) | async-done | bytes 393248 | tf_op jit(solution)/shard_map/all_to_all | solution.py:250
  21.5 0.0 copy-done.3
  21.5 1.5 %channels.1 = (f32[16,48,128]{2,1,0:T(8,128)S(1)}, bf16[6,384,384]{2,1,0:T(8,128)(2,1)S(1)}) custom-call(f32[32,24,128]{2,1,0:T(8,128)S(1)} %bitcast.9, f32[16,128]{1,0:T(8,128)S(1)} %copy-done.3, bf16[768,256]{1,0:T(8,128)(2,1)S(1)} %get-tuple-element.18.table_ref, f32[8,2,24,128]{3,2,1,0:T(8,128)S(1)} %copy_bitcast_fusion.taps_ref, ...), custom_call_target="tpu_custom_call" | custom-call | tf_op jit(solution)/shard_map/channels/pallas_call | solution.py:296
  23.0 15.5 %all_to_all.10 = f32[16,48,128]{2,1,0:T(8,128)S(1)} all-to-all(f32[16,48,128]{2,1,0:T(8,128)S(1)} %get-tuple-element.20), channel_id=1, replica_groups=mesh['grp'=2,'band'=16] {'band'}, dimensions={0} | all-to-all | bytes 786432 | tf_op jit(solution)/shard_map/all_to_all | solution.py:250
  38.5 1.9 %beams.1 = f32[8,8,192]{2,1,0:T(8,128)} custom-call(f32[768,128]{1,0:T(8,128)S(1)} %bitcast.10, bf16[2,384,384]{2,1,0:T(8,128)(2,1)S(1)} %get-tuple-element.21.early_ref, bf16[6,384,384]{2,1,0:T(8,128)(2,1)S(1)} %get-tuple-element.22.late_ref), custom_call_target="tpu_custom_call" | custom-call | tf_op jit(solution)/shard_map/beams/pallas_call | solution.py:321
  (3 shorter events, 0.1 us)
Async XLA Ops:
  0.0 16.3 %copy-start = (f32[2,8,192,128]{3,2,1,0:T(8,128)S(1)}, f32[2,8,192,128]{3,2,1,0:T(8,128)}, u32[]{:S(2)}) copy-start(f32[2,8,192,128]{3,2,1,0:T(8,128)} %param.9) | copy-start | bytes 4718596
  0.0 1.1 %copy-start.1 = (f32[2,192,256]{2,1,0:T(8,128)S(1)}, f32[2,192,256]{2,1,0:T(8,128)}, u32[]{:S(2)}) copy-start(f32[2,192,256]{2,1,0:T(8,128)} %x_ref.1) | copy-start | bytes 1179652
  1.9 19.6 %all-to-all-start = ((f32[16,2,24,128]{3,2,1,0:T(8,128)}), f32[16,2,24,128]{3,2,1,0:T(8,128)S(1)}, u32[]{:S(2)}, u32[]{:S(2)}) async-start(f32[16,2,24,128]{3,2,1,0:T(8,128)} %pieces.1), calls=%async_computation | async-start | bytes 786432 | tf_op jit(solution)/shard_map/all_to_all | solution.py:250
  9.3 0.9 %copy-start.2 = (s32[192,1]{1,0:T(8,128)S(1)}, s32[192,1]{1,0:T(8,128)}, u32[]{:S(2)}) copy-start(s32[192,1]{1,0:T(8,128)} %constant.21.clone.slot_ref) | copy-start | bytes 2308
  10.2 0.7 %copy-start.4 = (s32[192]{0:T(256)S(1)}, s32[192]{0:T(256)}, u32[]{:S(2)}) copy-start(s32[192]{0:T(256)} %param.11) | copy-start | bytes 2308
  10.9 10.6 %copy-start.3 = (f32[16,128]{1,0:T(8,128)S(1)}, f32[16,128]{1,0:T(8,128)}, u32[]{:S(2)}) copy-start(f32[16,128]{1,0:T(8,128)} %proto_ref.1) | copy-start | bytes 24580
